TPU v7x, 32 devices: a whole 2x2x4 slice. The times are simulated.
32 devices in a mesh: dp: 4 (over x, core), seq: 8 (over z, y).
Axes of the slice: x: 2, y: 2, z: 4, core: 2. Of those that a mesh axis runs over, the one named last changes fastest.
Arguments:
- tokens: bfloat16 [8, 2048, 768], P('dp', 'seq'), may hold values from -6 to 6
- cotangent: bfloat16 [8, 2048, 768], P('dp', 'seq'), may hold values from -6 to 6
- lengths: int32 [8], P('dp'), may hold values from 1024 to 2048, as said below
- w_mx: bfloat16 [768, 3200], P(('dp', 'seq')), may hold values from -0.21875 to 0.21875
- w_value: bfloat16 [768, 1536], P(('dp', 'seq')), may hold values from -0.21875 to 0.21875
- w_out: bfloat16 [1536, 768], P(('dp', 'seq')), may hold values from -0.4375 to 0.4375
- w_up: bfloat16 [768, 1536], P(('dp', 'seq')), may hold values from -0.21875 to 0.21875
- w_down: bfloat16 [1536, 768], P(('dp', 'seq')), may hold values from -0.15625 to 0.15625
- ema_rate: bfloat16 [768, 16], P(('dp', 'seq'))
- ema_in: bfloat16 [768, 16], P(('dp', 'seq')), may hold values from -4 to 4
- ema_out: bfloat16 [768, 16], P(('dp', 'seq')), may hold values from -1.5 to 1.5
- gains: bfloat16 [768, 3], P(('dp', 'seq')), may hold values from 0.5 to 1.5
- qk_affine: bfloat16 [3, 128], replicated, may hold values from -6 to 6
Outputs:
- result: bfloat16 [8, 2048, 768], P('dp', 'seq')
- grad_tokens: float32 [8, 2048, 768], P('dp', 'seq')
- grad_w_mx: float32 [768, 3200], P(('dp', 'seq'))
- grad_w_value: float32 [768, 1536], P(('dp', 'seq'))
- grad_w_out: float32 [1536, 768], P(('dp', 'seq'))
- grad_w_up: float32 [768, 1536], P(('dp', 'seq'))
- grad_w_down: float32 [1536, 768], P(('dp', 'seq'))
- grad_ema_rate: float32 [768, 16], P(('dp', 'seq'))
- grad_ema_in: float32 [768, 16], P(('dp', 'seq'))
- grad_ema_out: float32 [768, 16], P(('dp', 'seq'))
- grad_gains: float32 [768, 3], P(('dp', 'seq'))
- grad_qk_affine: float32 [3, 128], replicated
- rms_values: float32 [3], replicated
Inputs may be any that keep to these rules, and one draw needn't show every extreme that they name: `lengths`: in each aligned pair of rows 2i, 2i + 1 one row, which one is drawn, has length 2048.
All inputs are finite; a program needn't handle non-finite values.
Results may differ from a plain program's by a relative error of at most 0.0169.
The roundings to bfloat16 on the way count: a program that leaves them out, or rounds other values in their place, can miss the bound.
Values may be sent and summed in bfloat16 or wider, within the bound.
A program may use at most 320 MiB of HBM per device.

v0:
```python
import jax
import jax.numpy as jnp
from jax import lax
from jax.sharding import PartitionSpec as P

D = 768
Z = 128
V = 1536
SPAN = 128
SEQ_DEV = 256


EPSILON = 1e-06
TOP_PRECISION = lax.Precision.HIGHEST


def prefix(value, axis, join, neutral):
    count, mine = (lax.axis_size(axis), lax.axis_index(axis))
    pieces = jax.tree.map(lambda part: lax.all_gather(part, axis), value)
    so_far = jax.tree.map(
        lambda part, zero: jnp.full_like(part, 0) + jnp.asarray(zero, part.dtype), value, neutral
    )

    def lap(position, so_far):
        longer = join(so_far, jax.tree.map(lambda part: part[position], pieces))
        return jax.tree.map(lambda new, old: jnp.where(position < mine, new, old), longer, so_far)

    return lax.fori_loop(0, count - 1, lap, so_far)


def prefix_2(value, axis, combine, identity):
    length, here = (lax.axis_size(axis), lax.axis_index(axis))
    everything = jax.tree.map(
        lambda part, kind: lax.all_gather(part.astype(kind), axis),
        value,
        jax.tree.map(lambda a: jnp.bfloat16 if a.dtype == jnp.float32 else a.dtype, value),
    )
    start = jax.tree.map(
        lambda part, zero: jnp.broadcast_to(jnp.asarray(zero, part.dtype), part.shape),
        value,
        identity,
    )

    def lap(k, before):
        at = length - 1 - k
        reached = at > here
        new = combine(
            before, jax.tree.map(lambda part, own: part[at].astype(own.dtype), everything, value)
        )
        return jax.tree.map(lambda a, b: jnp.where(reached, a, b), new, before)

    return lax.fori_loop(0, length, lap, start)


def silu_slope(values):
    sigmoid = jax.nn.sigmoid(values)
    return sigmoid * (1.0 + values * (1.0 - sigmoid))


def chain_combine(earlier, later):
    return (earlier[0] * later[0], later[0] * earlier[1] + later[1])


def ema_local(rate, beta, eta, input_signal):
    rows_here, length, channels = input_signal.shape
    block_len = min(64, length)
    blocks_count = length // block_len
    lag_values = jnp.arange(block_len, dtype=jnp.float32)
    powers = jnp.exp(-lag_values[:, None, None] * rate[None])
    scale_in = jnp.sqrt(-jnp.expm1(-2.0 * rate)) * beta
    kernel = jnp.sum(powers * (eta * scale_in)[None], axis=2)
    step_ids = jnp.arange(block_len)
    lag_index = jnp.clip(step_ids[:, None] - step_ids[None, :], 0, block_len - 1)
    toeplitz = jnp.where(
        (step_ids[:, None] >= step_ids[None, :])[:, :, None], kernel[lag_index], 0.0
    )
    leading = jnp.exp(-(lag_values[:, None, None] + 1.0) * rate[None]) * eta[None]
    trailing = powers[::-1] * scale_in[None]
    block_decay = jnp.exp(-block_len * rate)
    blocks = jnp.swapaxes(input_signal.reshape(rows_here, blocks_count, block_len, channels), 0, 1)

    def advance(carried, segment):
        smooth = jnp.einsum("tsd,bsd->btd", toeplitz, segment, precision=TOP_PRECISION)
        smooth = smooth + jnp.einsum("tdh,bdh->btd", leading, carried, precision=TOP_PRECISION)
        carried = block_decay * carried + jnp.einsum(
            "sdh,bsd->bdh", trailing, segment, precision=TOP_PRECISION
        )
        return (carried, smooth)

    initial = jnp.zeros((rows_here, channels, rate.shape[1]), jnp.float32)
    final_state, smooth = lax.scan(advance, initial, blocks)
    return (jnp.swapaxes(smooth, 0, 1).reshape(rows_here, length, channels), final_state)


def ema_carry(rate, eta, incoming):
    block_len = min(64, SEQ_DEV)
    blocks_count = SEQ_DEV // block_len
    lag_values = jnp.arange(block_len, dtype=jnp.float32)
    leading = jnp.exp(-(lag_values[:, None, None] + 1.0) * rate[None]) * eta[None]
    block_decay = jnp.exp(-block_len * rate)

    def advance(carried, unused):
        return (
            block_decay * carried,
            jnp.einsum("tdh,bdh->btd", leading, carried, precision=TOP_PRECISION),
        )

    _, smooth = lax.scan(advance, incoming, None, length=blocks_count)
    return jnp.swapaxes(smooth, 0, 1).reshape(incoming.shape[0], SEQ_DEV, incoming.shape[1])


def per_device(
    tokens,
    cotangent,
    lengths,
    w_mx,
    w_value,
    w_out,
    w_up,
    w_down,
    ema_rate,
    ema_in,
    ema_out,
    gains,
    qk_affine,
):
    gathered = (
        lax.all_gather(w_mx, ("dp", "seq"), axis=0, tiled=True),
        lax.all_gather(w_value, ("dp", "seq"), axis=0, tiled=True),
        lax.all_gather(w_out, ("dp", "seq"), axis=0, tiled=True),
        lax.all_gather(w_up, ("dp", "seq"), axis=0, tiled=True),
        lax.all_gather(w_down, ("dp", "seq"), axis=0, tiled=True),
        lax.all_gather(ema_rate, ("dp", "seq"), axis=0, tiled=True),
        lax.all_gather(ema_in, ("dp", "seq"), axis=0, tiled=True),
        lax.all_gather(ema_out, ("dp", "seq"), axis=0, tiled=True),
        lax.all_gather(gains, ("dp", "seq"), axis=0, tiled=True),
    )
    mx_full, value_full, out_full, up_full, down_full, rate_low, beta_low, eta_low, gain_low = (
        gathered
    )
    rate = rate_low.astype(jnp.float32)
    beta = beta_low.astype(jnp.float32)
    eta = eta_low.astype(jnp.float32)
    gain_all = gain_low.astype(jnp.float32)
    gain_first = gain_all[:, 0]
    gain_second = gain_all[:, 1]
    omega_gain = gain_all[:, 2]
    affine = qk_affine.astype(jnp.float32)
    rows_here = tokens.shape[0]
    spans_dev = SEQ_DEV // SPAN
    score_scale = Z ** (-0.5)
    inputs = tokens.astype(jnp.float32)
    seq_pos = lax.axis_index("seq") * SEQ_DEV + jnp.arange(SEQ_DEV, dtype=jnp.int32)
    valid_rows = (seq_pos[None, :] < lengths[:, None]).astype(jnp.float32)[:, :, None]
    inverse1 = lax.rsqrt(jnp.mean(inputs * inputs, axis=-1, keepdims=True) + EPSILON)
    unit1 = inputs * inverse1
    normed = unit1 * gain_first
    normed_low = normed.astype(jnp.bfloat16)
    value_pre = jnp.einsum(
        "bsd,dv->bsv", normed_low, value_full, preferred_element_type=jnp.float32
    )
    value_low = jax.nn.silu(value_pre).astype(jnp.bfloat16)
    (smooth_local, end_local), pull_local = jax.vjp(ema_local, rate, beta, eta, normed)
    growth = jnp.exp(-SEQ_DEV * rate)
    start_state = prefix(
        (growth, end_local),
        "seq",
        chain_combine,
        (jnp.ones_like(growth), jnp.zeros_like(end_local)),
    )[1]
    smooth_carry, pull_carry = jax.vjp(ema_carry, rate, eta, start_state)
    blend = smooth_local + smooth_carry + omega_gain * normed
    shifted_low = jax.nn.silu(blend).astype(jnp.bfloat16)
    mixed = jnp.einsum("bsd,dk->bsk", shifted_low, mx_full, preferred_element_type=jnp.float32)
    update = jax.nn.sigmoid(mixed[..., :D])
    shared_pre = mixed[..., D : D + Z]
    shared = jax.nn.silu(shared_pre)
    reset_pre = mixed[..., D + Z : D + Z + V]
    reset = jax.nn.silu(reset_pre)
    direct = mixed[..., D + Z + V :]
    query_low = (
        (shared * affine[0] + affine[1]).astype(jnp.bfloat16).reshape(rows_here, spans_dev, SPAN, Z)
    )
    key_low = (shared * affine[2]).astype(jnp.bfloat16).reshape(rows_here, spans_dev, SPAN, Z)
    value_tiles = value_low.reshape(rows_here, spans_dev, SPAN, V)
    scores = (
        jnp.einsum("bnqz,bnkz->bnqk", query_low, key_low, preferred_element_type=jnp.float32)
        * score_scale
    )
    causal = jnp.arange(SPAN)[:, None] >= jnp.arange(SPAN)[None, :]
    masked = jnp.where(causal, scores, -1e30)
    peak = jnp.max(masked, axis=-1, keepdims=True)
    expo = jnp.exp(masked - peak)
    attention_weights = expo / jnp.sum(expo, axis=-1, keepdims=True)
    probs_low = attention_weights.astype(jnp.bfloat16)
    attended_output = jnp.einsum(
        "bnqk,bnkv->bnqv", probs_low, value_tiles, preferred_element_type=jnp.float32
    ).reshape(rows_here, SEQ_DEV, V)
    gated_low = (reset * attended_output).astype(jnp.bfloat16)
    cand_pre = direct + jnp.einsum(
        "bsv,vd->bsd", gated_low, out_full, preferred_element_type=jnp.float32
    )
    candidate = jax.nn.silu(cand_pre)
    attn_branch = update * (candidate - inputs)
    middle = inputs + attn_branch
    inverse2 = lax.rsqrt(jnp.mean(middle * middle, axis=-1, keepdims=True) + EPSILON)
    unit2 = middle * inverse2
    normed2_low = (unit2 * gain_second).astype(jnp.bfloat16)
    up_pre = jnp.einsum("bsd,df->bsf", normed2_low, up_full, preferred_element_type=jnp.float32)
    hidden_low = jax.nn.silu(up_pre).astype(jnp.bfloat16)
    ffn_branch = jnp.einsum(
        "bsf,fd->bsd", hidden_low, down_full, preferred_element_type=jnp.float32
    )
    output = middle + ffn_branch
    again = (
        lax.all_gather(w_mx, ("dp", "seq"), axis=0, tiled=True),
        lax.all_gather(w_value, ("dp", "seq"), axis=0, tiled=True),
        lax.all_gather(w_out, ("dp", "seq"), axis=0, tiled=True),
        lax.all_gather(w_up, ("dp", "seq"), axis=0, tiled=True),
        lax.all_gather(w_down, ("dp", "seq"), axis=0, tiled=True),
    )
    mixer_backward, value_back, out_back, up_back, down_back = again
    grad_out = cotangent.astype(jnp.float32) * valid_rows
    grad_out_low = grad_out.astype(jnp.bfloat16)
    grad_down = jnp.einsum(
        "bsf,bsd->fd", hidden_low, grad_out_low, preferred_element_type=jnp.float32
    )
    grad_hidden = jnp.einsum(
        "bsd,fd->bsf", grad_out_low, down_back, preferred_element_type=jnp.float32
    )
    grad_up_low = (grad_hidden * silu_slope(up_pre)).astype(jnp.bfloat16)
    grad_up = jnp.einsum(
        "bsd,bsf->df", normed2_low, grad_up_low, preferred_element_type=jnp.float32
    )
    grad_normed2 = jnp.einsum(
        "bsf,df->bsd", grad_up_low, up_back, preferred_element_type=jnp.float32
    )
    grad_gain_second = jnp.sum(grad_normed2 * unit2, axis=(0, 1))
    scaled2 = grad_normed2 * gain_second
    grad_middle = grad_out + inverse2 * (
        scaled2 - unit2 * jnp.mean(scaled2 * unit2, axis=-1, keepdims=True)
    )
    grad_update = grad_middle * (candidate - inputs)
    grad_cand_pre = grad_middle * update * silu_slope(cand_pre)
    grad_cand_low = grad_cand_pre.astype(jnp.bfloat16)
    grad_out_proj = jnp.einsum(
        "bsv,bsd->vd", gated_low, grad_cand_low, preferred_element_type=jnp.float32
    )
    grad_gated = jnp.einsum(
        "bsd,vd->bsv", grad_cand_low, out_back, preferred_element_type=jnp.float32
    )
    grad_reset = grad_gated * attended_output
    grad_attended_low = (
        (grad_gated * reset).astype(jnp.bfloat16).reshape(rows_here, spans_dev, SPAN, V)
    )
    grad_probs = jnp.einsum(
        "bnqv,bnkv->bnqk", grad_attended_low, value_tiles, preferred_element_type=jnp.float32
    )
    grad_values = jnp.einsum(
        "bnqk,bnqv->bnkv", probs_low, grad_attended_low, preferred_element_type=jnp.float32
    ).reshape(rows_here, SEQ_DEV, V)
    grad_scores_low = (
        attention_weights
        * (grad_probs - jnp.sum(grad_probs * attention_weights, axis=-1, keepdims=True))
    ).astype(jnp.bfloat16)
    grad_query = (
        jnp.einsum("bnqk,bnkz->bnqz", grad_scores_low, key_low, preferred_element_type=jnp.float32)
        * score_scale
    ).reshape(rows_here, SEQ_DEV, Z)
    grad_key = (
        jnp.einsum(
            "bnqk,bnqz->bnkz", grad_scores_low, query_low, preferred_element_type=jnp.float32
        )
        * score_scale
    ).reshape(rows_here, SEQ_DEV, Z)
    grad_affine = jnp.stack(
        [
            jnp.sum(grad_query * shared, axis=(0, 1)),
            jnp.sum(grad_query, axis=(0, 1)),
            jnp.sum(grad_key * shared, axis=(0, 1)),
        ]
    )
    grad_shared = grad_query * affine[0] + grad_key * affine[2]
    grad_mixed_low = jnp.concatenate(
        [
            grad_update * update * (1.0 - update),
            grad_shared * silu_slope(shared_pre),
            grad_reset * silu_slope(reset_pre),
            grad_cand_pre,
        ],
        axis=-1,
    ).astype(jnp.bfloat16)
    grad_mx = jnp.einsum(
        "bsd,bsk->dk", shifted_low, grad_mixed_low, preferred_element_type=jnp.float32
    )
    grad_shifted = jnp.einsum(
        "bsk,dk->bsd", grad_mixed_low, mixer_backward, preferred_element_type=jnp.float32
    )
    grad_blend = grad_shifted * silu_slope(blend)
    grad_omega = jnp.sum(grad_blend * normed, axis=(0, 1))
    grad_value_low = (grad_values * silu_slope(value_pre)).astype(jnp.bfloat16)
    grad_value_proj = jnp.einsum(
        "bsd,bsv->dv", normed_low, grad_value_low, preferred_element_type=jnp.float32
    )
    grad_normed = grad_blend * omega_gain + jnp.einsum(
        "bsv,dv->bsd", grad_value_low, value_back, preferred_element_type=jnp.float32
    )
    rate_from_carry, eta_from_carry, direct_adjoint = pull_carry(grad_blend)
    later_adjoint = prefix_2(
        (growth, direct_adjoint),
        "seq",
        chain_combine,
        (jnp.ones_like(growth), jnp.zeros_like(direct_adjoint)),
    )[1]
    rate_from_local, grad_beta, eta_from_local, normed_from_ema = pull_local(
        (grad_blend, later_adjoint)
    )
    rate_from_growth = jnp.sum(later_adjoint * start_state, axis=0) * (-SEQ_DEV * growth)
    grad_rate = rate_from_carry + rate_from_local + rate_from_growth
    grad_eta = eta_from_carry + eta_from_local
    grad_normed = grad_normed + normed_from_ema
    grad_gain_first = jnp.sum(grad_normed * unit1, axis=(0, 1))
    scaled1 = grad_normed * gain_first
    grad_tokens = grad_middle * (1.0 - update) + inverse1 * (
        scaled1 - unit1 * jnp.mean(scaled1 * unit1, axis=-1, keepdims=True)
    )
    grad_gains = jnp.stack([grad_gain_first, grad_gain_second, grad_omega], axis=1)
    shards = (
        lax.psum_scatter(grad_mx, ("dp", "seq"), scatter_dimension=0, tiled=True),
        lax.psum_scatter(grad_value_proj, ("dp", "seq"), scatter_dimension=0, tiled=True),
        lax.psum_scatter(grad_out_proj, ("dp", "seq"), scatter_dimension=0, tiled=True),
        lax.psum_scatter(grad_up, ("dp", "seq"), scatter_dimension=0, tiled=True),
        lax.psum_scatter(grad_down, ("dp", "seq"), scatter_dimension=0, tiled=True),
        lax.psum_scatter(grad_rate, ("dp", "seq"), scatter_dimension=0, tiled=True),
        lax.psum_scatter(grad_beta, ("dp", "seq"), scatter_dimension=0, tiled=True),
        lax.psum_scatter(grad_eta, ("dp", "seq"), scatter_dimension=0, tiled=True),
        lax.psum_scatter(grad_gains, ("dp", "seq"), scatter_dimension=0, tiled=True),
    )
    squares = jnp.stack(
        [
            jnp.sum(valid_rows * output * output),
            jnp.sum(valid_rows * attn_branch * attn_branch),
            jnp.sum(valid_rows * ffn_branch * ffn_branch),
            jnp.sum(valid_rows),
        ]
    )
    affine_total, square_total = lax.psum((grad_affine, squares), ("dp", "seq"))
    rms_values = jnp.sqrt(square_total[:3] / (square_total[3] * D))
    return (
        output.astype(jnp.bfloat16),
        grad_tokens,
        shards[0],
        shards[1],
        shards[2],
        shards[3],
        shards[4],
        shards[5],
        shards[6],
        shards[7],
        shards[8],
        affine_total,
        rms_values,
    )


def solution(mesh):
    placed = (
        P("dp", "seq", None),
        P("dp", "seq", None),
        P("dp"),
        P(("dp", "seq"), None),
        P(("dp", "seq"), None),
        P(("dp", "seq"), None),
        P(("dp", "seq"), None),
        P(("dp", "seq"), None),
        P(("dp", "seq"), None),
        P(("dp", "seq"), None),
        P(("dp", "seq"), None),
        P(("dp", "seq"), None),
        P(),
    )
    return jax.shard_map(
        per_device,
        mesh=mesh,
        in_specs=placed,
        out_specs=(
            P("dp", "seq", None),
            P("dp", "seq", None),
            P(("dp", "seq"), None),
            P(("dp", "seq"), None),
            P(("dp", "seq"), None),
            P(("dp", "seq"), None),
            P(("dp", "seq"), None),
            P(("dp", "seq"), None),
            P(("dp", "seq"), None),
            P(("dp", "seq"), None),
            P(("dp", "seq"), None),
            P(),
            P(),
        ),
        check_vma=False,
    )
```

profile of v0, /device:TPU:0, one launch (start us, length us, event | category | flops | bytes accessed | tf_op | source)
XLA Modules:
  0.0 2444.7 jit_solution(5525015418152541947)
XLA Ops:
  16.8 70.0 %all-gather.5 = bf16[32,24,3]{1,2,0:T(4,128)(2,1)S(1)} all-gather(bf16[1,24,3]{1,2,0:T(4,128)(2,1)} %bitcast.405), channel_id=1, replica_groups=mesh['dp'=4,'seq'=8] {'dp','seq'}, dimensions={0}, use_global_device_ids=true | all-gather | bytes 4752 | tf_op jit(solution)/shard_map/all_gather | solution.py:136
  88.4 65.0 %all-gather.4 = bf16[32,24,16]{1,2,0:T(8,128)(2,1)S(1)} all-gather(bf16[1,24,16]{1,2,0:T(8,128)(2,1)} %bitcast.399), channel_id=1, replica_groups=mesh['dp'=4,'seq'=8] {'dp','seq'}, dimensions={0}, use_global_device_ids=true | all-gather | bytes 25344 | tf_op jit(solution)/shard_map/all_gather | solution.py:133
  153.6 66.7 %all-gather.6 = bf16[32,24,16]{1,2,0:T(8,128)(2,1)S(1)} all-gather(bf16[1,24,16]{1,2,0:T(8,128)(2,1)} %bitcast.400), channel_id=1, replica_groups=mesh['dp'=4,'seq'=8] {'dp','seq'}, dimensions={0}, use_global_device_ids=true | all-gather | bytes 25344 | tf_op jit(solution)/shard_map/all_gather | solution.py:134
  220.5 65.0 %all-gather.7 = bf16[32,24,16]{1,2,0:T(8,128)(2,1)S(1)} all-gather(bf16[1,24,16]{1,2,0:T(8,128)(2,1)} %bitcast.401), channel_id=1, replica_groups=mesh['dp'=4,'seq'=8] {'dp','seq'}, dimensions={0}, use_global_device_ids=true | all-gather | bytes 25344 | tf_op jit(solution)/shard_map/all_gather | solution.py:135
  288.6 31.0 %all-gather.2 = bf16[6144,16]{0,1:T(8,128)(2,1)S(1)} all-gather(bf16[768,16]{0,1:T(8,128)(2,1)S(1)} %get-tuple-element.1458), channel_id=4, replica_groups=mesh['dp'=4,'seq'=8] {'seq'}, dimensions={0}, use_global_device_ids=true | all-gather | bytes 221184 | tf_op jit(solution)/shard_map/all_gather | solution.py:34
  320.7 31.3 %all-gather = f32[6144,16]{0,1:T(8,128)S(1)} all-gather(f32[768,16]{0,1:T(8,128)S(1)} %get-tuple-element.1459), channel_id=2, replica_groups=mesh['dp'=4,'seq'=8] {'seq'}, dimensions={0}, use_global_device_ids=true | all-gather | bytes 442368 | tf_op jit(solution)/shard_map/all_gather | solution.py:19
  405.5 23.4 copy.278
  441.2 275.5 %while.105 = (s32[]{:T(128)}, f32[2,768,16]{2,0,1:T(2,128)S(1)}, f32[4,2,64,768]{2,1,3,0:T(2,128)}, f32[4,2,768,16]{3,1,2,0:T(2,128)}, f32[1,768,16]{2,1,0:T(8,1...) while((s32[]{:T(128)}, f32[2,768,16]{2,0,1:T(2,128)S(1)}, ...), condition=%wide.region_3.4_spmd.clone, body=%wide.region_2.3_spmd.clone.sunk | while | flops 115040256 | bytes 46055864 | solution.py:91
  441.4 42.3 %fusion.259 = f32[768,2,64]{2,1,0:T(2,128)S(1)} fusion(f32[64,64,768]{1,0,2:T(8,128)} %get-tuple-element.1847, f32[4,2,64,768]{2,1,3,0:T(2,128)} %get-tuple-element.1845, s32[]{:T(128)S(6)} %copy.359), kind=kOutput, calls=%fused_computation.30.clone.1 | convolution fusion | flops 75497472 | bytes 26345476 | tf_op jit(solution)/shard_map/jvp()/while/body/eval_jaxpr/tsd,bsd->btd/dot_general | solution.py:83
  507.2 42.3 %fusion.259 = f32[768,2,64]{2,1,0:T(2,128)S(1)} fusion(f32[64,64,768]{1,0,2:T(8,128)} %get-tuple-element.1847, f32[4,2,64,768]{2,1,3,0:T(2,128)} %get-tuple-element.1845, s32[]{:T(128)S(6)} %copy.359), kind=kOutput, calls=%fused_computation.30.clone.1 | convolution fusion | flops 75497472 | bytes 26345476 | tf_op jit(solution)/shard_map/jvp()/while/body/eval_jaxpr/tsd,bsd->btd/dot_general | solution.py:83
  573.0 42.3 %fusion.259 = f32[768,2,64]{2,1,0:T(2,128)S(1)} fusion(f32[64,64,768]{1,0,2:T(8,128)} %get-tuple-element.1847, f32[4,2,64,768]{2,1,3,0:T(2,128)} %get-tuple-element.1845, s32[]{:T(128)S(6)} %copy.359), kind=kOutput, calls=%fused_computation.30.clone.1 | convolution fusion | flops 75497472 | bytes 26345476 | tf_op jit(solution)/shard_map/jvp()/while/body/eval_jaxpr/tsd,bsd->btd/dot_general | solution.py:83
  638.8 42.3 %fusion.259 = f32[768,2,64]{2,1,0:T(2,128)S(1)} fusion(f32[64,64,768]{1,0,2:T(8,128)} %get-tuple-element.1847, f32[4,2,64,768]{2,1,3,0:T(2,128)} %get-tuple-element.1845, s32[]{:T(128)S(6)} %copy.359), kind=kOutput, calls=%fused_computation.30.clone.1 | convolution fusion | flops 75497472 | bytes 26345476 | tf_op jit(solution)/shard_map/jvp()/while/body/eval_jaxpr/tsd,bsd->btd/dot_general | solution.py:83
  717.1 32.4 %all-gather.1 = f32[16,768,16]{1,2,0:T(8,128)S(1)} all-gather(f32[2,768,16]{1,2,0:T(8,128)S(1)} %copy.281), channel_id=3, replica_groups=mesh['dp'=4,'seq'=8] {'seq'}, dimensions={0}, use_global_device_ids=true | all-gather | bytes 884736 | tf_op jit(solution)/shard_map/all_gather | solution.py:19
  762.6 45.8 %while.104 = (s32[]{:T(128)}, f32[2,768,16]{2,0,1:T(2,128)S(1)}, f32[4,2,64,768]{2,1,3,0:T(2,128)}, f32[4,2,768,16]{3,1,2,0:T(2,128)}, f32[1,768,16]{2,1,0:T(8,1...) while((s32[]{:T(128)}, f32[2,768,16]{2,0,1:T(2,128)S(1)}, ...), condition=%wide.region_7.8_spmd.clone, body=%wide.region_6.7_spmd.clone.sunk | while | flops 20471808 | bytes 2802029 | solution.py:108
  897.6 128.4 %while.107 = (s32[]{:T(128)}, f32[768,16]{1,0:T(8,128)S(1)}, f32[64,768,16]{0,2,1:T(8,128)}, f32[2,768,16]{2,0,1:T(2,128)S(1)}, f32[4,2,768,16]{3,1,2,0:T(2,128)...) while((s32[]{:T(128)}, f32[768,16]{1,0:T(8,128)S(1)}, ...), condition=%wide.region_15.16_spmd.clone, body=%wide.region_13.15_spmd.clone.sunk | while | flops 41054212 | bytes 41535472 | solution.py:108
  1026.2 31.0 %all-gather.3 = bf16[16,768,16]{1,2,0:T(8,128)(2,1)S(1)} all-gather(bf16[2,768,16]{1,2,0:T(8,128)(2,1)S(1)} %copy.298), channel_id=5, replica_groups=mesh['dp'=4,'seq'=8] {'seq'}, dimensions={0}, use_global_device_ids=true | all-gather | bytes 442368 | tf_op jit(solution)/shard_map/all_gather | solution.py:34
  1069.2 519.3 %while.109 = (s32[]{:T(128)}, f32[64,64,768]{1,0,2:T(8,128)}, f32[64,768,16]{0,2,1:T(8,128)}, f32[768,16]{1,0:T(8,128)}, f32[64,768,16]{0,2,1:T(8,128)}, /*index...) while((s32[]{:T(128)}, f32[64,64,768]{1,0,2:T(8,128)}, ...), condition=%wide.region_20.21_spmd.clone, body=%wide.region_18.20_spmd.clone.sunk | while | flops 237711360 | bytes 284446592 | solution.py:91
  1072.8 25.1 %fusion.283 = f32[768,2,64]{2,1,0:T(2,128)S(1)} fusion(f32[64,64,768]{1,0,2:T(8,128)} %get-tuple-element.2017, f32[4,2,64,768]{2,1,3,0:T(2,128)} %get-tuple-element.2012, s32[]{:T(128)S(6)} %sub.152), kind=kOutput, calls=%fused_computation.89.clone.1 | convolution fusion | flops 75497472 | bytes 26345476 | tf_op jit(solution)/shard_map/transpose(jvp())/while/body/eval_jaxpr/tsd,bsd->btd/dot_general | solution.py:83
  1145.2 42.3 %bitcast_add_fusion.12 = f32[64,64,768]{1,0,2:T(8,128)S(1)} fusion(f32[64,64,768]{1,0,2:T(8,128)S(1)} %bitcast.360, pred[]{:T(512)S(6)} %compare.19, f32[4,2,64,768]{2,1,3,0:T(2,128)} %get-tuple-element.2013, s32[]{:T(128)S(6)} %sub.152, f32[4,2,64,768]{2,1,3,0:T(2,128)} %get-tuple-element.2012), kind=kOutput, calls=%fused_computation.69.clone.1 | convolution fusion | flops 81788928 | bytes 26740224 | tf_op jit(solution)/shard_map/transpose(jvp())/while/body/eval_jaxpr/tsd,bsd->btd/dot_general | solution.py:83
  1200.9 25.3 %fusion.283 = f32[768,2,64]{2,1,0:T(2,128)S(1)} fusion(f32[64,64,768]{1,0,2:T(8,128)} %get-tuple-element.2017, f32[4,2,64,768]{2,1,3,0:T(2,128)} %get-tuple-element.2012, s32[]{:T(128)S(6)} %sub.152), kind=kOutput, calls=%fused_computation.89.clone.1 | convolution fusion | flops 75497472 | bytes 26345476 | tf_op jit(solution)/shard_map/transpose(jvp())/while/body/eval_jaxpr/tsd,bsd->btd/dot_general | solution.py:83
  1273.2 42.6 %bitcast_add_fusion.12 = f32[64,64,768]{1,0,2:T(8,128)S(1)} fusion(f32[64,64,768]{1,0,2:T(8,128)S(1)} %bitcast.360, pred[]{:T(512)S(6)} %compare.19, f32[4,2,64,768]{2,1,3,0:T(2,128)} %get-tuple-element.2013, s32[]{:T(128)S(6)} %sub.152, f32[4,2,64,768]{2,1,3,0:T(2,128)} %get-tuple-element.2012), kind=kOutput, calls=%fused_computation.69.clone.1 | convolution fusion | flops 81788928 | bytes 26740224 | tf_op jit(solution)/shard_map/transpose(jvp())/while/body/eval_jaxpr/tsd,bsd->btd/dot_general | solution.py:83
  1328.8 25.3 %fusion.283 = f32[768,2,64]{2,1,0:T(2,128)S(1)} fusion(f32[64,64,768]{1,0,2:T(8,128)} %get-tuple-element.2017, f32[4,2,64,768]{2,1,3,0:T(2,128)} %get-tuple-element.2012, s32[]{:T(128)S(6)} %sub.152), kind=kOutput, calls=%fused_computation.89.clone.1 | convolution fusion | flops 75497472 | bytes 26345476 | tf_op jit(solution)/shard_map/transpose(jvp())/while/body/eval_jaxpr/tsd,bsd->btd/dot_general | solution.py:83
  1401.4 42.3 %bitcast_add_fusion.12 = f32[64,64,768]{1,0,2:T(8,128)S(1)} fusion(f32[64,64,768]{1,0,2:T(8,128)S(1)} %bitcast.360, pred[]{:T(512)S(6)} %compare.19, f32[4,2,64,768]{2,1,3,0:T(2,128)} %get-tuple-element.2013, s32[]{:T(128)S(6)} %sub.152, f32[4,2,64,768]{2,1,3,0:T(2,128)} %get-tuple-element.2012), kind=kOutput, calls=%fused_computation.69.clone.1 | convolution fusion | flops 81788928 | bytes 26740224 | tf_op jit(solution)/shard_map/transpose(jvp())/while/body/eval_jaxpr/tsd,bsd->btd/dot_general | solution.py:83
  1457.0 25.3 %fusion.283 = f32[768,2,64]{2,1,0:T(2,128)S(1)} fusion(f32[64,64,768]{1,0,2:T(8,128)} %get-tuple-element.2017, f32[4,2,64,768]{2,1,3,0:T(2,128)} %get-tuple-element.2012, s32[]{:T(128)S(6)} %sub.152), kind=kOutput, calls=%fused_computation.89.clone.1 | convolution fusion | flops 75497472 | bytes 26345476 | tf_op jit(solution)/shard_map/transpose(jvp())/while/body/eval_jaxpr/tsd,bsd->btd/dot_general | solution.py:83
  1529.3 42.6 %bitcast_add_fusion.12 = f32[64,64,768]{1,0,2:T(8,128)S(1)} fusion(f32[64,64,768]{1,0,2:T(8,128)S(1)} %bitcast.360, pred[]{:T(512)S(6)} %compare.19, f32[4,2,64,768]{2,1,3,0:T(2,128)} %get-tuple-element.2013, s32[]{:T(128)S(6)} %sub.152, f32[4,2,64,768]{2,1,3,0:T(2,128)} %get-tuple-element.2012), kind=kOutput, calls=%fused_computation.69.clone.1 | convolution fusion | flops 81788928 | bytes 26740224 | tf_op jit(solution)/shard_map/transpose(jvp())/while/body/eval_jaxpr/tsd,bsd->btd/dot_general | solution.py:83
  1655.2 28.2 %scatter_custom_fusion = f32[64,768]{1,0:T(8,128)S(1)} fusion(s32[4096]{0:T(1024)} %copy-done.55, f32[4096,768]{1,0:T(8,128)} %bitcast.378, f32[]{:T(128)} %constant.219.clone.1), kind=kCustom, calls=%fused_computation.233 | custom fusion | flops 3145728 | bytes 197120 | tf_op jit(solution)/shard_map/transpose(jvp())/scatter-add | solution.py:75
  1755.9 84.7 %all-reduce.8.cloned.1.call-done = (f32[768,16]{0,1:T(8,128)}, f32[768,16]{0,1:T(8,128)}, f32[768,16]{0,1:T(8,128)}, f32[768,3]{0,1:T(4,128)}, f32[3,128]{1,0:T(4,128)}, /*index=5*/f32[4]{0:T(128)}) async-done(((f32[768,16]{0,1:T(8,128)}, f32[768,16]{0,1:T(8,128)}, f32[768,16]{0,1:T(8,128)}, f32[768,3]{0,1:T(4,128)}, f32[3,128]{1,0:T(4,128)}, /*index=5*/f32[4]{0:T(128)}), (f32[768,16]{0,1:T(8,128)}, ...) | async-done | bytes 158240
  1849.1 106.0 %reduce-scatter.16.cloned.1.call-done = f32[24,1536]{1,0:T(8,128)} async-done(((f32[768,1536]{1,0:T(8,128)}), f32[24,1536]{1,0:T(8,128)}) %reduce-scatter.16.cloned.1.call-update) | async-done | bytes 147472 | tf_op jit(solution)/shard_map/reduce_scatter | solution.py:332
  1955.1 113.0 %reduce-scatter.18.cloned.1.call-done = f32[48,768]{1,0:T(8,128)} async-done(((f32[1536,768]{1,0:T(8,128)}), f32[48,768]{1,0:T(8,128)}) %reduce-scatter.18.cloned.1.call-update) | async-done | bytes 147472 | tf_op jit(solution)/shard_map/reduce_scatter | solution.py:333
  2068.1 112.2 %reduce-scatter.14.cloned.1.call-done = f32[48,768]{1,0:T(8,128)} async-done(((f32[1536,768]{1,0:T(8,128)}), f32[48,768]{1,0:T(8,128)}) %reduce-scatter.14.cloned.1.call-update) | async-done | bytes 147472 | tf_op jit(solution)/shard_map/reduce_scatter | solution.py:331
  2180.3 112.9 %reduce-scatter.12.cloned.1.call-done = f32[24,1536]{1,0:T(8,128)} async-done(((f32[768,1536]{1,0:T(8,128)}), f32[24,1536]{1,0:T(8,128)}) %reduce-scatter.12.cloned.1.call-update) | async-done | bytes 147472 | tf_op jit(solution)/shard_map/reduce_scatter | solution.py:330
  2293.2 143.3 %reduce-scatter.20.cloned.1.call-done = f32[24,3200]{1,0:T(8,128)} async-done(((f32[768,3200]{1,0:T(8,128)}), f32[24,3200]{1,0:T(8,128)}) %reduce-scatter.20.cloned.1.call-update) | async-done | bytes 307216
  (586 shorter events, 863.2 us)
Async XLA Ops:
  7.2 813.0 %all-gather.16.cloned.1.call-start = ((), (), s32[]{:S(2)}) async-start(), calls=%async_computation.6 | async-start | bytes 2433024 | tf_op jit(solution)/shard_map/all_gather | solution.py:129
  7.9 818.0 %all-gather.14.cloned.1.call-start = ((), (), s32[]{:S(2)}) async-start(), calls=%async_computation.5 | async-start | bytes 5068800 | tf_op jit(solution)/shard_map/all_gather | solution.py:128
  8.7 835.2 %all-gather.18.cloned.1.call-start = ((), (), s32[]{:S(2)}) async-start(), calls=%async_computation.7 | async-start | bytes 2433024 | tf_op jit(solution)/shard_map/all_gather | solution.py:130
  9.4 840.6 %all-gather.20.cloned.1.call-start = ((), (), s32[]{:S(2)}) async-start(), calls=%async_computation.8 | async-start | bytes 2433024 | tf_op jit(solution)/shard_map/all_gather | solution.py:131
  10.0 845.3 %all-gather.22.cloned.1.call-start = ((), (), s32[]{:S(2)}) async-start(), calls=%async_computation.9 | async-start | bytes 2433024 | tf_op jit(solution)/shard_map/all_gather | solution.py:132
  10.6 1830.0 %all-reduce.8.cloned.1.call-start = ((), (), s32[]{:S(2)}) async-start(), calls=%async_computation.15 | async-start | bytes 324608
  13.3 346.3 %copy-start.68 = (f32[64]{0:T(128)}, f32[64]{0:T(128)S(1)}, u32[]{:S(2)}) copy-start(f32[64]{0:T(128)S(1)} %get-tuple-element.1477) | copy-start | bytes 772
  13.4 382.0 %copy-start.50 = (pred[64,64]{1,0:T(8,128)(4,1)}, pred[64,64]{1,0:T(8,128)(4,1)S(1)}, u32[]{:S(2)}) copy-start(pred[64,64]{1,0:T(8,128)(4,1)S(1)} %iota_compare_fusion.1) | copy-start | bytes 12292
  16.8 336.1 %copy-start.52 = (f32[2,256]{1,0:T(2,128)}, f32[2,256]{1,0:T(2,128)S(1)}, u32[]{:S(2)}) copy-start(f32[2,256]{1,0:T(2,128)S(1)} %add_rsqrt_fusion.1) | copy-start | bytes 6148
  87.7 265.2 %copy-start.43 = (f32[768]{0:T(1024)}, f32[768]{0:T(1024)S(1)}, u32[]{:S(2)}) copy-start(f32[768]{0:T(1024)S(1)} %get-tuple-element.1322) | copy-start | bytes 9220
  285.7 67.2 %copy-start.6 = (bf16[2,256,768]{2,1,0:T(8,128)(2,1)S(1)}, bf16[2,256,768]{2,1,0:T(8,128)(2,1)}, u32[]{:S(2)}) copy-start(bf16[2,256,768]{2,1,0:T(8,128)(2,1)} %param.25) | copy-start | bytes 2359300
  286.0 68.3 %copy-start.37 = (f32[768,16]{0,1:T(8,128)}, f32[768,16]{0,1:T(8,128)S(1)}, u32[]{:S(2)}) copy-start(f32[768,16]{0,1:T(8,128)S(1)} %reshape.287) | copy-start | bytes 147460
  286.3 67.9 %copy-start.41 = (f32[768,16]{0,1:T(8,128)}, f32[768,16]{0,1:T(8,128)S(1)}, u32[]{:S(2)}) copy-start(f32[768,16]{0,1:T(8,128)S(1)} %reshape.286) | copy-start | bytes 147460
  286.6 67.6 %copy-start.38 = (f32[768,16]{0,1:T(8,128)}, f32[768,16]{0,1:T(8,128)S(1)}, u32[]{:S(2)}) copy-start(f32[768,16]{0,1:T(8,128)S(1)} %reshape.284) | copy-start | bytes 147460
  288.6 71.1 %copy-start.42 = (f32[768,16]{0,1:T(8,128)}, f32[768,16]{0,1:T(8,128)S(1)}, u32[]{:S(2)}) copy-start(f32[768,16]{0,1:T(8,128)S(1)} %get-tuple-element.1461) | copy-start | bytes 147460
  320.7 108.2 %copy-start.22 = (f32[768,16]{1,0:T(8,128)}, f32[768,16]{1,0:T(8,128)S(1)}, u32[]{:S(2)}) copy-start(f32[768,16]{1,0:T(8,128)S(1)} %copy.272) | copy-start | bytes 147460
  441.2 308.2 %copy-start.21 = (f32[2,768,16]{1,2,0:T(8,128)S(1)}, f32[2,768,16]{1,2,0:T(8,128)}, u32[]{:S(2)}) copy-start(f32[2,768,16]{1,2,0:T(8,128)} %custom-call.1) | copy-start | bytes 294916
  897.6 159.6 %copy-start.20 = (f32[2,768,16]{1,2,0:T(8,128)S(1)}, f32[2,768,16]{1,2,0:T(8,128)}, u32[]{:S(2)}) copy-start(f32[2,768,16]{1,2,0:T(8,128)} %custom-call.5) | copy-start | bytes 294916
  1097.9 47.2 %slice-start = ((s8[25165824]{0:T(1024)(128)(4,1)}), s8[4194304]{0:T(1024)(128)(4,1)S(1)}, s32[]{:S(2)}) async-start(s8[25165824]{0:T(1024)(128)(4,1)} %bitcast.359), calls=%async_computation.16 | async-start | bytes 8388608 | tf_op jit(solution)/shard_map/transpose(jvp())/while
  1097.9 47.2 %slice-start.1 = ((s8[25165824]{0:T(1024)(128)(4,1)}), s8[4194304]{0:T(1024)(128)(4,1)S(1)}, s32[]{:S(2)}) async-start(s8[25165824]{0:T(1024)(128)(4,1)} %bitcast.359), calls=%async_computation.17 | async-start | bytes 8388608 | tf_op jit(solution)/shard_map/transpose(jvp())/while
  1226.2 46.9 %slice-start = ((s8[25165824]{0:T(1024)(128)(4,1)}), s8[4194304]{0:T(1024)(128)(4,1)S(1)}, s32[]{:S(2)}) async-start(s8[25165824]{0:T(1024)(128)(4,1)} %bitcast.359), calls=%async_computation.16 | async-start | bytes 8388608 | tf_op jit(solution)/shard_map/transpose(jvp())/while
  1226.2 46.9 %slice-start.1 = ((s8[25165824]{0:T(1024)(128)(4,1)}), s8[4194304]{0:T(1024)(128)(4,1)S(1)}, s32[]{:S(2)}) async-start(s8[25165824]{0:T(1024)(128)(4,1)} %bitcast.359), calls=%async_computation.17 | async-start | bytes 8388608 | tf_op jit(solution)/shard_map/transpose(jvp())/while
  1273.2 42.6 %copy-start.3 = (f32[64,768,16]{0,2,1:T(8,128)}, f32[64,768,16]{0,2,1:T(8,128)S(1)}, u32[]{:S(2)}) copy-start(f32[64,768,16]{0,2,1:T(8,128)S(1)} %bitcast_add_fusion.13) | copy-start | bytes 9437188 | tf_op jit(solution)/shard_map/transpose(jvp())/while
  1354.1 47.2 %slice-start = ((s8[25165824]{0:T(1024)(128)(4,1)}), s8[4194304]{0:T(1024)(128)(4,1)S(1)}, s32[]{:S(2)}) async-start(s8[25165824]{0:T(1024)(128)(4,1)} %bitcast.359), calls=%async_computation.16 | async-start | bytes 8388608 | tf_op jit(solution)/shard_map/transpose(jvp())/while
  1354.1 47.2 %slice-start.1 = ((s8[25165824]{0:T(1024)(128)(4,1)}), s8[4194304]{0:T(1024)(128)(4,1)S(1)}, s32[]{:S(2)}) async-start(s8[25165824]{0:T(1024)(128)(4,1)} %bitcast.359), calls=%async_computation.17 | async-start | bytes 8388608 | tf_op jit(solution)/shard_map/transpose(jvp())/while
  1482.3 46.9 %slice-start = ((s8[25165824]{0:T(1024)(128)(4,1)}), s8[4194304]{0:T(1024)(128)(4,1)S(1)}, s32[]{:S(2)}) async-start(s8[25165824]{0:T(1024)(128)(4,1)} %bitcast.359), calls=%async_computation.16 | async-start | bytes 8388608 | tf_op jit(solution)/shard_map/transpose(jvp())/while
  1482.3 46.9 %slice-start.1 = ((s8[25165824]{0:T(1024)(128)(4,1)}), s8[4194304]{0:T(1024)(128)(4,1)S(1)}, s32[]{:S(2)}) async-start(s8[25165824]{0:T(1024)(128)(4,1)} %bitcast.359), calls=%async_computation.17 | async-start | bytes 8388608 | tf_op jit(solution)/shard_map/transpose(jvp())/while
  1718.6 236.5 %reduce-scatter.16.cloned.1.call-start = ((), (), s32[]{:S(2)}) async-start(), calls=%async_computation.12 | async-start | bytes 4866048 | tf_op jit(solution)/shard_map/reduce_scatter | solution.py:332
  1723.8 344.3 %reduce-scatter.18.cloned.1.call-start = ((), (), s32[]{:S(2)}) async-start(), calls=%async_computation.13 | async-start | bytes 4866048 | tf_op jit(solution)/shard_map/reduce_scatter | solution.py:333
  1730.6 449.7 %reduce-scatter.14.cloned.1.call-start = ((), (), s32[]{:S(2)}) async-start(), calls=%async_computation.11 | async-start | bytes 4866048 | tf_op jit(solution)/shard_map/reduce_scatter | solution.py:331
  1735.7 557.4 %reduce-scatter.12.cloned.1.call-start = ((), (), s32[]{:S(2)}) async-start(), calls=%async_computation.10 | async-start | bytes 4866048 | tf_op jit(solution)/shard_map/reduce_scatter | solution.py:330
  1740.8 695.7 %reduce-scatter.20.cloned.1.call-start = ((), (), s32[]{:S(2)}) async-start(), calls=%async_computation.14 | async-start | bytes 10137600
  (130 other events, 2039.3 us)
Sparse Core Ops, SparseCore 0:
  10.9 60.0 all-gather.15
  73.9 63.7 all-gather.13
  140.6 56.1 all-gather.17
  199.6 56.2 all-gather.19
  258.7 56.6 all-gather.21
  1718.7 121.8 all-reduce.7
  1846.6 108.3 reduce-scatter.15
  1962.0 106.0 reduce-scatter.17
  2074.2 106.0 reduce-scatter.13
  2187.1 106.0 reduce-scatter.11
  2299.7 136.7 reduce-scatter.19
where the time goes:
time: 2460 us; the launch traced here: 2440 us
  matrix products  951 us (39%)
  waiting for transfers between devices  675 us (27%)
  blocking collectives  392 us (16%)
  local copies, waits for them, and re-layouts  213 us (9%)
  other arithmetic  173 us (7%)
    dot_general x12, matrix products, advance(): jnp.einsum('tsd,bsd->btd', toeplitz, segment, precision=TOP_PRECISION)  440 us
    dot_general x24, matrix products, advance(): jnp.einsum('tdh,bdh->btd', leading, carried, precision=TOP_PRECISION)  299 us
    unnamed x13, waiting for transfers between devices  231 us
    dot_general x12, matrix products, advance(): jnp.einsum('sdh,bsd->bdh', trailing, segment, precision=TOP_PRECISION)  125 us
    reduce_scatter x1, waiting for transfers between devices, per_device(): lax.psum_scatter(grad_down, ('dp', 'seq'), scatter_dimension=0, tiled=True)  113 us
    reduce_scatter x1, waiting for transfers between devices, per_device(): lax.psum_scatter(grad_value_proj, ('dp', 'seq'), scatter_dimension=0, til...  113 us
    reduce_scatter x1, waiting for transfers between devices, per_device(): lax.psum_scatter(grad_out_proj, ('dp', 'seq'), scatter_dimension=0, tiled...  112 us
    reduce_scatter x1, waiting for transfers between devices, per_device(): lax.psum_scatter(grad_up, ('dp', 'seq'), scatter_dimension=0, tiled=True)  106 us
  transfers between devices with their start and end apart: 11, of which 6 were waited for; matrix products, arithmetic and copies ran while one was open for 21% of the time, Pallas kernels for 0%

commit v1 on v0

--- a/solution.py
+++ b/solution.py
@@ -1,8 +1,14 @@
+import functools
+
 import jax
 import jax.numpy as jnp
 from jax import lax
+from jax.experimental import pallas as pl
+from jax.experimental.pallas import tpu as pltpu
 from jax.sharding import PartitionSpec as P
 
+MESH = pl.DeviceIdType.MESH
+bf16, f32 = jnp.bfloat16, jnp.float32
 D = 768
 Z = 128
 V = 1536
@@ -363,6 +369,712 @@
     )
 
 
+HA, HB = 3200, 768
+RA, RB = 48, 96
+
+CHUNKS = [(0, 0, 640, "xy"), (0, 640, 640, "yx"), (0, 1280, 640, "xy"), (0, 1920, 640, "yx"), (0, 2560, 640, "xy"), (1, 0, 384, "yx"), (1, 384, 384, "xy")]
+
+class Pos:
+    def __init__(s):
+        s.dp, s.sq = lax.axis_index("dp"), lax.axis_index("seq")
+        s.x, s.c, s.z, s.y = s.dp // 2, s.dp % 2, s.sq // 2, s.sq % 2
+        s.sib = (s.dp + 1 - 2 * s.c, s.sq)
+        s.xn = (s.dp + 2 - 4 * s.x, s.sq)
+        s.yn = (s.dp, s.sq + 1 - 2 * s.y)
+        s.up = (s.dp, jnp.minimum(s.sq + 2, s.sq + 2 * (3 - s.z)))
+        s.dn = (s.dp, jnp.maximum(s.sq - 2, s.y))
+        s.dpx = s.dp + 2 - 4 * s.x
+
+def rcopy(src, dst, ss, rs, dev):
+    return pltpu.make_async_remote_copy(src_ref=src, dst_ref=dst, send_sem=ss, recv_sem=rs, device_id=dev, device_id_type=MESH)
+
+def barrier(pos):
+    bar = pltpu.get_barrier_semaphore()
+    sig = lambda d: pl.semaphore_signal(bar, inc=1, device_id=d, device_id_type=MESH)
+    sig(pos.sib); sig(pos.xn); sig(pos.yn)
+    @pl.when(pos.z < 3)
+    def _(): sig(pos.up)
+    @pl.when(pos.z > 0)
+    def _(): sig(pos.dn)
+    pl.semaphore_wait(bar, 3 + jnp.minimum(pos.z, 1) + jnp.minimum(3 - pos.z, 1))
+
+def at(ref, rows, nrows, half, w, off, width):
+    r = pl.ds(pl.multiple_of(rows, 48), nrows)
+    c = pl.ds(pl.multiple_of(half * w + off, 128), width)
+    return ref.at[r, c]
+
+class Gather:
+    def __init__(s, pos, bufs, ss, rs):
+        s.p, s.bufs, s.ss, s.rs = pos, bufs, ss, rs
+    def geom(s, i):
+        b, off, width, order = CHUNKS[i]
+        return s.bufs[b], (RA, RB)[b], (HA, HB)[b], off, width, order
+    def unit(s, i, dp, z, half, n=1):
+        ref, R, W, off, width, _ = s.geom(i)
+        return at(ref, (dp * 4 + z) * R, n * R, half, W, off, width)
+    def cp(s, i, k, ref, dev):
+        return rcopy(ref, ref, s.ss.at[i, k], s.rs.at[i, k], dev)
+    def z0(s, i):
+        p = s.p
+        u = s.unit(i, p.dp, p.z, p.y)
+        @pl.when(p.z < 3)
+        def _(): rcopy(u, u, s.ss.at[i, 0], s.rs.at[i, p.z], p.up).start()
+        @pl.when(p.z > 0)
+        def _(): rcopy(u, u, s.ss.at[i, 1], s.rs.at[i, p.z], p.dn).start()
+    def zrecv(s, i, zz):
+        u = s.unit(i, s.p.dp, zz, s.p.y)
+        rcopy(u, u, s.ss.at[i, 0], s.rs.at[i, zz], s.p.up).wait_recv()
+        return u
+    def zhop(s, i, h):
+        p = s.p
+        @pl.when(p.z >= h)
+        def _():
+            u = s.zrecv(i, p.z - h)
+            @pl.when(p.z < 3)
+            def _(): rcopy(u, u, s.ss.at[i, 1 + h], s.rs.at[i, p.z - h], p.up).start()
+        @pl.when(p.z + h <= 3)
+        def _():
+            u = s.zrecv(i, p.z + h)
+            @pl.when(p.z > 0)
+            def _(): rcopy(u, u, s.ss.at[i, 10 + h], s.rs.at[i, p.z + h], p.dn).start()
+    def s1(s, i):
+        p = s.p; order = CHUNKS[i][3]
+        u = s.unit(i, p.dp, 0, p.y, 4)
+        s.cp(i, 4, u, p.xn if order == "xy" else p.yn).start()
+        s.cp(i, 7, u, p.sib).start()
+    def s1_in(s, i):
+        p = s.p; order = CHUNKS[i][3]
+        return s.unit(i, p.dpx, 0, p.y, 4) if order == "xy" else s.unit(i, p.dp, 0, 1 - p.y, 4)
+    def s2(s, i):
+        p = s.p; order = CHUNKS[i][3]
+        r = s.s1_in(i)
+        s.cp(i, 4, r, p.xn).wait_recv()
+        nxt = p.yn if order == "xy" else p.xn
+        u = s.unit(i, p.dp, 0, p.y, 4)
+        s.cp(i, 5, u, nxt).start()
+        s.cp(i, 6, r, nxt).start()
+        s.cp(i, 8, r, p.sib).start()
+    def s2_in(s, i):
+        p = s.p; order = CHUNKS[i][3]
+        if order == "xy":
+            return s.unit(i, p.dp, 0, 1 - p.y, 4), s.unit(i, p.dpx, 0, 1 - p.y, 4)
+        return s.unit(i, p.dpx, 0, p.y, 4), s.unit(i, p.dpx, 0, 1 - p.y, 4)
+    def s3(s, i):
+        p = s.p
+        for k, r in enumerate(s.s2_in(i)):
+            s.cp(i, 5 + k, r, p.sib).wait_recv()
+            s.cp(i, 9 + k, r, p.sib).start()
+    def s4(s, i):
+        p = s.p
+        u = s.unit(i, p.dp, 0, p.y, 4)
+        for k in (7, 8, 9, 10):
+            s.cp(i, k, u, p.sib).wait_recv()
+    def drain(s, i):
+        p = s.p
+        u1 = s.unit(i, p.dp, 0, p.y)
+        u = s.unit(i, p.dp, 0, p.y, 4)
+        for k in (4, 5, 6, 7, 8, 9, 10):
+            s.cp(i, k, u, p.sib).wait_send()
+        w = lambda k: rcopy(u1, u1, s.ss.at[i, k], s.rs.at[i, 0], p.sib).wait_send()
+        @pl.when(p.z < 3)
+        def _(): w(0)
+        @pl.when(p.z > 0)
+        def _(): w(1)
+        for h in (1, 2):
+            @pl.when((p.z >= h) & (p.z < 3))
+            def _(): w(1 + h)
+            @pl.when((p.z + h <= 3) & (p.z > 0))
+            def _(): w(10 + h)
+
+def first_exchange(pos, wa_ref, wb_ref, WA, WB, land, ss, rs):
+    p = pos
+    ca = rcopy(wa_ref.at[:, pl.ds(pl.multiple_of((1 - p.y) * HA, 128), HA)], land, ss.at[0], rs.at[0], p.yn)
+    ca.start()
+    mine = (p.dp * 4 + p.z) * RB + p.y * 48
+    other = (p.dp * 4 + p.z) * RB + (1 - p.y) * 48
+    cb = rcopy(wb_ref.at[:, pl.ds(pl.multiple_of((1 - p.y) * HB, 128), HB)], at(WB, mine, 48, 1 - p.y, HB, 0, HB), ss.at[1], rs.at[1], p.yn)
+    cb.start()
+    at_own = at(WB, mine, 48, p.y, HB, 0, HB)
+    loc = pltpu.make_async_copy(wb_ref.at[:, pl.ds(pl.multiple_of(p.y * HB, 128), HB)], at_own, ss.at[2])
+    loc.start()
+    ca.wait()
+    own = wa_ref[:, pl.ds(pl.multiple_of(p.y * HA, 128), HA)].astype(jnp.float32)
+    got = land[...].astype(jnp.float32)
+    f = (p.y == 0)
+    lo = jnp.where(f, own, got); hi = jnp.where(f, got, own)
+    WA[pl.ds(pl.multiple_of((p.dp * 4 + p.z) * RA, 16), RA), pl.ds(pl.multiple_of(p.y * HA, 128), HA)] = jnp.concatenate([lo, hi], axis=0).astype(jnp.bfloat16)
+    cb.wait(); loc.wait()
+
+def ag_kernel(wa_ref, wb_ref, oa_ref, ob_ref, WA, WB, land, s0, r0, ss, rs, osem):
+    pos = Pos()
+    barrier(pos)
+    first_exchange(pos, wa_ref, wb_ref, WA, WB, land, s0, r0)
+    g = Gather(pos, (WA, WB), ss, rs)
+    n = len(CHUNKS)
+    for i in range(n): g.z0(i)
+    for t in range(n + 3):
+        if 0 <= t - 3 < n: g.s3(t - 3)
+        if 0 <= t - 2 < n: g.s2(t - 2)
+        if t < n:
+            g.zhop(t, 1)
+            g.zhop(t, 2)
+            g.zhop(t, 3)
+            g.s1(t)
+    for i in range(n): g.s4(i)
+    for i in range(n): g.drain(i)
+    a = pltpu.make_async_copy(WA, oa_ref, osem.at[0]); b = pltpu.make_async_copy(WB, ob_ref, osem.at[1])
+    a.start(); b.start(); a.wait(); b.wait()
+
+def gather_call(wa, wb):
+    n = len(CHUNKS)
+    return pl.pallas_call(
+        ag_kernel,
+        out_shape=(jax.ShapeDtypeStruct((768, 2 * HA), jnp.bfloat16), jax.ShapeDtypeStruct((1536, 2 * HB), jnp.bfloat16)),
+        in_specs=[pl.BlockSpec(memory_space=pltpu.VMEM)] * 2,
+        out_specs=[pl.BlockSpec(memory_space=pl.ANY)] * 2,
+        scratch_shapes=[pltpu.VMEM((768, 2 * HA), jnp.bfloat16), pltpu.VMEM((1536, 2 * HB), jnp.bfloat16), pltpu.VMEM((24, HA), jnp.bfloat16),
+            pltpu.SemaphoreType.DMA((3,)), pltpu.SemaphoreType.DMA((3,)), pltpu.SemaphoreType.DMA((n, 13)), pltpu.SemaphoreType.DMA((n, 13)), pltpu.SemaphoreType.DMA((2,))],
+        compiler_params=pltpu.CompilerParams(collective_id=0, has_side_effects=True, vmem_limit_bytes=60 * 2**20),
+    )(wa, wb)
+
+
+class Scatter:
+    NS = 14
+    def __init__(s, pos, P, L1, L2, L3, L4, F, G, out, ss, rs):
+        s.p, s.P, s.L1, s.L2, s.L3, s.L4, s.F, s.G, s.out, s.ss, s.rs = pos, P, L1, L2, L3, L4, F, G, out, ss, rs
+    def geom(s, i):
+        b, off, w, order = CHUNKS[i]
+        return b, (RA, RB)[b], (HA, HB)[b], off, w, order
+    def rows(s, i, xx, c, z=0):
+        R = (RA, RB)[CHUNKS[i][0]]
+        return pl.multiple_of(((xx * 2 + c) * 4 + z) * R, 48)
+    def cols(s, i, yy):
+        b, R, W, off, w, _ = s.geom(i)
+        return pl.ds(pl.multiple_of(yy * W + off, 128), w)
+    def piece(s, i, xx, c, yy, z=0, n=4):
+        b, R, W, off, w, _ = s.geom(i)
+        return s.P[b].at[pl.ds(s.rows(i, xx, c, z), n * R), s.cols(i, yy)]
+    def cp(s, i, k, src, dst, dev):
+        return rcopy(src, dst, s.ss.at[i, k], s.rs.at[i, k], dev)
+    def add(s, dst, src, nrows):
+        def body(r, _):
+            rr = pl.ds(pl.multiple_of(r * 48, 48), 48)
+            dst[rr, :] = (dst[rr, :].astype(f32) + src[rr, :].astype(f32)).astype(bf16)
+            return 0
+        lax.fori_loop(0, nrows // 48, body, 0)
+    def l1(s, i, xx, yy):
+        b, R, W, off, w, _ = s.geom(i)
+        return s.L1[b].at[xx, :, s.cols(i, yy)]
+    def st0(s, i):
+        p = s.p
+        for k, (xx, yy) in enumerate(((0, 0), (0, 1), (1, 0), (1, 1))):
+            s.cp(i, k, s.piece(i, xx, 1 - p.c, yy), s.l1(i, xx, yy), p.sib).start()
+    def a0(s, i):
+        b, R, W, off, w, _ = s.geom(i)
+        for k, (xx, yy) in enumerate(((0, 0), (0, 1), (1, 0), (1, 1))):
+            l = s.l1(i, xx, yy)
+            s.cp(i, k, l, l, s.p.sib).wait_recv()
+            s.add(s.piece(i, xx, s.p.c, yy), l, 4 * R)
+    def l2(s, i, k):
+        b, R, W, off, w, _ = s.geom(i)
+        return s.L2[b].at[k, :, pl.ds(off, w)]
+    def l3(s, i):
+        b, R, W, off, w, _ = s.geom(i)
+        return s.L3[b].at[:, pl.ds(off, w)]
+    def st1(s, i):
+        p, order = s.p, s.geom(i)[5]
+        for k in (0, 1):
+            src = s.piece(i, k, p.c, 1 - p.y) if order == "xy" else s.piece(i, 1 - p.x, p.c, k)
+            s.cp(i, 4 + k, src, s.l2(i, k), p.yn if order == "xy" else p.xn).start()
+    def a1(s, i):
+        p = s.p; b, R, W, off, w, order = s.geom(i)
+        for k in (0, 1):
+            l = s.l2(i, k)
+            s.cp(i, 4 + k, l, l, p.xn).wait_recv()
+            s.add(s.piece(i, k, p.c, p.y) if order == "xy" else s.piece(i, p.x, p.c, k), l, 4 * R)
+    def st2(s, i):
+        p, order = s.p, s.geom(i)[5]
+        src = s.piece(i, 1 - p.x, p.c, p.y) if order == "xy" else s.piece(i, p.x, p.c, 1 - p.y)
+        s.cp(i, 6, src, s.l3(i), p.xn if order == "xy" else p.yn).start()
+    def a2(s, i):
+        p = s.p; b, R, W, off, w, order = s.geom(i)
+        l = s.l3(i)
+        s.cp(i, 6, l, l, p.xn).wait_recv()
+        s.add(s.piece(i, p.x, p.c, p.y), l, 4 * R)
+    def l4(s, i, d, t):
+        b, R, W, off, w, _ = s.geom(i)
+        return s.L4[b].at[d, t, :, pl.ds(off, w)]
+    def own(s, i, t):
+        p = s.p
+        return s.piece(i, p.x, p.c, p.y, t, 1)
+    def zsem(s, d, t):
+        return 6 + t if d == 0 else 10 + t
+    def zflow(s, i, d, z):
+        p = s.p; R = s.geom(i)[1]
+        first = z == (0, 3)[d]
+        mine = () if first else (z,)
+        on = tuple(range(3, z, -1)) if d == 0 else tuple(range(0, z))
+        for t in on:
+            l = s.l4(i, d, t)
+            if not first:
+                s.cp(i, s.zsem(d, t), l, l, p.sib).wait_recv()
+                s.add(l, s.own(i, t), R)
+            s.cp(i, s.zsem(d, t), s.own(i, t) if first else l, l, p.up if d == 0 else p.dn).start()
+        for t in mine:
+            l = s.l4(i, d, t)
+            s.cp(i, s.zsem(d, t), l, l, p.sib).wait_recv()
+    def zstep(s, i, h):
+        p = s.p
+        for z, d in ((h, 0), (3 - h, 1)):
+            @pl.when(p.z == z)
+            def _(): s.zflow(i, d, z)
+    def fin(s, i):
+        p = s.p; b, R, W, off, w, _ = s.geom(i)
+        u = s.own(i, p.z)
+        hu, hd = (p.z > 0), (p.z < 3)
+        lu, ld = s.l4(i, 0, p.z), s.l4(i, 1, p.z)
+        F, G, out = s.F[b], s.G[b], s.out[b]
+        h = R // 2
+        for z in range(4):
+            @pl.when(p.z == z)
+            def _():
+                t = u[...].astype(f32)
+                if z > 0: t = t + lu[...].astype(f32)
+                if z < 3: t = t + ld[...].astype(f32)
+                F[:, pl.ds(off, w)] = t
+        src = F.at[pl.ds(pl.multiple_of((1 - p.y) * h, 8), h), pl.ds(off, w)]
+        s.cp(i, 13, src, G.at[:, pl.ds(off, w)], p.yn).start()
+        out[:, s.cols(i, p.y)] = F[pl.ds(pl.multiple_of(p.y * h, 8), h), pl.ds(off, w)]
+    def last(s, i):
+        p = s.p; b, R, W, off, w, _ = s.geom(i)
+        l = s.G[b].at[:, pl.ds(off, w)]
+        s.cp(i, 13, l, l, p.yn).wait_recv()
+        s.out[b][:, s.cols(i, 1 - p.y)] = l[...]
+    def drain(s, i):
+        p = s.p; b, R, W, off, w, _ = s.geom(i)
+        for k, ref in [(k, s.l1(i, 0, 0)) for k in range(4)] + [(4, s.l2(i, 0)), (5, s.l2(i, 1)), (6, s.l3(i)), (13, s.G[b].at[:, pl.ds(off, w)])]:
+            s.cp(i, k, ref, ref, p.sib).wait_send()
+        for d in (0, 1):
+            for t in ((1, 2, 3), (0, 1, 2))[d]:
+                l = s.l4(i, d, t)
+                @pl.when((p.z < t) if d == 0 else (p.z > t))
+                def _(): s.cp(i, s.zsem(d, t), l, l, p.sib).wait_send()
+
+def rs_schedule(g, n, before=lambda i: None):
+    for t in range(n + 9):
+        if t < n: before(t); g.st0(t)
+        if 0 <= t - 1 < n: g.a0(t - 1); g.st1(t - 1)
+        if 0 <= t - 2 < n: g.a1(t - 2); g.st2(t - 2)
+        if 0 <= t - 3 < n: g.a2(t - 3); g.zstep(t - 3, 0)
+        for h in (1, 2, 3):
+            if 0 <= t - 3 - h < n: g.zstep(t - 3 - h, h)
+        if 0 <= t - 6 < n: g.fin(t - 6)
+        if 0 <= t - 7 < n: g.last(t - 7)
+    for i in range(n): g.drain(i)
+
+def rs_kernel(pa_ref, pb_ref, oa, ob, PA, PB, L1A, L1B, L2A, L2B, L3A, L3B, L4A, L4B, FA, FB, GA, GB, ss, rs, ls):
+    pos = Pos(); barrier(pos)
+    n = len(CHUNKS)
+    a = pltpu.make_async_copy(pa_ref, PA, ls.at[0]); b = pltpu.make_async_copy(pb_ref, PB, ls.at[1])
+    a.start(); b.start(); a.wait(); b.wait()
+    g = Scatter(pos, (PA, PB), (L1A, L1B), (L2A, L2B), (L3A, L3B), (L4A, L4B), (FA, FB), (GA, GB), (oa, ob), ss, rs)
+    rs_schedule(g, n)
+
+def rs_scratch():
+    n = len(CHUNKS)
+    V = pltpu.VMEM
+    return [V((768, 2 * HA), bf16), V((1536, 2 * HB), bf16), V((2, 192, 2 * HA), bf16), V((2, 384, 2 * HB), bf16),
+        V((2, 192, HA), bf16), V((2, 384, HB), bf16), V((192, HA), bf16), V((384, HB), bf16),
+        V((2, 4, 48, HA), bf16), V((2, 4, 96, HB), bf16), V((48, HA), f32), V((96, HB), f32), V((24, HA), f32), V((48, HB), f32),
+        pltpu.SemaphoreType.DMA((n, Scatter.NS)), pltpu.SemaphoreType.DMA((n, Scatter.NS)), pltpu.SemaphoreType.DMA((2,))]
+
+def scatter_call(pa, pb):
+    return pl.pallas_call(rs_kernel,
+        out_shape=(jax.ShapeDtypeStruct((24, 2 * HA), f32), jax.ShapeDtypeStruct((48, 2 * HB), f32)),
+        in_specs=[pl.BlockSpec(memory_space=pl.ANY)] * 2,
+        out_specs=[pl.BlockSpec(memory_space=pltpu.VMEM)] * 2,
+        scratch_shapes=rs_scratch(),
+        compiler_params=pltpu.CompilerParams(collective_id=1, has_side_effects=True, vmem_limit_bytes=60 * 2**20))(pa, pb)
+
+NK = 32
+NB = 2
+
+def lanes(j): return pl.ds(pl.multiple_of(j * 128, 128), 128)
+def rows_(i): return pl.ds(pl.multiple_of(i * 8, 8), 8)
+def tree(xs):
+    xs = list(xs)
+    while len(xs) > 1:
+        xs = [xs[i] + xs[i + 1] if i + 1 < len(xs) else xs[i] for i in range(0, len(xs), 2)]
+    return xs[0]
+
+def fwd_states(U, rate, S, END, j, unroll=2):
+    ln = lanes(j)
+    r = rate[0:16, ln]
+    w = [jnp.exp(r * (s - 7.0)) for s in range(8)]
+    q8 = jnp.exp(r * -8.0)
+    def body(k, st):
+        new = []
+        for b in range(NB):
+            S[b * NK + k, :, ln] = st[b]
+            parts = [w[s] * U[b * NK + k, pl.ds(s, 1), ln] for s in range(8)]
+            new.append(q8 * st[b] + tree(parts))
+        return tuple(new)
+    st = lax.fori_loop(0, NK, body, tuple(jnp.zeros((16, 128), f32) for _ in range(NB)), unroll=unroll)
+    for b in range(NB): END[b, :, ln] = st[b]
+
+def conv_tables(rate, ec, j):
+    ln = lanes(j)
+    it = lax.broadcasted_iota(jnp.int32, (8, 128), 0).astype(f32)
+    E, K = [], []
+    for h in range(16):
+        rb = jnp.broadcast_to(rate[pl.ds(h, 1), ln], (8, 128)); eb = jnp.broadcast_to(ec[pl.ds(h, 1), ln], (8, 128))
+        K.append(jnp.exp(-it * rb) * eb)
+        E.append(jnp.exp(-(it + 1.0) * rb) * eb)
+    return E, tree(K)
+
+def fwd_smooth(U, S, S0, rate, ec, omega, BL, KS, j, unroll=1):
+    ln = lanes(j)
+    r = rate[0:16, ln]
+    q8 = jnp.exp(r * -8.0)
+    E, K = conv_tables(rate, ec, j)
+    KS[...] = K
+    ii = lax.broadcasted_iota(jnp.int32, (8, 128), 0)
+    KM = [jnp.where(ii >= l, jnp.broadcast_to(KS[pl.ds(l, 1), :], (8, 128)), 0.0) for l in range(8)]
+    om = jnp.broadcast_to(omega[:, ln], (8, 128))
+    KM[0] = KM[0] + om
+    def body(k, gs):
+        new = []
+        for b in range(NB):
+            i = b * NK + k
+            S[i, :, ln] = S[i, :, ln] + gs[b]
+            u = U[i, :, ln]
+            parts = [KM[0] * u] + [KM[l] * pltpu.roll(u, l, 0) for l in range(1, 8)]
+            parts += [E[h] * S[i, pl.ds(h, 1), ln] for h in range(16)]
+            BL[i, :, ln] = tree(parts)
+            new.append(q8 * gs[b])
+        return tuple(new)
+    lax.fori_loop(0, NK, body, tuple(S0[b, :, ln] for b in range(NB)), unroll=unroll)
+
+def bwd_states(Gr, U, S, rate, A, DIR, G1, H, CS, j, unroll=1):
+    ln = lanes(j)
+    r = rate[0:16, ln]
+    w = [jnp.exp(r * -float(s)) for s in range(8)]
+    q8 = jnp.exp(r * -8.0)
+    def body(kk, c):
+        k = NK - 1 - kk
+        st, g1, h1, C = c
+        new, C = [], list(C)
+        for b in range(NB):
+            i = b * NK + k
+            A[i, :, ln] = st[b]
+            p = [w[s] * Gr[i, pl.ds(s, 1), ln] for s in range(8)]
+            Bg = tree(p)
+            B1 = tree([p[s] if s == 1 else p[s] * float(s) for s in range(1, 8)])
+            Sk = S[i, :, ln]
+            g1 = g1 + Sk * Bg
+            h1 = h1 + Sk * B1
+            new.append(q8 * st[b] + Bg)
+            u, g = U[i, :, ln], Gr[i, :, ln]
+            C = [C[l] + g * (pltpu.roll(u, l, 0) if l else u) for l in range(8)]
+        return tuple(new), g1, h1, tuple(C)
+    z = jnp.zeros((16, 128), f32)
+    st, g1, h1, C = lax.fori_loop(0, NK, body, (tuple(z for _ in range(NB)), z, z, tuple(jnp.zeros((8, 128), f32) for _ in range(8))), unroll=unroll)
+    for b in range(NB): DIR[b, :, ln] = st[b]
+    ii = lax.broadcasted_iota(jnp.int32, (8, 128), 0)
+    g1, h1 = g1 * w[1], h1 * w[1]
+    for l in range(8):
+        cl = jnp.sum(jnp.where(ii >= l, C[l], 0.0), axis=0, keepdims=True)
+        t = w[l] * cl
+        g1 = g1 + t
+        if l: h1 = h1 + t * float(l)
+    G1[:, ln] = g1
+    H[:, ln] = h1
+
+def bwd_grad(Gr, U, S, A, A0, rate, ec, H, DU, KS, AT, j, unroll=1):
+    ln = lanes(j)
+    r = rate[0:16, ln]
+    q8 = jnp.exp(r * -8.0)
+    c8 = 8.0 * jnp.exp(r * -9.0)
+    wu = [jnp.exp(r * (s - 8.0)) * (8.0 - s) for s in range(8)]
+    it = lax.broadcasted_iota(jnp.int32, (8, 128), 0).astype(f32)
+    E, K = [], []
+    for h in range(16):
+        rb = jnp.broadcast_to(rate[pl.ds(h, 1), ln], (8, 128)); eb = jnp.broadcast_to(ec[pl.ds(h, 1), ln], (8, 128))
+        K.append(jnp.exp(-it * rb) * eb)
+        E.append(jnp.exp((it - 8.0) * rb) * eb)
+    KS[...] = tree(K)
+    ii = lax.broadcasted_iota(jnp.int32, (8, 128), 0)
+    KM = [jnp.where(ii < 8 - l, jnp.broadcast_to(KS[pl.ds(l, 1), :], (8, 128)), 0.0) for l in range(8)]
+    def body(kk, c):
+        k = NK - 1 - kk
+        gs, h1 = c
+        new = []
+        for b in range(NB):
+            i = b * NK + k
+            Ak = A[i, :, ln] + gs[b]
+            AT[b] = Ak
+            Bu = tree([wu[s] * U[i, pl.ds(s, 1), ln] for s in range(8)])
+            h1 = h1 + Ak * (Bu + c8 * S[i, :, ln])
+            g = Gr[i, :, ln]
+            parts = [KM[0] * g] + [KM[l] * pltpu.roll(g, 8 - l, 0) for l in range(1, 8)]
+            parts += [E[h] * AT[b, pl.ds(h, 1), :] for h in range(16)]
+            DU[i, :, ln] = tree(parts)
+            new.append(q8 * gs[b])
+        return tuple(new), h1
+    gs, h1 = lax.fori_loop(0, NK, body, (tuple(A0[b, :, ln] for b in range(NB)), H[:, ln]), unroll=unroll)
+    H[:, ln] = h1
+
+def six(f):
+    def body(j, _):
+        f(j); return 0
+    lax.fori_loop(0, 6, body, 0)
+
+vm = lambda s, t=f32: pltpu.VMEM(s, t)
+SH = jax.ShapeDtypeStruct
+CP = pltpu.CompilerParams(vmem_limit_bytes=56 * 2**20)
+
+def ema1(U, rate, unroll=2):
+    def k(U, rate, S, END): six(lambda j: fwd_states(U, rate, S, END, j, unroll))
+    return pl.pallas_call(k, out_shape=(SH((64, 16, 768), f32), SH((2, 16, 768), f32)), compiler_params=CP)(U, rate)
+def ema2(U, S, S0, rate, ec, omega, unroll=1):
+    def k(U, Sin, S0, rate, ec, omega, S, BL, KS):
+        S[...] = Sin[...]
+        six(lambda j: fwd_smooth(U, S, S0, rate, ec, omega, BL, KS, j, unroll))
+    return pl.pallas_call(k, out_shape=(SH((64, 16, 768), f32), SH((64, 8, 768), f32)), scratch_shapes=[vm((8, 128))], compiler_params=CP)(U, S, S0, rate, ec, omega)
+def emab1(Gr, U, S, rate, unroll=1):
+    def k(Gr, U, S, rate, A, DIR, G1, H, CS): six(lambda j: bwd_states(Gr, U, S, rate, A, DIR, G1, H, CS, j, unroll))
+    return pl.pallas_call(k, out_shape=(SH((64, 16, 768), f32), SH((2, 16, 768), f32), SH((16, 768), f32), SH((16, 768), f32)), scratch_shapes=[vm((8, 128))], compiler_params=CP)(Gr, U, S, rate)
+def emab2(Gr, U, S, A, A0, rate, ec, H, unroll=1):
+    def k(Gr, U, S, A, A0, rate, ec, Hin, H, DU, KS, AT):
+        H[...] = Hin[...]
+        six(lambda j: bwd_grad(Gr, U, S, A, A0, rate, ec, H, DU, KS, AT, j, unroll))
+    return pl.pallas_call(k, out_shape=(SH((16, 768), f32), SH((64, 8, 768), f32)), scratch_shapes=[vm((8, 128)), vm((2, 16, 128))], compiler_params=CP)(Gr, U, S, A, A0, rate, ec, H)
+
+def scan_kernel(way, e_ref, rate_ref, z_ref, W, L, ss, rs):
+    sq, dp = lax.axis_index("seq"), lax.axis_index("dp")
+    bar = pltpu.get_barrier_semaphore()
+    n = 8
+    has = lambda d: (sq + d < n) if d > 0 else (sq + d >= 0)
+    to = lambda d: (dp, jnp.clip(sq + d, 0, n - 1))
+    for s in (1, 2, 4):
+        for d in (s, -s):
+            @pl.when(has(d))
+            def _(): pl.semaphore_signal(bar, inc=1, device_id=to(d), device_id_type=MESH)
+    pl.semaphore_wait(bar, sum(jnp.clip(sq - s + 1, 0, 1) + jnp.clip(n - s - sq, 0, 1) for s in (1, 2, 4)))
+    W[0] = e_ref[...]
+    z_ref[...] = jnp.zeros_like(z_ref)
+    g = jnp.exp(rate_ref[...] * -256.0)
+    g2 = g * g
+    grow, keep = (g, g2, g2 * g2), (jnp.ones_like(g), g, g2 * g)
+    for k, s in enumerate((1, 2, 4)):
+        cp = rcopy(W.at[k], L.at[k], ss.at[k], rs.at[k], to(way * s))
+        @pl.when(has(way * s))
+        def _(): cp.start()
+        if k < 2: W[k + 1] = W[k]
+        @pl.when(has(-way * s))
+        def _():
+            cp.wait_recv()
+            z_ref[...] = z_ref[...] + keep[k][None] * L[k]
+            if k < 2: W[k + 1] = W[k + 1] + grow[k][None] * L[k]
+    for k, s in enumerate((1, 2, 4)):
+        @pl.when(has(way * s))
+        def _(): rcopy(W.at[k], L.at[k], ss.at[k], rs.at[k], to(way * s)).wait_send()
+def scan_call(e, rate, way, cid):
+    return pl.pallas_call(functools.partial(scan_kernel, way),
+        out_shape=jax.ShapeDtypeStruct(e.shape, f32),
+        scratch_shapes=[pltpu.VMEM((3,) + e.shape, f32), pltpu.VMEM((3,) + e.shape, f32), pltpu.SemaphoreType.DMA((3,)), pltpu.SemaphoreType.DMA((3,))],
+        compiler_params=pltpu.CompilerParams(collective_id=cid, has_side_effects=True, vmem_limit_bytes=40 * 2**20))(e, rate)
+
+
+def per_device_tuned(tokens, cotangent, lengths, w_mx, w_value, w_out, w_up, w_down, ema_rate, ema_in, ema_out, gains, qk_affine):
+    wa = jnp.pad(jnp.concatenate([w_mx, w_value, w_up], axis=1), ((0, 0), (0, 128)))
+    wb = jnp.concatenate([w_out, w_down], axis=1)
+    rate_own, in_own, out_own = (t.astype(f32) for t in (ema_rate, ema_in, ema_out))
+    scale_own = jnp.sqrt(-jnp.expm1(-2.0 * rate_own))
+    mine = jnp.pad(jnp.concatenate([rate_own, out_own * scale_own * in_own, gains.astype(f32)], axis=1), ((0, 0), (0, 93)))
+    small = lax.all_gather(mine, ("dp", "seq"), axis=0, tiled=True).T
+    full_a, full_b = gather_call(wa, wb)
+    rate, coef = small[:16], small[16:32]
+    gain_first, gain_second, omega_gain = small[32], small[33], small[34]
+    mx_full, value_full, up_full = full_a[:, :3200], full_a[:, 3200:4736], full_a[:, 4736:6272]
+    out_full, down_full = full_b[:, :768], full_b[:, 768:]
+    affine = qk_affine.astype(f32)
+    rows_here = tokens.shape[0]
+    spans_dev = SEQ_DEV // SPAN
+    score_scale = Z ** (-0.5)
+    inputs = tokens.astype(f32)
+    seq_pos = lax.axis_index("seq") * SEQ_DEV + jnp.arange(SEQ_DEV, dtype=jnp.int32)
+    valid_rows = (seq_pos[None, :] < lengths[:, None]).astype(f32)[:, :, None]
+    inverse1 = lax.rsqrt(jnp.mean(inputs * inputs, axis=-1, keepdims=True) + EPSILON)
+    unit1 = inputs * inverse1
+    normed = unit1 * gain_first
+    normed_low = normed.astype(bf16)
+    u3 = normed.reshape(64, 8, D)
+    states, ends = ema1(u3, rate, 4)
+    start_state = scan_call(ends, rate, 1, 2)
+    states, blend3 = ema2(u3, states, start_state, rate, coef, omega_gain[None], 2)
+    blend = blend3.reshape(normed.shape)
+    value_pre = jnp.einsum("bsd,dv->bsv", normed_low, value_full, preferred_element_type=f32)
+    value_low = jax.nn.silu(value_pre).astype(bf16)
+    shifted_low = jax.nn.silu(blend).astype(jnp.bfloat16)
+    mixed = jnp.einsum("bsd,dk->bsk", shifted_low, mx_full, preferred_element_type=jnp.float32)
+    update = jax.nn.sigmoid(mixed[..., :D])
+    shared_pre = mixed[..., D : D + Z]
+    shared = jax.nn.silu(shared_pre)
+    reset_pre = mixed[..., D + Z : D + Z + V]
+    reset = jax.nn.silu(reset_pre)
+    direct = mixed[..., D + Z + V :]
+    query_low = (
+        (shared * affine[0] + affine[1]).astype(jnp.bfloat16).reshape(rows_here, spans_dev, SPAN, Z)
+    )
+    key_low = (shared * affine[2]).astype(jnp.bfloat16).reshape(rows_here, spans_dev, SPAN, Z)
+    value_tiles = value_low.reshape(rows_here, spans_dev, SPAN, V)
+    scores = (
+        jnp.einsum("bnqz,bnkz->bnqk", query_low, key_low, preferred_element_type=jnp.float32)
+        * score_scale
+    )
+    causal = jnp.arange(SPAN)[:, None] >= jnp.arange(SPAN)[None, :]
+    masked = jnp.where(causal, scores, -1e30)
+    peak = jnp.max(masked, axis=-1, keepdims=True)
+    expo = jnp.exp(masked - peak)
+    attention_weights = expo / jnp.sum(expo, axis=-1, keepdims=True)
+    probs_low = attention_weights.astype(jnp.bfloat16)
+    attended_output = jnp.einsum(
+        "bnqk,bnkv->bnqv", probs_low, value_tiles, preferred_element_type=jnp.float32
+    ).reshape(rows_here, SEQ_DEV, V)
+    gated_low = (reset * attended_output).astype(jnp.bfloat16)
+    cand_pre = direct + jnp.einsum(
+        "bsv,vd->bsd", gated_low, out_full, preferred_element_type=jnp.float32
+    )
+    candidate = jax.nn.silu(cand_pre)
+    attn_branch = update * (candidate - inputs)
+    middle = inputs + attn_branch
+    inverse2 = lax.rsqrt(jnp.mean(middle * middle, axis=-1, keepdims=True) + EPSILON)
+    unit2 = middle * inverse2
+    normed2_low = (unit2 * gain_second).astype(jnp.bfloat16)
+    up_pre = jnp.einsum("bsd,df->bsf", normed2_low, up_full, preferred_element_type=jnp.float32)
+    hidden_low = jax.nn.silu(up_pre).astype(jnp.bfloat16)
+    ffn_branch = jnp.einsum(
+        "bsf,fd->bsd", hidden_low, down_full, preferred_element_type=jnp.float32
+    )
+    output = middle + ffn_branch
+    mixer_backward, value_back, out_back, up_back, down_back = mx_full, value_full, out_full, up_full, down_full
+    grad_out = cotangent.astype(jnp.float32) * valid_rows
+    grad_out_low = grad_out.astype(jnp.bfloat16)
+    grad_down = jnp.einsum(
+        "bsf,bsd->fd", hidden_low, grad_out_low, preferred_element_type=jnp.float32
+    )
+    grad_hidden = jnp.einsum(
+        "bsd,fd->bsf", grad_out_low, down_back, preferred_element_type=jnp.float32
+    )
+    grad_up_low = (grad_hidden * silu_slope(up_pre)).astype(jnp.bfloat16)
+    grad_up = jnp.einsum(
+        "bsd,bsf->df", normed2_low, grad_up_low, preferred_element_type=jnp.float32
+    )
+    grad_normed2 = jnp.einsum(
+        "bsf,df->bsd", grad_up_low, up_back, preferred_element_type=jnp.float32
+    )
+    grad_gain_second = jnp.sum(grad_normed2 * unit2, axis=(0, 1))
+    scaled2 = grad_normed2 * gain_second
+    grad_middle = grad_out + inverse2 * (
+        scaled2 - unit2 * jnp.mean(scaled2 * unit2, axis=-1, keepdims=True)
+    )
+    grad_update = grad_middle * (candidate - inputs)
+    grad_cand_pre = grad_middle * update * silu_slope(cand_pre)
+    grad_cand_low = grad_cand_pre.astype(jnp.bfloat16)
+    grad_out_proj = jnp.einsum(
+        "bsv,bsd->vd", gated_low, grad_cand_low, preferred_element_type=jnp.float32
+    )
+    grad_gated = jnp.einsum(
+        "bsd,vd->bsv", grad_cand_low, out_back, preferred_element_type=jnp.float32
+    )
+    grad_reset = grad_gated * attended_output
+    grad_attended_low = (
+        (grad_gated * reset).astype(jnp.bfloat16).reshape(rows_here, spans_dev, SPAN, V)
+    )
+    grad_probs = jnp.einsum(
+        "bnqv,bnkv->bnqk", grad_attended_low, value_tiles, preferred_element_type=jnp.float32
+    )
+    grad_values = jnp.einsum(
+        "bnqk,bnqv->bnkv", probs_low, grad_attended_low, preferred_element_type=jnp.float32
+    ).reshape(rows_here, SEQ_DEV, V)
+    grad_scores_low = (
+        attention_weights
+        * (grad_probs - jnp.sum(grad_probs * attention_weights, axis=-1, keepdims=True))
+    ).astype(jnp.bfloat16)
+    grad_query = (
+        jnp.einsum("bnqk,bnkz->bnqz", grad_scores_low, key_low, preferred_element_type=jnp.float32)
+        * score_scale
+    ).reshape(rows_here, SEQ_DEV, Z)
+    grad_key = (
+        jnp.einsum(
+            "bnqk,bnqz->bnkz", grad_scores_low, query_low, preferred_element_type=jnp.float32
+        )
+        * score_scale
+    ).reshape(rows_here, SEQ_DEV, Z)
+    grad_affine = jnp.stack(
+        [
+            jnp.sum(grad_query * shared, axis=(0, 1)),
+            jnp.sum(grad_query, axis=(0, 1)),
+            jnp.sum(grad_key * shared, axis=(0, 1)),
+        ]
+    )
+    grad_shared = grad_query * affine[0] + grad_key * affine[2]
+    grad_mixed_low = jnp.concatenate(
+        [
+            grad_update * update * (1.0 - update),
+            grad_shared * silu_slope(shared_pre),
+            grad_reset * silu_slope(reset_pre),
+            grad_cand_pre,
+        ],
+        axis=-1,
+    ).astype(jnp.bfloat16)
+    grad_mx = jnp.einsum(
+        "bsd,bsk->dk", shifted_low, grad_mixed_low, preferred_element_type=jnp.float32
+    )
+    grad_shifted = jnp.einsum(
+        "bsk,dk->bsd", grad_mixed_low, mixer_backward, preferred_element_type=jnp.float32
+    )
+    grad_blend = grad_shifted * silu_slope(blend)
+    grad_omega = jnp.sum(grad_blend * normed, axis=(0, 1))
+    grad_value_low = (grad_values * silu_slope(value_pre)).astype(jnp.bfloat16)
+    grad_value_proj = jnp.einsum(
+        "bsd,bsv->dv", normed_low, grad_value_low, preferred_element_type=jnp.float32
+    )
+    grad_normed = grad_blend * omega_gain + jnp.einsum(
+        "bsv,dv->bsd", grad_value_low, value_back, preferred_element_type=jnp.float32
+    )
+    g3 = grad_blend.reshape(64, 8, D)
+    adj, direct, g1, h1 = emab1(g3, u3, states, rate, 2)
+    later = scan_call(direct, rate, -1, 3)
+    h1, du3 = emab2(g3, u3, states, adj, later, rate, coef, h1, 2)
+    grad_normed = grad_normed + du3.reshape(normed.shape)
+    grad_gain_first = jnp.sum(grad_normed * unit1, axis=(0, 1))
+    scaled1 = grad_normed * gain_first
+    grad_tokens = grad_middle * (1.0 - update) + inverse1 * (
+        scaled1 - unit1 * jnp.mean(scaled1 * unit1, axis=-1, keepdims=True)
+    )
+    pa = jnp.pad(jnp.concatenate([grad_mx, grad_value_proj, grad_up], axis=1).astype(bf16), ((0, 0), (0, 128)))
+    pb = jnp.concatenate([grad_out_proj, grad_down], axis=1).astype(bf16)
+    oa, ob = scatter_call(pa, pb)
+    tiny = jnp.concatenate([g1.T, h1.T, jnp.stack([grad_gain_first, grad_gain_second, grad_omega], axis=1)], axis=1)
+    tiny = lax.psum_scatter(jnp.pad(tiny, ((0, 0), (0, 93))), ("dp", "seq"), scatter_dimension=0, tiled=True)
+    g1, h1 = tiny[:, :16], tiny[:, 16:32]
+    grad_ema_out = in_own * scale_own * g1
+    grad_ema_in = out_own * scale_own * g1
+    grad_ema_rate = out_own * in_own * (jnp.exp(-2.0 * rate_own) / scale_own * g1 - scale_own * h1)
+    squares = jnp.stack([
+        jnp.sum(valid_rows * output * output),
+        jnp.sum(valid_rows * attn_branch * attn_branch),
+        jnp.sum(valid_rows * ffn_branch * ffn_branch),
+        jnp.sum(valid_rows),
+    ])
+    affine_total, square_total = lax.psum((grad_affine, squares), ("dp", "seq"))
+    rms_values = jnp.sqrt(square_total[:3] / (square_total[3] * D))
+    return (output.astype(bf16), grad_tokens, oa[:, :3200], oa[:, 3200:4736], ob[:, :768], oa[:, 4736:6272], ob[:, 768:],
+        grad_ema_rate, grad_ema_in, grad_ema_out, tiny[:, 32:35], affine_total, rms_values)
+
+
 def solution(mesh):
     placed = (
         P("dp", "seq", None),
@@ -379,8 +1091,9 @@
         P(("dp", "seq"), None),
         P(),
     )
+    step = per_device_tuned if dict(mesh.shape) == {"dp": 4, "seq": 8} else per_device
     return jax.shard_map(
-        per_device,
+        step,
         mesh=mesh,
         in_specs=placed,
         out_specs=(

time: 2460 us -> 532 us (0.22)
  matrix products: 951 us -> 59.1 us
  waiting for transfers between devices: 675 us -> 0.02 us
  blocking collectives: 392 us -> 109 us
  Pallas kernels: 0 us -> 272 us
  local copies, waits for them, and re-layouts: 213 us -> 25.5 us
  other arithmetic: 173 us -> 45.4 us
    dot_general x69 -> x21, matrix products: 951 us -> 59.1 us  [the longest x1 5.66 us: per_device_tuned(): jnp.einsum('bsd,dv->bsv', normed_low, value_full, preferred_element_type=...]
    reduce_scatter x4 -> x0, waiting for transfers between devices: 444 us -> none  [the longest x1 113 us: per_device(): lax.psum_scatter(grad_down, ('dp', 'seq'), scatter_dimension=0, tiled=True)]
    all_gather x8 -> x1, blocking collectives: 392 us -> 71.8 us  [per_device_tuned(): small = lax.all_gather(mine, ('dp', 'seq'), axis=0, tiled=True).T]
    pallas_call x0 -> x8, Pallas kernels: none -> 272 us  [the longest x1 115 us: gather_call(): pl.pallas_call(ag_kernel, out_shape=(jax.ShapeDtypeStruct((768, 2 * HA),...]
    unnamed x13 -> x2, waiting for transfers between devices: 231 us -> 0.02 us
    while x157 -> x0, local copies, waits for them, and re-layouts: 67.7 us -> none
    reduce_sum x15 -> x4, other arithmetic: 58.6 us -> 8.16 us  [the longest x1 4.92 us: per_device_tuned(): grad_gain_first = jnp.sum(grad_normed * unit1, axis=(0, 1))]
    psum x0 -> x1, blocking collectives: none -> 36.9 us  [per_device_tuned(): affine_total, square_total = lax.psum((grad_affine, squares), ('dp', 'seq'))]
  transfers between devices with their start and end apart: 11 -> 1, of which waited for: 6 -> 0; matrix products, arithmetic and copies ran while one was open for 21% -> 7% of each run, Pallas kernels for 0% -> 19%
where the time goes in v1:
time: 532 us; the launch traced here: 527 us
  Pallas kernels  272 us (51%)
  blocking collectives  109 us (20%)
  matrix products  59.1 us (11%)
  other arithmetic  45.4 us (9%)
  local copies, waits for them, and re-layouts  25.5 us (5%)
  between operations  15.8 us (3%)
    pallas_call x1, Pallas kernels, gather_call(): pl.pallas_call(ag_kernel, out_shape=(jax.ShapeDtypeStruct((768, 2 * HA),...  115 us
    pallas_call x1, Pallas kernels, scatter_call(): pl.pallas_call(rs_kernel, out_shape=(jax.ShapeDtypeStruct((24, 2 * HA), f...  102 us
    all_gather x1, blocking collectives, per_device_tuned(): small = lax.all_gather(mine, ('dp', 'seq'), axis=0, tiled=True).T  71.8 us
    psum x1, blocking collectives, per_device_tuned(): affine_total, square_total = lax.psum((grad_affine, squares), ('dp', 'seq'))  36.9 us
    pallas_call x2, Pallas kernels, scan_call(): pl.pallas_call(functools.partial(scan_kernel, way), out_shape=jax.ShapeDt...  17.7 us
    unnamed x160, local copies, waits for them, and re-layouts  13.6 us
    pallas_call x1, Pallas kernels, emab2(): pl.pallas_call(k, out_shape=(SH((16, 768), f32), SH((64, 8, 768), f32)),...  12.3 us
  transfers between devices with their start and end apart: 1, of which 0 were waited for; matrix products, arithmetic and copies ran while one was open for 7% of the time, Pallas kernels for 19%

profile of v1, /device:TPU:0, one launch (start us, length us, event | category | flops | bytes accessed | tf_op | source)
XLA Modules:
  0.0 526.8 jit_solution(8751842922153522604)
XLA Ops:
  10.5 71.8 %all_gather.3 = f32[768,128]{1,0:T(8,128)S(1)} all-gather(f32[24,128]{1,0:T(8,128)S(1)} %select_maximum_fusion), channel_id=1, replica_groups=mesh['dp'=4,'seq'=8] {'dp','seq'}, dimensions={0}, use_global_device_ids=true | all-gather | bytes 405504 | tf_op jit(solution)/shard_map/all_gather | solution.py:895
  86.6 5.3 %shard_map.228 = (f32[64,16,768]{2,1,0:T(8,128)}, f32[2,16,768]{2,1,0:T(8,128)}) custom-call(f32[64,8,768]{2,1,0:T(8,128)} %bitcast.151, f32[16,768]{1,0:T(8,128)} %get-tuple-element.101.rate.rate_ref), custom_call_target="tpu_custom_call" | custom-call | tf_op jit(solution)/shard_map/pallas_call | solution.py:838
  92.8 3.3 shard_map.229.S0
  96.7 9.2 %shard_map.230 = (f32[64,16,768]{2,1,0:T(8,128)}, f32[64,8,768]{2,1,0:T(8,128)}) custom-call(f32[64,8,768]{2,1,0:T(8,128)} %bitcast.152, f32[64,16,768]{2,1,0:T(8,128)} %get-tuple-element.27.Sin, f32[2,16,768]{2,1,0:T(8,128)} %copy-done.3, f32[16,768]{1,0:T(8,128)} %get-tuple-element.101.rate.rate_ref, f32[16,768]{1,0:T(8,128)} %get-tuple-element.100.ec, ...), custom_call_target="tpu_custom_call" | custom-call | tf_op jit(solution)/shard_map/pallas_call | solution.py:843
  109.4 115.1 %shard_map.231 = (bf16[768,6400]{1,0:T(8,128)(2,1)}, bf16[1536,1536]{1,0:T(8,128)(2,1)}) custom-call(bf16[24,6400]{1,0:T(8,128)(2,1)} %fusion.79.wa_ref, bf16[48,1536]{1,0:T(8,128)(2,1)} %pad_maximum_fusion.4.wb_ref), custom_call_target="tpu_custom_call" | custom-call | tf_op jit(solution)/shard_map/pallas_call | solution.py:530
  224.5 5.7 %multiply_convert_fusion.2 = (bf16[2,256,1536]{2,1,0:T(8,128)(2,1)}, f32[2,256,1536]{2,1,0:T(8,128)}) fusion(bf16[768,6400]{1,0:T(8,128)(2,1)} %get-tuple-element.30, f32[768]{0:T(1024)S(1)} %get-tuple-element.81, f32[2,256]{1,0:T(2,128)S(1)} %add_rsqrt_fusion.1, bf16[2,256,768]{2,1,0:T(8,128)(2,1)S(1)} %copy-done.7), kind=kOutput, calls=%fused_computation.31 | convolution fusion | flops 1213464576 | bytes 7869440 | tf_op jit(solution)/shard_map/bsd,dv->bsv/dot_general | solution.py:917
  230.2 2.8 fusion.8
  233.0 2.7 copy-done.8
  236.8 3.9 fusion.88
  240.8 3.9 fusion.13
  244.8 4.5 multiply_reduce_fusion.3
  249.5 4.1 fusion.27
  255.6 3.7 fusion.25
  259.3 4.2 fusion.45
  263.5 2.2 multiply_convert_fusion.4
  268.7 3.6 multiply_convert_fusion
  274.9 2.3 fusion.86
  277.5 3.9 fusion.12
  281.5 3.7 fusion.33
  286.9 5.3 %fusion.6 = f32[2,256,768]{2,1,0:T(8,128)S(1)} fusion(bf16[768,6400]{1,0:T(8,128)(2,1)} %get-tuple-element.30, bf16[2,256,768]{2,1,0:T(8,128)(2,1)S(1)} %copy-done.33, bf16[2,256,1536]{2,1,0:T(8,128)(2,1)S(1)} %copy-done.70, bf16[2,256,128]{2,1,0:T(8,128)(2,1)S(1)} %get-tuple-element.91, bf16[2,256,768]{2,1,0:T(8,128)(2,1)S(1)} %copy-done.29), kind=kOutput, calls=%fused_computation.8 | convolution fusion | flops 2529689600 | bytes 9764864 | tf_op jit(solution)/shard_map/bsk,dk->bsd/dot_general | solution.py:1035
  294.0 10.3 %shard_map.232 = (f32[64,16,768]{2,1,0:T(8,128)}, f32[2,16,768]{2,1,0:T(8,128)}, f32[16,768]{1,0:T(8,128)}, f32[16,768]{1,0:T(8,128)}) custom-call(f32[64,8,768]{2,1,0:T(8,128)} %bitcast.155, f32[64,8,768]{2,1,0:T(8,128)} %bitcast.153, f32[64,16,768]{2,1,0:T(8,128)} %get-tuple-element.32.S, f32[16,768]{1,0:T(8,128)} %get-tuple-element.101.rate.rate_ref), custom_call_target="tpu_custom_call" | custom-call | tf_op jit(solution)/shard_map/pallas_call | solution.py:846
  305.1 14.4 %shard_map.233.A0 = f32[2,16,768]{2,1,0:T(8,128)S(1)} custom-call(f32[2,16,768]{2,1,0:T(8,128)S(1)} %copy-done.4, f32[16,768]{1,0:T(8,128)S(1)} %copy-done.1), custom_call_target="tpu_custom_call" | custom-call | tf_op jit(solution)/shard_map/pallas_call | solution.py:883
  320.2 12.3 %shard_map.234 = (f32[16,768]{1,0:T(8,128)}, f32[64,8,768]{2,1,0:T(8,128)}) custom-call(f32[64,8,768]{2,1,0:T(8,128)} %bitcast.156, f32[64,8,768]{2,1,0:T(8,128)} %bitcast.154, f32[64,16,768]{2,1,0:T(8,128)} %get-tuple-element.32.S, f32[64,16,768]{2,1,0:T(8,128)} %get-tuple-element.33.A, f32[2,16,768]{2,1,0:T(8,128)} %copy-done.2, ...), custom_call_target="tpu_custom_call" | custom-call | tf_op jit(solution)/shard_map/pallas_call | solution.py:851
  332.6 4.9 fusion.52
  339.8 3.1 bitcast_convert_fusion.3
  347.7 3.7 bitcast_convert_fusion
  351.4 2.5 pad_maximum_fusion.pb_ref
  353.9 8.7 %fusion.5.pa_ref = bf16[768,6400]{1,0:T(8,128)(2,1)} fusion(bf16[768,1536]{1,0:T(8,128)(2,1)S(1)} %bitcast_convert_fusion.3, bf16[768,1536]{1,0:T(8,128)(2,1)S(1)} %bitcast_convert_fusion.4, bf16[768,3200]{1,0:T(8,128)(2,1)S(1)} %bitcast_convert_fusion), kind=kLoop, calls=%fused_computation.6 | loop fusion | flops 49152000 | bytes 19464192 | tf_op jit(solution)/shard_map/concatenate | solution.py:1057
  362.6 102.5 %shard_map.235 = (f32[24,6400]{1,0:T(8,128)}, f32[48,1536]{1,0:T(8,128)}) custom-call(bf16[768,6400]{1,0:T(8,128)(2,1)} %fusion.5.pa_ref, bf16[1536,1536]{1,0:T(8,128)(2,1)} %pad_maximum_fusion.pb_ref), custom_call_target="tpu_custom_call" | custom-call | tf_op jit(solution)/shard_map/pallas_call | solution.py:692
  470.4 2.6 pad_maximum_fusion.6
  473.0 36.9 %all-reduce.5 = (f32[3,128]{1,0:T(4,128)}, f32[4]{0:T(128)S(1)}) all-reduce(f32[3,128]{1,0:T(4,128)S(1)} %pad_maximum_fusion.5, f32[4]{0:T(128)S(1)} %pad_maximum_fusion.6), channel_id=1, replica_groups=mesh['dp'=4,'seq'=8] {'dp','seq'}, use_global_device_ids=true, to_apply=%region_14.15 | all-reduce | flops 388 | bytes 3104 | tf_op jit(solution)/shard_map/psum | solution.py:1072
  511.2 3.7 fusion.51
  (216 shorter events, 44.2 us)
Async XLA Ops:
  7.2 77.8 %copy-start.65 = (bf16[3,128]{1,0:T(4,128)(2,1)S(1)}, bf16[3,128]{1,0:T(4,128)(2,1)}, u32[]{:S(2)}) copy-start(bf16[3,128]{1,0:T(4,128)(2,1)} %param.25) | copy-start | bytes 2308
  7.2 77.8 %copy-start.7 = (bf16[2,256,768]{2,1,0:T(8,128)(2,1)S(1)}, bf16[2,256,768]{2,1,0:T(8,128)(2,1)}, u32[]{:S(2)}) copy-start(bf16[2,256,768]{2,1,0:T(8,128)(2,1)} %param.13) | copy-start | bytes 2359300
  7.2 508.2 %all-reduce.8.cloned.1.call-start = ((), (), s32[]{:S(2)}) async-start(), calls=%async_computation | async-start | bytes 786432
  85.0 148.0 %copy-start.55 = (f32[128]{0:T(128)}, f32[128]{0:T(128)S(1)}, u32[]{:S(2)}) copy-start(f32[128]{0:T(128)S(1)} %get-tuple-element.107) | copy-start | bytes 1540
  85.0 148.0 %copy-start.57 = (f32[128]{0:T(128)}, f32[128]{0:T(128)S(1)}, u32[]{:S(2)}) copy-start(f32[128]{0:T(128)S(1)} %get-tuple-element.109) | copy-start | bytes 1540
  85.2 139.2 %copy-start.46 = (f32[2,256]{1,0:T(2,128)}, f32[2,256]{1,0:T(2,128)S(1)}, u32[]{:S(2)}) copy-start(f32[2,256]{1,0:T(2,128)S(1)} %add_rsqrt_fusion.1) | copy-start | bytes 6148
  85.3 6.7 %copy-start = (f32[16,768]{1,0:T(8,128)S(1)}, f32[16,768]{1,0:T(8,128)}, u32[]{:S(2)}) copy-start(f32[16,768]{1,0:T(8,128)} %get-tuple-element.101.rate.rate_ref) | copy-start | bytes 147460
  107.9 122.3 %copy-start.30 = (bf16[2,256,768]{2,1,0:T(8,128)(2,1)}, bf16[2,256,768]{2,1,0:T(8,128)(2,1)S(1)}, u32[]{:S(2)}) copy-start(bf16[2,256,768]{2,1,0:T(8,128)(2,1)S(1)} %fusion.60) | copy-start | bytes 2359300
  224.5 5.7 %copy-start.66 = (bf16[768,6400]{1,0:T(8,128)(2,1)S(1)}, bf16[768,6400]{1,0:T(8,128)(2,1)}, u32[]{:S(2)}) copy-start(bf16[768,6400]{1,0:T(8,128)(2,1)} %get-tuple-element.30) | copy-start | bytes 29491204
  236.8 7.9 %slice-start = ((s8[6553600]{0:T(1024)(128)(4,1)}), s8[2359296]{0:T(1024)(128)(4,1)S(1)}, s32[]{:S(2)}) async-start(s8[6553600]{0:T(1024)(128)(4,1)} %bitcast.157), calls=%async_computation.1 | async-start | bytes 4718592
  240.8 12.9 %slice-start.2 = ((s8[4718592]{0:T(1024)(128)(4,1)}), s8[4194304]{0:T(1024)(128)(4,1)S(1)}, s32[]{:S(2)}) async-start(s8[4718592]{0:T(1024)(128)(4,1)} %bitcast.177), calls=%async_computation.3 | async-start | bytes 8388608
  244.8 8.8 %slice-start.3 = ((s8[4718592]{0:T(1024)(128)(4,1)}), s8[524288]{0:T(1024)(128)(4,1)S(1)}, s32[]{:S(2)}) async-start(s8[4718592]{0:T(1024)(128)(4,1)} %bitcast.177), calls=%async_computation.4 | async-start | bytes 1048576
  249.4 14.1 %copy-start.15 = (f32[2,256,768]{2,1,0:T(8,128)}, f32[2,256,768]{2,1,0:T(8,128)S(1)}, u32[]{:S(2)}) copy-start(f32[2,256,768]{2,1,0:T(8,128)S(1)} %get-tuple-element.88) | copy-start | bytes 4718596
  249.4 16.3 %copy-start.11 = (f32[2,256,768]{2,1,0:T(8,128)}, f32[2,256,768]{2,1,0:T(8,128)S(1)}, u32[]{:S(2)}) copy-start(f32[2,256,768]{2,1,0:T(8,128)S(1)} %get-tuple-element.114) | copy-start | bytes 4718596
  249.4 14.1 %copy-start.53 = (f32[2,256]{1,0:T(2,128)}, f32[2,256]{1,0:T(2,128)S(1)}, u32[]{:S(2)}) copy-start(f32[2,256]{1,0:T(2,128)S(1)} %add_rsqrt_fusion) | copy-start | bytes 6148
  249.5 14.0 %copy-start.48 = (f32[2,256]{1,0:T(2,128)}, f32[2,256]{1,0:T(2,128)S(1)}, u32[]{:S(2)}) copy-start(f32[2,256]{1,0:T(2,128)S(1)} %compare_convert_fusion.1) | copy-start | bytes 6148
  253.7 5.6 %copy-start.67 = (f32[2,256,1536]{2,1,0:T(8,128)}, f32[2,256,1536]{2,1,0:T(8,128)S(1)}, u32[]{:S(2)}) copy-start(f32[2,256,1536]{2,1,0:T(8,128)S(1)} %fusion.27) | copy-start | bytes 9437188
  281.5 5.4 %copy-start.29 = (bf16[2,256,768]{2,1,0:T(8,128)(2,1)S(1)}, bf16[2,256,768]{2,1,0:T(8,128)(2,1)}, u32[]{:S(2)}) copy-start(bf16[2,256,768]{2,1,0:T(8,128)(2,1)} %get-tuple-element.85) | copy-start | bytes 2359300
  281.5 5.4 %copy-start.33 = (bf16[2,256,768]{2,1,0:T(8,128)(2,1)S(1)}, bf16[2,256,768]{2,1,0:T(8,128)(2,1)}, u32[]{:S(2)}) copy-start(bf16[2,256,768]{2,1,0:T(8,128)(2,1)} %copy-done.32) | copy-start | bytes 2359300
  281.5 5.4 %copy-start.70 = (bf16[2,256,1536]{2,1,0:T(8,128)(2,1)S(1)}, bf16[2,256,1536]{2,1,0:T(8,128)(2,1)}, u32[]{:S(2)}) copy-start(bf16[2,256,1536]{2,1,0:T(8,128)(2,1)} %get-tuple-element.90) | copy-start | bytes 4718596
  286.9 5.4 %copy-start.14 = (f32[64,8,768]{2,1,0:T(8,128)S(1)}, f32[64,8,768]{2,1,0:T(8,128)}, u32[]{:S(2)}) copy-start(f32[64,8,768]{2,1,0:T(8,128)} %get-tuple-element.29) | copy-start | bytes 4718596
  294.0 10.3 %copy-start.1 = (f32[16,768]{1,0:T(8,128)S(1)}, f32[16,768]{1,0:T(8,128)}, u32[]{:S(2)}) copy-start(f32[16,768]{1,0:T(8,128)} %get-tuple-element.101.rate.rate_ref) | copy-start | bytes 147460
  320.2 12.3 %copy-start.6 = (f32[2,256,768]{2,1,0:T(8,128)S(1)}, f32[2,256,768]{2,1,0:T(8,128)}, u32[]{:S(2)}) copy-start(f32[2,256,768]{2,1,0:T(8,128)} %fusion.63) | copy-start | bytes 4718596
  320.2 12.3 %copy-start.12 = (f32[2,256,768]{2,1,0:T(8,128)S(1)}, f32[2,256,768]{2,1,0:T(8,128)}, u32[]{:S(2)}) copy-start(f32[2,256,768]{2,1,0:T(8,128)} %copy-done.11) | copy-start | bytes 4718596
  320.2 12.3 %copy-start.47 = (f32[2,256]{1,0:T(2,128)S(1)}, f32[2,256]{1,0:T(2,128)}, u32[]{:S(2)}) copy-start(f32[2,256]{1,0:T(2,128)} %copy-done.46) | copy-start | bytes 6148
  320.2 12.3 %copy-start.49 = (f32[2,256]{1,0:T(2,128)S(1)}, f32[2,256]{1,0:T(2,128)}, u32[]{:S(2)}) copy-start(f32[2,256]{1,0:T(2,128)} %copy-done.48) | copy-start | bytes 6148
  320.2 12.4 %copy-start.52 = (f32[768]{0:T(1024)S(1)}, f32[768]{0:T(1024)}, u32[]{:S(2)}) copy-start(f32[768]{0:T(1024)} %get-tuple-element.79) | copy-start | bytes 9220
  332.6 5.8 %copy-start.61 = (s32[256]{0:T(256)S(1)}, s32[256]{0:T(256)}, u32[]{:S(2)}) copy-start(s32[256]{0:T(256)} %iota_add_fusion) | copy-start | bytes 3076
  332.6 7.2 %copy-start.16 = (f32[2,256,768]{2,1,0:T(8,128)S(1)}, f32[2,256,768]{2,1,0:T(8,128)}, u32[]{:S(2)}) copy-start(f32[2,256,768]{2,1,0:T(8,128)} %copy-done.15) | copy-start | bytes 4718596
  332.6 7.2 %copy-start.51 = (f32[768]{0:T(1024)S(1)}, f32[768]{0:T(1024)}, u32[]{:S(2)}) copy-start(f32[768]{0:T(1024)} %get-tuple-element.80) | copy-start | bytes 9220
  332.6 7.1 %copy-start.54 = (f32[2,256]{1,0:T(2,128)S(1)}, f32[2,256]{1,0:T(2,128)}, u32[]{:S(2)}) copy-start(f32[2,256]{1,0:T(2,128)} %copy-done.53) | copy-start | bytes 6148
  465.1 46.0 %copy-start.10 = (f32[2,256,768]{2,1,0:T(8,128)S(1)}, f32[2,256,768]{2,1,0:T(8,128)}, u32[]{:S(2)}) copy-start(f32[2,256,768]{2,1,0:T(8,128)} %copy-done.9) | copy-start | bytes 4718596
  (45 other events, 128.0 us)
Sparse Core Ops, SparseCore 0:
  338.5 125.2 all-reduce.7

commit v2 on v1

--- a/solution.py
+++ b/solution.py
@@ -885,173 +885,434 @@
         scratch_shapes=[pltpu.VMEM((3,) + e.shape, f32), pltpu.VMEM((3,) + e.shape, f32), pltpu.SemaphoreType.DMA((3,)), pltpu.SemaphoreType.DMA((3,))],
         compiler_params=pltpu.CompilerParams(collective_id=cid, has_side_effects=True, vmem_limit_bytes=40 * 2**20))(e, rate)
 
+def sigmoid(v): return jax.nn.sigmoid(v)
+def dot(a, b): return jnp.dot(a, b, preferred_element_type=f32)
+def dot_nt(a, b): return lax.dot_general(a, b, (((1,), (1,)), ((), ())), preferred_element_type=f32)
+def dot_tn(a, b): return lax.dot_general(a, b, (((0,), (0,)), ((), ())), preferred_element_type=f32)
+def loop(n, f, unroll=1):
+    def body(i, _):
+        f(i); return 0
+    lax.fori_loop(0, n, body, 0, unroll=unroll)
+def ds(i, n): return pl.ds(pl.multiple_of(i * n, n), n)
+def silu_and_slope(v):
+    s = sigmoid(v)
+    y = v * s
+    return y, s + y * (1.0 - s)
+
+class Params:
+    def __init__(s, pos, ref, PRM, ss, rs):
+        s.p, s.ref, s.PRM, s.ss, s.rs = pos, ref, PRM, ss, rs
+    def r(s, row, n): return s.PRM.at[pl.ds(pl.multiple_of(row, 8), n), :]
+    def cp(s, k, src, dst, dev, kr=None):
+        return rcopy(src, dst, s.ss.at[k], s.rs.at[k if kr is None else kr], dev)
+    def y0(s):
+        p = s.p; row = (p.dp * 4 + p.z) * 48 + p.y * 24
+        s.cp(0, s.ref, s.r(row, 24), p.yn).start()
+        s.PRM[pl.ds(pl.multiple_of(row, 8), 24), :] = s.ref[...]
+    def y1(s):
+        p = s.p
+        l = s.r((p.dp * 4 + p.z) * 48, 24)
+        s.cp(0, l, l, p.yn).wait()
+    def z0(s):
+        p = s.p; u = s.r((p.dp * 4 + p.z) * 48, 48)
+        @pl.when(p.z < 3)
+        def _(): s.cp(1, u, u, p.up, 1 + p.z).start()
+        @pl.when(p.z > 0)
+        def _(): s.cp(2, u, u, p.dn, 1 + p.z).start()
+    def zhop(s, h):
+        p = s.p
+        @pl.when(p.z >= h)
+        def _():
+            u = s.r((p.dp * 4 + p.z - h) * 48, 48)
+            s.cp(1, u, u, p.up, 1 + p.z - h).wait_recv()
+            @pl.when(p.z < 3)
+            def _(): s.cp(2 + h, u, u, p.up, 1 + p.z - h).start()
+        @pl.when(p.z + h <= 3)
+        def _():
+            u = s.r((p.dp * 4 + p.z + h) * 48, 48)
+            s.cp(1, u, u, p.up, 1 + p.z + h).wait_recv()
+            @pl.when(p.z > 0)
+            def _(): s.cp(4 + h, u, u, p.dn, 1 + p.z + h).start()
+    def x0(s):
+        p = s.p; u = s.r(p.dp * 192, 192)
+        s.cp(7, u, u, p.xn).start()
+        s.cp(8, u, u, p.sib).start()
+    def x1(s):
+        p = s.p; u = s.r(p.dpx * 192, 192)
+        s.cp(7, u, u, p.xn).wait_recv()
+        s.cp(9, u, u, p.sib).start()
+    def end(s):
+        p = s.p; u = s.r(p.dp * 192, 192)
+        s.cp(8, u, u, p.sib).wait_recv()
+        s.cp(9, u, u, p.sib).wait_recv()
+    def drain(s):
+        p = s.p; u = s.r(p.dp * 192, 192); u1 = s.r(p.dp * 192, 48)
+        for k in (7, 8, 9): s.cp(k, u, u, p.sib).wait_send()
+        w = lambda k: s.cp(k, u1, u1, p.sib).wait_send()
+        @pl.when(p.z < 3)
+        def _(): w(1)
+        @pl.when(p.z > 0)
+        def _(): w(2)
+        for h in (1, 2):
+            @pl.when((p.z >= h) & (p.z < 3))
+            def _(): w(2 + h)
+            @pl.when((p.z + h <= 3) & (p.z > 0))
+            def _(): w(4 + h)
+
+class Scan:
+    def __init__(s, pos, way, rate, W, L, Z, GR, ss, rs):
+        s.p, s.way, s.rate, s.W, s.L, s.Z, s.GR, s.ss, s.rs = pos, way, rate, W, L, Z, GR, ss, rs
+    def has(s, d): return (s.p.sq + d < 8) if d > 0 else (s.p.sq + d >= 0)
+    def cp(s, k):
+        d = s.way * 2 ** k
+        return rcopy(s.W.at[k], s.L.at[k], s.ss.at[k], s.rs.at[k], (s.p.dp, jnp.clip(s.p.sq + d, 0, 7)))
+    def send(s, k):
+        @pl.when(s.has(s.way * 2 ** k))
+        def _(): s.cp(k).start()
+    def begin(s):
+        g = jnp.exp(s.rate[0:16, :] * -256.0)
+        s.GR[0] = g; s.GR[1] = g * g; s.GR[2] = g * g * g
+        s.Z[...] = jnp.zeros_like(s.Z)
+        s.send(0)
+    def step(s, k):
+        keep = lambda: (1.0, s.GR[0][None], s.GR[2][None])[k]
+        grow = lambda: (s.GR[0][None], s.GR[1][None])[k]
+        if k < 2: s.W[k + 1] = s.W[k].astype(s.W.dtype)
+        @pl.when(s.has(-s.way * 2 ** k))
+        def _():
+            s.cp(k).wait_recv()
+            s.Z[...] += keep() * s.L[k].astype(f32)
+            if k < 2: s.W[k + 1] = (s.W[k + 1].astype(f32) + grow() * s.L[k].astype(f32)).astype(s.W.dtype)
+        if k < 2: s.send(k + 1)
+    def drain(s):
+        for k in range(3):
+            @pl.when(s.has(s.way * 2 ** k))
+            def _(): s.cp(k).wait_send()
+
+def full_barrier(p):
+    bar = pltpu.get_barrier_semaphore()
+    sig = lambda d: pl.semaphore_signal(bar, inc=1, device_id=d, device_id_type=MESH)
+    sig(p.sib); sig(p.xn); sig(p.yn)
+    for d in (1, 2, 4):
+        @pl.when(p.sq + d < 8)
+        def _(): sig((p.dp, jnp.minimum(p.sq + d, 7)))
+        @pl.when(p.sq - d >= 0)
+        def _(): sig((p.dp, jnp.maximum(p.sq - d, 0)))
+    pl.semaphore_wait(bar, 3 + sum(jnp.clip(p.sq - d + 1, 0, 1) + jnp.clip(8 - d - p.sq, 0, 1) for d in (1, 2, 4)))
+
+def first_exchange_start(p, mx, va, wo, wu, wd, WB, land, s0, r0):
+    cps = {}
+    @pl.when(p.y == 0)
+    def _():
+        rcopy(va, land.at[:, pl.ds(0, 1536)], s0.at[0], r0.at[0], p.yn).start()
+        rcopy(wu, land.at[:, pl.ds(1536, 1536)], s0.at[1], r0.at[1], p.yn).start()
+    @pl.when(p.y == 1)
+    def _():
+        rcopy(mx, land, s0.at[0], r0.at[0], p.yn).start()
+    r = lambda yy: pl.ds(pl.multiple_of((p.dp * 4 + p.z) * RB + yy * 48, 48), 48)
+    for yy, (own, far) in ((0, (wo, wd)), (1, (wd, wo))):
+        @pl.when(p.y == yy)
+        def _():
+            rcopy(far, WB.at[r(yy), pl.ds((1 - yy) * HB, HB)], s0.at[2], r0.at[2], p.yn).start()
+            pltpu.make_async_copy(own, WB.at[r(yy), pl.ds(yy * HB, HB)], s0.at[3]).start()
+
+def first_exchange_end(p, mx, va, wo, wu, wd, WA, WB, land, s0, r0):
+    rows = pl.ds(pl.multiple_of((p.dp * 4 + p.z) * RA, 16), RA)
+    v1, v2 = land.at[:, pl.ds(0, 1536)], land.at[:, pl.ds(1536, 1536)]
+    put = lambda c, w, lo, hi: WA.__setitem__((rows, pl.ds(c, w)), jnp.concatenate([lo[...].astype(f32), hi[...].astype(f32)], axis=0).astype(bf16))
+    u = WB.at[pl.ds(pl.multiple_of((p.dp * 4 + p.z) * RB, 48), 48), pl.ds(0, HB)]
+    @pl.when(p.y == 0)
+    def _():
+        rcopy(mx, land, s0.at[0], r0.at[0], p.yn).wait_recv()
+        put(0, HA, mx, land)
+    @pl.when(p.y == 1)
+    def _():
+        rcopy(va, v1, s0.at[0], r0.at[0], p.yn).wait_recv()
+        rcopy(wu, v2, s0.at[1], r0.at[1], p.yn).wait_recv()
+        put(HA, 1536, v1, va)
+        put(HA + 1536, 1536, v2, wu)
+        WA[rows, pl.ds(HA + 3072, 128)] = jnp.zeros((RA, 128), bf16)
+    rcopy(u, u, s0.at[2], r0.at[2], p.yn).wait_recv()
+    pltpu.make_async_copy(u, u, s0.at[3]).wait()
+def first_exchange_drain(p, mx, va, wo, wu, wd, land, s0, r0):
+    v1 = land.at[:, pl.ds(0, 1536)]
+    @pl.when(p.y == 0)
+    def _():
+        rcopy(va, v1, s0.at[0], r0.at[0], p.yn).wait_send()
+        rcopy(wu, v1, s0.at[1], r0.at[1], p.yn).wait_send()
+    @pl.when(p.y == 1)
+    def _(): rcopy(mx, land, s0.at[0], r0.at[0], p.yn).wait_send()
+    rcopy(wo, wo, s0.at[2], r0.at[2], p.yn).wait_send()
+
+def norm_rows(tok, PT, U, NL, i):
+    x = tok[ds(i, 64), :].astype(f32)
+    r = lax.rsqrt(jnp.mean(x * x, axis=-1, keepdims=True) + EPSILON)
+    u = x * r * PT[32:33, :]
+    U[ds(i, 8), :, :] = u.reshape(8, 8, 768)
+    NL[ds(i, 64), :] = u.astype(bf16)
+
+def sub8(v):
+    return v.reshape(v.shape[0] // 8, 8, v.shape[1]).sum(axis=0)
+
+FORWARD_OUT = (("wa", (768, 2 * HA), bf16), ("wb", (1536, 2 * HB), bf16), ("vl", (512, 1536), bf16), ("vs", (512, 1536), bf16),
+    ("re", (512, 1536), bf16), ("rs", (512, 1536), bf16), ("at", (512, 1536), bf16), ("gt", (512, 1536), bf16), ("hi", (512, 1536), bf16), ("hs", (512, 1536), bf16),
+    ("uc", (512, 768), bf16), ("du", (512, 768), bf16), ("om", (512, 768), bf16), ("sh", (512, 768), bf16), ("bs", (512, 768), bf16), ("n2", (512, 768), bf16),
+    ("mi", (512, 768), f32), ("sp", (512, 128), f32), ("pr", (512, 128), f32), ("st", (64, 16, 768), f32), ("pt", (128, 768), f32), ("res", (512, 768), bf16), ("sq", (24, 768), f32))
+
+def forward_kernel(tok, valid, affine, prm, mx, va, wo, wu, wd, *refs):
+    no = len(FORWARD_OUT)
+    outs, bufs, rest = refs[:no], refs[no:2 * no], refs[2 * no:]
+    B = {name: r for (name, _, _), r in zip(FORWARD_OUT, bufs)}
+    O = {name: r for (name, _, _), r in zip(FORWARD_OUT, outs)}
+    osem = {name: i for i, (name, _, _) in enumerate(FORWARD_OUT)}
+    (PRM, land, U, NL, BL, RSF, UPD, DIR, ACC, KS, W, L, Z, GR, s0, r0, sp_, rp_, ss, rs, sx, rx, so) = rest
+    WA, WB, PT, S = B["wa"], B["wb"], B["pt"], B["st"]
+    p = Pos()
+    full_barrier(p)
+    out = lambda name: pltpu.make_async_copy(B[name], O[name], so.at[osem[name]])
+    def keep(*names):
+        for name in names: out(name).start()
+    par = Params(p, prm, PRM, sp_, rp_)
+    par.y0()
+    first_exchange_start(p, mx, va, wo, wu, wd, WB, land, s0, r0)
+    g = Gather(p, (WA, WB), ss, rs)
+    n = len(CHUNKS)
+    def link(t):
+        if t < n: g.z0(t)
+        if 0 <= t - 1 < n: g.zhop(t - 1, 1)
+        if 0 <= t - 2 < n: g.zhop(t - 2, 2)
+        if 0 <= t - 3 < n: g.zhop(t - 3, 3); g.s1(t - 3)
+        if 0 <= t - 4 < n: g.s2(t - 4)
+        if 0 <= t - 5 < n: g.s3(t - 5)
+        if 0 <= t - 6 < n: g.s4(t - 6)
+    par.y1(); par.z0()
+    first_exchange_end(p, mx, va, wo, wu, wd, WA, WB, land, s0, r0)
+    link(0); par.zhop(1)
+    link(1); par.zhop(2)
+    link(2); par.zhop(3); par.x0()
+    link(3); par.x1(); par.end()
+    for j in range(6): PT[:, j * 128:(j + 1) * 128] = PRM[j * 128:(j + 1) * 128, :].T
+    rate, ec, omega = PT.at[0:16, :], PT.at[16:32, :], PT.at[34:35, :]
+    loop(8, lambda i: norm_rows(tok, PT, U, NL, i))
+    link(4)
+    def some(lo, hi, f):
+        def body(j, _):
+            f(j); return 0
+        lax.fori_loop(lo, hi, body, 0)
+    states = lambda j: fwd_states(U, rate, S, W.at[0], j, 4)
+    some(0, 6, states)
+    sc = Scan(p, 1, PT, W, L, Z, GR, sx, rx)
+    sc.begin()
+    link(5)
+    sc.step(0); sc.step(1); sc.step(2)
+    smooth = lambda j: fwd_smooth(U, S, Z, rate, ec, omega, BL, KS, j, 2)
+    some(0, 3, smooth)
+    link(6)
+    some(3, 6, smooth)
+    def shift_rows(i):
+        y, s = silu_and_slope(BL[ds(i, 8), :, :].reshape(64, 768))
+        B["sh"][ds(i, 64), :] = y.astype(bf16)
+        B["bs"][ds(i, 64), :] = s.astype(bf16)
+    loop(8, shift_rows)
+    keep("st", "pt", "sh", "bs")
+    link(7)
+    def value(m):
+        ACC[...] = dot(NL[...], WA[:, pl.ds(pl.multiple_of(HA + m * 256, 128), 256)])
+        def rows(i):
+            y, s = silu_and_slope(ACC[ds(i, 64), :])
+            B["vl"][ds(i, 64), ds(m, 256)] = y.astype(bf16)
+            B["vs"][ds(i, 64), ds(m, 256)] = s.astype(bf16)
+        loop(8, rows)
+    some(0, 2, value)
+    def mixed(c, w=256): ACC[:, 0:w] = dot(B["sh"][...], WA[:, pl.ds(pl.multiple_of(c, 128), w)])
+    def update(m):
+        mixed(m * 256)
+        loop(8, lambda i: UPD.__setitem__((ds(i, 64), ds(m, 256)), sigmoid(ACC[ds(i, 64), :])))
+    def reset(m):
+        mixed(896 + m * 256)
+        def rows(i):
+            y, s = silu_and_slope(ACC[ds(i, 64), :])
+            RSF[ds(i, 64), ds(m, 256)] = y
+            B["re"][ds(i, 64), ds(m, 256)] = y.astype(bf16)
+            B["rs"][ds(i, 64), ds(m, 256)] = s.astype(bf16)
+        loop(8, rows)
+    def direct(m):
+        mixed(2432 + m * 256)
+        DIR[:, ds(m, 256)] = ACC[...]
+    some(0, 2, update)
+    link(8)
+    some(2, 6, value)
+    keep("vl", "vs")
+    some(2, 3, update)
+    mixed(768, 128)
+    B["sp"][...] = ACC[:, 0:128]
+    some(0, 1, reset)
+    link(9)
+    some(1, 6, reset)
+    keep("re", "rs", "sp")
+    link(10)
+    def attend(b):
+        rr = ds(b, 128)
+        s = B["sp"][rr, :]
+        s = s * sigmoid(s)
+        q = (s * affine[0:1, :] + affine[1:2, :]).astype(bf16)
+        k = (s * affine[2:3, :]).astype(bf16)
+        t = dot_nt(q, k) * Z_SCALE
+        ok = lax.broadcasted_iota(jnp.int32, (128, 128), 0) >= lax.broadcasted_iota(jnp.int32, (128, 128), 1)
+        t = jnp.where(ok, t, -1e30)
+        e = jnp.exp(t - jnp.max(t, axis=-1, keepdims=True))
+        e = e / jnp.sum(e, axis=-1, keepdims=True)
+        B["pr"][rr, :] = e
+        el = e.astype(bf16)
+        for m in range(6):
+            c = pl.ds(m * 256, 256)
+            a = dot(el, B["vl"][rr, c])
+            B["at"][rr, c] = a.astype(bf16)
+            B["gt"][rr, c] = (a * RSF[rr, c]).astype(bf16)
+    loop(4, attend)
+    some(0, 3, direct)
+    keep("pr", "at", "gt")
+    link(11)
+    link(12)
+    keep("wa", "wb")
+    SQ = B["sq"]
+    SQ[...] = jnp.zeros_like(SQ)
+    def candidate(m):
+        ACC[...] = dot(B["gt"][...], WB[:, ds(m, 256)])
+        def rows(i):
+            r, c = ds(i, 64), ds(m, 256)
+            y, s = silu_and_slope(DIR[r, c] + ACC[r, :])
+            u = UPD[r, c]
+            x = tok[r, c].astype(f32)
+            a = u * (y - x)
+            B["mi"][r, c] = x + a
+            B["uc"][r, c] = (u * s).astype(bf16)
+            B["du"][r, c] = (a * (1.0 - u)).astype(bf16)
+            B["om"][r, c] = (1.0 - u).astype(bf16)
+            SQ[8:16, c] += sub8(valid[r, :] * a * a)
+        loop(8, rows)
+    some(0, 3, candidate)
+    def second(i):
+        v = B["mi"][ds(i, 64), :]
+        r = lax.rsqrt(jnp.mean(v * v, axis=-1, keepdims=True) + EPSILON)
+        B["n2"][ds(i, 64), :] = (v * r * PT[33:34, :]).astype(bf16)
+    loop(8, second)
+    keep("mi", "uc", "du", "om", "n2")
+    def up(m):
+        ACC[...] = dot(B["n2"][...], WA[:, pl.ds(pl.multiple_of(HA + 1536 + m * 256, 128), 256)])
+        def rows(i):
+            y, s = silu_and_slope(ACC[ds(i, 64), :])
+            B["hi"][ds(i, 64), ds(m, 256)] = y.astype(bf16)
+            B["hs"][ds(i, 64), ds(m, 256)] = s.astype(bf16)
+        loop(8, rows)
+    some(0, 6, up)
+    keep("hi", "hs")
+    def down(m):
+        ACC[...] = dot(B["hi"][...], WB[:, pl.ds(pl.multiple_of(HB + m * 256, 128), 256)])
+        def rows(i):
+            r, c = ds(i, 64), ds(m, 256)
+            f = ACC[r, :]
+            o = B["mi"][r, c] + f
+            B["res"][r, c] = o.astype(bf16)
+            v = valid[r, :]
+            SQ[0:8, c] += sub8(v * o * o)
+            SQ[16:24, c] += sub8(v * f * f)
+        loop(8, rows)
+    some(0, 3, down)
+    keep("res", "sq")
+    for i in range(n): g.drain(i)
+    par.drain(); sc.drain()
+    first_exchange_drain(p, mx, va, wo, wu, wd, land, s0, r0)
+    for name, _, _ in FORWARD_OUT: out(name).wait()
+
+Z_SCALE = Z ** -0.5
+def forward_call(tok, valid, affine, prm, mx, va, wo, wu, wd):
+    n = len(CHUNKS)
+    v = pltpu.VMEM
+    D_ = pltpu.SemaphoreType.DMA
+    return pl.pallas_call(forward_kernel,
+        out_shape=tuple(jax.ShapeDtypeStruct(s, t) for _, s, t in FORWARD_OUT),
+        in_specs=[pl.BlockSpec(memory_space=pltpu.VMEM)] * 9,
+        out_specs=[pl.BlockSpec(memory_space=pl.ANY)] * len(FORWARD_OUT),
+        scratch_shapes=[v(s, t) for _, s, t in FORWARD_OUT] + [v((768, 128), f32), v((24, HA), bf16), v((64, 8, 768), f32), v((512, 768), bf16),
+            v((64, 8, 768), f32), v((512, 1536), f32), v((512, 768), f32), v((512, 768), f32), v((512, 256), f32), v((8, 128), f32),
+            v((3, 2, 16, 768), f32), v((3, 2, 16, 768), f32), v((2, 16, 768), f32), v((3, 16, 768), f32),
+            D_((4,)), D_((3,)), D_((10,)), D_((10,)), D_((n, 13)), D_((n, 13)), D_((3,)), D_((3,)), D_((len(FORWARD_OUT),))],
+        compiler_params=pltpu.CompilerParams(collective_id=0, has_side_effects=True, vmem_limit_bytes=62 * 2**20),
+    )(tok, valid, affine, prm, mx, va, wo, wu, wd)
+
 
 def per_device_tuned(tokens, cotangent, lengths, w_mx, w_value, w_out, w_up, w_down, ema_rate, ema_in, ema_out, gains, qk_affine):
-    wa = jnp.pad(jnp.concatenate([w_mx, w_value, w_up], axis=1), ((0, 0), (0, 128)))
-    wb = jnp.concatenate([w_out, w_down], axis=1)
     rate_own, in_own, out_own = (t.astype(f32) for t in (ema_rate, ema_in, ema_out))
     scale_own = jnp.sqrt(-jnp.expm1(-2.0 * rate_own))
     mine = jnp.pad(jnp.concatenate([rate_own, out_own * scale_own * in_own, gains.astype(f32)], axis=1), ((0, 0), (0, 93)))
-    small = lax.all_gather(mine, ("dp", "seq"), axis=0, tiled=True).T
-    full_a, full_b = gather_call(wa, wb)
+    seq_pos = lax.axis_index("seq") * SEQ_DEV + jnp.arange(SEQ_DEV, dtype=jnp.int32)
+    valid = (seq_pos[None, :] < lengths[:, None]).astype(f32).reshape(512, 1)
+    tok = tokens.reshape(512, D)
+    affine = jnp.pad(qk_affine.astype(f32), ((0, 5), (0, 0)))
+    kept = forward_call(tok, valid, affine, mine, w_mx, w_value, w_out, w_up, w_down)
+    K = {name: t for (name, _, _), t in zip(FORWARD_OUT, kept)}
+    full_a, full_b = K["wa"], K["wb"]
+    small = K["pt"]
     rate, coef = small[:16], small[16:32]
     gain_first, gain_second, omega_gain = small[32], small[33], small[34]
     mx_full, value_full, up_full = full_a[:, :3200], full_a[:, 3200:4736], full_a[:, 4736:6272]
     out_full, down_full = full_b[:, :768], full_b[:, 768:]
-    affine = qk_affine.astype(f32)
-    rows_here = tokens.shape[0]
-    spans_dev = SEQ_DEV // SPAN
-    score_scale = Z ** (-0.5)
-    inputs = tokens.astype(f32)
-    seq_pos = lax.axis_index("seq") * SEQ_DEV + jnp.arange(SEQ_DEV, dtype=jnp.int32)
-    valid_rows = (seq_pos[None, :] < lengths[:, None]).astype(f32)[:, :, None]
+    inputs = tok.astype(f32)
     inverse1 = lax.rsqrt(jnp.mean(inputs * inputs, axis=-1, keepdims=True) + EPSILON)
     unit1 = inputs * inverse1
     normed = unit1 * gain_first
     normed_low = normed.astype(bf16)
     u3 = normed.reshape(64, 8, D)
-    states, ends = ema1(u3, rate, 4)
-    start_state = scan_call(ends, rate, 1, 2)
-    states, blend3 = ema2(u3, states, start_state, rate, coef, omega_gain[None], 2)
-    blend = blend3.reshape(normed.shape)
-    value_pre = jnp.einsum("bsd,dv->bsv", normed_low, value_full, preferred_element_type=f32)
-    value_low = jax.nn.silu(value_pre).astype(bf16)
-    shifted_low = jax.nn.silu(blend).astype(jnp.bfloat16)
-    mixed = jnp.einsum("bsd,dk->bsk", shifted_low, mx_full, preferred_element_type=jnp.float32)
-    update = jax.nn.sigmoid(mixed[..., :D])
-    shared_pre = mixed[..., D : D + Z]
-    shared = jax.nn.silu(shared_pre)
-    reset_pre = mixed[..., D + Z : D + Z + V]
-    reset = jax.nn.silu(reset_pre)
-    direct = mixed[..., D + Z + V :]
-    query_low = (
-        (shared * affine[0] + affine[1]).astype(jnp.bfloat16).reshape(rows_here, spans_dev, SPAN, Z)
-    )
-    key_low = (shared * affine[2]).astype(jnp.bfloat16).reshape(rows_here, spans_dev, SPAN, Z)
-    value_tiles = value_low.reshape(rows_here, spans_dev, SPAN, V)
-    scores = (
-        jnp.einsum("bnqz,bnkz->bnqk", query_low, key_low, preferred_element_type=jnp.float32)
-        * score_scale
-    )
-    causal = jnp.arange(SPAN)[:, None] >= jnp.arange(SPAN)[None, :]
-    masked = jnp.where(causal, scores, -1e30)
-    peak = jnp.max(masked, axis=-1, keepdims=True)
-    expo = jnp.exp(masked - peak)
-    attention_weights = expo / jnp.sum(expo, axis=-1, keepdims=True)
-    probs_low = attention_weights.astype(jnp.bfloat16)
-    attended_output = jnp.einsum(
-        "bnqk,bnkv->bnqv", probs_low, value_tiles, preferred_element_type=jnp.float32
-    ).reshape(rows_here, SEQ_DEV, V)
-    gated_low = (reset * attended_output).astype(jnp.bfloat16)
-    cand_pre = direct + jnp.einsum(
-        "bsv,vd->bsd", gated_low, out_full, preferred_element_type=jnp.float32
-    )
-    candidate = jax.nn.silu(cand_pre)
-    attn_branch = update * (candidate - inputs)
-    middle = inputs + attn_branch
+    dn = lambda a, b, ca, cb: lax.dot_general(a, b, (((ca,), (cb,)), ((), ())), preferred_element_type=f32)
+    middle = K["mi"]
     inverse2 = lax.rsqrt(jnp.mean(middle * middle, axis=-1, keepdims=True) + EPSILON)
     unit2 = middle * inverse2
-    normed2_low = (unit2 * gain_second).astype(jnp.bfloat16)
-    up_pre = jnp.einsum("bsd,df->bsf", normed2_low, up_full, preferred_element_type=jnp.float32)
-    hidden_low = jax.nn.silu(up_pre).astype(jnp.bfloat16)
-    ffn_branch = jnp.einsum(
-        "bsf,fd->bsd", hidden_low, down_full, preferred_element_type=jnp.float32
-    )
-    output = middle + ffn_branch
-    mixer_backward, value_back, out_back, up_back, down_back = mx_full, value_full, out_full, up_full, down_full
-    grad_out = cotangent.astype(jnp.float32) * valid_rows
-    grad_out_low = grad_out.astype(jnp.bfloat16)
-    grad_down = jnp.einsum(
-        "bsf,bsd->fd", hidden_low, grad_out_low, preferred_element_type=jnp.float32
-    )
-    grad_hidden = jnp.einsum(
-        "bsd,fd->bsf", grad_out_low, down_back, preferred_element_type=jnp.float32
-    )
-    grad_up_low = (grad_hidden * silu_slope(up_pre)).astype(jnp.bfloat16)
-    grad_up = jnp.einsum(
-        "bsd,bsf->df", normed2_low, grad_up_low, preferred_element_type=jnp.float32
-    )
-    grad_normed2 = jnp.einsum(
-        "bsf,df->bsd", grad_up_low, up_back, preferred_element_type=jnp.float32
-    )
-    grad_gain_second = jnp.sum(grad_normed2 * unit2, axis=(0, 1))
-    scaled2 = grad_normed2 * gain_second
-    grad_middle = grad_out + inverse2 * (
-        scaled2 - unit2 * jnp.mean(scaled2 * unit2, axis=-1, keepdims=True)
-    )
-    grad_update = grad_middle * (candidate - inputs)
-    grad_cand_pre = grad_middle * update * silu_slope(cand_pre)
-    grad_cand_low = grad_cand_pre.astype(jnp.bfloat16)
-    grad_out_proj = jnp.einsum(
-        "bsv,bsd->vd", gated_low, grad_cand_low, preferred_element_type=jnp.float32
-    )
-    grad_gated = jnp.einsum(
-        "bsd,vd->bsv", grad_cand_low, out_back, preferred_element_type=jnp.float32
-    )
-    grad_reset = grad_gated * attended_output
-    grad_attended_low = (
-        (grad_gated * reset).astype(jnp.bfloat16).reshape(rows_here, spans_dev, SPAN, V)
-    )
-    grad_probs = jnp.einsum(
-        "bnqv,bnkv->bnqk", grad_attended_low, value_tiles, preferred_element_type=jnp.float32
-    )
-    grad_values = jnp.einsum(
-        "bnqk,bnqv->bnkv", probs_low, grad_attended_low, preferred_element_type=jnp.float32
-    ).reshape(rows_here, SEQ_DEV, V)
-    grad_scores_low = (
-        attention_weights
-        * (grad_probs - jnp.sum(grad_probs * attention_weights, axis=-1, keepdims=True))
-    ).astype(jnp.bfloat16)
-    grad_query = (
-        jnp.einsum("bnqk,bnkz->bnqz", grad_scores_low, key_low, preferred_element_type=jnp.float32)
-        * score_scale
-    ).reshape(rows_here, SEQ_DEV, Z)
-    grad_key = (
-        jnp.einsum(
-            "bnqk,bnqz->bnkz", grad_scores_low, query_low, preferred_element_type=jnp.float32
-        )
-        * score_scale
-    ).reshape(rows_here, SEQ_DEV, Z)
-    grad_affine = jnp.stack(
-        [
-            jnp.sum(grad_query * shared, axis=(0, 1)),
-            jnp.sum(grad_query, axis=(0, 1)),
-            jnp.sum(grad_key * shared, axis=(0, 1)),
-        ]
-    )
-    grad_shared = grad_query * affine[0] + grad_key * affine[2]
-    grad_mixed_low = jnp.concatenate(
-        [
-            grad_update * update * (1.0 - update),
-            grad_shared * silu_slope(shared_pre),
-            grad_reset * silu_slope(reset_pre),
-            grad_cand_pre,
-        ],
-        axis=-1,
-    ).astype(jnp.bfloat16)
-    grad_mx = jnp.einsum(
-        "bsd,bsk->dk", shifted_low, grad_mixed_low, preferred_element_type=jnp.float32
-    )
-    grad_shifted = jnp.einsum(
-        "bsk,dk->bsd", grad_mixed_low, mixer_backward, preferred_element_type=jnp.float32
-    )
-    grad_blend = grad_shifted * silu_slope(blend)
-    grad_omega = jnp.sum(grad_blend * normed, axis=(0, 1))
-    grad_value_low = (grad_values * silu_slope(value_pre)).astype(jnp.bfloat16)
-    grad_value_proj = jnp.einsum(
-        "bsd,bsv->dv", normed_low, grad_value_low, preferred_element_type=jnp.float32
-    )
-    grad_normed = grad_blend * omega_gain + jnp.einsum(
-        "bsv,dv->bsd", grad_value_low, value_back, preferred_element_type=jnp.float32
-    )
+    grad_out = cotangent.reshape(512, D).astype(f32) * valid
+    g_low = grad_out.astype(bf16)
+    grad_down = dn(K["hi"], g_low, 0, 0)
+    gu_low = (dn(g_low, down_full, 1, 1) * K["hs"].astype(f32)).astype(bf16)
+    grad_up = dn(K["n2"], gu_low, 0, 0)
+    grad_n2 = dn(gu_low, up_full, 1, 1)
+    grad_gain_second = jnp.sum(grad_n2 * unit2, axis=0)
+    scaled2 = grad_n2 * gain_second
+    grad_middle = grad_out + inverse2 * (scaled2 - unit2 * jnp.mean(scaled2 * unit2, axis=-1, keepdims=True))
+    gc_low = (grad_middle * K["uc"].astype(f32)).astype(bf16)
+    grad_out_proj = dn(K["gt"], gc_low, 0, 0)
+    grad_gated = dn(gc_low, out_full, 1, 1)
+    grad_reset = grad_gated * K["at"].astype(f32)
+    go = (grad_gated * K["re"].astype(f32)).astype(bf16).reshape(4, SPAN, V)
+    vl = K["vl"].reshape(4, SPAN, V)
+    probs = K["pr"].reshape(4, SPAN, SPAN)
+    probs_low = probs.astype(bf16)
+    grad_probs = jnp.einsum("nqv,nkv->nqk", go, vl, preferred_element_type=f32)
+    grad_values = jnp.einsum("nqk,nqv->nkv", probs_low, go, preferred_element_type=f32).reshape(512, V)
+    gs = (probs * (grad_probs - jnp.sum(grad_probs * probs, axis=-1, keepdims=True))).astype(bf16)
+    shared_pre = K["sp"]
+    shared = jax.nn.silu(shared_pre)
+    ql = (shared * affine[0] + affine[1]).astype(bf16).reshape(4, SPAN, Z)
+    kl = (shared * affine[2]).astype(bf16).reshape(4, SPAN, Z)
+    gq = (jnp.einsum("nqk,nkz->nqz", gs, kl, preferred_element_type=f32) * Z_SCALE).reshape(512, Z)
+    gk = (jnp.einsum("nqk,nqz->nkz", gs, ql, preferred_element_type=f32) * Z_SCALE).reshape(512, Z)
+    grad_affine = jnp.stack([jnp.sum(gq * shared, axis=0), jnp.sum(gq, axis=0), jnp.sum(gk * shared, axis=0)])
+    grad_shared = gq * affine[0] + gk * affine[2]
+    gm_low = jnp.concatenate([(grad_middle * K["du"].astype(f32)).astype(bf16), (grad_shared * silu_slope(shared_pre)).astype(bf16),
+        (grad_reset * K["rs"].astype(f32)).astype(bf16), gc_low], axis=1)
+    grad_mx = dn(K["sh"], gm_low, 0, 0)
+    grad_blend = dn(gm_low, mx_full, 1, 1) * K["bs"].astype(f32)
+    grad_omega = jnp.sum(grad_blend * normed, axis=0)
+    gv_low = (grad_values * K["vs"].astype(f32)).astype(bf16)
+    grad_value_proj = dn(normed_low, gv_low, 0, 0)
+    grad_normed = grad_blend * omega_gain + dn(gv_low, value_full, 1, 1)
     g3 = grad_blend.reshape(64, 8, D)
+    states = K["st"]
     adj, direct, g1, h1 = emab1(g3, u3, states, rate, 2)
     later = scan_call(direct, rate, -1, 3)
     h1, du3 = emab2(g3, u3, states, adj, later, rate, coef, h1, 2)
     grad_normed = grad_normed + du3.reshape(normed.shape)
-    grad_gain_first = jnp.sum(grad_normed * unit1, axis=(0, 1))
+    grad_gain_first = jnp.sum(grad_normed * unit1, axis=0)
     scaled1 = grad_normed * gain_first
-    grad_tokens = grad_middle * (1.0 - update) + inverse1 * (
+    grad_tokens = grad_middle * K["om"].astype(f32) + inverse1 * (
         scaled1 - unit1 * jnp.mean(scaled1 * unit1, axis=-1, keepdims=True)
     )
     pa = jnp.pad(jnp.concatenate([grad_mx, grad_value_proj, grad_up], axis=1).astype(bf16), ((0, 0), (0, 128)))
@@ -1063,15 +1324,10 @@
     grad_ema_out = in_own * scale_own * g1
     grad_ema_in = out_own * scale_own * g1
     grad_ema_rate = out_own * in_own * (jnp.exp(-2.0 * rate_own) / scale_own * g1 - scale_own * h1)
-    squares = jnp.stack([
-        jnp.sum(valid_rows * output * output),
-        jnp.sum(valid_rows * attn_branch * attn_branch),
-        jnp.sum(valid_rows * ffn_branch * ffn_branch),
-        jnp.sum(valid_rows),
-    ])
+    squares = jnp.append(jnp.sum(K["sq"].reshape(3, -1), axis=1), jnp.sum(valid))
     affine_total, square_total = lax.psum((grad_affine, squares), ("dp", "seq"))
     rms_values = jnp.sqrt(square_total[:3] / (square_total[3] * D))
-    return (output.astype(bf16), grad_tokens, oa[:, :3200], oa[:, 3200:4736], ob[:, :768], oa[:, 4736:6272], ob[:, 768:],
+    return (K["res"].reshape(tokens.shape), grad_tokens.reshape(tokens.shape), oa[:, :3200], oa[:, 3200:4736], ob[:, :768], oa[:, 4736:6272], ob[:, 768:],
         grad_ema_rate, grad_ema_in, grad_ema_out, tiny[:, 32:35], affine_total, rms_values)
 
 

time: 532 us -> 412 us (0.77)
  blocking collectives: 109 us -> 38.3 us
  matrix products: 59.1 us -> 39 us
  other arithmetic: 45.4 us -> 29.1 us
  Pallas kernels: 272 us -> 264 us
    all_gather x1 -> x0, blocking collectives: 71.8 us -> none  [per_device_tuned(): small = lax.all_gather(mine, ('dp', 'seq'), axis=0, tiled=True).T]
    dot_general x21 -> x14, matrix products: 59.1 us -> 39 us  [the longest x10 35.8 us: per_device_tuned(): lax.dot_general(a, b, (((ca,), (cb,)), ((), ())), preferred_element_type=...]
    pallas_call x3 -> x1, Pallas kernels: 130 us -> 119 us  [forward_call(): pl.pallas_call(forward_kernel, out_shape=tuple((jax.ShapeDtypeStruct(s, t...]
    convert_element_type x8 -> x7, other arithmetic: 10.8 us -> 6.38 us  [the longest x1 3.48 us: per_device_tuned(): (grad_middle * K['du'].astype(f32)).astype(bf16)]
    pallas_call x2 -> x1, Pallas kernels: 17.7 us -> 21.5 us  [scan_call(): pl.pallas_call(functools.partial(scan_kernel, way), out_shape=jax.ShapeDt...]
    unnamed x160 -> x91, local copies, waits for them, and re-layouts: 13.6 us -> 11.8 us
  transfers between devices with their start and end apart: 1 -> 1, of which waited for: 0 -> 0; matrix products, arithmetic and copies ran while one was open for 7% -> 8% of each run, Pallas kernels for 19% -> 24%
where the time goes in v2:
time: 412 us; the launch traced here: 411 us
  Pallas kernels  264 us (64%)
  matrix products  39 us (9%)
  blocking collectives  38.3 us (9%)
  other arithmetic  29.1 us (7%)
  local copies, waits for them, and re-layouts  25.3 us (6%)
  between operations  15.2 us (4%)
    pallas_call x1, Pallas kernels, forward_call(): pl.pallas_call(forward_kernel, out_shape=tuple((jax.ShapeDtypeStruct(s, t...  119 us
    pallas_call x1, Pallas kernels, scatter_call(): pl.pallas_call(rs_kernel, out_shape=(jax.ShapeDtypeStruct((24, 2 * HA), f...  101 us
    psum x1, blocking collectives, per_device_tuned(): affine_total, square_total = lax.psum((grad_affine, squares), ('dp', 'seq'))  38.3 us
    dot_general x10, matrix products, per_device_tuned(): lax.dot_general(a, b, (((ca,), (cb,)), ((), ())), preferred_element_type=...  35.8 us
    pallas_call x1, Pallas kernels, scan_call(): pl.pallas_call(functools.partial(scan_kernel, way), out_shape=jax.ShapeDt...  21.5 us
    pallas_call x1, Pallas kernels, emab2(): pl.pallas_call(k, out_shape=(SH((16, 768), f32), SH((64, 8, 768), f32)),...  12.3 us
    unnamed x91, local copies, waits for them, and re-layouts  11.8 us
    pallas_call x1, Pallas kernels, emab1(): pl.pallas_call(k, out_shape=(SH((64, 16, 768), f32), SH((2, 16, 768), f32...  10.4 us
  transfers between devices with their start and end apart: 1, of which 0 were waited for; matrix products, arithmetic and copies ran while one was open for 8% of the time, Pallas kernels for 24%

profile of v2, /device:TPU:0, one launch (start us, length us, event | category | flops | bytes accessed | tf_op | source)
XLA Modules:
  0.0 411.3 jit_solution(5685859963396013)
XLA Ops:
  13.9 1.4 multiply_reduce_fusion.4
  15.9 119.5 %shard_map.228 = (bf16[768,6400]{1,0:T(8,128)(2,1)}, bf16[1536,1536]{1,0:T(8,128)(2,1)}, bf16[512,1536]{1,0:T(8,128)(2,1)}, bf16[512,1536]{1,0:T(8,128)(2,1)}, b...) custom-call(bf16[512,768]{1,0:T(8,128)(2,1)} %bitcast.89, ...), custom_call_target="tpu_custom_call" | custom-call | tf_op jit(solution)/shard_map/pallas_call | solution.py:1233
  136.3 1.5 fusion.46
  137.8 1.7 multiply_reduce_fusion.6
  139.7 3.4 fusion.8
  143.2 4.9 %multiply_reduce_fusion.1 = (f32[768]{0:T(1024)S(1)}, f32[512]{0:T(512)S(1)}, f32[512,768]{1,0:T(8,128)}) fusion(f32[512,768]{1,0:T(8,128)S(1)} %copy-done.6, f32[512]{0:T(512)S(1)} %add_rsqrt_fusion.1, f32[768]{0:T(1024)S(1)} %get-tuple-element.95, bf16[512,1536]{1,0:T(8,128)(2,1)S(1)} %fusion.8, bf16[768,6400]{1,0:T(8,128)(2,1)} %get-tuple-element.48), kind=kOutput, calls=%fused_computation.33 | convolution fusion | flops 1210317568 | bytes 7088128 | tf_op jit(solution)/shard_map/dot_general | solution.py:1267
  148.3 3.5 multiply_convert_fusion.3
  152.0 1.5 copy-done.29
  153.9 4.5 %multiply_convert_fusion.1 = (bf16[512,1536]{1,0:T(8,128)(2,1)S(1)}, bf16[512,1536]{1,0:T(8,128)(2,1)}) fusion(bf16[512,1536]{1,0:T(8,128)(2,1)S(1)} %copy-done.29, bf16[512,1536]{1,0:T(8,128)(2,1)S(1)} %copy-done.30, bf16[512,1536]{1,0:T(8,128)(2,1)S(1)} %copy-done.31, bf16[512,768]{1,0:T(8,128)(2,1)S(1)} %multiply_convert_fusion.2, ...), kind=kOutput, calls=%fused_computation.19 | convolution fusion | flops 1214251008 | bytes 11010048 | tf_op jit(solution)/shard_map/dot_general | solution.py:1267
  158.4 2.2 fusion.33
  162.5 1.5 multiply_multiply_fusion.U
  164.5 6.9 %convert_multiply_fusion.2 = f32[512,768]{1,0:T(8,128)} fusion(bf16[512,768]{1,0:T(8,128)(2,1)S(1)} %copy-done.35, bf16[768,6400]{1,0:T(8,128)(2,1)} %get-tuple-element.48, bf16[512,768]{1,0:T(8,128)(2,1)S(1)} %copy-done.19, bf16[512,1536]{1,0:T(8,128)(2,1)} %get-tuple-element.103, bf16[512,128]{1,0:T(8,128)(2,1)S(1)} %get-tuple-element.104, ...), kind=kOutput, calls=%fused_computation.41 | convolution fusion | flops 2530476032 | bytes 10551296 | tf_op jit(solution)/shard_map/dot_general | solution.py:1267
  171.3 10.4 %shard_map.229 = (f32[64,16,768]{2,1,0:T(8,128)}, f32[2,16,768]{2,1,0:T(8,128)}, f32[16,768]{1,0:T(8,128)}, f32[16,768]{1,0:T(8,128)}) custom-call(f32[64,8,768]{2,1,0:T(8,128)} %bitcast.92, f32[64,8,768]{2,1,0:T(8,128)} %multiply_multiply_fusion.U, f32[64,16,768]{2,1,0:T(8,128)} %get-tuple-element.61.S, f32[16,768]{1,0:T(8,128)} %get-tuple-element.110.rate.rate_ref), custom_call_target="tpu_custom_call" | custom-call | tf_op jit(solution)/shard_map/pallas_call | solution.py:846
  182.6 21.5 %shard_map.230.A0 = f32[2,16,768]{2,1,0:T(8,128)S(1)} custom-call(f32[2,16,768]{2,1,0:T(8,128)S(1)} %copy-done.2, f32[16,768]{1,0:T(8,128)S(1)} %copy-done), custom_call_target="tpu_custom_call" | custom-call | tf_op jit(solution)/shard_map/pallas_call | solution.py:883
  204.2 1.6 fusion.7
  205.8 12.3 %shard_map.231 = (f32[16,768]{1,0:T(8,128)}, f32[64,8,768]{2,1,0:T(8,128)}) custom-call(f32[64,8,768]{2,1,0:T(8,128)} %bitcast.93, f32[64,8,768]{2,1,0:T(8,128)} %multiply_multiply_fusion.U, f32[64,16,768]{2,1,0:T(8,128)} %get-tuple-element.61.S, f32[64,16,768]{2,1,0:T(8,128)} %get-tuple-element.62.A, f32[2,16,768]{2,1,0:T(8,128)} %copy-done.1, ...), custom_call_target="tpu_custom_call" | custom-call | tf_op jit(solution)/shard_map/pallas_call | solution.py:851
  218.2 5.1 %multiply_reduce_fusion.2 = (f32[768]{0:T(1024)S(1)}, f32[512]{0:T(512)S(1)}, f32[768]{0:T(1024)S(1)}, f32[512,768]{1,0:T(8,128)}) fusion(f32[512]{0:T(512)S(1)} %bitcast.107, bf16[2,256,768]{2,1,0:T(8,128)(2,1)S(1)} %copy-done.4, f32[768]{0:T(1024)S(1)} %get-tuple-element.94, f32[512,768]{1,0:T(8,128)S(1)} %copy-done.5, ...), kind=kOutput, calls=%fused_computation.34 | convolution fusion | flops 1213069312 | bytes 9453568 | tf_op jit(solution)/shard_map/dot_general | solution.py:1267
  224.8 3.1 convolution_convert_fusion.4
  228.0 1.4 convolution_convert_fusion.2
  229.6 1.4 convolution_convert_fusion.1
  231.5 3.6 convolution_convert_fusion
  235.2 1.4 convolution_convert_fusion.3
  236.6 2.6 pad_maximum_fusion.pb_ref
  239.2 8.7 %fusion.4.pa_ref = bf16[768,6400]{1,0:T(8,128)(2,1)} fusion(bf16[768,1536]{1,0:T(8,128)(2,1)S(1)} %convolution_convert_fusion.3, bf16[768,1536]{1,0:T(8,128)(2,1)S(1)} %convolution_convert_fusion.4, bf16[768,3200]{1,0:T(8,128)(2,1)S(1)} %convolution_convert_fusion), kind=kLoop, calls=%fused_computation.5 | loop fusion | flops 49152000 | bytes 19464192 | tf_op jit(solution)/shard_map/concatenate | solution.py:1318
  248.0 100.7 %shard_map.232 = (f32[24,6400]{1,0:T(8,128)}, f32[48,1536]{1,0:T(8,128)}) custom-call(bf16[768,6400]{1,0:T(8,128)(2,1)} %fusion.4.pa_ref, bf16[1536,1536]{1,0:T(8,128)(2,1)} %pad_maximum_fusion.pb_ref), custom_call_target="tpu_custom_call" | custom-call | tf_op jit(solution)/shard_map/pallas_call | solution.py:692
  348.7 1.8 slice.87
  350.4 1.7 fusion.45
  353.2 38.3 %all-reduce.5 = (f32[3,128]{1,0:T(4,128)}, f32[4]{0:T(128)S(1)}) all-reduce(f32[3,128]{1,0:T(4,128)S(1)} %pad_maximum_fusion.4, f32[4]{0:T(128)S(1)} %pad_maximum_fusion.5), channel_id=1, replica_groups=mesh['dp'=4,'seq'=8] {'dp','seq'}, use_global_device_ids=true, to_apply=%region_12.13 | all-reduce | flops 388 | bytes 3104 | tf_op jit(solution)/shard_map/psum | solution.py:1328
  392.1 1.7 fusion.47
  394.5 3.1 multiply_add_fusion
  401.1 1.4 dynamic-slice.3
  402.4 2.1 copy.70
  (131 shorter events, 19.9 us)
Async XLA Ops:
  7.2 390.9 %all-reduce.8.cloned.1.call-start = ((), (), s32[]{:S(2)}) async-start(), calls=%async_computation | async-start | bytes 786432
  15.9 123.5 %copy-start.7 = (bf16[2,256,768]{2,1,0:T(8,128)(2,1)S(1)}, bf16[2,256,768]{2,1,0:T(8,128)(2,1)}, u32[]{:S(2)}) copy-start(bf16[2,256,768]{2,1,0:T(8,128)(2,1)} %param.14) | copy-start | bytes 2359300
  137.8 2.0 copy-start.32
  139.7 3.4 copy-start.16
  139.7 3.4 copy-start.6
  143.2 4.9 %copy-start.37 = (bf16[512,1536]{1,0:T(8,128)(2,1)}, bf16[512,1536]{1,0:T(8,128)(2,1)S(1)}, u32[]{:S(2)}) copy-start(bf16[512,1536]{1,0:T(8,128)(2,1)S(1)} %fusion.8) | copy-start | bytes 4718596
  143.2 4.9 %copy-start.22 = (f32[512,128]{1,0:T(8,128)S(1)}, f32[512,128]{1,0:T(8,128)}, u32[]{:S(2)}) copy-start(f32[512,128]{1,0:T(8,128)} %get-tuple-element.52) | copy-start | bytes 786436
  148.2 3.5 copy-start.21
  148.2 3.7 copy-start.31
  151.7 1.7 copy-start.29
  151.7 2.2 copy-start.30
  151.9 6.5 %copy-start.18 = (bf16[512,768]{1,0:T(8,128)(2,1)}, bf16[512,768]{1,0:T(8,128)(2,1)S(1)}, u32[]{:S(2)}) copy-start(bf16[512,768]{1,0:T(8,128)(2,1)S(1)} %multiply_convert_fusion.2) | copy-start | bytes 2359300
  158.4 2.2 copy-start.8
  162.2 1.7 copy-start.14
  162.2 1.7 copy-start.19
  162.3 2.2 copy-start.35
  171.3 10.4 %copy-start = (f32[16,768]{1,0:T(8,128)S(1)}, f32[16,768]{1,0:T(8,128)}, u32[]{:S(2)}) copy-start(f32[16,768]{1,0:T(8,128)} %get-tuple-element.110.rate.rate_ref) | copy-start | bytes 147460
  171.3 32.8 %copy-start.3 = (f32[4,128,1536]{2,1,0:T(8,128)S(1)}, f32[4,128,1536]{2,1,0:T(8,128)}, u32[]{:S(2)}) copy-start(f32[4,128,1536]{2,1,0:T(8,128)} %fusion.33) | copy-start | bytes 9437188
  171.3 32.8 %copy-start.9 = (bf16[512,1536]{1,0:T(8,128)(2,1)S(1)}, bf16[512,1536]{1,0:T(8,128)(2,1)}, u32[]{:S(2)}) copy-start(bf16[512,1536]{1,0:T(8,128)(2,1)} %get-tuple-element.60) | copy-start | bytes 4718596
  204.1 1.7 copy-start.1
  205.8 12.4 %copy-start.5 = (f32[512,768]{1,0:T(8,128)S(1)}, f32[512,768]{1,0:T(8,128)}, u32[]{:S(2)}) copy-start(f32[512,768]{1,0:T(8,128)} %convert_multiply_fusion.2) | copy-start | bytes 4718596
  205.8 12.4 %copy-start.10 = (bf16[512,1536]{1,0:T(8,128)(2,1)S(1)}, bf16[512,1536]{1,0:T(8,128)(2,1)}, u32[]{:S(2)}) copy-start(bf16[512,1536]{1,0:T(8,128)(2,1)} %fusion.7) | copy-start | bytes 4718596
  218.2 5.1 %copy-start.24 = (f32[16,768]{1,0:T(8,128)S(1)}, f32[16,768]{1,0:T(8,128)}, u32[]{:S(2)}) copy-start(f32[16,768]{1,0:T(8,128)} %get-tuple-element.72) | copy-start | bytes 147460
  218.2 5.1 %copy-start.25 = (f32[16,768]{1,0:T(8,128)S(1)}, f32[16,768]{1,0:T(8,128)}, u32[]{:S(2)}) copy-start(f32[16,768]{1,0:T(8,128)} %get-tuple-element.73) | copy-start | bytes 147460
  218.2 6.0 %copy-start.26 = (s32[2]{0:T(128)S(1)}, s32[2]{0:T(128)}, u32[]{:S(2)}) copy-start(s32[2]{0:T(128)} %param.15) | copy-start | bytes 28
  224.8 3.1 copy-start.20
  224.8 3.1 copy-start.28
  229.6 1.9 copy-start.36
  231.5 3.7 copy-start.33
  231.5 3.7 copy-start.38
  248.0 104.2 %copy-start.23 = (f32[24,768]{1,0:T(8,128)S(1)}, f32[24,768]{1,0:T(8,128)}, u32[]{:S(2)}) copy-start(f32[24,768]{1,0:T(8,128)} %get-tuple-element.74) | copy-start | bytes 221188
  348.7 45.8 %copy-start.13 = (bf16[512,768]{1,0:T(8,128)(2,1)S(1)}, bf16[512,768]{1,0:T(8,128)(2,1)}, u32[]{:S(2)}) copy-start(bf16[512,768]{1,0:T(8,128)(2,1)} %get-tuple-element.50) | copy-start | bytes 2359300
  (8 other events, 10.1 us)
Sparse Core Ops, SparseCore 0:
  224.3 123.9 all-reduce.7

commit v3 on v2

--- a/solution.py
+++ b/solution.py
@@ -485,57 +485,6 @@
             def _(): w(1 + h)
             @pl.when((p.z + h <= 3) & (p.z > 0))
             def _(): w(10 + h)
-
-def first_exchange(pos, wa_ref, wb_ref, WA, WB, land, ss, rs):
-    p = pos
-    ca = rcopy(wa_ref.at[:, pl.ds(pl.multiple_of((1 - p.y) * HA, 128), HA)], land, ss.at[0], rs.at[0], p.yn)
-    ca.start()
-    mine = (p.dp * 4 + p.z) * RB + p.y * 48
-    other = (p.dp * 4 + p.z) * RB + (1 - p.y) * 48
-    cb = rcopy(wb_ref.at[:, pl.ds(pl.multiple_of((1 - p.y) * HB, 128), HB)], at(WB, mine, 48, 1 - p.y, HB, 0, HB), ss.at[1], rs.at[1], p.yn)
-    cb.start()
-    at_own = at(WB, mine, 48, p.y, HB, 0, HB)
-    loc = pltpu.make_async_copy(wb_ref.at[:, pl.ds(pl.multiple_of(p.y * HB, 128), HB)], at_own, ss.at[2])
-    loc.start()
-    ca.wait()
-    own = wa_ref[:, pl.ds(pl.multiple_of(p.y * HA, 128), HA)].astype(jnp.float32)
-    got = land[...].astype(jnp.float32)
-    f = (p.y == 0)
-    lo = jnp.where(f, own, got); hi = jnp.where(f, got, own)
-    WA[pl.ds(pl.multiple_of((p.dp * 4 + p.z) * RA, 16), RA), pl.ds(pl.multiple_of(p.y * HA, 128), HA)] = jnp.concatenate([lo, hi], axis=0).astype(jnp.bfloat16)
-    cb.wait(); loc.wait()
-
-def ag_kernel(wa_ref, wb_ref, oa_ref, ob_ref, WA, WB, land, s0, r0, ss, rs, osem):
-    pos = Pos()
-    barrier(pos)
-    first_exchange(pos, wa_ref, wb_ref, WA, WB, land, s0, r0)
-    g = Gather(pos, (WA, WB), ss, rs)
-    n = len(CHUNKS)
-    for i in range(n): g.z0(i)
-    for t in range(n + 3):
-        if 0 <= t - 3 < n: g.s3(t - 3)
-        if 0 <= t - 2 < n: g.s2(t - 2)
-        if t < n:
-            g.zhop(t, 1)
-            g.zhop(t, 2)
-            g.zhop(t, 3)
-            g.s1(t)
-    for i in range(n): g.s4(i)
-    for i in range(n): g.drain(i)
-    a = pltpu.make_async_copy(WA, oa_ref, osem.at[0]); b = pltpu.make_async_copy(WB, ob_ref, osem.at[1])
-    a.start(); b.start(); a.wait(); b.wait()
-
-def gather_call(wa, wb):
-    n = len(CHUNKS)
-    return pl.pallas_call(
-        ag_kernel,
-        out_shape=(jax.ShapeDtypeStruct((768, 2 * HA), jnp.bfloat16), jax.ShapeDtypeStruct((1536, 2 * HB), jnp.bfloat16)),
-        in_specs=[pl.BlockSpec(memory_space=pltpu.VMEM)] * 2,
-        out_specs=[pl.BlockSpec(memory_space=pl.ANY)] * 2,
-        scratch_shapes=[pltpu.VMEM((768, 2 * HA), jnp.bfloat16), pltpu.VMEM((1536, 2 * HB), jnp.bfloat16), pltpu.VMEM((24, HA), jnp.bfloat16),
-            pltpu.SemaphoreType.DMA((3,)), pltpu.SemaphoreType.DMA((3,)), pltpu.SemaphoreType.DMA((n, 13)), pltpu.SemaphoreType.DMA((n, 13)), pltpu.SemaphoreType.DMA((2,))],
-        compiler_params=pltpu.CompilerParams(collective_id=0, has_side_effects=True, vmem_limit_bytes=60 * 2**20),
-    )(wa, wb)
 
 
 class Scatter:
@@ -633,7 +582,7 @@
         u = s.own(i, p.z)
         hu, hd = (p.z > 0), (p.z < 3)
         lu, ld = s.l4(i, 0, p.z), s.l4(i, 1, p.z)
-        F, G, out = s.F[b], s.G[b], s.out[b]
+        F, G, out = s.F[b], s.G[b], s.out
         h = R // 2
         for z in range(4):
             @pl.when(p.z == z)
@@ -644,12 +593,16 @@
                 F[:, pl.ds(off, w)] = t
         src = F.at[pl.ds(pl.multiple_of((1 - p.y) * h, 8), h), pl.ds(off, w)]
         s.cp(i, 13, src, G.at[:, pl.ds(off, w)], p.yn).start()
-        out[:, s.cols(i, p.y)] = F[pl.ds(pl.multiple_of(p.y * h, 8), h), pl.ds(off, w)]
+        for yy in (0, 1):
+            @pl.when(p.y == yy)
+            def _(): out(b, yy, off, w, lambda o, k: F[pl.ds(yy * h, h), pl.ds(off + o, k)])
     def last(s, i):
         p = s.p; b, R, W, off, w, _ = s.geom(i)
         l = s.G[b].at[:, pl.ds(off, w)]
         s.cp(i, 13, l, l, p.yn).wait_recv()
-        s.out[b][:, s.cols(i, 1 - p.y)] = l[...]
+        for yy in (0, 1):
+            @pl.when(p.y == 1 - yy)
+            def _(): s.out(b, yy, off, w, lambda o, k: l[:, pl.ds(o, k)])
     def drain(s, i):
         p = s.p; b, R, W, off, w, _ = s.geom(i)
         for k, ref in [(k, s.l1(i, 0, 0)) for k in range(4)] + [(4, s.l2(i, 0)), (5, s.l2(i, 1)), (6, s.l3(i)), (13, s.G[b].at[:, pl.ds(off, w)])]:
@@ -660,26 +613,6 @@
                 @pl.when((p.z < t) if d == 0 else (p.z > t))
                 def _(): s.cp(i, s.zsem(d, t), l, l, p.sib).wait_send()
 
-def rs_schedule(g, n, before=lambda i: None):
-    for t in range(n + 9):
-        if t < n: before(t); g.st0(t)
-        if 0 <= t - 1 < n: g.a0(t - 1); g.st1(t - 1)
-        if 0 <= t - 2 < n: g.a1(t - 2); g.st2(t - 2)
-        if 0 <= t - 3 < n: g.a2(t - 3); g.zstep(t - 3, 0)
-        for h in (1, 2, 3):
-            if 0 <= t - 3 - h < n: g.zstep(t - 3 - h, h)
-        if 0 <= t - 6 < n: g.fin(t - 6)
-        if 0 <= t - 7 < n: g.last(t - 7)
-    for i in range(n): g.drain(i)
-
-def rs_kernel(pa_ref, pb_ref, oa, ob, PA, PB, L1A, L1B, L2A, L2B, L3A, L3B, L4A, L4B, FA, FB, GA, GB, ss, rs, ls):
-    pos = Pos(); barrier(pos)
-    n = len(CHUNKS)
-    a = pltpu.make_async_copy(pa_ref, PA, ls.at[0]); b = pltpu.make_async_copy(pb_ref, PB, ls.at[1])
-    a.start(); b.start(); a.wait(); b.wait()
-    g = Scatter(pos, (PA, PB), (L1A, L1B), (L2A, L2B), (L3A, L3B), (L4A, L4B), (FA, FB), (GA, GB), (oa, ob), ss, rs)
-    rs_schedule(g, n)
-
 def rs_scratch():
     n = len(CHUNKS)
     V = pltpu.VMEM
@@ -688,13 +621,6 @@
         V((2, 4, 48, HA), bf16), V((2, 4, 96, HB), bf16), V((48, HA), f32), V((96, HB), f32), V((24, HA), f32), V((48, HB), f32),
         pltpu.SemaphoreType.DMA((n, Scatter.NS)), pltpu.SemaphoreType.DMA((n, Scatter.NS)), pltpu.SemaphoreType.DMA((2,))]
 
-def scatter_call(pa, pb):
-    return pl.pallas_call(rs_kernel,
-        out_shape=(jax.ShapeDtypeStruct((24, 2 * HA), f32), jax.ShapeDtypeStruct((48, 2 * HB), f32)),
-        in_specs=[pl.BlockSpec(memory_space=pl.ANY)] * 2,
-        out_specs=[pl.BlockSpec(memory_space=pltpu.VMEM)] * 2,
-        scratch_shapes=rs_scratch(),
-        compiler_params=pltpu.CompilerParams(collective_id=1, has_side_effects=True, vmem_limit_bytes=60 * 2**20))(pa, pb)
 
 NK = 32
 NB = 2
@@ -779,7 +705,7 @@
         return tuple(new), g1, h1, tuple(C)
     z = jnp.zeros((16, 128), f32)
     st, g1, h1, C = lax.fori_loop(0, NK, body, (tuple(z for _ in range(NB)), z, z, tuple(jnp.zeros((8, 128), f32) for _ in range(8))), unroll=unroll)
-    for b in range(NB): DIR[b, :, ln] = st[b]
+    for b in range(NB): DIR[b, :, ln] = st[b].astype(DIR.dtype)
     ii = lax.broadcasted_iota(jnp.int32, (8, 128), 0)
     g1, h1 = g1 * w[1], h1 * w[1]
     for l in range(8):
@@ -818,72 +744,12 @@
             g = Gr[i, :, ln]
             parts = [KM[0] * g] + [KM[l] * pltpu.roll(g, 8 - l, 0) for l in range(1, 8)]
             parts += [E[h] * AT[b, pl.ds(h, 1), :] for h in range(16)]
-            DU[i, :, ln] = tree(parts)
+            DU[i, :, ln] += tree(parts)
             new.append(q8 * gs[b])
         return tuple(new), h1
     gs, h1 = lax.fori_loop(0, NK, body, (tuple(A0[b, :, ln] for b in range(NB)), H[:, ln]), unroll=unroll)
     H[:, ln] = h1
 
-def six(f):
-    def body(j, _):
-        f(j); return 0
-    lax.fori_loop(0, 6, body, 0)
-
-vm = lambda s, t=f32: pltpu.VMEM(s, t)
-SH = jax.ShapeDtypeStruct
-CP = pltpu.CompilerParams(vmem_limit_bytes=56 * 2**20)
-
-def ema1(U, rate, unroll=2):
-    def k(U, rate, S, END): six(lambda j: fwd_states(U, rate, S, END, j, unroll))
-    return pl.pallas_call(k, out_shape=(SH((64, 16, 768), f32), SH((2, 16, 768), f32)), compiler_params=CP)(U, rate)
-def ema2(U, S, S0, rate, ec, omega, unroll=1):
-    def k(U, Sin, S0, rate, ec, omega, S, BL, KS):
-        S[...] = Sin[...]
-        six(lambda j: fwd_smooth(U, S, S0, rate, ec, omega, BL, KS, j, unroll))
-    return pl.pallas_call(k, out_shape=(SH((64, 16, 768), f32), SH((64, 8, 768), f32)), scratch_shapes=[vm((8, 128))], compiler_params=CP)(U, S, S0, rate, ec, omega)
-def emab1(Gr, U, S, rate, unroll=1):
-    def k(Gr, U, S, rate, A, DIR, G1, H, CS): six(lambda j: bwd_states(Gr, U, S, rate, A, DIR, G1, H, CS, j, unroll))
-    return pl.pallas_call(k, out_shape=(SH((64, 16, 768), f32), SH((2, 16, 768), f32), SH((16, 768), f32), SH((16, 768), f32)), scratch_shapes=[vm((8, 128))], compiler_params=CP)(Gr, U, S, rate)
-def emab2(Gr, U, S, A, A0, rate, ec, H, unroll=1):
-    def k(Gr, U, S, A, A0, rate, ec, Hin, H, DU, KS, AT):
-        H[...] = Hin[...]
-        six(lambda j: bwd_grad(Gr, U, S, A, A0, rate, ec, H, DU, KS, AT, j, unroll))
-    return pl.pallas_call(k, out_shape=(SH((16, 768), f32), SH((64, 8, 768), f32)), scratch_shapes=[vm((8, 128)), vm((2, 16, 128))], compiler_params=CP)(Gr, U, S, A, A0, rate, ec, H)
-
-def scan_kernel(way, e_ref, rate_ref, z_ref, W, L, ss, rs):
-    sq, dp = lax.axis_index("seq"), lax.axis_index("dp")
-    bar = pltpu.get_barrier_semaphore()
-    n = 8
-    has = lambda d: (sq + d < n) if d > 0 else (sq + d >= 0)
-    to = lambda d: (dp, jnp.clip(sq + d, 0, n - 1))
-    for s in (1, 2, 4):
-        for d in (s, -s):
-            @pl.when(has(d))
-            def _(): pl.semaphore_signal(bar, inc=1, device_id=to(d), device_id_type=MESH)
-    pl.semaphore_wait(bar, sum(jnp.clip(sq - s + 1, 0, 1) + jnp.clip(n - s - sq, 0, 1) for s in (1, 2, 4)))
-    W[0] = e_ref[...]
-    z_ref[...] = jnp.zeros_like(z_ref)
-    g = jnp.exp(rate_ref[...] * -256.0)
-    g2 = g * g
-    grow, keep = (g, g2, g2 * g2), (jnp.ones_like(g), g, g2 * g)
-    for k, s in enumerate((1, 2, 4)):
-        cp = rcopy(W.at[k], L.at[k], ss.at[k], rs.at[k], to(way * s))
-        @pl.when(has(way * s))
-        def _(): cp.start()
-        if k < 2: W[k + 1] = W[k]
-        @pl.when(has(-way * s))
-        def _():
-            cp.wait_recv()
-            z_ref[...] = z_ref[...] + keep[k][None] * L[k]
-            if k < 2: W[k + 1] = W[k + 1] + grow[k][None] * L[k]
-    for k, s in enumerate((1, 2, 4)):
-        @pl.when(has(way * s))
-        def _(): rcopy(W.at[k], L.at[k], ss.at[k], rs.at[k], to(way * s)).wait_send()
-def scan_call(e, rate, way, cid):
-    return pl.pallas_call(functools.partial(scan_kernel, way),
-        out_shape=jax.ShapeDtypeStruct(e.shape, f32),
-        scratch_shapes=[pltpu.VMEM((3,) + e.shape, f32), pltpu.VMEM((3,) + e.shape, f32), pltpu.SemaphoreType.DMA((3,)), pltpu.SemaphoreType.DMA((3,))],
-        compiler_params=pltpu.CompilerParams(collective_id=cid, has_side_effects=True, vmem_limit_bytes=40 * 2**20))(e, rate)
 
 def sigmoid(v): return jax.nn.sigmoid(v)
 def dot(a, b): return jnp.dot(a, b, preferred_element_type=f32)
@@ -1241,6 +1107,316 @@
         compiler_params=pltpu.CompilerParams(collective_id=0, has_side_effects=True, vmem_limit_bytes=62 * 2**20),
     )(tok, valid, affine, prm, mx, va, wo, wu, wd)
 
+class Tiny:
+    def __init__(s, pos, T, L1, L2, L4, OUT, G, ss, rs):
+        s.p, s.T, s.L1, s.L2, s.L4, s.OUT, s.G, s.ss, s.rs = pos, T, L1, L2, L4, OUT, G, ss, rs
+    def r(s, xx, c, z=0, n=4): return s.T.at[pl.ds(pl.multiple_of(((xx * 2 + c) * 4 + z) * 48, 8), n * 48), :]
+    def cp(s, k, src, dst, dev): return rcopy(src, dst, s.ss.at[k], s.rs.at[k], dev)
+    def st0(s):
+        for xx in (0, 1): s.cp(xx, s.r(xx, 1 - s.p.c), s.L1.at[xx], s.p.sib).start()
+    def a0(s):
+        p = s.p
+        for xx in (0, 1):
+            l = s.L1.at[xx]
+            s.cp(xx, l, l, p.sib).wait_recv()
+            t = s.r(xx, p.c)
+            t[...] = t[...] + l[...]
+        s.cp(2, s.r(1 - p.x, p.c), s.L2, p.xn).start()
+    def a1(s):
+        p = s.p
+        s.cp(2, s.L2, s.L2, p.xn).wait_recv()
+        t = s.r(p.x, p.c)
+        t[...] = t[...] + s.L2[...]
+    def own(s, t): return s.r(s.p.x, s.p.c, t, 1)
+    def zsem(s, d, t): return 2 + t if d == 0 else 6 + t
+    def zflow(s, d, z):
+        p = s.p
+        first = z == (0, 3)[d]
+        on = tuple(range(3, z, -1)) if d == 0 else tuple(range(0, z))
+        for t in on:
+            l = s.L4.at[d, t]
+            if not first:
+                s.cp(s.zsem(d, t), l, l, p.sib).wait_recv()
+                l[...] = l[...] + s.own(t)[...]
+            s.cp(s.zsem(d, t), s.own(t) if first else l, l, p.up if d == 0 else p.dn).start()
+        if not first:
+            l = s.L4.at[d, z]
+            s.cp(s.zsem(d, z), l, l, p.sib).wait_recv()
+    def zstep(s, h):
+        for z, d in ((h, 0), (3 - h, 1)):
+            @pl.when(s.p.z == z)
+            def _(): s.zflow(d, z)
+    def fin(s):
+        p = s.p
+        for z in range(4):
+            @pl.when(p.z == z)
+            def _():
+                t = s.own(z)
+                v = t[...]
+                if z > 0: v = v + s.L4[0, z]
+                if z < 3: v = v + s.L4[1, z]
+                t[...] = v
+        row = ((p.x * 2 + p.c) * 4 + p.z) * 48
+        far = s.T.at[pl.ds(pl.multiple_of(row + (1 - p.y) * 24, 8), 24), :]
+        s.cp(9, far, s.G, p.yn).start()
+    def last(s):
+        p = s.p
+        row = ((p.x * 2 + p.c) * 4 + p.z) * 48
+        s.cp(9, s.G, s.G, p.yn).wait_recv()
+        s.OUT[...] = s.T[pl.ds(pl.multiple_of(row + p.y * 24, 8), 24), :] + s.G[...]
+    def drain(s):
+        p = s.p
+        for k, l in ((0, s.L1.at[0]), (1, s.L1.at[1]), (2, s.L2), (9, s.G)): s.cp(k, l, l, p.sib).wait_send()
+        for d in (0, 1):
+            for t in ((1, 2, 3), (0, 1, 2))[d]:
+                l = s.L4.at[d, t]
+                @pl.when((p.z < t) if d == 0 else (p.z > t))
+                def _(): s.cp(s.zsem(d, t), l, l, p.sib).wait_send()
+
+class Total:
+    def __init__(s, pos, R, L, ss, rs):
+        p = pos
+        z1 = (p.dp, p.sq + 2 - 4 * (p.z % 2)); z2 = (p.dp, p.sq + 4 - 8 * (p.z // 2))
+        s.to, s.R, s.L, s.ss, s.rs = (p.sib, p.xn, p.yn, z1, z2), R, L, ss, rs
+    def cp(s, k): return rcopy(s.R.at[k], s.L.at[k], s.ss.at[k], s.rs.at[k], s.to[k])
+    def send(s, k): s.cp(k).start()
+    def step(s, k):
+        s.cp(k).wait_recv()
+        s.R[k + 1] = s.R[k] + s.L[k]
+        if k < 4: s.send(k + 1)
+    def drain(s):
+        for k in range(5): s.cp(k).wait_send()
+
+BACK_IN = ("wa", "wb", "vl", "vs", "re", "rs", "at", "gt", "hi", "hs", "uc", "du", "om", "sh", "bs", "n2", "mi", "sp", "pr", "st", "pt", "tok", "cot")
+ORDER = (5, 6, 0, 1, 2, 3, 4)
+ENTER = {5: 0, 6: 1, 0: 4, 1: 5, 2: 6, 3: 7, 4: 8}
+
+def backward_kernel(valid, affine, sq, *refs):
+    ni = len(BACK_IN)
+    I = dict(zip(BACK_IN, refs[:ni]))
+    (o_mx, o_va, o_up, o_wo, o_wd, o_gt, o_tiny, o_red) = refs[ni:ni + 8]
+    (WA, WB, L1A, L1B, L2A, L2B, L3A, L3B, L4A, L4B, FA, FB, GA, GB_, TOK, PT, U, X0, X1, GT, GG, G1, H, KS, AT, ACC, W, L, Zb, GR,
+     T, TL1, TL2, TL4, TG, TP, RR, RL, ss, rs, sx, rx, st_, rt_, sr, rr_, li, lo) = refs[ni + 8:]
+    p = Pos()
+    sem = {name: i for i, name in enumerate(BACK_IN)}
+    def load(name, dst): pltpu.make_async_copy(I[name], dst, li.at[sem[name]]).start()
+    def ready(name, dst): pltpu.make_async_copy(I[name], dst, li.at[sem[name]]).wait()
+    n = len(CHUNKS)
+    parts = ((0, 1536), (1536, 3072))
+    def put(b, half, off, w, get):
+        if b == 1: (o_wo, o_wd)[half][:, pl.ds(off, w)] = get(0, w)
+        elif half == 0: o_mx[:, pl.ds(off, w)] = get(0, w)
+        else:
+            for (lo_, hi_), o in zip(parts, (o_va, o_up)):
+                a, e = max(off, lo_), min(off + w, hi_)
+                if a < e: o[:, pl.ds(a - lo_, e - a)] = get(a - off, e - a)
+    g = Scatter(p, (WA, WB), (L1A, L1B), (L2A, L2B), (L3A, L3B), (L4A, L4B), (FA, FB), (GA, GB_), put, ss, rs)
+    def link(t):
+        for i in ORDER:
+            r = t - ENTER[i]
+            if r == 0: g.st0(i)
+            if r == 1: g.a0(i); g.st1(i)
+            if r == 2: g.a1(i); g.st2(i)
+            if r == 3: g.a2(i); g.zstep(i, 0)
+            if r in (4, 5, 6): g.zstep(i, r - 3)
+            if r == 6: g.fin(i)
+            if r == 7: g.last(i)
+    v = lambda s, t: pltpu.VMEM(s, t)
+    big, mid = v((512, 1536), bf16), v((512, 768), bf16)
+    rate, ec, omega = PT.at[0:16, :], PT.at[16:32, :], PT.at[34:35, :]
+    gain1, gain2 = PT.at[32:33, :], PT.at[33:34, :]
+    def some(lo, hi, f):
+        def body(j, _):
+            f(j); return 0
+        lax.fori_loop(lo, hi, body, 0)
+    def at3(X, i): return X[ds(i, 8), :, :].reshape(64, 768)
+    def dense(P0, P1, P2, P3, P4, P5, P6, GMX, Q0, Q1, Q2, Q3, Q4, SP, PR):
+        load("cot", Q4); load("wb", WB); load("hi", P1); load("hs", P0); load("wa", WA); load("n2", Q1); load("tok", TOK); load("pt", PT)
+        load("gt", P3); load("mi", X0); load("uc", Q2); load("du", Q3); load("rs", P4); load("vl", P5); load("vs", P6); load("sp", SP); load("pr", PR)
+        full_barrier(p)
+        GG[...] = jnp.zeros_like(GG)
+        ready("cot", Q4)
+        def low(i): Q0[ds(i, 64), :] = (Q4[ds(i, 64), :].astype(f32) * valid[ds(i, 64), :]).astype(bf16)
+        loop(8, low)
+        ready("wb", WB); ready("hs", P0); ready("hi", P1)
+        def f_hidden(m):
+            c = ds(m, 256)
+            ACC[...] = dot_nt(Q0[...], WB[c, HB:])
+            WB[c, HB:] = dot_tn(P1[:, c], Q0[...]).astype(bf16)
+            def rows(i):
+                r = ds(i, 64)
+                P2[r, c] = (ACC[r, :] * P0[r, c].astype(f32)).astype(bf16)
+            loop(8, rows)
+        some(0, 6, f_hidden)
+        load("at", P0); load("re", P1)
+        ready("wa", WA); ready("n2", Q1)
+        def f_up(m):
+            c = ds(m, 256)
+            X1[:, :, c] = dot_nt(P2[...], WA[c, HA + 1536:HA + 3072]).reshape(64, 8, 256)
+            WA[c, HA + 1536:HA + 3072] = dot_tn(Q1[:, c], P2[...]).astype(bf16)
+        some(0, 3, f_up)
+        ready("mi", X0); ready("uc", Q2); ready("du", Q3); ready("pt", PT)
+        load("sh", Q0);
+        load("om", Q1)
+        ready("om", Q1)
+        def f_norm2(i):
+            r = ds(i, 64)
+            m_, k = at3(X0, i), at3(X1, i)
+            inv = lax.rsqrt(jnp.mean(m_ * m_, axis=-1, keepdims=True) + EPSILON)
+            unit = m_ * inv
+            GG[0:8, :] += sub8(k * unit)
+            k = k * gain2[...]
+            gm = Q4[r, :].astype(f32) * valid[r, :] + inv * (k - unit * jnp.mean(k * unit, axis=-1, keepdims=True))
+            GMX[r, 0:768] = (gm * Q3[r, :].astype(f32)).astype(bf16)
+            GMX[r, 2432:3200] = (gm * Q2[r, :].astype(f32)).astype(bf16)
+            GT[r, :] = gm * Q1[r, :].astype(f32)
+        loop(8, f_norm2)
+        ready("gt", P3); ready("at", P0); ready("re", P1); ready("rs", P4)
+        def f_gated(m):
+            c = ds(m, 256)
+            ACC[...] = dot_nt(GMX[:, 2432:3200], WB[c, 0:HB])
+            WB[c, 0:HB] = dot_tn(P3[:, c], GMX[:, 2432:3200]).astype(bf16)
+            c2 = pl.ds(pl.multiple_of(896 + m * 256, 128), 256)
+            def rows(i):
+                r = ds(i, 64)
+                a = ACC[r, :]
+                P2[r, c] = (a * P1[r, c].astype(f32)).astype(bf16)
+                GMX[r, c2] = (a * P0[r, c].astype(f32) * P4[r, c].astype(f32)).astype(bf16)
+            loop(8, rows)
+        some(0, 6, f_gated)
+        link(0)
+        load("bs", Q1)
+        ready("tok", TOK)
+        loop(8, lambda i: norm_rows(TOK, PT, U, Q2, i))
+        link(1)
+        ready("vl", P5); ready("vs", P6); ready("sp", SP); ready("pr", PR)
+        RR[0] = jnp.zeros((8, 128), f32)
+        def f_attend(b):
+            r = ds(b, 128)
+            pr = PR[r, :]
+            gp = dot_nt(P2[r, :], P5[r, :])
+            gs = (pr * (gp - jnp.sum(gp * pr, axis=-1, keepdims=True))).astype(bf16)
+            el = pr.astype(bf16)
+            for m in range(6):
+                c = pl.ds(m * 256, 256)
+                P6[r, c] = (dot_tn(el, P2[r, c]) * P6[r, c].astype(f32)).astype(bf16)
+            s, slope = silu_and_slope(SP[r, :])
+            q = (s * affine[0:1, :] + affine[1:2, :]).astype(bf16)
+            k = (s * affine[2:3, :]).astype(bf16)
+            gq = dot(gs, k) * Z_SCALE
+            gk = dot_tn(gs, q) * Z_SCALE
+            GMX[r, 768:896] = ((gq * affine[0:1, :] + gk * affine[2:3, :]) * slope).astype(bf16)
+            for i, t in enumerate((gq * s, gq, gk * s)):
+                RR[0, i:i + 1, :] += jnp.sum(t, axis=0, keepdims=True)
+        loop(4, f_attend)
+        link(2)
+        ready("bs", Q1); ready("sh", Q0)
+        def f_blend(m):
+            c = ds(m, 256)
+            ACC[...] = dot_nt(GMX[...], WA[c, 0:HA])
+            X1[:, :, c] = dot_nt(P6[...], WA[c, HA:HA + 1536]).reshape(64, 8, 256)
+            def rows(i):
+                r, k = ds(i, 64), ds(i, 8)
+                gb = ACC[r, :] * Q1[r, c].astype(f32)
+                X0[k, :, c] = gb.reshape(8, 8, 256)
+                GG[8:16, c] += sub8(gb * U[k, :, c].reshape(64, 256))
+                X1[k, :, c] += (gb * omega[:, c]).reshape(8, 8, 256)
+            loop(8, rows)
+        some(0, 3, f_blend)
+        link(3)
+        for i in range(5):
+            lo_, w = CHUNKS[i][1], CHUNKS[i][2]
+            WA[:, lo_:lo_ + w] = dot_tn(Q0[...], GMX[:, lo_:lo_ + w]).astype(bf16)
+            e = min(lo_ + w, 1536)
+            if lo_ < e: WA[:, HA + lo_:HA + e] = dot_tn(Q2[...], P6[:, lo_:e]).astype(bf16)
+            if lo_ + w == HA: WA[:, 2 * HA - 128:] = jnp.zeros((768, 128), bf16)
+            link(4 + i)
+    pl.run_scoped(dense, big, big, big, big, big, big, big, v((512, HA), bf16), mid, mid, mid, mid, mid, v((512, 128), f32), v((512, 128), f32))
+    tot = Total(p, RR, RL, sr, rr_)
+    for k in range(3):
+        t = sub8(sq[pl.ds(k * 8, 8), :]).sum(axis=0, keepdims=True)
+        RR[0, 3 + k:4 + k, :] = sum(t[:, j * 128:(j + 1) * 128] for j in range(6))
+    RR[0, 6:7, :] = jnp.broadcast_to(jnp.sum(valid[...], axis=0, keepdims=True) * (1.0 / 128.0), (1, 128))
+    tot.send(0)
+    def average(S, A):
+        load("st", S)
+        ready("st", S)
+        back = lambda j: bwd_states(X0, U, S, rate, A, W.at[0], G1, H, KS, j, 2)
+        some(0, 3, back)
+        link(9)
+        some(3, 6, back)
+        sc = Scan(p, -1, PT, W, L, Zb, GR, sx, rx)
+        sc.begin()
+        tot.step(0)
+        link(10)
+        sc.step(0)
+        tot.step(1)
+        sc.step(1)
+        tot.step(2)
+        sc.step(2)
+        link(11)
+        grad = lambda j: bwd_grad(X0, U, S, A, Zb, rate, ec, H, X1, KS, AT, j, 2)
+        some(0, 3, grad)
+        tot.step(3)
+        link(12)
+        some(3, 6, grad)
+        tot.step(4)
+        sc.drain()
+    pl.run_scoped(average, v((64, 16, 768), f32), v((64, 16, 768), f32))
+    o_red[...] = RR[5]
+    GG[16:24, :] = jnp.zeros((8, 768), f32)
+    def f_last(i):
+        r = ds(i, 64)
+        x = TOK[r, :].astype(f32)
+        inv = lax.rsqrt(jnp.mean(x * x, axis=-1, keepdims=True) + EPSILON)
+        unit = x * inv
+        gn = at3(X1, i)
+        GG[16:24, :] += sub8(gn * unit)
+        k = gn * gain1[...]
+        GT[r, :] += inv * (k - unit * jnp.mean(k * unit, axis=-1, keepdims=True))
+    loop(8, f_last)
+    fin = pltpu.make_async_copy(GT, o_gt, lo.at[0])
+    fin.start()
+    TP[...] = jnp.zeros_like(TP)
+    TP[0:16, :] = G1[...]
+    TP[16:32, :] = H[...]
+    for k, i in ((32, 2), (33, 0), (34, 1)):
+        TP[k:k + 1, :] = jnp.sum(GG[pl.ds(i * 8, 8), :], axis=0, keepdims=True)
+    for j in range(6): T[j * 128:(j + 1) * 128, :] = TP[:, j * 128:(j + 1) * 128].T
+    tiny = Tiny(p, T, TL1, TL2, TL4, o_tiny, TG, st_, rt_)
+    tiny.st0()
+    link(13)
+    tiny.a0()
+    link(14)
+    tiny.a1(); tiny.zstep(0)
+    link(15)
+    for h in (1, 2, 3): tiny.zstep(h)
+    tiny.fin()
+    link(16)
+    tiny.last()
+    for i in range(n): g.drain(i)
+    tiny.drain(); tot.drain()
+    fin.wait()
+
+def backward_call(valid, affine, sq, ins):
+    n = len(CHUNKS)
+    v = pltpu.VMEM
+    D_ = pltpu.SemaphoreType.DMA
+    sds = jax.ShapeDtypeStruct
+    vm_, any_ = pl.BlockSpec(memory_space=pltpu.VMEM), pl.BlockSpec(memory_space=pl.ANY)
+    return pl.pallas_call(backward_kernel,
+        out_shape=(sds((24, 3200), f32), sds((24, 1536), f32), sds((24, 1536), f32), sds((48, 768), f32), sds((48, 768), f32), sds((512, 768), f32), sds((24, 128), f32), sds((8, 128), f32)),
+        in_specs=[vm_] * 3 + [any_] * len(ins),
+        out_specs=[vm_] * 5 + [any_] + [vm_] * 2,
+        scratch_shapes=rs_scratch()[:14] + [v((512, 768), bf16), v((128, 768), f32), v((64, 8, 768), f32), v((64, 8, 768), f32), v((64, 8, 768), f32), v((512, 768), f32),
+            v((24, 768), f32), v((16, 768), f32), v((16, 768), f32), v((8, 128), f32), v((2, 16, 128), f32), v((512, 256), f32),
+            v((3, 2, 16, 768), bf16), v((3, 2, 16, 768), bf16), v((2, 16, 768), f32), v((3, 16, 768), f32),
+            v((768, 128), f32), v((2, 192, 128), f32), v((192, 128), f32), v((2, 4, 48, 128), f32), v((24, 128), f32), v((128, 768), f32),
+            v((6, 8, 128), f32), v((5, 8, 128), f32),
+            D_((n, Scatter.NS)), D_((n, Scatter.NS)), D_((3,)), D_((3,)), D_((10,)), D_((10,)), D_((5,)), D_((5,)), D_((len(BACK_IN),)), D_((1,))],
+        compiler_params=pltpu.CompilerParams(collective_id=1, has_side_effects=True, vmem_limit_bytes=63 * 2**20),
+    )(valid, affine, sq, *ins)
+
 
 def per_device_tuned(tokens, cotangent, lengths, w_mx, w_value, w_out, w_up, w_down, ema_rate, ema_in, ema_out, gains, qk_affine):
     rate_own, in_own, out_own = (t.astype(f32) for t in (ema_rate, ema_in, ema_out))
@@ -1252,83 +1428,16 @@
     affine = jnp.pad(qk_affine.astype(f32), ((0, 5), (0, 0)))
     kept = forward_call(tok, valid, affine, mine, w_mx, w_value, w_out, w_up, w_down)
     K = {name: t for (name, _, _), t in zip(FORWARD_OUT, kept)}
-    full_a, full_b = K["wa"], K["wb"]
-    small = K["pt"]
-    rate, coef = small[:16], small[16:32]
-    gain_first, gain_second, omega_gain = small[32], small[33], small[34]
-    mx_full, value_full, up_full = full_a[:, :3200], full_a[:, 3200:4736], full_a[:, 4736:6272]
-    out_full, down_full = full_b[:, :768], full_b[:, 768:]
-    inputs = tok.astype(f32)
-    inverse1 = lax.rsqrt(jnp.mean(inputs * inputs, axis=-1, keepdims=True) + EPSILON)
-    unit1 = inputs * inverse1
-    normed = unit1 * gain_first
-    normed_low = normed.astype(bf16)
-    u3 = normed.reshape(64, 8, D)
-    dn = lambda a, b, ca, cb: lax.dot_general(a, b, (((ca,), (cb,)), ((), ())), preferred_element_type=f32)
-    middle = K["mi"]
-    inverse2 = lax.rsqrt(jnp.mean(middle * middle, axis=-1, keepdims=True) + EPSILON)
-    unit2 = middle * inverse2
-    grad_out = cotangent.reshape(512, D).astype(f32) * valid
-    g_low = grad_out.astype(bf16)
-    grad_down = dn(K["hi"], g_low, 0, 0)
-    gu_low = (dn(g_low, down_full, 1, 1) * K["hs"].astype(f32)).astype(bf16)
-    grad_up = dn(K["n2"], gu_low, 0, 0)
-    grad_n2 = dn(gu_low, up_full, 1, 1)
-    grad_gain_second = jnp.sum(grad_n2 * unit2, axis=0)
-    scaled2 = grad_n2 * gain_second
-    grad_middle = grad_out + inverse2 * (scaled2 - unit2 * jnp.mean(scaled2 * unit2, axis=-1, keepdims=True))
-    gc_low = (grad_middle * K["uc"].astype(f32)).astype(bf16)
-    grad_out_proj = dn(K["gt"], gc_low, 0, 0)
-    grad_gated = dn(gc_low, out_full, 1, 1)
-    grad_reset = grad_gated * K["at"].astype(f32)
-    go = (grad_gated * K["re"].astype(f32)).astype(bf16).reshape(4, SPAN, V)
-    vl = K["vl"].reshape(4, SPAN, V)
-    probs = K["pr"].reshape(4, SPAN, SPAN)
-    probs_low = probs.astype(bf16)
-    grad_probs = jnp.einsum("nqv,nkv->nqk", go, vl, preferred_element_type=f32)
-    grad_values = jnp.einsum("nqk,nqv->nkv", probs_low, go, preferred_element_type=f32).reshape(512, V)
-    gs = (probs * (grad_probs - jnp.sum(grad_probs * probs, axis=-1, keepdims=True))).astype(bf16)
-    shared_pre = K["sp"]
-    shared = jax.nn.silu(shared_pre)
-    ql = (shared * affine[0] + affine[1]).astype(bf16).reshape(4, SPAN, Z)
-    kl = (shared * affine[2]).astype(bf16).reshape(4, SPAN, Z)
-    gq = (jnp.einsum("nqk,nkz->nqz", gs, kl, preferred_element_type=f32) * Z_SCALE).reshape(512, Z)
-    gk = (jnp.einsum("nqk,nqz->nkz", gs, ql, preferred_element_type=f32) * Z_SCALE).reshape(512, Z)
-    grad_affine = jnp.stack([jnp.sum(gq * shared, axis=0), jnp.sum(gq, axis=0), jnp.sum(gk * shared, axis=0)])
-    grad_shared = gq * affine[0] + gk * affine[2]
-    gm_low = jnp.concatenate([(grad_middle * K["du"].astype(f32)).astype(bf16), (grad_shared * silu_slope(shared_pre)).astype(bf16),
-        (grad_reset * K["rs"].astype(f32)).astype(bf16), gc_low], axis=1)
-    grad_mx = dn(K["sh"], gm_low, 0, 0)
-    grad_blend = dn(gm_low, mx_full, 1, 1) * K["bs"].astype(f32)
-    grad_omega = jnp.sum(grad_blend * normed, axis=0)
-    gv_low = (grad_values * K["vs"].astype(f32)).astype(bf16)
-    grad_value_proj = dn(normed_low, gv_low, 0, 0)
-    grad_normed = grad_blend * omega_gain + dn(gv_low, value_full, 1, 1)
-    g3 = grad_blend.reshape(64, 8, D)
-    states = K["st"]
-    adj, direct, g1, h1 = emab1(g3, u3, states, rate, 2)
-    later = scan_call(direct, rate, -1, 3)
-    h1, du3 = emab2(g3, u3, states, adj, later, rate, coef, h1, 2)
-    grad_normed = grad_normed + du3.reshape(normed.shape)
-    grad_gain_first = jnp.sum(grad_normed * unit1, axis=0)
-    scaled1 = grad_normed * gain_first
-    grad_tokens = grad_middle * K["om"].astype(f32) + inverse1 * (
-        scaled1 - unit1 * jnp.mean(scaled1 * unit1, axis=-1, keepdims=True)
-    )
-    pa = jnp.pad(jnp.concatenate([grad_mx, grad_value_proj, grad_up], axis=1).astype(bf16), ((0, 0), (0, 128)))
-    pb = jnp.concatenate([grad_out_proj, grad_down], axis=1).astype(bf16)
-    oa, ob = scatter_call(pa, pb)
-    tiny = jnp.concatenate([g1.T, h1.T, jnp.stack([grad_gain_first, grad_gain_second, grad_omega], axis=1)], axis=1)
-    tiny = lax.psum_scatter(jnp.pad(tiny, ((0, 0), (0, 93))), ("dp", "seq"), scatter_dimension=0, tiled=True)
+    K["tok"], K["cot"], K["mi"] = tok, cotangent.reshape(512, D), K["mi"].reshape(64, 8, 768)
+    g_mx, g_va, g_up, g_wo, g_wd, g_tok, tiny, red = backward_call(valid, affine, K["sq"], [K[name] for name in BACK_IN])
     g1, h1 = tiny[:, :16], tiny[:, 16:32]
     grad_ema_out = in_own * scale_own * g1
     grad_ema_in = out_own * scale_own * g1
     grad_ema_rate = out_own * in_own * (jnp.exp(-2.0 * rate_own) / scale_own * g1 - scale_own * h1)
-    squares = jnp.append(jnp.sum(K["sq"].reshape(3, -1), axis=1), jnp.sum(valid))
-    affine_total, square_total = lax.psum((grad_affine, squares), ("dp", "seq"))
-    rms_values = jnp.sqrt(square_total[:3] / (square_total[3] * D))
-    return (K["res"].reshape(tokens.shape), grad_tokens.reshape(tokens.shape), oa[:, :3200], oa[:, 3200:4736], ob[:, :768], oa[:, 4736:6272], ob[:, 768:],
-        grad_ema_rate, grad_ema_in, grad_ema_out, tiny[:, 32:35], affine_total, rms_values)
+    sums = jnp.sum(red[3:7], axis=1)
+    rms_values = jnp.sqrt(sums[:3] / (sums[3] * D))
+    return (K["res"].reshape(tokens.shape), g_tok.reshape(tokens.shape), g_mx, g_va, g_wo, g_up, g_wd,
+        grad_ema_rate, grad_ema_in, grad_ema_out, tiny[:, 32:35], red[:3], rms_values)
 
 
 def solution(mesh):

time: 412 us -> 331 us (0.80)
  Pallas kernels: 264 us -> 309 us
  matrix products: 39 us -> 0 us
  blocking collectives: 38.3 us -> 0 us
  other arithmetic: 29.1 us -> 5.01 us
  between operations: 15.2 us -> 1.39 us
  local copies, waits for them, and re-layouts: 25.3 us -> 14.6 us
    pallas_call x4 -> x1, Pallas kernels: 145 us -> 190 us  [backward_call(): pl.pallas_call(backward_kernel, out_shape=(sds((24, 3200), f32), sds((24,...]
    dot_general x14 -> x0, matrix products: 39 us -> none  [the longest x10 35.8 us: per_device_tuned(): lax.dot_general(a, b, (((ca,), (cb,)), ((), ())), preferred_element_type=...]
    psum x1 -> x0, blocking collectives: 38.3 us -> none  [per_device_tuned(): affine_total, square_total = lax.psum((grad_affine, squares), ('dp', 'seq'))]
    concatenate x3 -> x0, other arithmetic: 12.1 us -> none  [the longest x1 8.75 us: per_device_tuned(): jnp.concatenate([grad_mx, grad_value_proj, grad_up], axis=1).astype(bf16)]
    slice x7 -> x2, local copies, waits for them, and re-layouts: 8.95 us -> 1.85 us  [the longest x1 1.26 us: per_device_tuned(): red[:3]]
    convert_element_type x7 -> x0, other arithmetic: 6.38 us -> none  [the longest x1 3.48 us: per_device_tuned(): (grad_middle * K['du'].astype(f32)).astype(bf16)]
    unnamed x91 -> x30, local copies, waits for them, and re-layouts: 11.8 us -> 11.2 us
  transfers between devices with their start and end apart: 1 -> 0, of which waited for: 0 -> 0; matrix products, arithmetic and copies ran while one was open for 8% -> 0% of each run, Pallas kernels for 24% -> 0%
where the time goes in v3:
time: 331 us; the launch traced here: 330 us
  Pallas kernels  309 us (93%)
  local copies, waits for them, and re-layouts  14.6 us (4%)
  other arithmetic  5.01 us (2%)
    pallas_call x1, Pallas kernels, backward_call(): pl.pallas_call(backward_kernel, out_shape=(sds((24, 3200), f32), sds((24,...  190 us
    pallas_call x1, Pallas kernels, forward_call(): pl.pallas_call(forward_kernel, out_shape=tuple((jax.ShapeDtypeStruct(s, t...  119 us
    unnamed x30, local copies, waits for them, and re-layouts  11.2 us

profile of v3, /device:TPU:0, one launch (start us, length us, event | category | flops | bytes accessed | tf_op | source)
XLA Modules:
  0.0 330.3 jit_solution(2828618148377708076)
XLA Ops:
  0.7 0.7 fusion.2
  1.4 1.3 pad_convert_fusion.affine
  2.7 0.8 copy.34
  3.4 0.8 copy.36
  4.2 0.8 copy.35
  5.0 0.8 copy.37
  5.8 0.7 select_maximum_fusion.prm
  6.5 0.9 copy.45
  7.3 119.4 %shard_map.228 = (bf16[768,6400]{1,0:T(8,128)(2,1)}, bf16[1536,1536]{1,0:T(8,128)(2,1)}, bf16[512,1536]{1,0:T(8,128)(2,1)}, bf16[512,1536]{1,0:T(8,128)(2,1)}, b...) custom-call(bf16[512,768]{1,0:T(8,128)(2,1)} %bitcast.11, ...), custom_call_target="tpu_custom_call" | custom-call | tf_op jit(solution)/shard_map/pallas_call | solution.py:1099
  126.7 0.0 copy-start.1
  126.7 189.8 %shard_map.229 = (f32[24,3200]{1,0:T(8,128)}, f32[24,1536]{1,0:T(8,128)}, f32[24,1536]{1,0:T(8,128)}, f32[48,768]{1,0:T(8,128)}, f32[48,768]{1,0:T(8,128)}, /*in...) custom-call(f32[512,1]{1,0:T(8,128)} %bitcast.14, f32[8,128]{1,0:T(8,128)} %pad_convert_fusion.affine, ...), custom_call_target="tpu_custom_call" | custom-call | tf_op jit(solution)/shard_map/pallas_call | solution.py:1407
  316.6 0.0 copy-start
  316.6 0.9 slice_reduce_fusion
  317.5 0.6 slice.27
  318.7 1.3 slice.24
  320.0 0.5 divide_sqrt_fusion
  320.5 0.8 slice.23
  321.3 0.7 copy.43
  321.9 0.9 fusion.1
  322.8 0.7 copy.42
  323.5 0.7 copy.40
  324.1 0.7 copy.41
  324.8 0.9 copy.53
  325.7 0.0 copy-done
  325.7 1.1 copy.54
  326.9 0.7 copy.55
  327.6 0.0 copy-done.6
  327.6 0.7 copy.56
  328.3 0.7 copy.57
  328.9 0.0 copy-done.4
  328.9 0.7 copy.58
  329.6 0.7 copy.59
  (13 shorter events, 0.1 us)
Async XLA Ops:
  126.7 198.1 %copy-start.1 = (bf16[512,768]{1,0:T(8,128)(2,1)S(1)}, bf16[512,768]{1,0:T(8,128)(2,1)}, u32[]{:S(2)}) copy-start(bf16[512,768]{1,0:T(8,128)(2,1)} %get-tuple-element.44) | copy-start | bytes 2359300
  316.6 9.1 %copy-start = (f32[512,768]{1,0:T(8,128)S(1)}, f32[512,768]{1,0:T(8,128)}, u32[]{:S(2)}) copy-start(f32[512,768]{1,0:T(8,128)} %get-tuple-element.67) | copy-start | bytes 4718596
  325.7 1.2 copy-start.2
  325.7 1.9 copy-start.6
  325.7 2.6 copy-start.5
  325.7 3.2 copy-start.4
  325.7 3.9 %copy-start.3 = (f32[48,768]{1,0:T(8,128)S(1)}, f32[48,768]{1,0:T(8,128)}, u32[]{:S(2)}) copy-start(f32[48,768]{1,0:T(8,128)} %get-tuple-element.123) | copy-start | bytes 442372

commit v4 on v3

--- a/solution.py
+++ b/solution.py
@@ -372,7 +372,11 @@
 HA, HB = 3200, 768
 RA, RB = 48, 96
 
-CHUNKS = [(0, 0, 640, "xy"), (0, 640, 640, "yx"), (0, 1280, 640, "xy"), (0, 1920, 640, "yx"), (0, 2560, 640, "xy"), (1, 0, 384, "yx"), (1, 384, 384, "xy")]
+CHUNKS = [(0, 0, 256, "xy"), (0, 256, 256, "yx"), (0, 512, 384, "xy"), (0, 896, 384, "yx"), (0, 1280, 384, "xy"), (0, 1664, 384, "yx"),
+    (0, 2048, 384, "xy"), (0, 2432, 384, "yx"), (0, 2816, 256, "xy"), (0, 3072, 128, "yx"),
+    (1, 0, 256, "xy"), (1, 256, 128, "yx"), (1, 384, 128, "xy"), (1, 512, 256, "yx")]
+GATHER_GROUPS = ((0, 1), (2, 3), (4, 5), (6, 7), (8, 9, 11, 12), (10, 13))
+SCATTER_GROUPS = ((10, 13), (11, 12), (0, 1), (2, 3), (4, 5), (6, 7), (8, 9))
 
 class Pos:
     def __init__(s):
@@ -381,128 +385,98 @@
         s.sib = (s.dp + 1 - 2 * s.c, s.sq)
         s.xn = (s.dp + 2 - 4 * s.x, s.sq)
         s.yn = (s.dp, s.sq + 1 - 2 * s.y)
-        s.up = (s.dp, jnp.minimum(s.sq + 2, s.sq + 2 * (3 - s.z)))
-        s.dn = (s.dp, jnp.maximum(s.sq - 2, s.y))
         s.dpx = s.dp + 2 - 4 * s.x
+    def zof(s, d): return (s.z + d) % 4
+    def zn(s, d): return (s.dp, s.zof(d) * 2 + s.y)
 
 def rcopy(src, dst, ss, rs, dev):
     return pltpu.make_async_remote_copy(src_ref=src, dst_ref=dst, send_sem=ss, recv_sem=rs, device_id=dev, device_id_type=MESH)
 
-def barrier(pos):
+def full_barrier(p):
     bar = pltpu.get_barrier_semaphore()
     sig = lambda d: pl.semaphore_signal(bar, inc=1, device_id=d, device_id_type=MESH)
-    sig(pos.sib); sig(pos.xn); sig(pos.yn)
-    @pl.when(pos.z < 3)
-    def _(): sig(pos.up)
-    @pl.when(pos.z > 0)
-    def _(): sig(pos.dn)
-    pl.semaphore_wait(bar, 3 + jnp.minimum(pos.z, 1) + jnp.minimum(3 - pos.z, 1))
+    for d in (p.sib, p.xn, p.yn, p.zn(1), p.zn(2), p.zn(3)): sig(d)
+    @pl.when(p.sq < 7)
+    def _(): sig((p.dp, jnp.minimum(p.sq + 1, 7)))
+    @pl.when(p.sq > 0)
+    def _(): sig((p.dp, jnp.maximum(p.sq - 1, 0)))
+    pl.semaphore_wait(bar, 6 + jnp.clip(p.sq, 0, 1) + jnp.clip(7 - p.sq, 0, 1))
 
 def at(ref, rows, nrows, half, w, off, width):
-    r = pl.ds(pl.multiple_of(rows, 48), nrows)
-    c = pl.ds(pl.multiple_of(half * w + off, 128), width)
-    return ref.at[r, c]
+    return ref.at[pl.ds(pl.multiple_of(rows, 48), nrows), pl.ds(pl.multiple_of(half * w + off, 128), width)]
 
 class Gather:
     def __init__(s, pos, bufs, ss, rs):
         s.p, s.bufs, s.ss, s.rs = pos, bufs, ss, rs
-    def geom(s, i):
-        b, off, width, order = CHUNKS[i]
-        return s.bufs[b], (RA, RB)[b], (HA, HB)[b], off, width, order
     def unit(s, i, dp, z, half, n=1):
-        ref, R, W, off, width, _ = s.geom(i)
-        return at(ref, (dp * 4 + z) * R, n * R, half, W, off, width)
+        b, off, width, _ = CHUNKS[i]
+        R = (RA, RB)[b]
+        return at(s.bufs[b], (dp * 4 + z) * R, n * R, half, (HA, HB)[b], off, width)
     def cp(s, i, k, ref, dev):
         return rcopy(ref, ref, s.ss.at[i, k], s.rs.at[i, k], dev)
     def z0(s, i):
         p = s.p
         u = s.unit(i, p.dp, p.z, p.y)
-        @pl.when(p.z < 3)
-        def _(): rcopy(u, u, s.ss.at[i, 0], s.rs.at[i, p.z], p.up).start()
-        @pl.when(p.z > 0)
-        def _(): rcopy(u, u, s.ss.at[i, 1], s.rs.at[i, p.z], p.dn).start()
-    def zrecv(s, i, zz):
-        u = s.unit(i, s.p.dp, zz, s.p.y)
-        rcopy(u, u, s.ss.at[i, 0], s.rs.at[i, zz], s.p.up).wait_recv()
-        return u
-    def zhop(s, i, h):
-        p = s.p
-        @pl.when(p.z >= h)
-        def _():
-            u = s.zrecv(i, p.z - h)
-            @pl.when(p.z < 3)
-            def _(): rcopy(u, u, s.ss.at[i, 1 + h], s.rs.at[i, p.z - h], p.up).start()
-        @pl.when(p.z + h <= 3)
-        def _():
-            u = s.zrecv(i, p.z + h)
-            @pl.when(p.z > 0)
-            def _(): rcopy(u, u, s.ss.at[i, 10 + h], s.rs.at[i, p.z + h], p.dn).start()
+        for d in (1, 3, 2): rcopy(u, u, s.ss.at[i, d - 1], s.rs.at[i, p.z], p.zn(d)).start()
     def s1(s, i):
-        p = s.p; order = CHUNKS[i][3]
+        p = s.p
+        for d in (1, 2, 3):
+            u = s.unit(i, p.dp, p.zof(d), p.y)
+            rcopy(u, u, s.ss.at[i, 0], s.rs.at[i, p.zof(d)], p.sib).wait_recv()
         u = s.unit(i, p.dp, 0, p.y, 4)
-        s.cp(i, 4, u, p.xn if order == "xy" else p.yn).start()
+        s.cp(i, 4, u, p.xn if CHUNKS[i][3] == "xy" else p.yn).start()
         s.cp(i, 7, u, p.sib).start()
     def s1_in(s, i):
-        p = s.p; order = CHUNKS[i][3]
-        return s.unit(i, p.dpx, 0, p.y, 4) if order == "xy" else s.unit(i, p.dp, 0, 1 - p.y, 4)
+        p = s.p
+        return s.unit(i, p.dpx, 0, p.y, 4) if CHUNKS[i][3] == "xy" else s.unit(i, p.dp, 0, 1 - p.y, 4)
     def s2(s, i):
-        p = s.p; order = CHUNKS[i][3]
+        p = s.p
         r = s.s1_in(i)
         s.cp(i, 4, r, p.xn).wait_recv()
-        nxt = p.yn if order == "xy" else p.xn
-        u = s.unit(i, p.dp, 0, p.y, 4)
-        s.cp(i, 5, u, nxt).start()
+        nxt = p.yn if CHUNKS[i][3] == "xy" else p.xn
+        s.cp(i, 5, s.unit(i, p.dp, 0, p.y, 4), nxt).start()
         s.cp(i, 6, r, nxt).start()
         s.cp(i, 8, r, p.sib).start()
     def s2_in(s, i):
-        p = s.p; order = CHUNKS[i][3]
-        if order == "xy":
+        p = s.p
+        if CHUNKS[i][3] == "xy":
             return s.unit(i, p.dp, 0, 1 - p.y, 4), s.unit(i, p.dpx, 0, 1 - p.y, 4)
         return s.unit(i, p.dpx, 0, p.y, 4), s.unit(i, p.dpx, 0, 1 - p.y, 4)
     def s3(s, i):
-        p = s.p
         for k, r in enumerate(s.s2_in(i)):
-            s.cp(i, 5 + k, r, p.sib).wait_recv()
-            s.cp(i, 9 + k, r, p.sib).start()
+            s.cp(i, 5 + k, r, s.p.sib).wait_recv()
+            s.cp(i, 9 + k, r, s.p.sib).start()
     def s4(s, i):
-        p = s.p
-        u = s.unit(i, p.dp, 0, p.y, 4)
-        for k in (7, 8, 9, 10):
-            s.cp(i, k, u, p.sib).wait_recv()
-    def drain(s, i):
-        p = s.p
-        u1 = s.unit(i, p.dp, 0, p.y)
-        u = s.unit(i, p.dp, 0, p.y, 4)
-        for k in (4, 5, 6, 7, 8, 9, 10):
-            s.cp(i, k, u, p.sib).wait_send()
-        w = lambda k: rcopy(u1, u1, s.ss.at[i, k], s.rs.at[i, 0], p.sib).wait_send()
-        @pl.when(p.z < 3)
-        def _(): w(0)
-        @pl.when(p.z > 0)
-        def _(): w(1)
-        for h in (1, 2):
-            @pl.when((p.z >= h) & (p.z < 3))
-            def _(): w(1 + h)
-            @pl.when((p.z + h <= 3) & (p.z > 0))
-            def _(): w(10 + h)
-
+        u = s.unit(i, s.p.dp, 0, s.p.y, 4)
+        for k in (7, 8, 9, 10): s.cp(i, k, u, s.p.sib).wait_recv()
+    def tick(s, t):
+        at_ = lambda k: GATHER_GROUPS[k] if 0 <= k < len(GATHER_GROUPS) else ()
+        for i in at_(t): s.s1(i)
+        for i in at_(t - 1): s.s2(i)
+        for i in at_(t + 1): s.z0(i)
+        for i in at_(t - 2): s.s3(i)
+        for i in at_(t - 3): s.s4(i)
+    def drain(s):
+        p = s.p
+        for i in range(len(CHUNKS)):
+            u1 = s.unit(i, p.dp, 0, p.y)
+            u = s.unit(i, p.dp, 0, p.y, 4)
+            for k in (4, 5, 6, 7, 8, 9, 10): s.cp(i, k, u, p.sib).wait_send()
+            for k in (0, 1, 2): s.cp(i, k, u1, p.sib).wait_send()
 
 class Scatter:
-    NS = 14
+    NS = 11
     def __init__(s, pos, P, L1, L2, L3, L4, F, G, out, ss, rs):
         s.p, s.P, s.L1, s.L2, s.L3, s.L4, s.F, s.G, s.out, s.ss, s.rs = pos, P, L1, L2, L3, L4, F, G, out, ss, rs
     def geom(s, i):
         b, off, w, order = CHUNKS[i]
         return b, (RA, RB)[b], (HA, HB)[b], off, w, order
-    def rows(s, i, xx, c, z=0):
-        R = (RA, RB)[CHUNKS[i][0]]
-        return pl.multiple_of(((xx * 2 + c) * 4 + z) * R, 48)
     def cols(s, i, yy):
         b, R, W, off, w, _ = s.geom(i)
         return pl.ds(pl.multiple_of(yy * W + off, 128), w)
     def piece(s, i, xx, c, yy, z=0, n=4):
         b, R, W, off, w, _ = s.geom(i)
-        return s.P[b].at[pl.ds(s.rows(i, xx, c, z), n * R), s.cols(i, yy)]
+        return s.P[b].at[pl.ds(pl.multiple_of(((xx * 2 + c) * 4 + z) * R, 48), n * R), s.cols(i, yy)]
     def cp(s, i, k, src, dst, dev):
         return rcopy(src, dst, s.ss.at[i, k], s.rs.at[i, k], dev)
     def add(s, dst, src, nrows):
@@ -512,14 +486,13 @@
             return 0
         lax.fori_loop(0, nrows // 48, body, 0)
     def l1(s, i, xx, yy):
-        b, R, W, off, w, _ = s.geom(i)
-        return s.L1[b].at[xx, :, s.cols(i, yy)]
+        return s.L1[CHUNKS[i][0]].at[xx, :, s.cols(i, yy)]
     def st0(s, i):
         p = s.p
         for k, (xx, yy) in enumerate(((0, 0), (0, 1), (1, 0), (1, 1))):
             s.cp(i, k, s.piece(i, xx, 1 - p.c, yy), s.l1(i, xx, yy), p.sib).start()
     def a0(s, i):
-        b, R, W, off, w, _ = s.geom(i)
+        R = s.geom(i)[1]
         for k, (xx, yy) in enumerate(((0, 0), (0, 1), (1, 0), (1, 1))):
             l = s.l1(i, xx, yy)
             s.cp(i, k, l, l, s.p.sib).wait_recv()
@@ -546,81 +519,64 @@
         src = s.piece(i, 1 - p.x, p.c, p.y) if order == "xy" else s.piece(i, p.x, p.c, 1 - p.y)
         s.cp(i, 6, src, s.l3(i), p.xn if order == "xy" else p.yn).start()
     def a2(s, i):
-        p = s.p; b, R, W, off, w, order = s.geom(i)
         l = s.l3(i)
-        s.cp(i, 6, l, l, p.xn).wait_recv()
-        s.add(s.piece(i, p.x, p.c, p.y), l, 4 * R)
-    def l4(s, i, d, t):
+        s.cp(i, 6, l, l, s.p.xn).wait_recv()
+        s.add(s.piece(i, s.p.x, s.p.c, s.p.y), l, 4 * s.geom(i)[1])
+    def l4(s, i, k):
         b, R, W, off, w, _ = s.geom(i)
-        return s.L4[b].at[d, t, :, pl.ds(off, w)]
-    def own(s, i, t):
-        p = s.p
-        return s.piece(i, p.x, p.c, p.y, t, 1)
-    def zsem(s, d, t):
-        return 6 + t if d == 0 else 10 + t
-    def zflow(s, i, d, z):
-        p = s.p; R = s.geom(i)[1]
-        first = z == (0, 3)[d]
-        mine = () if first else (z,)
-        on = tuple(range(3, z, -1)) if d == 0 else tuple(range(0, z))
-        for t in on:
-            l = s.l4(i, d, t)
-            if not first:
-                s.cp(i, s.zsem(d, t), l, l, p.sib).wait_recv()
-                s.add(l, s.own(i, t), R)
-            s.cp(i, s.zsem(d, t), s.own(i, t) if first else l, l, p.up if d == 0 else p.dn).start()
-        for t in mine:
-            l = s.l4(i, d, t)
-            s.cp(i, s.zsem(d, t), l, l, p.sib).wait_recv()
-    def zstep(s, i, h):
-        p = s.p
-        for z, d in ((h, 0), (3 - h, 1)):
-            @pl.when(p.z == z)
-            def _(): s.zflow(i, d, z)
+        return s.L4[b].at[k, :, pl.ds(off, w)]
+    def zsend(s, i):
+        p = s.p
+        for d in (1, 3, 2):
+            rcopy(s.piece(i, p.x, p.c, p.y, p.zof(d), 1), s.l4(i, 3 - d), s.ss.at[i, 6 + d], s.rs.at[i, 10 - d], p.zn(d)).start()
     def fin(s, i):
         p = s.p; b, R, W, off, w, _ = s.geom(i)
-        u = s.own(i, p.z)
-        hu, hd = (p.z > 0), (p.z < 3)
-        lu, ld = s.l4(i, 0, p.z), s.l4(i, 1, p.z)
         F, G, out = s.F[b], s.G[b], s.out
         h = R // 2
-        for z in range(4):
-            @pl.when(p.z == z)
-            def _():
-                t = u[...].astype(f32)
-                if z > 0: t = t + lu[...].astype(f32)
-                if z < 3: t = t + ld[...].astype(f32)
-                F[:, pl.ds(off, w)] = t
+        t = s.piece(i, p.x, p.c, p.y, p.z, 1)[...].astype(f32)
+        for k in range(3):
+            l = s.l4(i, k)
+            s.cp(i, 7 + k, l, l, p.sib).wait_recv()
+            t = t + l[...].astype(f32)
+        F[:, pl.ds(off, w)] = t
         src = F.at[pl.ds(pl.multiple_of((1 - p.y) * h, 8), h), pl.ds(off, w)]
-        s.cp(i, 13, src, G.at[:, pl.ds(off, w)], p.yn).start()
+        s.cp(i, 10, src, G.at[:, pl.ds(off, w)], p.yn).start()
         for yy in (0, 1):
             @pl.when(p.y == yy)
             def _(): out(b, yy, off, w, lambda o, k: F[pl.ds(yy * h, h), pl.ds(off + o, k)])
     def last(s, i):
         p = s.p; b, R, W, off, w, _ = s.geom(i)
         l = s.G[b].at[:, pl.ds(off, w)]
-        s.cp(i, 13, l, l, p.yn).wait_recv()
+        s.cp(i, 10, l, l, p.yn).wait_recv()
         for yy in (0, 1):
             @pl.when(p.y == 1 - yy)
             def _(): s.out(b, yy, off, w, lambda o, k: l[:, pl.ds(o, k)])
-    def drain(s, i):
-        p = s.p; b, R, W, off, w, _ = s.geom(i)
-        for k, ref in [(k, s.l1(i, 0, 0)) for k in range(4)] + [(4, s.l2(i, 0)), (5, s.l2(i, 1)), (6, s.l3(i)), (13, s.G[b].at[:, pl.ds(off, w)])]:
-            s.cp(i, k, ref, ref, p.sib).wait_send()
-        for d in (0, 1):
-            for t in ((1, 2, 3), (0, 1, 2))[d]:
-                l = s.l4(i, d, t)
-                @pl.when((p.z < t) if d == 0 else (p.z > t))
-                def _(): s.cp(i, s.zsem(d, t), l, l, p.sib).wait_send()
+    def tick(s, t, enter):
+        st = [(t - e, grp) for e, grp in zip(enter, SCATTER_GROUPS)]
+        for r, grp in st:
+            for i in grp:
+                if r == 1: s.a0(i); s.st1(i)
+        for r, grp in st:
+            for i in grp:
+                if r == 2: s.a1(i); s.st2(i)
+        for r, grp in st:
+            for i in grp:
+                if r == 0: s.st0(i)
+                if r == 3: s.a2(i); s.zsend(i)
+                if r == 4: s.fin(i)
+                if r == 5: s.last(i)
+    def drain(s):
+        p = s.p
+        for i in range(len(CHUNKS)):
+            b, R, W, off, w, _ = s.geom(i)
+            for k, ref in [(k, s.l1(i, 0, 0)) for k in range(4)] + [(4, s.l2(i, 0)), (5, s.l2(i, 1)), (6, s.l3(i)), (10, s.G[b].at[:, pl.ds(off, w)])] + [(7 + k, s.l4(i, k)) for k in range(3)]:
+                s.cp(i, k, ref, ref, p.sib).wait_send()
 
 def rs_scratch():
-    n = len(CHUNKS)
-    V = pltpu.VMEM
-    return [V((768, 2 * HA), bf16), V((1536, 2 * HB), bf16), V((2, 192, 2 * HA), bf16), V((2, 384, 2 * HB), bf16),
-        V((2, 192, HA), bf16), V((2, 384, HB), bf16), V((192, HA), bf16), V((384, HB), bf16),
-        V((2, 4, 48, HA), bf16), V((2, 4, 96, HB), bf16), V((48, HA), f32), V((96, HB), f32), V((24, HA), f32), V((48, HB), f32),
-        pltpu.SemaphoreType.DMA((n, Scatter.NS)), pltpu.SemaphoreType.DMA((n, Scatter.NS)), pltpu.SemaphoreType.DMA((2,))]
-
+    v = pltpu.VMEM
+    return [v((768, 2 * HA), bf16), v((1536, 2 * HB), bf16), v((2, 192, 2 * HA), bf16), v((2, 384, 2 * HB), bf16),
+        v((2, 192, HA), bf16), v((2, 384, HB), bf16), v((192, HA), bf16), v((384, HB), bf16),
+        v((3, 48, HA), bf16), v((3, 96, HB), bf16), v((48, HA), f32), v((96, HB), f32), v((24, HA), f32), v((48, HB), f32)]
 
 NK = 32
 NB = 2
@@ -781,26 +737,12 @@
         s.cp(0, l, l, p.yn).wait()
     def z0(s):
         p = s.p; u = s.r((p.dp * 4 + p.z) * 48, 48)
-        @pl.when(p.z < 3)
-        def _(): s.cp(1, u, u, p.up, 1 + p.z).start()
-        @pl.when(p.z > 0)
-        def _(): s.cp(2, u, u, p.dn, 1 + p.z).start()
-    def zhop(s, h):
-        p = s.p
-        @pl.when(p.z >= h)
-        def _():
-            u = s.r((p.dp * 4 + p.z - h) * 48, 48)
-            s.cp(1, u, u, p.up, 1 + p.z - h).wait_recv()
-            @pl.when(p.z < 3)
-            def _(): s.cp(2 + h, u, u, p.up, 1 + p.z - h).start()
-        @pl.when(p.z + h <= 3)
-        def _():
-            u = s.r((p.dp * 4 + p.z + h) * 48, 48)
-            s.cp(1, u, u, p.up, 1 + p.z + h).wait_recv()
-            @pl.when(p.z > 0)
-            def _(): s.cp(4 + h, u, u, p.dn, 1 + p.z + h).start()
+        for d in (1, 3, 2): s.cp(d, u, u, p.zn(d), 1 + p.z).start()
     def x0(s):
         p = s.p; u = s.r(p.dp * 192, 192)
+        for d in (1, 2, 3):
+            l = s.r((p.dp * 4 + p.zof(d)) * 48, 48)
+            s.cp(1, l, l, p.sib, 1 + p.zof(d)).wait_recv()
         s.cp(7, u, u, p.xn).start()
         s.cp(8, u, u, p.sib).start()
     def x1(s):
@@ -814,16 +756,7 @@
     def drain(s):
         p = s.p; u = s.r(p.dp * 192, 192); u1 = s.r(p.dp * 192, 48)
         for k in (7, 8, 9): s.cp(k, u, u, p.sib).wait_send()
-        w = lambda k: s.cp(k, u1, u1, p.sib).wait_send()
-        @pl.when(p.z < 3)
-        def _(): w(1)
-        @pl.when(p.z > 0)
-        def _(): w(2)
-        for h in (1, 2):
-            @pl.when((p.z >= h) & (p.z < 3))
-            def _(): w(2 + h)
-            @pl.when((p.z + h <= 3) & (p.z > 0))
-            def _(): w(4 + h)
+        for k in (1, 2, 3): s.cp(k, u1, u1, p.sib).wait_send()
 
 class Scan:
     def __init__(s, pos, way, rate, W, L, Z, GR, ss, rs):
@@ -855,17 +788,6 @@
             @pl.when(s.has(s.way * 2 ** k))
             def _(): s.cp(k).wait_send()
 
-def full_barrier(p):
-    bar = pltpu.get_barrier_semaphore()
-    sig = lambda d: pl.semaphore_signal(bar, inc=1, device_id=d, device_id_type=MESH)
-    sig(p.sib); sig(p.xn); sig(p.yn)
-    for d in (1, 2, 4):
-        @pl.when(p.sq + d < 8)
-        def _(): sig((p.dp, jnp.minimum(p.sq + d, 7)))
-        @pl.when(p.sq - d >= 0)
-        def _(): sig((p.dp, jnp.maximum(p.sq - d, 0)))
-    pl.semaphore_wait(bar, 3 + sum(jnp.clip(p.sq - d + 1, 0, 1) + jnp.clip(8 - d - p.sq, 0, 1) for d in (1, 2, 4)))
-
 def first_exchange_start(p, mx, va, wo, wu, wd, WB, land, s0, r0):
     cps = {}
     @pl.when(p.y == 0)
@@ -942,25 +864,15 @@
     par.y0()
     first_exchange_start(p, mx, va, wo, wu, wd, WB, land, s0, r0)
     g = Gather(p, (WA, WB), ss, rs)
-    n = len(CHUNKS)
-    def link(t):
-        if t < n: g.z0(t)
-        if 0 <= t - 1 < n: g.zhop(t - 1, 1)
-        if 0 <= t - 2 < n: g.zhop(t - 2, 2)
-        if 0 <= t - 3 < n: g.zhop(t - 3, 3); g.s1(t - 3)
-        if 0 <= t - 4 < n: g.s2(t - 4)
-        if 0 <= t - 5 < n: g.s3(t - 5)
-        if 0 <= t - 6 < n: g.s4(t - 6)
+    link = g.tick
     par.y1(); par.z0()
     first_exchange_end(p, mx, va, wo, wu, wd, WA, WB, land, s0, r0)
-    link(0); par.zhop(1)
-    link(1); par.zhop(2)
-    link(2); par.zhop(3); par.x0()
-    link(3); par.x1(); par.end()
+    for i in GATHER_GROUPS[0]: g.z0(i)
+    par.x0(); par.x1(); par.end()
+    link(0)
     for j in range(6): PT[:, j * 128:(j + 1) * 128] = PRM[j * 128:(j + 1) * 128, :].T
     rate, ec, omega = PT.at[0:16, :], PT.at[16:32, :], PT.at[34:35, :]
     loop(8, lambda i: norm_rows(tok, PT, U, NL, i))
-    link(4)
     def some(lo, hi, f):
         def body(j, _):
             f(j); return 0
@@ -969,19 +881,17 @@
     some(0, 6, states)
     sc = Scan(p, 1, PT, W, L, Z, GR, sx, rx)
     sc.begin()
-    link(5)
+    link(1)
     sc.step(0); sc.step(1); sc.step(2)
     smooth = lambda j: fwd_smooth(U, S, Z, rate, ec, omega, BL, KS, j, 2)
-    some(0, 3, smooth)
-    link(6)
-    some(3, 6, smooth)
+    some(0, 6, smooth)
+    link(2)
     def shift_rows(i):
         y, s = silu_and_slope(BL[ds(i, 8), :, :].reshape(64, 768))
         B["sh"][ds(i, 64), :] = y.astype(bf16)
         B["bs"][ds(i, 64), :] = s.astype(bf16)
     loop(8, shift_rows)
     keep("st", "pt", "sh", "bs")
-    link(7)
     def value(m):
         ACC[...] = dot(NL[...], WA[:, pl.ds(pl.multiple_of(HA + m * 256, 128), 256)])
         def rows(i):
@@ -989,7 +899,6 @@
             B["vl"][ds(i, 64), ds(m, 256)] = y.astype(bf16)
             B["vs"][ds(i, 64), ds(m, 256)] = s.astype(bf16)
         loop(8, rows)
-    some(0, 2, value)
     def mixed(c, w=256): ACC[:, 0:w] = dot(B["sh"][...], WA[:, pl.ds(pl.multiple_of(c, 128), w)])
     def update(m):
         mixed(m * 256)
@@ -1005,18 +914,6 @@
     def direct(m):
         mixed(2432 + m * 256)
         DIR[:, ds(m, 256)] = ACC[...]
-    some(0, 2, update)
-    link(8)
-    some(2, 6, value)
-    keep("vl", "vs")
-    some(2, 3, update)
-    mixed(768, 128)
-    B["sp"][...] = ACC[:, 0:128]
-    some(0, 1, reset)
-    link(9)
-    some(1, 6, reset)
-    keep("re", "rs", "sp")
-    link(10)
     def attend(b):
         rr = ds(b, 128)
         s = B["sp"][rr, :]
@@ -1035,11 +932,28 @@
             a = dot(el, B["vl"][rr, c])
             B["at"][rr, c] = a.astype(bf16)
             B["gt"][rr, c] = (a * RSF[rr, c]).astype(bf16)
+    link(3)
+    some(0, 2, value)
+    some(0, 2, update)
+    link(4)
+    some(2, 5, value)
+    some(2, 3, update)
+    mixed(768, 128)
+    B["sp"][...] = ACC[:, 0:128]
+    some(0, 1, reset)
+    link(5)
+    some(5, 6, value)
+    keep("vl", "vs", "sp")
+    some(1, 4, reset)
+    link(6)
+    some(4, 6, reset)
+    keep("re", "rs")
+    some(0, 1, direct)
     loop(4, attend)
-    some(0, 3, direct)
     keep("pr", "at", "gt")
-    link(11)
-    link(12)
+    link(7)
+    some(1, 3, direct)
+    link(8)
     keep("wa", "wb")
     SQ = B["sq"]
     SQ[...] = jnp.zeros_like(SQ)
@@ -1086,7 +1000,7 @@
         loop(8, rows)
     some(0, 3, down)
     keep("res", "sq")
-    for i in range(n): g.drain(i)
+    g.drain()
     par.drain(); sc.drain()
     first_exchange_drain(p, mx, va, wo, wu, wd, land, s0, r0)
     for name, _, _ in FORWARD_OUT: out(name).wait()
@@ -1103,7 +1017,7 @@
         scratch_shapes=[v(s, t) for _, s, t in FORWARD_OUT] + [v((768, 128), f32), v((24, HA), bf16), v((64, 8, 768), f32), v((512, 768), bf16),
             v((64, 8, 768), f32), v((512, 1536), f32), v((512, 768), f32), v((512, 768), f32), v((512, 256), f32), v((8, 128), f32),
             v((3, 2, 16, 768), f32), v((3, 2, 16, 768), f32), v((2, 16, 768), f32), v((3, 16, 768), f32),
-            D_((4,)), D_((3,)), D_((10,)), D_((10,)), D_((n, 13)), D_((n, 13)), D_((3,)), D_((3,)), D_((len(FORWARD_OUT),))],
+            D_((4,)), D_((3,)), D_((10,)), D_((10,)), D_((n, 11)), D_((n, 11)), D_((3,)), D_((3,)), D_((len(FORWARD_OUT),))],
         compiler_params=pltpu.CompilerParams(collective_id=0, has_side_effects=True, vmem_limit_bytes=62 * 2**20),
     )(tok, valid, affine, prm, mx, va, wo, wu, wd)
 
@@ -1127,35 +1041,18 @@
         s.cp(2, s.L2, s.L2, p.xn).wait_recv()
         t = s.r(p.x, p.c)
         t[...] = t[...] + s.L2[...]
-    def own(s, t): return s.r(s.p.x, s.p.c, t, 1)
-    def zsem(s, d, t): return 2 + t if d == 0 else 6 + t
-    def zflow(s, d, z):
-        p = s.p
-        first = z == (0, 3)[d]
-        on = tuple(range(3, z, -1)) if d == 0 else tuple(range(0, z))
-        for t in on:
-            l = s.L4.at[d, t]
-            if not first:
-                s.cp(s.zsem(d, t), l, l, p.sib).wait_recv()
-                l[...] = l[...] + s.own(t)[...]
-            s.cp(s.zsem(d, t), s.own(t) if first else l, l, p.up if d == 0 else p.dn).start()
-        if not first:
-            l = s.L4.at[d, z]
-            s.cp(s.zsem(d, z), l, l, p.sib).wait_recv()
-    def zstep(s, h):
-        for z, d in ((h, 0), (3 - h, 1)):
-            @pl.when(s.p.z == z)
-            def _(): s.zflow(d, z)
+    def zsend(s):
+        p = s.p
+        for d in (1, 3, 2): rcopy(s.r(p.x, p.c, p.zof(d), 1), s.L4.at[3 - d], s.ss.at[2 + d], s.rs.at[6 - d], p.zn(d)).start()
     def fin(s):
         p = s.p
-        for z in range(4):
-            @pl.when(p.z == z)
-            def _():
-                t = s.own(z)
-                v = t[...]
-                if z > 0: v = v + s.L4[0, z]
-                if z < 3: v = v + s.L4[1, z]
-                t[...] = v
+        t = s.r(p.x, p.c, p.z, 1)
+        v = t[...]
+        for k in range(3):
+            l = s.L4.at[k]
+            s.cp(3 + k, l, l, p.sib).wait_recv()
+            v = v + l[...]
+        t[...] = v
         row = ((p.x * 2 + p.c) * 4 + p.z) * 48
         far = s.T.at[pl.ds(pl.multiple_of(row + (1 - p.y) * 24, 8), 24), :]
         s.cp(9, far, s.G, p.yn).start()
@@ -1167,11 +1064,7 @@
     def drain(s):
         p = s.p
         for k, l in ((0, s.L1.at[0]), (1, s.L1.at[1]), (2, s.L2), (9, s.G)): s.cp(k, l, l, p.sib).wait_send()
-        for d in (0, 1):
-            for t in ((1, 2, 3), (0, 1, 2))[d]:
-                l = s.L4.at[d, t]
-                @pl.when((p.z < t) if d == 0 else (p.z > t))
-                def _(): s.cp(s.zsem(d, t), l, l, p.sib).wait_send()
+        for k in range(3): s.cp(3 + k, s.L4.at[k], s.L4.at[k], p.sib).wait_send()
 
 class Total:
     def __init__(s, pos, R, L, ss, rs):
@@ -1188,20 +1081,23 @@
         for k in range(5): s.cp(k).wait_send()
 
 BACK_IN = ("wa", "wb", "vl", "vs", "re", "rs", "at", "gt", "hi", "hs", "uc", "du", "om", "sh", "bs", "n2", "mi", "sp", "pr", "st", "pt", "tok", "cot")
-ORDER = (5, 6, 0, 1, 2, 3, 4)
-ENTER = {5: 0, 6: 1, 0: 4, 1: 5, 2: 6, 3: 7, 4: 8}
+ENTER = (0, 1, 3, 4, 5, 6, 7)
 
 def backward_kernel(valid, affine, sq, *refs):
     ni = len(BACK_IN)
     I = dict(zip(BACK_IN, refs[:ni]))
     (o_mx, o_va, o_up, o_wo, o_wd, o_gt, o_tiny, o_red) = refs[ni:ni + 8]
     (WA, WB, L1A, L1B, L2A, L2B, L3A, L3B, L4A, L4B, FA, FB, GA, GB_, TOK, PT, U, X0, X1, GT, GG, G1, H, KS, AT, ACC, W, L, Zb, GR,
-     T, TL1, TL2, TL4, TG, TP, RR, RL, ss, rs, sx, rx, st_, rt_, sr, rr_, li, lo) = refs[ni + 8:]
+     T, TL1, TL2, TL4, TG, TP, RR, RL, ss, rs, sx, rx, st_, rt_, sr, rr_, li, lo, lw) = refs[ni + 8:]
     p = Pos()
     sem = {name: i for i, name in enumerate(BACK_IN)}
     def load(name, dst): pltpu.make_async_copy(I[name], dst, li.at[sem[name]]).start()
     def ready(name, dst): pltpu.make_async_copy(I[name], dst, li.at[sem[name]]).wait()
-    n = len(CHUNKS)
+    whole = ((WB, "wb", HB, HB), (WA, "wa", HA + 1536, 1536), (WB, "wb", 0, HB), (WA, "wa", 0, HA + 1536))
+    def part_copy(k):
+        ref, name, c, w = whole[k]
+        return pltpu.make_async_copy(I[name].at[:, pl.ds(c, w)], ref.at[:, pl.ds(c, w)], lw.at[k])
+    def part(k): part_copy(k).start()
     parts = ((0, 1536), (1536, 3072))
     def put(b, half, off, w, get):
         if b == 1: (o_wo, o_wd)[half][:, pl.ds(off, w)] = get(0, w)
@@ -1211,16 +1107,7 @@
                 a, e = max(off, lo_), min(off + w, hi_)
                 if a < e: o[:, pl.ds(a - lo_, e - a)] = get(a - off, e - a)
     g = Scatter(p, (WA, WB), (L1A, L1B), (L2A, L2B), (L3A, L3B), (L4A, L4B), (FA, FB), (GA, GB_), put, ss, rs)
-    def link(t):
-        for i in ORDER:
-            r = t - ENTER[i]
-            if r == 0: g.st0(i)
-            if r == 1: g.a0(i); g.st1(i)
-            if r == 2: g.a1(i); g.st2(i)
-            if r == 3: g.a2(i); g.zstep(i, 0)
-            if r in (4, 5, 6): g.zstep(i, r - 3)
-            if r == 6: g.fin(i)
-            if r == 7: g.last(i)
+    def link(t): g.tick(t, ENTER)
     v = lambda s, t: pltpu.VMEM(s, t)
     big, mid = v((512, 1536), bf16), v((512, 768), bf16)
     rate, ec, omega = PT.at[0:16, :], PT.at[16:32, :], PT.at[34:35, :]
@@ -1230,15 +1117,15 @@
             f(j); return 0
         lax.fori_loop(lo, hi, body, 0)
     def at3(X, i): return X[ds(i, 8), :, :].reshape(64, 768)
-    def dense(P0, P1, P2, P3, P4, P5, P6, GMX, Q0, Q1, Q2, Q3, Q4, SP, PR):
-        load("cot", Q4); load("wb", WB); load("hi", P1); load("hs", P0); load("wa", WA); load("n2", Q1); load("tok", TOK); load("pt", PT)
-        load("gt", P3); load("mi", X0); load("uc", Q2); load("du", Q3); load("rs", P4); load("vl", P5); load("vs", P6); load("sp", SP); load("pr", PR)
+    def dense(P0, P1, P2, P3, P4, P5, P6, GMX, Q0, Q1, Q2, Q3, Q4, SP, PR, SHT, NLT):
+        load("cot", Q4); part(0); load("hs", P0); load("hi", P1); part(1); load("n2", Q1); load("mi", X0); load("uc", Q2); load("du", Q3); load("pt", PT)
+        part(2); load("gt", P3); load("rs", P4); load("vl", P5); load("vs", P6); load("sp", SP); load("pr", PR); part(3); load("tok", TOK)
         full_barrier(p)
         GG[...] = jnp.zeros_like(GG)
         ready("cot", Q4)
         def low(i): Q0[ds(i, 64), :] = (Q4[ds(i, 64), :].astype(f32) * valid[ds(i, 64), :]).astype(bf16)
         loop(8, low)
-        ready("wb", WB); ready("hs", P0); ready("hi", P1)
+        part_copy(0).wait(); ready("hs", P0); ready("hi", P1)
         def f_hidden(m):
             c = ds(m, 256)
             ACC[...] = dot_nt(Q0[...], WB[c, HB:])
@@ -1249,7 +1136,7 @@
             loop(8, rows)
         some(0, 6, f_hidden)
         load("at", P0); load("re", P1)
-        ready("wa", WA); ready("n2", Q1)
+        part_copy(1).wait(); ready("n2", Q1)
         def f_up(m):
             c = ds(m, 256)
             X1[:, :, c] = dot_nt(P2[...], WA[c, HA + 1536:HA + 3072]).reshape(64, 8, 256)
@@ -1271,7 +1158,7 @@
             GMX[r, 2432:3200] = (gm * Q2[r, :].astype(f32)).astype(bf16)
             GT[r, :] = gm * Q1[r, :].astype(f32)
         loop(8, f_norm2)
-        ready("gt", P3); ready("at", P0); ready("re", P1); ready("rs", P4)
+        part_copy(2).wait(); ready("gt", P3); ready("at", P0); ready("re", P1); ready("rs", P4)
         def f_gated(m):
             c = ds(m, 256)
             ACC[...] = dot_nt(GMX[:, 2432:3200], WB[c, 0:HB])
@@ -1310,7 +1197,7 @@
                 RR[0, i:i + 1, :] += jnp.sum(t, axis=0, keepdims=True)
         loop(4, f_attend)
         link(2)
-        ready("bs", Q1); ready("sh", Q0)
+        part_copy(3).wait(); ready("bs", Q1); ready("sh", Q0)
         def f_blend(m):
             c = ds(m, 256)
             ACC[...] = dot_nt(GMX[...], WA[c, 0:HA])
@@ -1323,15 +1210,15 @@
                 X1[k, :, c] += (gb * omega[:, c]).reshape(8, 8, 256)
             loop(8, rows)
         some(0, 3, f_blend)
-        link(3)
-        for i in range(5):
-            lo_, w = CHUNKS[i][1], CHUNKS[i][2]
-            WA[:, lo_:lo_ + w] = dot_tn(Q0[...], GMX[:, lo_:lo_ + w]).astype(bf16)
-            e = min(lo_ + w, 1536)
-            if lo_ < e: WA[:, HA + lo_:HA + e] = dot_tn(Q2[...], P6[:, lo_:e]).astype(bf16)
-            if lo_ + w == HA: WA[:, 2 * HA - 128:] = jnp.zeros((768, 128), bf16)
-            link(4 + i)
-    pl.run_scoped(dense, big, big, big, big, big, big, big, v((512, HA), bf16), mid, mid, mid, mid, mid, v((512, 128), f32), v((512, 128), f32))
+        SHT[...] = Q0[...].T
+        NLT[...] = Q2[...].T
+        for k, (lo_, hi_) in enumerate(((0, 512), (512, 1280), (1280, 2048), (2048, 2816), (2816, 3200))):
+            WA[:, lo_:hi_] = dot(SHT[...], GMX[:, lo_:hi_]).astype(bf16)
+            e = min(hi_, 1536)
+            if lo_ < e: WA[:, HA + lo_:HA + e] = dot(NLT[...], P6[:, lo_:e]).astype(bf16)
+            if hi_ == HA: WA[:, 2 * HA - 128:] = jnp.zeros((768, 128), bf16)
+            link(3 + k)
+    pl.run_scoped(dense, big, big, big, big, big, big, big, v((512, HA), bf16), mid, mid, mid, mid, mid, v((512, 128), f32), v((512, 128), f32), v((768, 512), bf16), v((768, 512), bf16))
     tot = Total(p, RR, RL, sr, rr_)
     for k in range(3):
         t = sub8(sq[pl.ds(k * 8, 8), :]).sum(axis=0, keepdims=True)
@@ -1343,22 +1230,22 @@
         ready("st", S)
         back = lambda j: bwd_states(X0, U, S, rate, A, W.at[0], G1, H, KS, j, 2)
         some(0, 3, back)
-        link(9)
+        link(8)
         some(3, 6, back)
         sc = Scan(p, -1, PT, W, L, Zb, GR, sx, rx)
         sc.begin()
         tot.step(0)
-        link(10)
+        link(9)
         sc.step(0)
         tot.step(1)
         sc.step(1)
         tot.step(2)
         sc.step(2)
-        link(11)
+        link(10)
         grad = lambda j: bwd_grad(X0, U, S, A, Zb, rate, ec, H, X1, KS, AT, j, 2)
         some(0, 3, grad)
         tot.step(3)
-        link(12)
+        link(11)
         some(3, 6, grad)
         tot.step(4)
         sc.drain()
@@ -1385,16 +1272,12 @@
     for j in range(6): T[j * 128:(j + 1) * 128, :] = TP[:, j * 128:(j + 1) * 128].T
     tiny = Tiny(p, T, TL1, TL2, TL4, o_tiny, TG, st_, rt_)
     tiny.st0()
-    link(13)
     tiny.a0()
-    link(14)
-    tiny.a1(); tiny.zstep(0)
-    link(15)
-    for h in (1, 2, 3): tiny.zstep(h)
+    tiny.a1(); tiny.zsend()
+    link(12)
     tiny.fin()
-    link(16)
     tiny.last()
-    for i in range(n): g.drain(i)
+    g.drain()
     tiny.drain(); tot.drain()
     fin.wait()
 
@@ -1408,12 +1291,12 @@
         out_shape=(sds((24, 3200), f32), sds((24, 1536), f32), sds((24, 1536), f32), sds((48, 768), f32), sds((48, 768), f32), sds((512, 768), f32), sds((24, 128), f32), sds((8, 128), f32)),
         in_specs=[vm_] * 3 + [any_] * len(ins),
         out_specs=[vm_] * 5 + [any_] + [vm_] * 2,
-        scratch_shapes=rs_scratch()[:14] + [v((512, 768), bf16), v((128, 768), f32), v((64, 8, 768), f32), v((64, 8, 768), f32), v((64, 8, 768), f32), v((512, 768), f32),
+        scratch_shapes=rs_scratch() + [v((512, 768), bf16), v((128, 768), f32), v((64, 8, 768), f32), v((64, 8, 768), f32), v((64, 8, 768), f32), v((512, 768), f32),
             v((24, 768), f32), v((16, 768), f32), v((16, 768), f32), v((8, 128), f32), v((2, 16, 128), f32), v((512, 256), f32),
             v((3, 2, 16, 768), bf16), v((3, 2, 16, 768), bf16), v((2, 16, 768), f32), v((3, 16, 768), f32),
-            v((768, 128), f32), v((2, 192, 128), f32), v((192, 128), f32), v((2, 4, 48, 128), f32), v((24, 128), f32), v((128, 768), f32),
+            v((768, 128), f32), v((2, 192, 128), f32), v((192, 128), f32), v((3, 48, 128), f32), v((24, 128), f32), v((128, 768), f32),
             v((6, 8, 128), f32), v((5, 8, 128), f32),
-            D_((n, Scatter.NS)), D_((n, Scatter.NS)), D_((3,)), D_((3,)), D_((10,)), D_((10,)), D_((5,)), D_((5,)), D_((len(BACK_IN),)), D_((1,))],
+            D_((n, Scatter.NS)), D_((n, Scatter.NS)), D_((3,)), D_((3,)), D_((10,)), D_((10,)), D_((5,)), D_((5,)), D_((len(BACK_IN),)), D_((1,)), D_((4,))],
         compiler_params=pltpu.CompilerParams(collective_id=1, has_side_effects=True, vmem_limit_bytes=63 * 2**20),
     )(valid, affine, sq, *ins)
 

time: 331 us -> 273 us (0.82)
  Pallas kernels: 309 us -> 251 us
    pallas_call x1, Pallas kernels: 190 us -> 140 us  [backward_call(): pl.pallas_call(backward_kernel, out_shape=(sds((24, 3200), f32), sds((24,...]
    pallas_call x1, Pallas kernels: 119 us -> 111 us  [forward_call(): pl.pallas_call(forward_kernel, out_shape=tuple((jax.ShapeDtypeStruct(s, t...]
where the time goes in v4:
time: 273 us; the launch traced here: 272 us
  Pallas kernels  251 us (92%)
  local copies, waits for them, and re-layouts  14.6 us (5%)
  other arithmetic  5.01 us (2%)
    pallas_call x1, Pallas kernels, backward_call(): pl.pallas_call(backward_kernel, out_shape=(sds((24, 3200), f32), sds((24,...  140 us
    pallas_call x1, Pallas kernels, forward_call(): pl.pallas_call(forward_kernel, out_shape=tuple((jax.ShapeDtypeStruct(s, t...  111 us
    unnamed x30, local copies, waits for them, and re-layouts  11.2 us

profile of v4, /device:TPU:0, one launch (start us, length us, event | category | flops | bytes accessed | tf_op | source)
XLA Modules:
  0.0 272.4 jit_solution(2844023019545341930)
XLA Ops:
  0.7 0.7 fusion.2
  1.4 1.3 pad_convert_fusion.affine
  2.7 0.8 copy.34
  3.4 0.8 copy.36
  4.2 0.8 copy.35
  5.0 0.8 copy.37
  5.8 0.7 select_maximum_fusion.prm
  6.5 0.9 copy.45
  7.3 111.4 %shard_map.228 = (bf16[768,6400]{1,0:T(8,128)(2,1)}, bf16[1536,1536]{1,0:T(8,128)(2,1)}, bf16[512,1536]{1,0:T(8,128)(2,1)}, bf16[512,1536]{1,0:T(8,128)(2,1)}, b...) custom-call(bf16[512,768]{1,0:T(8,128)(2,1)} %bitcast.11, ...), custom_call_target="tpu_custom_call" | custom-call | tf_op jit(solution)/shard_map/pallas_call | solution.py:1013
  118.8 139.9 %shard_map.229 = (f32[24,3200]{1,0:T(8,128)}, f32[24,1536]{1,0:T(8,128)}, f32[24,1536]{1,0:T(8,128)}, f32[48,768]{1,0:T(8,128)}, f32[48,768]{1,0:T(8,128)}, /*in...) custom-call(f32[512,1]{1,0:T(8,128)} %bitcast.14, f32[8,128]{1,0:T(8,128)} %pad_convert_fusion.affine, ...), custom_call_target="tpu_custom_call" | custom-call | tf_op jit(solution)/shard_map/pallas_call | solution.py:1290
  258.7 0.9 slice_reduce_fusion
  259.7 0.6 slice.27
  260.9 1.3 slice.24
  262.2 0.5 divide_sqrt_fusion
  262.7 0.8 slice.23
  263.5 0.7 copy.43
  264.1 0.9 fusion.1
  265.0 0.7 copy.42
  265.6 0.7 copy.40
  266.3 0.7 copy.41
  267.0 0.9 copy.53
  267.9 0.0 copy-done
  267.9 0.0 copy-start.4
  267.9 0.0 copy-start.3
  267.9 1.1 copy.54
  269.0 0.7 copy.55
  269.8 0.0 copy-done.6
  269.8 0.7 copy.56
  270.4 0.7 copy.57
  271.1 0.0 copy-done.4
  271.1 0.7 copy.58
  271.8 0.7 copy.59
  (13 shorter events, 0.1 us)
Async XLA Ops:
  118.8 148.2 %copy-start.1 = (bf16[512,768]{1,0:T(8,128)(2,1)S(1)}, bf16[512,768]{1,0:T(8,128)(2,1)}, u32[]{:S(2)}) copy-start(bf16[512,768]{1,0:T(8,128)(2,1)} %get-tuple-element.44) | copy-start | bytes 2359300
  258.7 9.1 %copy-start = (f32[512,768]{1,0:T(8,128)S(1)}, f32[512,768]{1,0:T(8,128)}, u32[]{:S(2)}) copy-start(f32[512,768]{1,0:T(8,128)} %get-tuple-element.67) | copy-start | bytes 4718596
  267.9 1.2 copy-start.2
  267.9 1.9 copy-start.6
  267.9 2.6 copy-start.5
  267.9 3.2 %copy-start.4 = (f32[24,1536]{1,0:T(8,128)S(1)}, f32[24,1536]{1,0:T(8,128)}, u32[]{:S(2)}) copy-start(f32[24,1536]{1,0:T(8,128)} %get-tuple-element.122) | copy-start | bytes 442372
  267.9 3.9 %copy-start.3 = (f32[48,768]{1,0:T(8,128)S(1)}, f32[48,768]{1,0:T(8,128)}, u32[]{:S(2)}) copy-start(f32[48,768]{1,0:T(8,128)} %get-tuple-element.123) | copy-start | bytes 442372

commit v5 on v4

--- a/solution.py
+++ b/solution.py
@@ -372,11 +372,10 @@
 HA, HB = 3200, 768
 RA, RB = 48, 96
 
-CHUNKS = [(0, 0, 256, "xy"), (0, 256, 256, "yx"), (0, 512, 384, "xy"), (0, 896, 384, "yx"), (0, 1280, 384, "xy"), (0, 1664, 384, "yx"),
-    (0, 2048, 384, "xy"), (0, 2432, 384, "yx"), (0, 2816, 256, "xy"), (0, 3072, 128, "yx"),
-    (1, 0, 256, "xy"), (1, 256, 128, "yx"), (1, 384, 128, "xy"), (1, 512, 256, "yx")]
-GATHER_GROUPS = ((0, 1), (2, 3), (4, 5), (6, 7), (8, 9, 11, 12), (10, 13))
-SCATTER_GROUPS = ((10, 13), (11, 12), (0, 1), (2, 3), (4, 5), (6, 7), (8, 9))
+MXL, VAL, UPL, ONE, DWL = 1664, 1664, 2432, 768, 384
+KINDS = ((0, 0, 1664), (0, 1664, 768), (0, 2432, 768), (1, 0, 384), (1, 384, 384))
+GATHER_CHUNKS = ((0, 1664, 128, "xy"), (0, 1792, 128, "yx"), (0, 1920, 256, "xy"), (0, 2176, 256, "yx"), (0, 0, 384, "xy"), (0, 384, 384, "yx"), (0, 768, 384, "xy"), (0, 1152, 512, "yx"), (1, 0, 128, "xy"), (1, 128, 256, "yx"), (0, 2432, 128, "xy"), (0, 2560, 128, "yx"), (0, 2688, 128, "z"), (0, 2816, 128, "z"), (0, 2944, 128, "z"), (0, 3072, 128, "z"), (1, 384, 128, "xy"), (1, 512, 256, "yx"))
+SCATTER_CHUNKS = ((1, 384, 128, "xy"), (1, 512, 128, "yx"), (1, 640, 128, "yx"), (0, 2432, 384, "xy"), (0, 2816, 384, "yx"), (1, 0, 256, "xy"), (1, 256, 128, "yx"), (0, 1664, 512, "yx"), (0, 2176, 256, "xy"), (0, 0, 384, "xy"), (0, 384, 384, "yx"), (0, 768, 256, "xy"), (0, 1024, 256, "yx"), (0, 1280, 128, "xy"), (0, 1408, 256, "yx"))
 
 class Pos:
     def __init__(s):
@@ -396,20 +395,16 @@
     bar = pltpu.get_barrier_semaphore()
     sig = lambda d: pl.semaphore_signal(bar, inc=1, device_id=d, device_id_type=MESH)
     for d in (p.sib, p.xn, p.yn, p.zn(1), p.zn(2), p.zn(3)): sig(d)
-    @pl.when(p.sq < 7)
-    def _(): sig((p.dp, jnp.minimum(p.sq + 1, 7)))
-    @pl.when(p.sq > 0)
-    def _(): sig((p.dp, jnp.maximum(p.sq - 1, 0)))
-    pl.semaphore_wait(bar, 6 + jnp.clip(p.sq, 0, 1) + jnp.clip(7 - p.sq, 0, 1))
+    pl.semaphore_wait(bar, 6)
 
 def at(ref, rows, nrows, half, w, off, width):
     return ref.at[pl.ds(pl.multiple_of(rows, 48), nrows), pl.ds(pl.multiple_of(half * w + off, 128), width)]
 
 class Gather:
     def __init__(s, pos, bufs, ss, rs):
-        s.p, s.bufs, s.ss, s.rs = pos, bufs, ss, rs
+        s.p, s.bufs, s.ss, s.rs, s.here = pos, bufs, ss, rs, set()
     def unit(s, i, dp, z, half, n=1):
-        b, off, width, _ = CHUNKS[i]
+        b, off, width, _ = GATHER_CHUNKS[i]
         R = (RA, RB)[b]
         return at(s.bufs[b], (dp * 4 + z) * R, n * R, half, (HA, HB)[b], off, width)
     def cp(s, i, k, ref, dev):
@@ -424,52 +419,74 @@
             u = s.unit(i, p.dp, p.zof(d), p.y)
             rcopy(u, u, s.ss.at[i, 0], s.rs.at[i, p.zof(d)], p.sib).wait_recv()
         u = s.unit(i, p.dp, 0, p.y, 4)
-        s.cp(i, 4, u, p.xn if CHUNKS[i][3] == "xy" else p.yn).start()
+        s.cp(i, 4, u, p.xn if GATHER_CHUNKS[i][3] == "xy" else p.yn).start()
         s.cp(i, 7, u, p.sib).start()
-    def s1_in(s, i):
-        p = s.p
-        return s.unit(i, p.dpx, 0, p.y, 4) if CHUNKS[i][3] == "xy" else s.unit(i, p.dp, 0, 1 - p.y, 4)
     def s2(s, i):
         p = s.p
-        r = s.s1_in(i)
+        xy = GATHER_CHUNKS[i][3] == "xy"
+        r = s.unit(i, p.dpx, 0, p.y, 4) if xy else s.unit(i, p.dp, 0, 1 - p.y, 4)
         s.cp(i, 4, r, p.xn).wait_recv()
-        nxt = p.yn if CHUNKS[i][3] == "xy" else p.xn
+        nxt = p.yn if xy else p.xn
         s.cp(i, 5, s.unit(i, p.dp, 0, p.y, 4), nxt).start()
         s.cp(i, 6, r, nxt).start()
         s.cp(i, 8, r, p.sib).start()
-    def s2_in(s, i):
-        p = s.p
-        if CHUNKS[i][3] == "xy":
-            return s.unit(i, p.dp, 0, 1 - p.y, 4), s.unit(i, p.dpx, 0, 1 - p.y, 4)
-        return s.unit(i, p.dpx, 0, p.y, 4), s.unit(i, p.dpx, 0, 1 - p.y, 4)
-    def s3(s, i):
-        for k, r in enumerate(s.s2_in(i)):
-            s.cp(i, 5 + k, r, s.p.sib).wait_recv()
-            s.cp(i, 9 + k, r, s.p.sib).start()
-    def s4(s, i):
-        u = s.unit(i, s.p.dp, 0, s.p.y, 4)
-        for k in (7, 8, 9, 10): s.cp(i, k, u, s.p.sib).wait_recv()
-    def tick(s, t):
-        at_ = lambda k: GATHER_GROUPS[k] if 0 <= k < len(GATHER_GROUPS) else ()
-        for i in at_(t): s.s1(i)
-        for i in at_(t - 1): s.s2(i)
-        for i in at_(t + 1): s.z0(i)
-        for i in at_(t - 2): s.s3(i)
-        for i in at_(t - 3): s.s4(i)
+    def s3(s, i, k):
+        p = s.p
+        if GATHER_CHUNKS[i][3] == "xy": r = s.unit(i, (p.dp, p.dpx)[k], 0, 1 - p.y, 4)
+        else: r = s.unit(i, p.dpx, 0, (p.y, 1 - p.y)[k], 4)
+        s.cp(i, 5 + k, r, p.sib).wait_recv()
+        s.cp(i, 9 + k, r, p.sib).start()
+    def sa(s, i): s.s3(i, 0)
+    def sb(s, i): s.s3(i, 1)
+    def need(s, b, lo, hi):
+        for i, (bb, off, w, _) in enumerate(GATHER_CHUNKS):
+            if bb == b and off < hi and off + w > lo and i not in s.here:
+                s.here.add(i)
+                u = s.unit(i, s.p.dp, 0, s.p.y, 4)
+                for k in (7, 8, 9, 10): s.cp(i, k, u, s.p.sib).wait_recv()
+    def c1(s, i):
+        s.cp(i, 4, s.unit(i, s.p.dp, s.p.z, s.p.y), s.p.xn).start()
+    def c2(s, i):
+        p = s.p
+        r = s.unit(i, p.dpx, p.z, p.y)
+        s.cp(i, 4, r, p.xn).wait_recv()
+        s.cp(i, 5, s.unit(i, p.dp, p.z, p.y), p.yn).start()
+        s.cp(i, 6, r, p.yn).start()
+    def four(s, i, z):
+        p = s.p
+        return [s.unit(i, d, z, h) for d in (p.dp, p.dpx) for h in (p.y, 1 - p.y)]
+    def c3(s, i):
+        p = s.p
+        us = s.four(i, p.z)
+        s.cp(i, 5, us[1], p.yn).wait_recv()
+        s.cp(i, 6, us[3], p.yn).wait_recv()
+        for d in (1, 3, 2):
+            for k, u in enumerate(us):
+                rcopy(u, u, s.ss.at[i, 7 + 4 * d + k], s.rs.at[i, 11 + 4 * (d - 1) + k], p.zn(d)).start()
+    def c4(s, i):
+        p = s.p
+        for d in (1, 2, 3):
+            for k, u in enumerate(s.four(i, p.z)):
+                rcopy(u, u, s.ss.at[i, 0], s.rs.at[i, 11 + 4 * (d - 1) + k], p.sib).wait_recv()
+        for k, (d, h) in enumerate(((p.dp, p.y), (p.dpx, p.y), (p.dp, 1 - p.y), (p.dpx, 1 - p.y))):
+            s.cp(i, 7 + k, s.unit(i, d, 0, h, 4), p.sib).start()
+    def steps(s): return (s.z0, s.s1, s.s2, s.sa, s.sb, s.c1, s.c2, s.c3, s.c4)
     def drain(s):
         p = s.p
-        for i in range(len(CHUNKS)):
+        for i, (_, _, _, order) in enumerate(GATHER_CHUNKS):
             u1 = s.unit(i, p.dp, 0, p.y)
             u = s.unit(i, p.dp, 0, p.y, 4)
-            for k in (4, 5, 6, 7, 8, 9, 10): s.cp(i, k, u, p.sib).wait_send()
-            for k in (0, 1, 2): s.cp(i, k, u1, p.sib).wait_send()
+            one = (4, 5, 6) + tuple(range(11, 23)) if order == "z" else (0, 1, 2)
+            for k in one: s.cp(i, k, u1, p.sib).wait_send()
+            for k in range(4, 11):
+                if k not in one: s.cp(i, k, u, p.sib).wait_send()
 
 class Scatter:
     NS = 11
     def __init__(s, pos, P, L1, L2, L3, L4, F, G, out, ss, rs):
         s.p, s.P, s.L1, s.L2, s.L3, s.L4, s.F, s.G, s.out, s.ss, s.rs = pos, P, L1, L2, L3, L4, F, G, out, ss, rs
     def geom(s, i):
-        b, off, w, order = CHUNKS[i]
+        b, off, w, order = SCATTER_CHUNKS[i]
         return b, (RA, RB)[b], (HA, HB)[b], off, w, order
     def cols(s, i, yy):
         b, R, W, off, w, _ = s.geom(i)
@@ -486,7 +503,7 @@
             return 0
         lax.fori_loop(0, nrows // 48, body, 0)
     def l1(s, i, xx, yy):
-        return s.L1[CHUNKS[i][0]].at[xx, :, s.cols(i, yy)]
+        return s.L1[SCATTER_CHUNKS[i][0]].at[xx, :, s.cols(i, yy)]
     def st0(s, i):
         p = s.p
         for k, (xx, yy) in enumerate(((0, 0), (0, 1), (1, 0), (1, 1))):
@@ -551,23 +568,16 @@
         for yy in (0, 1):
             @pl.when(p.y == 1 - yy)
             def _(): s.out(b, yy, off, w, lambda o, k: l[:, pl.ds(o, k)])
-    def tick(s, t, enter):
-        st = [(t - e, grp) for e, grp in zip(enter, SCATTER_GROUPS)]
-        for r, grp in st:
-            for i in grp:
-                if r == 1: s.a0(i); s.st1(i)
-        for r, grp in st:
-            for i in grp:
-                if r == 2: s.a1(i); s.st2(i)
-        for r, grp in st:
-            for i in grp:
-                if r == 0: s.st0(i)
-                if r == 3: s.a2(i); s.zsend(i)
-                if r == 4: s.fin(i)
-                if r == 5: s.last(i)
+    def r0(s, i): s.st0(i)
+    def r1(s, i): s.a0(i); s.st1(i)
+    def r2(s, i): s.a1(i); s.st2(i)
+    def r3(s, i): s.a2(i); s.zsend(i)
+    def r4(s, i): s.fin(i)
+    def r5(s, i): s.last(i)
+    def steps(s): return (s.r0, s.r1, s.r2, s.r3, s.r4, s.r5)
     def drain(s):
         p = s.p
-        for i in range(len(CHUNKS)):
+        for i in range(len(SCATTER_CHUNKS)):
             b, R, W, off, w, _ = s.geom(i)
             for k, ref in [(k, s.l1(i, 0, 0)) for k in range(4)] + [(4, s.l2(i, 0)), (5, s.l2(i, 1)), (6, s.l3(i)), (10, s.G[b].at[:, pl.ds(off, w)])] + [(7 + k, s.l4(i, k)) for k in range(3)]:
                 s.cp(i, k, ref, ref, p.sib).wait_send()
@@ -602,7 +612,7 @@
             new.append(q8 * st[b] + tree(parts))
         return tuple(new)
     st = lax.fori_loop(0, NK, body, tuple(jnp.zeros((16, 128), f32) for _ in range(NB)), unroll=unroll)
-    for b in range(NB): END[b, :, ln] = st[b]
+    for b in range(NB): END[b, :, ln] = st[b].astype(END.dtype)
 
 def conv_tables(rate, ec, j):
     ln = lanes(j)
@@ -649,9 +659,12 @@
         for b in range(NB):
             i = b * NK + k
             A[i, :, ln] = st[b]
-            p = [w[s] * Gr[i, pl.ds(s, 1), ln] for s in range(8)]
-            Bg = tree(p)
-            B1 = tree([p[s] if s == 1 else p[s] * float(s) for s in range(1, 8)])
+            p = [Gr[i, pl.ds(0, 1), ln]] + [w[s] * Gr[i, pl.ds(s, 1), ln] for s in range(1, 8)]
+            later = B1 = p[7]
+            for t in range(6, 0, -1):
+                later = later + p[t]
+                B1 = B1 + later
+            Bg = later + p[0]
             Sk = S[i, :, ln]
             g1 = g1 + Sk * Bg
             h1 = h1 + Sk * B1
@@ -759,78 +772,85 @@
         for k in (1, 2, 3): s.cp(k, u1, u1, p.sib).wait_send()
 
 class Scan:
-    def __init__(s, pos, way, rate, W, L, Z, GR, ss, rs):
-        s.p, s.way, s.rate, s.W, s.L, s.Z, s.GR, s.ss, s.rs = pos, way, rate, W, L, Z, GR, ss, rs
-    def has(s, d): return (s.p.sq + d < 8) if d > 0 else (s.p.sq + d >= 0)
-    def cp(s, k):
-        d = s.way * 2 ** k
-        return rcopy(s.W.at[k], s.L.at[k], s.ss.at[k], s.rs.at[k], (s.p.dp, jnp.clip(s.p.sq + d, 0, 7)))
-    def send(s, k):
-        @pl.when(s.has(s.way * 2 ** k))
-        def _(): s.cp(k).start()
-    def begin(s):
-        g = jnp.exp(s.rate[0:16, :] * -256.0)
-        s.GR[0] = g; s.GR[1] = g * g; s.GR[2] = g * g * g
-        s.Z[...] = jnp.zeros_like(s.Z)
-        s.send(0)
-    def step(s, k):
-        keep = lambda: (1.0, s.GR[0][None], s.GR[2][None])[k]
-        grow = lambda: (s.GR[0][None], s.GR[1][None])[k]
-        if k < 2: s.W[k + 1] = s.W[k].astype(s.W.dtype)
-        @pl.when(s.has(-s.way * 2 ** k))
-        def _():
-            s.cp(k).wait_recv()
-            s.Z[...] += keep() * s.L[k].astype(f32)
-            if k < 2: s.W[k + 1] = (s.W[k + 1].astype(f32) + grow() * s.L[k].astype(f32)).astype(s.W.dtype)
-        if k < 2: s.send(k + 1)
+    def __init__(s, pos, way, rate, E, L, Z, ss, rs):
+        s.p, s.way, s.rate, s.E, s.L, s.Z, s.ss, s.rs = pos, way, rate, E, L, Z, ss, rs
+    def grow(s, k): return jnp.exp(s.rate[0:16, :] * (-256.0 * k))[None]
+    def cp(s, d):
+        return rcopy(s.E.at[0 if d == 0 else 1], s.L.at[d], s.ss.at[d], s.rs.at[d], s.p.yn if d == 0 else s.p.zn(s.way * d))
+    def sc0(s): s.cp(0).start()
+    def sc1(s):
+        p = s.p
+        s.cp(0).wait_recv()
+        own, got = s.E[0].astype(f32), s.L[0].astype(f32)
+        second = p.y == (1 if s.way > 0 else 0)
+        s.Z[...] = jnp.where(second, got, 0.0)
+        pair = jnp.where(second, own, got) + s.grow(1) * jnp.where(second, got, own)
+        s.E[1] = pair.astype(s.E.dtype)
+        for d in (1, 2, 3):
+            @pl.when((p.z + d <= 3) if s.way > 0 else (p.z - d >= 0))
+            def _(): s.cp(d).start()
+    def sc2(s):
+        p = s.p
+        k = (p.y if s.way > 0 else 1 - p.y).astype(f32)
+        for d in (1, 2, 3):
+            @pl.when((p.z - d >= 0) if s.way > 0 else (p.z + d <= 3))
+            def _():
+                s.cp(d).wait_recv()
+                s.Z[...] += s.grow(k + 2.0 * (d - 1)) * s.L[d].astype(f32)
     def drain(s):
-        for k in range(3):
-            @pl.when(s.has(s.way * 2 ** k))
-            def _(): s.cp(k).wait_send()
-
-def first_exchange_start(p, mx, va, wo, wu, wd, WB, land, s0, r0):
-    cps = {}
-    @pl.when(p.y == 0)
-    def _():
-        rcopy(va, land.at[:, pl.ds(0, 1536)], s0.at[0], r0.at[0], p.yn).start()
-        rcopy(wu, land.at[:, pl.ds(1536, 1536)], s0.at[1], r0.at[1], p.yn).start()
-    @pl.when(p.y == 1)
-    def _():
-        rcopy(mx, land, s0.at[0], r0.at[0], p.yn).start()
-    r = lambda yy: pl.ds(pl.multiple_of((p.dp * 4 + p.z) * RB + yy * 48, 48), 48)
-    for yy, (own, far) in ((0, (wo, wd)), (1, (wd, wo))):
-        @pl.when(p.y == yy)
-        def _():
-            rcopy(far, WB.at[r(yy), pl.ds((1 - yy) * HB, HB)], s0.at[2], r0.at[2], p.yn).start()
-            pltpu.make_async_copy(own, WB.at[r(yy), pl.ds(yy * HB, HB)], s0.at[3]).start()
-
-def first_exchange_end(p, mx, va, wo, wu, wd, WA, WB, land, s0, r0):
-    rows = pl.ds(pl.multiple_of((p.dp * 4 + p.z) * RA, 16), RA)
-    v1, v2 = land.at[:, pl.ds(0, 1536)], land.at[:, pl.ds(1536, 1536)]
-    put = lambda c, w, lo, hi: WA.__setitem__((rows, pl.ds(c, w)), jnp.concatenate([lo[...].astype(f32), hi[...].astype(f32)], axis=0).astype(bf16))
-    u = WB.at[pl.ds(pl.multiple_of((p.dp * 4 + p.z) * RB, 48), 48), pl.ds(0, HB)]
-    @pl.when(p.y == 0)
-    def _():
-        rcopy(mx, land, s0.at[0], r0.at[0], p.yn).wait_recv()
-        put(0, HA, mx, land)
-    @pl.when(p.y == 1)
-    def _():
-        rcopy(va, v1, s0.at[0], r0.at[0], p.yn).wait_recv()
-        rcopy(wu, v2, s0.at[1], r0.at[1], p.yn).wait_recv()
-        put(HA, 1536, v1, va)
-        put(HA + 1536, 1536, v2, wu)
-        WA[rows, pl.ds(HA + 3072, 128)] = jnp.zeros((RA, 128), bf16)
-    rcopy(u, u, s0.at[2], r0.at[2], p.yn).wait_recv()
-    pltpu.make_async_copy(u, u, s0.at[3]).wait()
-def first_exchange_drain(p, mx, va, wo, wu, wd, land, s0, r0):
-    v1 = land.at[:, pl.ds(0, 1536)]
-    @pl.when(p.y == 0)
-    def _():
-        rcopy(va, v1, s0.at[0], r0.at[0], p.yn).wait_send()
-        rcopy(wu, v1, s0.at[1], r0.at[1], p.yn).wait_send()
-    @pl.when(p.y == 1)
-    def _(): rcopy(mx, land, s0.at[0], r0.at[0], p.yn).wait_send()
-    rcopy(wo, wo, s0.at[2], r0.at[2], p.yn).wait_send()
+        p = s.p
+        s.cp(0).wait_send()
+        for d in (1, 2, 3):
+            @pl.when((p.z + d <= 3) if s.way > 0 else (p.z - d >= 0))
+            def _(): s.cp(d).wait_send()
+
+class Halves:
+    def __init__(s, pos, mx, va, wo, wu, wd, WA, WB, land, ss, rs):
+        s.p, s.mx, s.va, s.wo, s.wu, s.wd, s.WA, s.WB, s.land, s.ss, s.rs = pos, mx, va, wo, wu, wd, WA, WB, land, ss, rs
+    def pieces(s, y):
+        return ((s.va, y * 768, VAL, 768), (s.mx, y * MXL, 0, 1536 if y else MXL), (s.wu, y * 768, UPL, 768))
+    def rb(s, yy): return pl.ds(pl.multiple_of((s.p.dp * 4 + s.p.z) * RB + yy * 48, 48), 48)
+    def wb(s, yy, half, k): return s.WB.at[s.rb(yy), pl.ds(half * HB + k * DWL, DWL)]
+    def start(s):
+        p = s.p
+        for yy in (0, 1):
+            @pl.when(p.y == yy)
+            def _():
+                for k, (ref, a, c, w) in enumerate(s.pieces(1 - yy)):
+                    rcopy(ref.at[:, pl.ds(a, w)], s.land.at[:, pl.ds(c, w)], s.ss.at[k], s.rs.at[k], p.yn).start()
+                for k, ref in enumerate((s.wo, s.wd)):
+                    rcopy(ref.at[:, pl.ds((1 - yy) * DWL, DWL)], s.wb(yy, 1 - yy, k), s.ss.at[3 + k], s.rs.at[3 + k], p.yn).start()
+                    pltpu.make_async_copy(ref.at[:, pl.ds(yy * DWL, DWL)], s.wb(yy, yy, k), s.ss.at[5 + k]).start()
+    def end(s, ks):
+        p = s.p
+        rows = pl.ds(pl.multiple_of((p.dp * 4 + p.z) * RA, 16), RA)
+        for yy in (0, 1):
+            @pl.when(p.y == yy)
+            def _():
+                for k, (ref, a, c, w) in enumerate(s.pieces(yy)):
+                    if k not in ks: continue
+                    l = s.land.at[:, pl.ds(c, w)]
+                    rcopy(l, l, s.ss.at[k], s.rs.at[k], p.yn).wait_recv()
+                    both = (ref[:, pl.ds(a, w)], l[...]) if yy == 0 else (l[...], ref[:, pl.ds(a, w)])
+                    s.WA[rows, pl.ds(yy * HA + c, w)] = jnp.concatenate([t.astype(f32) for t in both], axis=0).astype(bf16)
+                if yy == 1 and 1 in ks: s.WA[rows, pl.ds(HA + 1536, 128)] = jnp.zeros((RA, 128), bf16)
+        if 1 in ks:
+            u = s.wb(0, 0, 0)
+            for k in (0, 1):
+                rcopy(u, u, s.ss.at[3 + k], s.rs.at[3 + k], p.yn).wait_recv()
+                pltpu.make_async_copy(u, u, s.ss.at[5 + k]).wait()
+    def hv0(s): s.end((0,))
+    def hv1(s): s.end((1, 2))
+    def drain(s):
+        p = s.p
+        for yy in (0, 1):
+            @pl.when(p.y == yy)
+            def _():
+                for k, (ref, a, c, w) in enumerate(s.pieces(1 - yy)):
+                    l = s.land.at[:, pl.ds(c, w)]
+                    rcopy(l, l, s.ss.at[k], s.rs.at[k], p.yn).wait_send()
+        u = s.wb(0, 0, 0)
+        for k in (0, 1): rcopy(u, u, s.ss.at[3 + k], s.rs.at[3 + k], p.yn).wait_send()
 
 def norm_rows(tok, PT, U, NL, i):
     x = tok[ds(i, 64), :].astype(f32)
@@ -839,6 +859,11 @@
     U[ds(i, 8), :, :] = u.reshape(8, 8, 768)
     NL[ds(i, 64), :] = u.astype(bf16)
 
+def run_plan(plan, steps):
+    for e in plan:
+        if e % 100 == 0: steps[0][e // 100]()
+        else: steps[1][e // 100](e % 100 - 1)
+
 def sub8(v):
     return v.reshape(v.shape[0] // 8, 8, v.shape[1]).sum(axis=0)
 
@@ -846,6 +871,15 @@
     ("re", (512, 1536), bf16), ("rs", (512, 1536), bf16), ("at", (512, 1536), bf16), ("gt", (512, 1536), bf16), ("hi", (512, 1536), bf16), ("hs", (512, 1536), bf16),
     ("uc", (512, 768), bf16), ("du", (512, 768), bf16), ("om", (512, 768), bf16), ("sh", (512, 768), bf16), ("bs", (512, 768), bf16), ("n2", (512, 768), bf16),
     ("mi", (512, 768), f32), ("sp", (512, 128), f32), ("pr", (512, 128), f32), ("st", (64, 16, 768), f32), ("pt", (128, 768), f32), ("res", (512, 768), bf16), ("sq", (24, 768), f32))
+
+FORWARD_PLAN = (
+    0, 100, 200, 300, 704, 701, 500, 400, 703, 804, 600, 1213, 707, 801, 803, 1216, 1313, 700, 901, 708, 904, 903, 800, 1215, 1001, 702, 1,
+    1101, 2, 705, 1316, 807, 808, 1315, 3, 4, 5, 6, 1003, 706, 1214, 712, 900, 805, 908, 1103, 802, 710, 806, 902, 812, 1000, 1004, 1104,
+    905, 912, 907, 906, 1008, 709, 1002, 1005, 1102, 1108, 201, 717, 711, 202, 810, 101, 102, 809, 1007, 718, 103, 1314, 104, 105, 106,
+    1006, 1107, 811, 1416, 817, 1106, 1100, 1012, 909, 401, 910, 203, 1112, 1105, 818, 911, 402, 1413, 1200, 301, 917, 302, 1009, 303, 1109,
+    1414, 403, 918, 1010, 501, 1516, 1110, 1011, 1513, 1415, 502, 503, 504, 1111, 1300, 1017, 1514, 1018, 1117, 1400, 601, 1515, 602, 1118,
+    603, 1500,
+)
 
 def forward_kernel(tok, valid, affine, prm, mx, va, wo, wu, wd, *refs):
     no = len(FORWARD_OUT)
@@ -853,68 +887,72 @@
     B = {name: r for (name, _, _), r in zip(FORWARD_OUT, bufs)}
     O = {name: r for (name, _, _), r in zip(FORWARD_OUT, outs)}
     osem = {name: i for i, (name, _, _) in enumerate(FORWARD_OUT)}
-    (PRM, land, U, NL, BL, RSF, UPD, DIR, ACC, KS, W, L, Z, GR, s0, r0, sp_, rp_, ss, rs, sx, rx, so) = rest
+    (PRM, land, U, NL, BL, RSF, UPD, DIR, ACC, KS, E, L, Z, s0, r0, sp_, rp_, ss, rs, sx, rx, so, sw) = rest
     WA, WB, PT, S = B["wa"], B["wb"], B["pt"], B["st"]
     p = Pos()
     full_barrier(p)
     out = lambda name: pltpu.make_async_copy(B[name], O[name], so.at[osem[name]])
     def keep(*names):
         for name in names: out(name).start()
+    def weight(k, h):
+        b, c, w = KINDS[k]
+        a, o = ((WA, O["wa"]), (WB, O["wb"]))[b]
+        cols = pl.ds((HA, HB)[b] * h + c, w)
+        return pltpu.make_async_copy(a.at[:, cols], o.at[:, cols], sw.at[k, h])
+    def keep_weight(k):
+        for h in (0, 1): weight(k, h).start()
     par = Params(p, prm, PRM, sp_, rp_)
-    par.y0()
-    first_exchange_start(p, mx, va, wo, wu, wd, WB, land, s0, r0)
+    hv = Halves(p, mx, va, wo, wu, wd, WA, WB, land, s0, r0)
     g = Gather(p, (WA, WB), ss, rs)
-    link = g.tick
-    par.y1(); par.z0()
-    first_exchange_end(p, mx, va, wo, wu, wd, WA, WB, land, s0, r0)
-    for i in GATHER_GROUPS[0]: g.z0(i)
-    par.x0(); par.x1(); par.end()
-    link(0)
-    for j in range(6): PT[:, j * 128:(j + 1) * 128] = PRM[j * 128:(j + 1) * 128, :].T
     rate, ec, omega = PT.at[0:16, :], PT.at[16:32, :], PT.at[34:35, :]
-    loop(8, lambda i: norm_rows(tok, PT, U, NL, i))
-    def some(lo, hi, f):
-        def body(j, _):
-            f(j); return 0
-        lax.fori_loop(lo, hi, body, 0)
-    states = lambda j: fwd_states(U, rate, S, W.at[0], j, 4)
-    some(0, 6, states)
-    sc = Scan(p, 1, PT, W, L, Z, GR, sx, rx)
-    sc.begin()
-    link(1)
-    sc.step(0); sc.step(1); sc.step(2)
-    smooth = lambda j: fwd_smooth(U, S, Z, rate, ec, omega, BL, KS, j, 2)
-    some(0, 6, smooth)
-    link(2)
-    def shift_rows(i):
-        y, s = silu_and_slope(BL[ds(i, 8), :, :].reshape(64, 768))
-        B["sh"][ds(i, 64), :] = y.astype(bf16)
-        B["bs"][ds(i, 64), :] = s.astype(bf16)
-    loop(8, shift_rows)
-    keep("st", "pt", "sh", "bs")
-    def value(m):
-        ACC[...] = dot(NL[...], WA[:, pl.ds(pl.multiple_of(HA + m * 256, 128), 256)])
+    sc = Scan(p, 1, PT, E, L, Z, sx, rx)
+    SQ = B["sq"]
+    def par1(): par.y1(); par.z0()
+    def pt():
+        par.end()
+        for j in range(6): PT[:, j * 128:(j + 1) * 128] = PRM[j * 128:(j + 1) * 128, :].T
+    def norm(): loop(8, lambda i: norm_rows(tok, PT, U, NL, i))
+    def st(j): fwd_states(U, rate, S, E.at[0], j, 4)
+    def sm(j):
+        if j == 0: sc.sc2()
+        fwd_smooth(U, S, Z, rate, ec, omega, BL, KS, j, 2)
+    def sh():
         def rows(i):
-            y, s = silu_and_slope(ACC[ds(i, 64), :])
-            B["vl"][ds(i, 64), ds(m, 256)] = y.astype(bf16)
-            B["vs"][ds(i, 64), ds(m, 256)] = s.astype(bf16)
+            y, s = silu_and_slope(BL[ds(i, 8), :, :].reshape(64, 768))
+            B["sh"][ds(i, 64), :] = y.astype(bf16)
+            B["bs"][ds(i, 64), :] = s.astype(bf16)
         loop(8, rows)
-    def mixed(c, w=256): ACC[:, 0:w] = dot(B["sh"][...], WA[:, pl.ds(pl.multiple_of(c, 128), w)])
-    def update(m):
-        mixed(m * 256)
-        loop(8, lambda i: UPD.__setitem__((ds(i, 64), ds(m, 256)), sigmoid(ACC[ds(i, 64), :])))
-    def reset(m):
-        mixed(896 + m * 256)
+        keep("st", "pt", "sh", "bs")
+    def both(name, slope, m, c, w=256):
         def rows(i):
-            y, s = silu_and_slope(ACC[ds(i, 64), :])
-            RSF[ds(i, 64), ds(m, 256)] = y
-            B["re"][ds(i, 64), ds(m, 256)] = y.astype(bf16)
-            B["rs"][ds(i, 64), ds(m, 256)] = s.astype(bf16)
+            y, s = silu_and_slope(ACC[ds(i, 64), 0:256])
+            B[name][ds(i, 64), ds(m, 256)] = y.astype(bf16)
+            B[slope][ds(i, 64), ds(m, 256)] = s.astype(bf16)
+            if name == "re": RSF[ds(i, 64), ds(m, 256)] = y
         loop(8, rows)
-    def direct(m):
-        mixed(2432 + m * 256)
-        DIR[:, ds(m, 256)] = ACC[...]
-    def attend(b):
+    def mul(x, ref, c, w=256): ACC[:, 0:w] = dot(x[...], ref[:, c:c + w])
+    def va_(k):
+        g.need(0, VAL + 256 * k, VAL + 256 * k + 256)
+        for h in (0, 1):
+            mul(NL, WA, h * HA + VAL + 256 * k)
+            both("vl", "vs", 3 * h + k, 0)
+        if k == 2: keep("vl", "vs"); keep_weight(1)
+    def mu(k):
+        g.need(0, 256 * k, 256 * k + 256)
+        mul(B["sh"], WA, 256 * k)
+        loop(8, lambda i: UPD.__setitem__((ds(i, 64), ds(k, 256)), sigmoid(ACC[ds(i, 64), 0:256])))
+        mul(B["sh"], WA, HA + 256 * k)
+        both("re", "rs", 3 + k, 0)
+    def ms():
+        g.need(0, 768, 896)
+        mul(B["sh"], WA, 768, 128)
+        B["sp"][...] = ACC[:, 0:128]
+    def md(k):
+        g.need(0, 768 + 256 * k, 1152 + 256 * k)
+        mul(B["sh"], WA, 896 + 256 * k)
+        both("re", "rs", k, 0)
+        DIR[:, ds(k, 256)] = dot(B["sh"][...], WA[:, HA + 768 + 256 * k:HA + 1024 + 256 * k])
+    def at_(b):
         rr = ds(b, 128)
         s = B["sp"][rr, :]
         s = s * sigmoid(s)
@@ -932,82 +970,64 @@
             a = dot(el, B["vl"][rr, c])
             B["at"][rr, c] = a.astype(bf16)
             B["gt"][rr, c] = (a * RSF[rr, c]).astype(bf16)
-    link(3)
-    some(0, 2, value)
-    some(0, 2, update)
-    link(4)
-    some(2, 5, value)
-    some(2, 3, update)
-    mixed(768, 128)
-    B["sp"][...] = ACC[:, 0:128]
-    some(0, 1, reset)
-    link(5)
-    some(5, 6, value)
-    keep("vl", "vs", "sp")
-    some(1, 4, reset)
-    link(6)
-    some(4, 6, reset)
-    keep("re", "rs")
-    some(0, 1, direct)
-    loop(4, attend)
-    keep("pr", "at", "gt")
-    link(7)
-    some(1, 3, direct)
-    link(8)
-    keep("wa", "wb")
-    SQ = B["sq"]
-    SQ[...] = jnp.zeros_like(SQ)
-    def candidate(m):
-        ACC[...] = dot(B["gt"][...], WB[:, ds(m, 256)])
+        if b == 3: keep("re", "rs", "sp", "pr", "at", "gt"); keep_weight(0)
+    def ca():
+        g.need(1, 0, DWL)
+        SQ[...] = jnp.zeros_like(SQ)
+        for m in range(2):
+            ACC[...] = dot(B["gt"][...], WB[:, m * HB:m * HB + DWL])
+            def rows(i):
+                r, c = ds(i, 64), pl.ds(m * DWL, DWL)
+                y, s = silu_and_slope(DIR[r, c] + ACC[r, :])
+                u = UPD[r, c]
+                x = tok[r, c].astype(f32)
+                a = u * (y - x)
+                B["mi"][r, c] = x + a
+                B["uc"][r, c] = (u * s).astype(bf16)
+                B["du"][r, c] = (a * (1.0 - u)).astype(bf16)
+                B["om"][r, c] = (1.0 - u).astype(bf16)
+                SQ[8:16, c] += sub8(valid[r, :] * a * a)
+            loop(8, rows)
+        keep_weight(3)
+    def n2():
         def rows(i):
-            r, c = ds(i, 64), ds(m, 256)
-            y, s = silu_and_slope(DIR[r, c] + ACC[r, :])
-            u = UPD[r, c]
-            x = tok[r, c].astype(f32)
-            a = u * (y - x)
-            B["mi"][r, c] = x + a
-            B["uc"][r, c] = (u * s).astype(bf16)
-            B["du"][r, c] = (a * (1.0 - u)).astype(bf16)
-            B["om"][r, c] = (1.0 - u).astype(bf16)
-            SQ[8:16, c] += sub8(valid[r, :] * a * a)
+            v = B["mi"][ds(i, 64), :]
+            r = lax.rsqrt(jnp.mean(v * v, axis=-1, keepdims=True) + EPSILON)
+            B["n2"][ds(i, 64), :] = (v * r * PT[33:34, :]).astype(bf16)
         loop(8, rows)
-    some(0, 3, candidate)
-    def second(i):
-        v = B["mi"][ds(i, 64), :]
-        r = lax.rsqrt(jnp.mean(v * v, axis=-1, keepdims=True) + EPSILON)
-        B["n2"][ds(i, 64), :] = (v * r * PT[33:34, :]).astype(bf16)
-    loop(8, second)
-    keep("mi", "uc", "du", "om", "n2")
-    def up(m):
-        ACC[...] = dot(B["n2"][...], WA[:, pl.ds(pl.multiple_of(HA + 1536 + m * 256, 128), 256)])
-        def rows(i):
-            y, s = silu_and_slope(ACC[ds(i, 64), :])
-            B["hi"][ds(i, 64), ds(m, 256)] = y.astype(bf16)
-            B["hs"][ds(i, 64), ds(m, 256)] = s.astype(bf16)
-        loop(8, rows)
-    some(0, 6, up)
-    keep("hi", "hs")
-    def down(m):
-        ACC[...] = dot(B["hi"][...], WB[:, pl.ds(pl.multiple_of(HB + m * 256, 128), 256)])
-        def rows(i):
-            r, c = ds(i, 64), ds(m, 256)
-            f = ACC[r, :]
-            o = B["mi"][r, c] + f
-            B["res"][r, c] = o.astype(bf16)
-            v = valid[r, :]
-            SQ[0:8, c] += sub8(v * o * o)
-            SQ[16:24, c] += sub8(v * f * f)
-        loop(8, rows)
-    some(0, 3, down)
-    keep("res", "sq")
-    g.drain()
-    par.drain(); sc.drain()
-    first_exchange_drain(p, mx, va, wo, wu, wd, land, s0, r0)
-    for name, _, _ in FORWARD_OUT: out(name).wait()
+        keep("mi", "uc", "du", "om", "n2")
+    def up(k):
+        g.need(0, UPL + 256 * k, UPL + 256 * k + 256)
+        for h in (0, 1):
+            mul(B["n2"], WA, h * HA + UPL + 256 * k)
+            both("hi", "hs", 3 * h + k, 0)
+    def do():
+        keep("hi", "hs"); keep_weight(2)
+        g.need(1, DWL, 2 * DWL)
+        keep_weight(4)
+        for m in range(2):
+            ACC[...] = dot(B["hi"][...], WB[:, m * HB + DWL:m * HB + 2 * DWL])
+            def rows(i):
+                r, c = ds(i, 64), pl.ds(m * DWL, DWL)
+                f = ACC[r, :]
+                o = B["mi"][r, c] + f
+                B["res"][r, c] = o.astype(bf16)
+                v = valid[r, :]
+                SQ[0:8, c] += sub8(v * o * o)
+                SQ[16:24, c] += sub8(v * f * f)
+            loop(8, rows)
+        keep("res", "sq")
+    steps = (par.y0, hv.start, par1, hv.hv0, hv.hv1, par.x0, par.x1, pt, norm, sc.sc0, sc.sc1, sh, ms, ca, n2, do), (st, sm, va_, mu, md, at_, up) + g.steps()
+    run_plan(FORWARD_PLAN, steps)
+    g.drain(); par.drain(); sc.drain(); hv.drain()
+    for name, _, _ in FORWARD_OUT[2:]: out(name).wait()
+    for k in range(len(KINDS)):
+        for h in (0, 1): weight(k, h).wait()
 
 Z_SCALE = Z ** -0.5
+SCAN_TYPE = f32
 def forward_call(tok, valid, affine, prm, mx, va, wo, wu, wd):
-    n = len(CHUNKS)
+    n = len(GATHER_CHUNKS)
     v = pltpu.VMEM
     D_ = pltpu.SemaphoreType.DMA
     return pl.pallas_call(forward_kernel,
@@ -1015,9 +1035,9 @@
         in_specs=[pl.BlockSpec(memory_space=pltpu.VMEM)] * 9,
         out_specs=[pl.BlockSpec(memory_space=pl.ANY)] * len(FORWARD_OUT),
         scratch_shapes=[v(s, t) for _, s, t in FORWARD_OUT] + [v((768, 128), f32), v((24, HA), bf16), v((64, 8, 768), f32), v((512, 768), bf16),
-            v((64, 8, 768), f32), v((512, 1536), f32), v((512, 768), f32), v((512, 768), f32), v((512, 256), f32), v((8, 128), f32),
-            v((3, 2, 16, 768), f32), v((3, 2, 16, 768), f32), v((2, 16, 768), f32), v((3, 16, 768), f32),
-            D_((4,)), D_((3,)), D_((10,)), D_((10,)), D_((n, 11)), D_((n, 11)), D_((3,)), D_((3,)), D_((len(FORWARD_OUT),))],
+            v((64, 8, 768), f32), v((512, 1536), f32), v((512, 768), f32), v((512, 768), f32), v((512, 384), f32), v((8, 128), f32),
+            v((2, 2, 16, 768), SCAN_TYPE), v((4, 2, 16, 768), SCAN_TYPE), v((2, 16, 768), f32),
+            D_((7,)), D_((5,)), D_((10,)), D_((10,)), D_((n, 23)), D_((n, 23)), D_((4,)), D_((4,)), D_((len(FORWARD_OUT),)), D_((len(KINDS), 2))],
         compiler_params=pltpu.CompilerParams(collective_id=0, has_side_effects=True, vmem_limit_bytes=62 * 2**20),
     )(tok, valid, affine, prm, mx, va, wo, wu, wd)
 
@@ -1081,104 +1101,124 @@
         for k in range(5): s.cp(k).wait_send()
 
 BACK_IN = ("wa", "wb", "vl", "vs", "re", "rs", "at", "gt", "hi", "hs", "uc", "du", "om", "sh", "bs", "n2", "mi", "sp", "pr", "st", "pt", "tok", "cot")
-ENTER = (0, 1, 3, 4, 5, 6, 7)
+MX_PARTS = ((0, 384), (384, 384), (768, 256), (1024, 256), (1280, 128), (1408, 256))
+BACKWARD_PLAN = (
+    800, 701, 702, 703, 704, 705, 706, 2, 1, 3, 801, 802, 102, 803, 101, 4, 900, 103, 901, 5, 104, 902, 903, 904, 905, 201, 906, 6, 105,
+    202, 7, 1001, 1002, 1000, 106, 1003, 1004, 701, 204, 702, 301, 703, 107, 302, 700, 901, 801, 902, 802, 803, 205, 903, 800, 206, 304, 8,
+    1106, 203, 1101, 1001, 10, 207, 305, 108, 15, 1102, 1002, 110, 1003, 1105, 306, 1104, 9, 14, 13, 1004, 1005, 303, 307, 1006, 11, 113, 0,
+    601, 1103, 114, 208, 100, 111, 213, 602, 308, 210, 109, 12, 1201, 115, 1202, 211, 313, 603, 112, 1203, 1204, 310, 214, 408, 404, 1205,
+    1206, 311, 209, 401, 900, 212, 314, 413, 200, 407, 215, 309, 312, 406, 300, 402, 409, 414, 315, 411, 509, 504, 400, 412, 403, 405, 501,
+    514, 410, 511, 502, 415, 604, 512, 500, 505, 605, 507, 506, 513, 515, 503, 508, 510, 600,
+)
+CUT = 37
 
 def backward_kernel(valid, affine, sq, *refs):
     ni = len(BACK_IN)
     I = dict(zip(BACK_IN, refs[:ni]))
     (o_mx, o_va, o_up, o_wo, o_wd, o_gt, o_tiny, o_red) = refs[ni:ni + 8]
-    (WA, WB, L1A, L1B, L2A, L2B, L3A, L3B, L4A, L4B, FA, FB, GA, GB_, TOK, PT, U, X0, X1, GT, GG, G1, H, KS, AT, ACC, W, L, Zb, GR,
-     T, TL1, TL2, TL4, TG, TP, RR, RL, ss, rs, sx, rx, st_, rt_, sr, rr_, li, lo, lw) = refs[ni + 8:]
+    (WA, WB, L1A, L1B, L2A, L2B, L3A, L3B, L4A, L4B, FA, FB, GA, GB_, TOK, PT, U, X0, X1, GT, GG, G1, H, KS, AT, ACC, E, L, Zb,
+     T, TL1, TL2, TL4, TG, TP, RR, RL, P6, GMX, Q0, Q1, Q2, SHT, SP, ss, rs, sx, rx, st_, rt_, sr, rr_, li, lo, lw) = refs[ni + 8:]
     p = Pos()
     sem = {name: i for i, name in enumerate(BACK_IN)}
     def load(name, dst): pltpu.make_async_copy(I[name], dst, li.at[sem[name]]).start()
-    def ready(name, dst): pltpu.make_async_copy(I[name], dst, li.at[sem[name]]).wait()
-    whole = ((WB, "wb", HB, HB), (WA, "wa", HA + 1536, 1536), (WB, "wb", 0, HB), (WA, "wa", 0, HA + 1536))
-    def part_copy(k):
-        ref, name, c, w = whole[k]
-        return pltpu.make_async_copy(I[name].at[:, pl.ds(c, w)], ref.at[:, pl.ds(c, w)], lw.at[k])
-    def part(k): part_copy(k).start()
-    parts = ((0, 1536), (1536, 3072))
+    def ready(*pairs):
+        for name, dst in pairs: pltpu.make_async_copy(I[name], dst, li.at[sem[name]]).wait()
+    def part_copies(k):
+        b, c, w = KINDS[k]
+        for h in (0, 1):
+            cols = pl.ds((HA, HB)[b] * h + c, w)
+            yield pltpu.make_async_copy(I[("wa", "wb")[b]].at[:, cols], (WA, WB)[b].at[:, cols], lw.at[k, h])
+    def part(k):
+        for cp in part_copies(k): cp.start()
+    def part_ready(k):
+        for cp in part_copies(k): cp.wait()
     def put(b, half, off, w, get):
-        if b == 1: (o_wo, o_wd)[half][:, pl.ds(off, w)] = get(0, w)
-        elif half == 0: o_mx[:, pl.ds(off, w)] = get(0, w)
-        else:
-            for (lo_, hi_), o in zip(parts, (o_va, o_up)):
-                a, e = max(off, lo_), min(off + w, hi_)
-                if a < e: o[:, pl.ds(a - lo_, e - a)] = get(a - off, e - a)
+        outs = ((o_wo, 0, 384, 384), (o_wd, 384, 768, 384)) if b else ((o_mx, 0, 1536 if half else MXL, MXL), (o_va, VAL, UPL, 768), (o_up, UPL, HA, 768))
+        for o, lo_, hi_, step in outs:
+            a, e = max(off, lo_), min(off + w, hi_)
+            if a < e: o[:, pl.ds(a - lo_ + half * step, e - a)] = get(a - off, e - a)
     g = Scatter(p, (WA, WB), (L1A, L1B), (L2A, L2B), (L3A, L3B), (L4A, L4B), (FA, FB), (GA, GB_), put, ss, rs)
-    def link(t): g.tick(t, ENTER)
+    tot = Total(p, RR, RL, sr, rr_)
+    sc = Scan(p, -1, PT, E, L, Zb, sx, rx)
+    tiny = Tiny(p, T, TL1, TL2, TL4, o_tiny, TG, st_, rt_)
     v = lambda s, t: pltpu.VMEM(s, t)
     big, mid = v((512, 1536), bf16), v((512, 768), bf16)
     rate, ec, omega = PT.at[0:16, :], PT.at[16:32, :], PT.at[34:35, :]
     gain1, gain2 = PT.at[32:33, :], PT.at[33:34, :]
-    def some(lo, hi, f):
-        def body(j, _):
-            f(j); return 0
-        lax.fori_loop(lo, hi, body, 0)
     def at3(X, i): return X[ds(i, 8), :, :].reshape(64, 768)
-    def dense(P0, P1, P2, P3, P4, P5, P6, GMX, Q0, Q1, Q2, Q3, Q4, SP, PR, SHT, NLT):
-        load("cot", Q4); part(0); load("hs", P0); load("hi", P1); part(1); load("n2", Q1); load("mi", X0); load("uc", Q2); load("du", Q3); load("pt", PT)
-        part(2); load("gt", P3); load("rs", P4); load("vl", P5); load("vs", P6); load("sp", SP); load("pr", PR); part(3); load("tok", TOK)
+    def pair(ref, rows, c, w, step): return jnp.concatenate([ref[rows, c:c + w], ref[rows, c + step:c + step + w]], axis=1)
+    def ti2(): tiny.a1(); tiny.zsend()
+    def to0():
+        for k in range(3):
+            t = sub8(sq[pl.ds(k * 8, 8), :]).sum(axis=0, keepdims=True)
+            RR[0, 3 + k:4 + k, :] = sum(t[:, j * 128:(j + 1) * 128] for j in range(6))
+        RR[0, 6:7, :] = jnp.broadcast_to(jnp.sum(valid[...], axis=0, keepdims=True) * (1.0 / 128.0), (1, 128))
+        tot.send(0)
+    alone = (sc.sc0, sc.sc1, tiny.st0, tiny.a0, ti2, tiny.fin, tiny.last, to0)
+    many = g.steps() + (tot.step,)
+    def first(P0, P1, P2, P3, P4, P5, Q3, Q4, PR):
+        load("cot", Q4); part(4); load("hs", P0); load("hi", P1); part(2); load("n2", Q1); load("mi", X0); load("uc", Q2); load("du", Q3); load("pt", PT)
+        part(3); load("gt", P3); load("rs", P4); load("vl", P5); load("vs", P6); load("sp", SP); load("pr", PR); part(1); load("tok", TOK); part(0)
         full_barrier(p)
-        GG[...] = jnp.zeros_like(GG)
-        ready("cot", Q4)
-        def low(i): Q0[ds(i, 64), :] = (Q4[ds(i, 64), :].astype(f32) * valid[ds(i, 64), :]).astype(bf16)
-        loop(8, low)
-        part_copy(0).wait(); ready("hs", P0); ready("hi", P1)
-        def f_hidden(m):
-            c = ds(m, 256)
-            ACC[...] = dot_nt(Q0[...], WB[c, HB:])
-            WB[c, HB:] = dot_tn(P1[:, c], Q0[...]).astype(bf16)
+        def lo_():
+            GG[...] = jnp.zeros_like(GG)
+            RR[0] = jnp.zeros((8, 128), f32)
+            ready(("cot", Q4))
+            def rows(i): Q0[ds(i, 64), :] = (Q4[ds(i, 64), :].astype(f32) * valid[ds(i, 64), :]).astype(bf16)
+            loop(8, rows)
+            part_ready(4); ready(("hs", P0), ("hi", P1))
+        def hi(m):
+            c = pl.ds(m * 256, 256)
+            ACC[...] = dot_nt(Q0[...], pair(WB, c, DWL, DWL, HB))
+            t = dot_tn(P1[:, c], Q0[...]).astype(bf16)
+            WB[c, DWL:HB], WB[c, HB + DWL:] = t[:, :DWL], t[:, DWL:]
             def rows(i):
                 r = ds(i, 64)
                 P2[r, c] = (ACC[r, :] * P0[r, c].astype(f32)).astype(bf16)
             loop(8, rows)
-        some(0, 6, f_hidden)
-        load("at", P0); load("re", P1)
-        part_copy(1).wait(); ready("n2", Q1)
-        def f_up(m):
-            c = ds(m, 256)
-            X1[:, :, c] = dot_nt(P2[...], WA[c, HA + 1536:HA + 3072]).reshape(64, 8, 256)
-            WA[c, HA + 1536:HA + 3072] = dot_tn(Q1[:, c], P2[...]).astype(bf16)
-        some(0, 3, f_up)
-        ready("mi", X0); ready("uc", Q2); ready("du", Q3); ready("pt", PT)
-        load("sh", Q0);
-        load("om", Q1)
-        ready("om", Q1)
-        def f_norm2(i):
-            r = ds(i, 64)
-            m_, k = at3(X0, i), at3(X1, i)
-            inv = lax.rsqrt(jnp.mean(m_ * m_, axis=-1, keepdims=True) + EPSILON)
-            unit = m_ * inv
-            GG[0:8, :] += sub8(k * unit)
-            k = k * gain2[...]
-            gm = Q4[r, :].astype(f32) * valid[r, :] + inv * (k - unit * jnp.mean(k * unit, axis=-1, keepdims=True))
-            GMX[r, 0:768] = (gm * Q3[r, :].astype(f32)).astype(bf16)
-            GMX[r, 2432:3200] = (gm * Q2[r, :].astype(f32)).astype(bf16)
-            GT[r, :] = gm * Q1[r, :].astype(f32)
-        loop(8, f_norm2)
-        part_copy(2).wait(); ready("gt", P3); ready("at", P0); ready("re", P1); ready("rs", P4)
-        def f_gated(m):
-            c = ds(m, 256)
-            ACC[...] = dot_nt(GMX[:, 2432:3200], WB[c, 0:HB])
-            WB[c, 0:HB] = dot_tn(P3[:, c], GMX[:, 2432:3200]).astype(bf16)
-            c2 = pl.ds(pl.multiple_of(896 + m * 256, 128), 256)
+            if m == 5: load("at", P0); load("re", P1)
+        def ub(m):
+            if m == 0: part_ready(2); ready(("n2", Q1))
+            c = pl.ds(m * 256, 256)
+            X1[:, :, c] = (dot_nt(P2[:, 0:768], WA[c, UPL:HA]) + dot_nt(P2[:, 768:], WA[c, HA + UPL:])).reshape(64, 8, 256)
+            WA[c, UPL:HA] = dot_tn(Q1[:, c], P2[:, 0:768]).astype(bf16)
+            WA[c, HA + UPL:] = dot_tn(Q1[:, c], P2[:, 768:]).astype(bf16)
+        def nb():
+            load("sh", Q0)
+            load("om", Q1)
+            ready(("mi", X0), ("uc", Q2), ("du", Q3), ("pt", PT), ("om", Q1))
+            def rows(i):
+                r = ds(i, 64)
+                m_, k = at3(X0, i), at3(X1, i)
+                inv = lax.rsqrt(jnp.mean(m_ * m_, axis=-1, keepdims=True) + EPSILON)
+                unit = m_ * inv
+                GG[0:8, :] += sub8(k * unit)
+                k = k * gain2[...]
+                gm = Q4[r, :].astype(f32) * valid[r, :] + inv * (k - unit * jnp.mean(k * unit, axis=-1, keepdims=True))
+                GMX[r, 0:768] = (gm * Q3[r, :].astype(f32)).astype(bf16)
+                GMX[r, 2432:3200] = (gm * Q2[r, :].astype(f32)).astype(bf16)
+                GT[r, :] = gm * Q1[r, :].astype(f32)
+            loop(8, rows)
+            load("bs", Q1)
+        def ga(m):
+            if m == 0: part_ready(3); ready(("gt", P3), ("at", P0), ("re", P1), ("rs", P4))
+            c = pl.ds(m * 256, 256)
+            gc = GMX[:, 2432:3200]
+            ACC[...] = dot_nt(gc, pair(WB, c, 0, DWL, HB))
+            t = dot_tn(P3[:, c], gc).astype(bf16)
+            WB[c, 0:DWL], WB[c, HB:HB + DWL] = t[:, :DWL], t[:, DWL:]
+            c2 = pl.ds(896 + m * 256, 256)
             def rows(i):
                 r = ds(i, 64)
                 a = ACC[r, :]
                 P2[r, c] = (a * P1[r, c].astype(f32)).astype(bf16)
                 GMX[r, c2] = (a * P0[r, c].astype(f32) * P4[r, c].astype(f32)).astype(bf16)
             loop(8, rows)
-        some(0, 6, f_gated)
-        link(0)
-        load("bs", Q1)
-        ready("tok", TOK)
-        loop(8, lambda i: norm_rows(TOK, PT, U, Q2, i))
-        link(1)
-        ready("vl", P5); ready("vs", P6); ready("sp", SP); ready("pr", PR)
-        RR[0] = jnp.zeros((8, 128), f32)
-        def f_attend(b):
+        def nr():
+            ready(("tok", TOK))
+            loop(8, lambda i: norm_rows(TOK, PT, U, Q2, i))
+        def at_(b):
+            if b == 0: ready(("vl", P5), ("vs", P6), ("sp", SP), ("pr", PR))
             r = ds(b, 128)
             pr = PR[r, :]
             gp = dot_nt(P2[r, :], P5[r, :])
@@ -1195,13 +1235,22 @@
             GMX[r, 768:896] = ((gq * affine[0:1, :] + gk * affine[2:3, :]) * slope).astype(bf16)
             for i, t in enumerate((gq * s, gq, gk * s)):
                 RR[0, i:i + 1, :] += jnp.sum(t, axis=0, keepdims=True)
-        loop(4, f_attend)
-        link(2)
-        part_copy(3).wait(); ready("bs", Q1); ready("sh", Q0)
-        def f_blend(m):
-            c = ds(m, 256)
-            ACC[...] = dot_nt(GMX[...], WA[c, 0:HA])
-            X1[:, :, c] = dot_nt(P6[...], WA[c, HA:HA + 1536]).reshape(64, 8, 256)
+        run_plan(BACKWARD_PLAN[:CUT], (alone + (lo_, nb, nr), many + (hi, ub, ga, at_)))
+    pl.run_scoped(first, big, big, big, big, big, big, mid, mid, v((512, 128), f32))
+    def second(S, A):
+        load("st", S)
+        def vb(m):
+            if m == 0: part_ready(1)
+            c = pl.ds(m * 256, 256)
+            X1[:, :, c] = (dot_nt(P6[:, 0:768], WA[c, VAL:UPL]) + dot_nt(P6[:, 768:], WA[c, HA + VAL:HA + UPL])).reshape(64, 8, 256)
+        def dv(m):
+            c = pl.ds(m * 256, 256)
+            WA[c, VAL:UPL] = dot_tn(Q2[:, c], P6[:, 0:768]).astype(bf16)
+            WA[c, HA + VAL:HA + UPL] = dot_tn(Q2[:, c], P6[:, 768:]).astype(bf16)
+        def bl(m):
+            if m == 0: part_ready(0); ready(("bs", Q1), ("sh", Q0))
+            c = pl.ds(m * 256, 256)
+            ACC[...] = dot_nt(GMX[:, 0:MXL], WA[c, 0:MXL]) + dot_nt(GMX[:, MXL:], WA[c, HA:HA + 1536])
             def rows(i):
                 r, k = ds(i, 64), ds(i, 8)
                 gb = ACC[r, :] * Q1[r, c].astype(f32)
@@ -1209,80 +1258,46 @@
                 GG[8:16, c] += sub8(gb * U[k, :, c].reshape(64, 256))
                 X1[k, :, c] += (gb * omega[:, c]).reshape(8, 8, 256)
             loop(8, rows)
-        some(0, 3, f_blend)
-        SHT[...] = Q0[...].T
-        NLT[...] = Q2[...].T
-        for k, (lo_, hi_) in enumerate(((0, 512), (512, 1280), (1280, 2048), (2048, 2816), (2816, 3200))):
-            WA[:, lo_:hi_] = dot(SHT[...], GMX[:, lo_:hi_]).astype(bf16)
-            e = min(hi_, 1536)
-            if lo_ < e: WA[:, HA + lo_:HA + e] = dot(NLT[...], P6[:, lo_:e]).astype(bf16)
-            if hi_ == HA: WA[:, 2 * HA - 128:] = jnp.zeros((768, 128), bf16)
-            link(3 + k)
-    pl.run_scoped(dense, big, big, big, big, big, big, big, v((512, HA), bf16), mid, mid, mid, mid, mid, v((512, 128), f32), v((512, 128), f32), v((768, 512), bf16), v((768, 512), bf16))
-    tot = Total(p, RR, RL, sr, rr_)
-    for k in range(3):
-        t = sub8(sq[pl.ds(k * 8, 8), :]).sum(axis=0, keepdims=True)
-        RR[0, 3 + k:4 + k, :] = sum(t[:, j * 128:(j + 1) * 128] for j in range(6))
-    RR[0, 6:7, :] = jnp.broadcast_to(jnp.sum(valid[...], axis=0, keepdims=True) * (1.0 / 128.0), (1, 128))
-    tot.send(0)
-    def average(S, A):
-        load("st", S)
-        ready("st", S)
-        back = lambda j: bwd_states(X0, U, S, rate, A, W.at[0], G1, H, KS, j, 2)
-        some(0, 3, back)
-        link(8)
-        some(3, 6, back)
-        sc = Scan(p, -1, PT, W, L, Zb, GR, sx, rx)
-        sc.begin()
-        tot.step(0)
-        link(9)
-        sc.step(0)
-        tot.step(1)
-        sc.step(1)
-        tot.step(2)
-        sc.step(2)
-        link(10)
-        grad = lambda j: bwd_grad(X0, U, S, A, Zb, rate, ec, H, X1, KS, AT, j, 2)
-        some(0, 3, grad)
-        tot.step(3)
-        link(11)
-        some(3, 6, grad)
-        tot.step(4)
-        sc.drain()
-    pl.run_scoped(average, v((64, 16, 768), f32), v((64, 16, 768), f32))
+        def bk(j):
+            if j == 0: ready(("st", S))
+            bwd_states(X0, U, S, rate, A, E.at[0], G1, H, KS, j, 2)
+        def tr(): SHT[...] = Q0[...].T
+        def dm(k):
+            off, w = MX_PARTS[k]
+            WA[:, off:off + w] = dot(SHT[...], GMX[:, off:off + w]).astype(bf16)
+            e = min(off + w, 1536)
+            if off < e: WA[:, HA + off:HA + e] = dot(SHT[...], GMX[:, MXL + off:MXL + e]).astype(bf16)
+            if off + w > 1536: WA[:, HA + 1536:HA + MXL] = jnp.zeros((768, 128), bf16)
+        def gr(j):
+            if j == 0: sc.sc2()
+            bwd_grad(X0, U, S, A, Zb, rate, ec, H, X1, KS, AT, j, 2)
+        def la():
+            GG[16:24, :] = jnp.zeros((8, 768), f32)
+            def rows(i):
+                r = ds(i, 64)
+                x = TOK[r, :].astype(f32)
+                inv = lax.rsqrt(jnp.mean(x * x, axis=-1, keepdims=True) + EPSILON)
+                unit = x * inv
+                gn = at3(X1, i)
+                GG[16:24, :] += sub8(gn * unit)
+                k = gn * gain1[...]
+                GT[r, :] += inv * (k - unit * jnp.mean(k * unit, axis=-1, keepdims=True))
+            loop(8, rows)
+            pltpu.make_async_copy(GT, o_gt, lo.at[0]).start()
+            TP[...] = jnp.zeros_like(TP)
+            TP[0:16, :] = G1[...]
+            TP[16:32, :] = H[...]
+            for k, i in ((32, 2), (33, 0), (34, 1)):
+                TP[k:k + 1, :] = jnp.sum(GG[pl.ds(i * 8, 8), :], axis=0, keepdims=True)
+            for j in range(6): T[j * 128:(j + 1) * 128, :] = TP[:, j * 128:(j + 1) * 128].T
+        run_plan(BACKWARD_PLAN[CUT:], (alone + (tr, la), many + (vb, dv, bl, bk, dm, gr)))
+    pl.run_scoped(second, v((64, 16, 768), f32), v((64, 16, 768), f32))
     o_red[...] = RR[5]
-    GG[16:24, :] = jnp.zeros((8, 768), f32)
-    def f_last(i):
-        r = ds(i, 64)
-        x = TOK[r, :].astype(f32)
-        inv = lax.rsqrt(jnp.mean(x * x, axis=-1, keepdims=True) + EPSILON)
-        unit = x * inv
-        gn = at3(X1, i)
-        GG[16:24, :] += sub8(gn * unit)
-        k = gn * gain1[...]
-        GT[r, :] += inv * (k - unit * jnp.mean(k * unit, axis=-1, keepdims=True))
-    loop(8, f_last)
-    fin = pltpu.make_async_copy(GT, o_gt, lo.at[0])
-    fin.start()
-    TP[...] = jnp.zeros_like(TP)
-    TP[0:16, :] = G1[...]
-    TP[16:32, :] = H[...]
-    for k, i in ((32, 2), (33, 0), (34, 1)):
-        TP[k:k + 1, :] = jnp.sum(GG[pl.ds(i * 8, 8), :], axis=0, keepdims=True)
-    for j in range(6): T[j * 128:(j + 1) * 128, :] = TP[:, j * 128:(j + 1) * 128].T
-    tiny = Tiny(p, T, TL1, TL2, TL4, o_tiny, TG, st_, rt_)
-    tiny.st0()
-    tiny.a0()
-    tiny.a1(); tiny.zsend()
-    link(12)
-    tiny.fin()
-    tiny.last()
-    g.drain()
-    tiny.drain(); tot.drain()
-    fin.wait()
+    g.drain(); tiny.drain(); tot.drain(); sc.drain()
+    pltpu.make_async_copy(GT, o_gt, lo.at[0]).wait()
 
 def backward_call(valid, affine, sq, ins):
-    n = len(CHUNKS)
+    n = len(SCATTER_CHUNKS)
     v = pltpu.VMEM
     D_ = pltpu.SemaphoreType.DMA
     sds = jax.ShapeDtypeStruct
@@ -1293,10 +1308,10 @@
         out_specs=[vm_] * 5 + [any_] + [vm_] * 2,
         scratch_shapes=rs_scratch() + [v((512, 768), bf16), v((128, 768), f32), v((64, 8, 768), f32), v((64, 8, 768), f32), v((64, 8, 768), f32), v((512, 768), f32),
             v((24, 768), f32), v((16, 768), f32), v((16, 768), f32), v((8, 128), f32), v((2, 16, 128), f32), v((512, 256), f32),
-            v((3, 2, 16, 768), bf16), v((3, 2, 16, 768), bf16), v((2, 16, 768), f32), v((3, 16, 768), f32),
+            v((2, 2, 16, 768), bf16), v((4, 2, 16, 768), bf16), v((2, 16, 768), f32),
             v((768, 128), f32), v((2, 192, 128), f32), v((192, 128), f32), v((3, 48, 128), f32), v((24, 128), f32), v((128, 768), f32),
-            v((6, 8, 128), f32), v((5, 8, 128), f32),
-            D_((n, Scatter.NS)), D_((n, Scatter.NS)), D_((3,)), D_((3,)), D_((10,)), D_((10,)), D_((5,)), D_((5,)), D_((len(BACK_IN),)), D_((1,)), D_((4,))],
+            v((6, 8, 128), f32), v((5, 8, 128), f32), v((512, 1536), bf16), v((512, 3200), bf16), v((512, 768), bf16), v((512, 768), bf16), v((512, 768), bf16), v((768, 512), bf16), v((512, 128), f32),
+            D_((n, 11)), D_((n, 11)), D_((4,)), D_((4,)), D_((10,)), D_((10,)), D_((5,)), D_((5,)), D_((len(BACK_IN),)), D_((1,)), D_((len(KINDS), 2))],
         compiler_params=pltpu.CompilerParams(collective_id=1, has_side_effects=True, vmem_limit_bytes=63 * 2**20),
     )(valid, affine, sq, *ins)
 

time: 273 us -> 213 us (0.78); the launches traced: 272 us -> 210 us
  Pallas kernels: 251 us -> 188 us
    pallas_call x1, Pallas kernels: 140 us -> 94.1 us  [backward_call(): pl.pallas_call(backward_kernel, out_shape=(sds((24, 3200), f32), sds((24,...]
    pallas_call x1, Pallas kernels: 111 us -> 94.3 us  [forward_call(): pl.pallas_call(forward_kernel, out_shape=tuple((jax.ShapeDtypeStruct(s, t...]
where the time goes in v5:
time: 213 us; the launch traced here: 210 us
  Pallas kernels  188 us (88%)
  local copies, waits for them, and re-layouts  14.6 us (7%)
  other arithmetic  5.01 us (2%)
    pallas_call x1, Pallas kernels, forward_call(): pl.pallas_call(forward_kernel, out_shape=tuple((jax.ShapeDtypeStruct(s, t...  94.3 us
    pallas_call x1, Pallas kernels, backward_call(): pl.pallas_call(backward_kernel, out_shape=(sds((24, 3200), f32), sds((24,...  94.1 us
    unnamed x30, local copies, waits for them, and re-layouts  11.2 us

profile of v5, /device:TPU:0, one launch (start us, length us, event | category | flops | bytes accessed | tf_op | source)
XLA Modules:
  0.0 209.6 jit_solution(14276665721393743864)
XLA Ops:
  0.7 0.7 fusion.2
  1.4 1.3 pad_convert_fusion.affine
  2.7 0.8 copy.34
  3.4 0.8 copy.36
  4.2 0.8 copy.35
  5.0 0.8 copy.37
  5.8 0.7 select_maximum_fusion.prm
  6.5 0.9 copy.45
  7.3 94.3 %shard_map.228 = (bf16[768,6400]{1,0:T(8,128)(2,1)}, bf16[1536,1536]{1,0:T(8,128)(2,1)}, bf16[512,1536]{1,0:T(8,128)(2,1)}, bf16[512,1536]{1,0:T(8,128)(2,1)}, b...) custom-call(bf16[512,768]{1,0:T(8,128)(2,1)} %bitcast.11, ...), custom_call_target="tpu_custom_call" | custom-call | tf_op jit(solution)/shard_map/pallas_call | solution.py:1033
  101.6 0.0 copy-start.1
  101.6 94.1 %shard_map.229 = (f32[24,3200]{1,0:T(8,128)}, f32[24,1536]{1,0:T(8,128)}, f32[24,1536]{1,0:T(8,128)}, f32[48,768]{1,0:T(8,128)}, f32[48,768]{1,0:T(8,128)}, /*in...) custom-call(f32[512,1]{1,0:T(8,128)} %bitcast.14, f32[8,128]{1,0:T(8,128)} %pad_convert_fusion.affine, ...), custom_call_target="tpu_custom_call" | custom-call | tf_op jit(solution)/shard_map/pallas_call | solution.py:1305
  195.7 0.0 copy-start
  195.8 0.9 slice_reduce_fusion
  196.7 0.6 slice.27
  197.9 1.3 slice.24
  199.2 0.5 divide_sqrt_fusion
  199.7 0.8 slice.23
  200.5 0.7 copy.43
  201.1 0.9 fusion.1
  202.0 0.7 copy.42
  202.7 0.7 copy.40
  203.3 0.7 copy.41
  204.0 0.0 copy-done.1
  204.0 0.9 copy.53
  204.9 0.0 copy-done
  204.9 0.0 copy-start.4
  204.9 1.1 copy.54
  206.1 0.7 copy.55
  206.8 0.7 copy.56
  207.4 0.7 copy.57
  208.1 0.7 copy.58
  208.8 0.7 copy.59
  (13 shorter events, 0.1 us)
Async XLA Ops:
  101.6 102.4 %copy-start.1 = (bf16[512,768]{1,0:T(8,128)(2,1)S(1)}, bf16[512,768]{1,0:T(8,128)(2,1)}, u32[]{:S(2)}) copy-start(bf16[512,768]{1,0:T(8,128)(2,1)} %get-tuple-element.44) | copy-start | bytes 2359300
  195.7 9.1 %copy-start = (f32[512,768]{1,0:T(8,128)S(1)}, f32[512,768]{1,0:T(8,128)}, u32[]{:S(2)}) copy-start(f32[512,768]{1,0:T(8,128)} %get-tuple-element.67) | copy-start | bytes 4718596
  204.9 1.2 copy-start.2
  204.9 1.9 copy-start.6
  204.9 2.6 %copy-start.5 = (f32[48,768]{1,0:T(8,128)S(1)}, f32[48,768]{1,0:T(8,128)}, u32[]{:S(2)}) copy-start(f32[48,768]{1,0:T(8,128)} %get-tuple-element.121) | copy-start | bytes 442372
  204.9 3.2 %copy-start.4 = (f32[24,1536]{1,0:T(8,128)S(1)}, f32[24,1536]{1,0:T(8,128)}, u32[]{:S(2)}) copy-start(f32[24,1536]{1,0:T(8,128)} %get-tuple-element.122) | copy-start | bytes 442372
  204.9 3.9 %copy-start.3 = (f32[48,768]{1,0:T(8,128)S(1)}, f32[48,768]{1,0:T(8,128)}, u32[]{:S(2)}) copy-start(f32[48,768]{1,0:T(8,128)} %get-tuple-element.123) | copy-start | bytes 442372

commit v6 on v5

--- a/solution.py
+++ b/solution.py
@@ -374,8 +374,8 @@
 
 MXL, VAL, UPL, ONE, DWL = 1664, 1664, 2432, 768, 384
 KINDS = ((0, 0, 1664), (0, 1664, 768), (0, 2432, 768), (1, 0, 384), (1, 384, 384))
-GATHER_CHUNKS = ((0, 1664, 128, "xy"), (0, 1792, 128, "yx"), (0, 1920, 256, "xy"), (0, 2176, 256, "yx"), (0, 0, 384, "xy"), (0, 384, 384, "yx"), (0, 768, 384, "xy"), (0, 1152, 512, "yx"), (1, 0, 128, "xy"), (1, 128, 256, "yx"), (0, 2432, 128, "xy"), (0, 2560, 128, "yx"), (0, 2688, 128, "z"), (0, 2816, 128, "z"), (0, 2944, 128, "z"), (0, 3072, 128, "z"), (1, 384, 128, "xy"), (1, 512, 256, "yx"))
-SCATTER_CHUNKS = ((1, 384, 128, "xy"), (1, 512, 128, "yx"), (1, 640, 128, "yx"), (0, 2432, 384, "xy"), (0, 2816, 384, "yx"), (1, 0, 256, "xy"), (1, 256, 128, "yx"), (0, 1664, 512, "yx"), (0, 2176, 256, "xy"), (0, 0, 384, "xy"), (0, 384, 384, "yx"), (0, 768, 256, "xy"), (0, 1024, 256, "yx"), (0, 1280, 128, "xy"), (0, 1408, 256, "yx"))
+GATHER_CHUNKS = ((0, 1664, 128, "xy"), (0, 1792, 256, "yx"), (0, 2048, 256, "xy"), (0, 2304, 128, "yx"), (0, 0, 256, "xy"), (0, 256, 256, "yx"), (0, 512, 256, "xy"), (0, 768, 384, "yx"), (0, 1152, 256, "xy"), (0, 1408, 256, "yx"), (1, 0, 128, "xy"), (1, 128, 256, "yx"), (0, 2432, 128, "xy"), (0, 2560, 128, "yx"), (0, 2688, 128, "z"), (0, 2816, 128, "z"), (0, 2944, 128, "z"), (0, 3072, 128, "z"), (1, 384, 128, "xy"), (1, 512, 128, "yx"), (1, 640, 128, "xy"))
+SCATTER_CHUNKS = ((1, 384, 128, "xy"), (1, 512, 128, "yx"), (1, 640, 128, "yx"), (0, 2432, 512, "xy"), (0, 2944, 256, "yx"), (1, 0, 128, "yx"), (1, 128, 256, "xy"), (0, 1664, 512, "yx"), (0, 2176, 256, "xy"), (0, 0, 384, "yx"), (0, 384, 384, "xy"), (0, 768, 384, "yx"), (0, 1152, 256, "xy"), (0, 1408, 256, "yx"))
 
 class Pos:
     def __init__(s):
@@ -864,6 +864,14 @@
         if e % 100 == 0: steps[0][e // 100]()
         else: steps[1][e // 100](e % 100 - 1)
 
+def state_scale(rate):
+    return jnp.sqrt(jnp.tanh(rate) * (1.0 + jnp.exp(-2.0 * rate)))
+
+def row_masks(lens, valid, p):
+    for b in range(2):
+        t = lax.broadcasted_iota(jnp.int32, (SEQ_DEV, 1), 0) + p.sq * SEQ_DEV
+        valid[b * SEQ_DEV:(b + 1) * SEQ_DEV, :] = jnp.where(t < lens[b], 1.0, 0.0)
+
 def sub8(v):
     return v.reshape(v.shape[0] // 8, 8, v.shape[1]).sum(axis=0)
 
@@ -873,24 +881,23 @@
     ("mi", (512, 768), f32), ("sp", (512, 128), f32), ("pr", (512, 128), f32), ("st", (64, 16, 768), f32), ("pt", (128, 768), f32), ("res", (512, 768), bf16), ("sq", (24, 768), f32))
 
 FORWARD_PLAN = (
-    0, 100, 200, 300, 704, 701, 500, 400, 703, 804, 600, 1213, 707, 801, 803, 1216, 1313, 700, 901, 708, 904, 903, 800, 1215, 1001, 702, 1,
-    1101, 2, 705, 1316, 807, 808, 1315, 3, 4, 5, 6, 1003, 706, 1214, 712, 900, 805, 908, 1103, 802, 710, 806, 902, 812, 1000, 1004, 1104,
-    905, 912, 907, 906, 1008, 709, 1002, 1005, 1102, 1108, 201, 717, 711, 202, 810, 101, 102, 809, 1007, 718, 103, 1314, 104, 105, 106,
-    1006, 1107, 811, 1416, 817, 1106, 1100, 1012, 909, 401, 910, 203, 1112, 1105, 818, 911, 402, 1413, 1200, 301, 917, 302, 1009, 303, 1109,
-    1414, 403, 918, 1010, 501, 1516, 1110, 1011, 1513, 1415, 502, 503, 504, 1111, 1300, 1017, 1514, 1018, 1117, 1400, 601, 1515, 602, 1118,
-    603, 1500,
+    0, 100, 200, 300, 702, 500, 701, 703, 802, 400, 704, 1216, 1218, 600, 710, 801, 902, 709, 700, 901, 800, 804, 1001, 1002, 705, 803,
+    1316, 706, 810, 1, 2, 1101, 1318, 3, 4, 707, 809, 5, 1102, 1217, 903, 714, 6, 805, 900, 904, 910, 713, 708, 1215, 201, 1003, 711, 806,
+    909, 1000, 1103, 813, 1004, 807, 906, 808, 907, 202, 905, 908, 1104, 1010, 1006, 712, 1009, 1109, 811, 1110, 101, 102, 1007, 1107, 721,
+    103, 104, 812, 720, 913, 814, 1106, 105, 1008, 1005, 106, 821, 1105, 719, 1418, 1100, 203, 820, 912, 1317, 1108, 1315, 301, 401, 1416,
+    302, 819, 911, 914, 402, 303, 1415, 1012, 1013, 403, 921, 920, 1200, 501, 1011, 1516, 502, 1111, 1112, 1113, 503, 1417, 1518, 504, 919,
+    1300, 1014, 1114, 1021, 1515, 1121, 1400, 601, 1517, 602, 1020, 1019, 1119, 1120, 603, 1500,
 )
 
-def forward_kernel(tok, valid, affine, prm, mx, va, wo, wu, wd, *refs):
+def forward_kernel(lens, tok, qk, rate_t, in_t, out_t, gain_t, mx, va, wo, wu, wd, *refs):
     no = len(FORWARD_OUT)
     outs, bufs, rest = refs[:no], refs[no:2 * no], refs[2 * no:]
     B = {name: r for (name, _, _), r in zip(FORWARD_OUT, bufs)}
     O = {name: r for (name, _, _), r in zip(FORWARD_OUT, outs)}
     osem = {name: i for i, (name, _, _) in enumerate(FORWARD_OUT)}
-    (PRM, land, U, NL, BL, RSF, UPD, DIR, ACC, KS, E, L, Z, s0, r0, sp_, rp_, ss, rs, sx, rx, so, sw) = rest
+    (PRM, land, U, NL, BL, RSF, UPD, DIR, ACC, KS, E, L, Z, valid, affine, prm, s0, r0, sp_, rp_, ss, rs, sx, rx, so, sw) = rest
     WA, WB, PT, S = B["wa"], B["wb"], B["pt"], B["st"]
     p = Pos()
-    full_barrier(p)
     out = lambda name: pltpu.make_async_copy(B[name], O[name], so.at[osem[name]])
     def keep(*names):
         for name in names: out(name).start()
@@ -901,6 +908,17 @@
         return pltpu.make_async_copy(a.at[:, cols], o.at[:, cols], sw.at[k, h])
     def keep_weight(k):
         for h in (0, 1): weight(k, h).start()
+    def small():
+        PT[...] = jnp.zeros_like(PT)
+        r = rate_t[...].astype(f32)
+        PT[0:16, 0:24] = r
+        PT[16:32, 0:24] = out_t[...].astype(f32) * state_scale(r) * in_t[...].astype(f32)
+        PT[32:35, 0:24] = gain_t[...].astype(f32)
+        prm[...] = PT[:, 0:128].T[0:24, :]
+    small()
+    full_barrier(p)
+    row_masks(lens, valid, p)
+    affine[0:3, :] = qk[...].astype(f32)
     par = Params(p, prm, PRM, sp_, rp_)
     hv = Halves(p, mx, va, wo, wu, wd, WA, WB, land, s0, r0)
     g = Gather(p, (WA, WB), ss, rs)
@@ -1026,20 +1044,21 @@
 
 Z_SCALE = Z ** -0.5
 SCAN_TYPE = f32
-def forward_call(tok, valid, affine, prm, mx, va, wo, wu, wd):
+def forward_call(*args):
     n = len(GATHER_CHUNKS)
     v = pltpu.VMEM
     D_ = pltpu.SemaphoreType.DMA
     return pl.pallas_call(forward_kernel,
         out_shape=tuple(jax.ShapeDtypeStruct(s, t) for _, s, t in FORWARD_OUT),
-        in_specs=[pl.BlockSpec(memory_space=pltpu.VMEM)] * 9,
+        in_specs=[pl.BlockSpec(memory_space=pltpu.SMEM)] + [pl.BlockSpec(memory_space=pltpu.VMEM)] * 11,
         out_specs=[pl.BlockSpec(memory_space=pl.ANY)] * len(FORWARD_OUT),
         scratch_shapes=[v(s, t) for _, s, t in FORWARD_OUT] + [v((768, 128), f32), v((24, HA), bf16), v((64, 8, 768), f32), v((512, 768), bf16),
             v((64, 8, 768), f32), v((512, 1536), f32), v((512, 768), f32), v((512, 768), f32), v((512, 384), f32), v((8, 128), f32),
             v((2, 2, 16, 768), SCAN_TYPE), v((4, 2, 16, 768), SCAN_TYPE), v((2, 16, 768), f32),
+            v((512, 1), f32), v((8, 128), f32), v((24, 128), f32),
             D_((7,)), D_((5,)), D_((10,)), D_((10,)), D_((n, 23)), D_((n, 23)), D_((4,)), D_((4,)), D_((len(FORWARD_OUT),)), D_((len(KINDS), 2))],
         compiler_params=pltpu.CompilerParams(collective_id=0, has_side_effects=True, vmem_limit_bytes=62 * 2**20),
-    )(tok, valid, affine, prm, mx, va, wo, wu, wd)
+    )(*args)
 
 class Tiny:
     def __init__(s, pos, T, L1, L2, L4, OUT, G, ss, rs):
@@ -1101,23 +1120,23 @@
         for k in range(5): s.cp(k).wait_send()
 
 BACK_IN = ("wa", "wb", "vl", "vs", "re", "rs", "at", "gt", "hi", "hs", "uc", "du", "om", "sh", "bs", "n2", "mi", "sp", "pr", "st", "pt", "tok", "cot")
-MX_PARTS = ((0, 384), (384, 384), (768, 256), (1024, 256), (1280, 128), (1408, 256))
+MX_PARTS = ((0, 384), (384, 384), (768, 384), (1152, 256), (1408, 256))
 BACKWARD_PLAN = (
-    800, 701, 702, 703, 704, 705, 706, 2, 1, 3, 801, 802, 102, 803, 101, 4, 900, 103, 901, 5, 104, 902, 903, 904, 905, 201, 906, 6, 105,
-    202, 7, 1001, 1002, 1000, 106, 1003, 1004, 701, 204, 702, 301, 703, 107, 302, 700, 901, 801, 902, 802, 803, 205, 903, 800, 206, 304, 8,
-    1106, 203, 1101, 1001, 10, 207, 305, 108, 15, 1102, 1002, 110, 1003, 1105, 306, 1104, 9, 14, 13, 1004, 1005, 303, 307, 1006, 11, 113, 0,
-    601, 1103, 114, 208, 100, 111, 213, 602, 308, 210, 109, 12, 1201, 115, 1202, 211, 313, 603, 112, 1203, 1204, 310, 214, 408, 404, 1205,
-    1206, 311, 209, 401, 900, 212, 314, 413, 200, 407, 215, 309, 312, 406, 300, 402, 409, 414, 315, 411, 509, 504, 400, 412, 403, 405, 501,
-    514, 410, 511, 502, 415, 604, 512, 500, 505, 605, 507, 506, 513, 515, 503, 508, 510, 600,
+    800, 701, 702, 703, 704, 705, 706, 1, 801, 3, 802, 803, 5, 4, 101, 103, 2, 900, 104, 901, 105, 1000, 902, 102, 903, 203, 904, 905, 906,
+    205, 6, 1001, 1002, 201, 1003, 7, 1004, 701, 702, 703, 202, 106, 204, 801, 802, 803, 8, 301, 107, 901, 108, 902, 9, 305, 903, 109, 303,
+    1001, 304, 1002, 1003, 1004, 1005, 1006, 207, 0, 206, 302, 800, 1101, 10, 100, 208, 700, 209, 1102, 601, 1104, 110, 307, 1105, 11, 1103,
+    13, 12, 306, 111, 14, 602, 112, 1201, 1202, 308, 210, 1203, 1204, 211, 113, 309, 212, 114, 310, 1205, 1206, 406, 311, 900, 214, 312,
+    200, 409, 300, 603, 403, 407, 314, 401, 213, 410, 412, 503, 400, 404, 507, 411, 313, 402, 414, 408, 405, 509, 500, 504, 604, 512, 514,
+    502, 413, 506, 605, 511, 510, 508, 501, 600, 505, 513,
 )
 CUT = 37
 
-def backward_kernel(valid, affine, sq, *refs):
+def backward_kernel(lens, qk, sq, *refs):
     ni = len(BACK_IN)
     I = dict(zip(BACK_IN, refs[:ni]))
     (o_mx, o_va, o_up, o_wo, o_wd, o_gt, o_tiny, o_red) = refs[ni:ni + 8]
     (WA, WB, L1A, L1B, L2A, L2B, L3A, L3B, L4A, L4B, FA, FB, GA, GB_, TOK, PT, U, X0, X1, GT, GG, G1, H, KS, AT, ACC, E, L, Zb,
-     T, TL1, TL2, TL4, TG, TP, RR, RL, P6, GMX, Q0, Q1, Q2, SHT, SP, ss, rs, sx, rx, st_, rt_, sr, rr_, li, lo, lw) = refs[ni + 8:]
+     T, TL1, TL2, TL4, TG, TP, RR, RL, P6, GMX, Q0, Q1, Q2, SHT, SP, valid, affine, ss, rs, sx, rx, st_, rt_, sr, rr_, li, lo, lw) = refs[ni + 8:]
     p = Pos()
     sem = {name: i for i, name in enumerate(BACK_IN)}
     def load(name, dst): pltpu.make_async_copy(I[name], dst, li.at[sem[name]]).start()
@@ -1160,6 +1179,8 @@
         load("cot", Q4); part(4); load("hs", P0); load("hi", P1); part(2); load("n2", Q1); load("mi", X0); load("uc", Q2); load("du", Q3); load("pt", PT)
         part(3); load("gt", P3); load("rs", P4); load("vl", P5); load("vs", P6); load("sp", SP); load("pr", PR); part(1); load("tok", TOK); part(0)
         full_barrier(p)
+        row_masks(lens, valid, p)
+        affine[0:3, :] = qk[...].astype(f32)
         def lo_():
             GG[...] = jnp.zeros_like(GG)
             RR[0] = jnp.zeros((8, 128), f32)
@@ -1296,7 +1317,7 @@
     g.drain(); tiny.drain(); tot.drain(); sc.drain()
     pltpu.make_async_copy(GT, o_gt, lo.at[0]).wait()
 
-def backward_call(valid, affine, sq, ins):
+def backward_call(lens, qk, sq, ins):
     n = len(SCATTER_CHUNKS)
     v = pltpu.VMEM
     D_ = pltpu.SemaphoreType.DMA
@@ -1304,38 +1325,59 @@
     vm_, any_ = pl.BlockSpec(memory_space=pltpu.VMEM), pl.BlockSpec(memory_space=pl.ANY)
     return pl.pallas_call(backward_kernel,
         out_shape=(sds((24, 3200), f32), sds((24, 1536), f32), sds((24, 1536), f32), sds((48, 768), f32), sds((48, 768), f32), sds((512, 768), f32), sds((24, 128), f32), sds((8, 128), f32)),
-        in_specs=[vm_] * 3 + [any_] * len(ins),
+        in_specs=[pl.BlockSpec(memory_space=pltpu.SMEM)] + [vm_] * 2 + [any_] * len(ins),
         out_specs=[vm_] * 5 + [any_] + [vm_] * 2,
         scratch_shapes=rs_scratch() + [v((512, 768), bf16), v((128, 768), f32), v((64, 8, 768), f32), v((64, 8, 768), f32), v((64, 8, 768), f32), v((512, 768), f32),
             v((24, 768), f32), v((16, 768), f32), v((16, 768), f32), v((8, 128), f32), v((2, 16, 128), f32), v((512, 256), f32),
             v((2, 2, 16, 768), bf16), v((4, 2, 16, 768), bf16), v((2, 16, 768), f32),
             v((768, 128), f32), v((2, 192, 128), f32), v((192, 128), f32), v((3, 48, 128), f32), v((24, 128), f32), v((128, 768), f32),
-            v((6, 8, 128), f32), v((5, 8, 128), f32), v((512, 1536), bf16), v((512, 3200), bf16), v((512, 768), bf16), v((512, 768), bf16), v((512, 768), bf16), v((768, 512), bf16), v((512, 128), f32),
+            v((6, 8, 128), f32), v((5, 8, 128), f32), v((512, 1536), bf16), v((512, 3200), bf16), v((512, 768), bf16), v((512, 768), bf16), v((512, 768), bf16), v((768, 512), bf16), v((512, 128), f32), v((512, 1), f32), v((8, 128), f32),
             D_((n, 11)), D_((n, 11)), D_((4,)), D_((4,)), D_((10,)), D_((10,)), D_((5,)), D_((5,)), D_((len(BACK_IN),)), D_((1,)), D_((len(KINDS), 2))],
         compiler_params=pltpu.CompilerParams(collective_id=1, has_side_effects=True, vmem_limit_bytes=63 * 2**20),
-    )(valid, affine, sq, *ins)
+    )(lens, qk, sq, *ins)
+
+def last_kernel(res, gtok, mx, va, wo, wu, wd, tiny, red, rate_t, in_t, out_t, o_res, o_gtok, o_mx, o_va, o_wo, o_wu, o_wd, o_rate, o_in, o_out, o_gain, o_qk, o_rms, *rest):
+    mid, ss = rest[:7], rest[7]
+    into = [pltpu.make_async_copy(a, m, ss.at[0, k]) for k, (a, m) in enumerate(zip((res, gtok, mx, va, wo, wu, wd), mid))]
+    big = [pltpu.make_async_copy(m, o, ss.at[1, k]) for k, (m, o) in enumerate(zip(mid, (o_res, o_gtok, o_mx, o_va, o_wo, o_wu, o_wd)))]
+    for cp in into: cp.start()
+    for a, b in zip(into, big):
+        a.wait()
+        b.start()
+    t = jnp.concatenate([tiny[...], jnp.zeros((104, 128), f32)], axis=0).T
+    g1, h1 = t[0:16, 0:24], t[16:32, 0:24]
+    r, a, b = (x[...].astype(f32) for x in (rate_t, in_t, out_t))
+    scale = state_scale(r)
+    o_out[...] = a * scale * g1
+    o_in[...] = b * scale * g1
+    o_rate[...] = b * a * (jnp.exp(-2.0 * r) / scale * g1 - scale * h1)
+    o_gain[...] = t[32:35, 0:24]
+    o_qk[...] = red[0:3, :]
+    s = jnp.sum(jnp.concatenate([red[...], jnp.zeros((120, 128), f32)], axis=0).T, axis=0, keepdims=True)
+    o_rms[...] = jnp.sqrt(s[:, 3:6] / (s[:, 6:7] * D))
+    for cp in big: cp.wait()
+
+def last_call(*args):
+    vm_, any_ = pl.BlockSpec(memory_space=pltpu.VMEM), pl.BlockSpec(memory_space=pl.ANY)
+    sds = jax.ShapeDtypeStruct
+    return pl.pallas_call(last_kernel,
+        out_shape=tuple(sds(a.shape, a.dtype) for a in args[:7]) + (sds((16, 24), f32),) * 3 + (sds((3, 24), f32), sds((3, 128), f32), sds((1, 3), f32)),
+        in_specs=[any_] * 7 + [vm_] * 5,
+        out_specs=[any_] * 7 + [vm_] * 6,
+        scratch_shapes=[pltpu.VMEM(a.shape, a.dtype) for a in args[:7]] + [pltpu.SemaphoreType.DMA((2, 7))],
+        compiler_params=pltpu.CompilerParams(vmem_limit_bytes=63 * 2**20))(*args)
 
 
 def per_device_tuned(tokens, cotangent, lengths, w_mx, w_value, w_out, w_up, w_down, ema_rate, ema_in, ema_out, gains, qk_affine):
-    rate_own, in_own, out_own = (t.astype(f32) for t in (ema_rate, ema_in, ema_out))
-    scale_own = jnp.sqrt(-jnp.expm1(-2.0 * rate_own))
-    mine = jnp.pad(jnp.concatenate([rate_own, out_own * scale_own * in_own, gains.astype(f32)], axis=1), ((0, 0), (0, 93)))
-    seq_pos = lax.axis_index("seq") * SEQ_DEV + jnp.arange(SEQ_DEV, dtype=jnp.int32)
-    valid = (seq_pos[None, :] < lengths[:, None]).astype(f32).reshape(512, 1)
     tok = tokens.reshape(512, D)
-    affine = jnp.pad(qk_affine.astype(f32), ((0, 5), (0, 0)))
-    kept = forward_call(tok, valid, affine, mine, w_mx, w_value, w_out, w_up, w_down)
+    rate_t, in_t, out_t, gain_t = ema_rate.T, ema_in.T, ema_out.T, gains.T
+    kept = forward_call(lengths, tok, qk_affine, rate_t, in_t, out_t, gain_t, w_mx, w_value, w_out, w_up, w_down)
     K = {name: t for (name, _, _), t in zip(FORWARD_OUT, kept)}
     K["tok"], K["cot"], K["mi"] = tok, cotangent.reshape(512, D), K["mi"].reshape(64, 8, 768)
-    g_mx, g_va, g_up, g_wo, g_wd, g_tok, tiny, red = backward_call(valid, affine, K["sq"], [K[name] for name in BACK_IN])
-    g1, h1 = tiny[:, :16], tiny[:, 16:32]
-    grad_ema_out = in_own * scale_own * g1
-    grad_ema_in = out_own * scale_own * g1
-    grad_ema_rate = out_own * in_own * (jnp.exp(-2.0 * rate_own) / scale_own * g1 - scale_own * h1)
-    sums = jnp.sum(red[3:7], axis=1)
-    rms_values = jnp.sqrt(sums[:3] / (sums[3] * D))
-    return (K["res"].reshape(tokens.shape), g_tok.reshape(tokens.shape), g_mx, g_va, g_wo, g_up, g_wd,
-        grad_ema_rate, grad_ema_in, grad_ema_out, tiny[:, 32:35], red[:3], rms_values)
+    g_mx, g_va, g_up, g_wo, g_wd, g_tok, tiny, red = backward_call(lengths, qk_affine, K["sq"], [K[name] for name in BACK_IN])
+    res, g_tok, g_mx, g_va, g_wo, g_up, g_wd, g_rate, g_in, g_out, g_gain, g_qk, rms = last_call(
+        K["res"], g_tok, g_mx, g_va, g_wo, g_up, g_wd, tiny, red, rate_t, in_t, out_t)
+    return (res.reshape(tokens.shape), g_tok.reshape(tokens.shape), g_mx, g_va, g_wo, g_up, g_wd, g_rate.T, g_in.T, g_out.T, g_gain.T, g_qk, rms.reshape(3))
 
 
 def solution(mesh):

time: 213 us -> 197 us (0.925)
  local copies, waits for them, and re-layouts: 14.6 us -> 0 us
  other arithmetic: 5.01 us -> 0 us
  Pallas kernels: 188 us -> 193 us
    unnamed x30 -> x0, local copies, waits for them, and re-layouts: 11.2 us -> none
    pallas_call x0 -> x1, Pallas kernels: none -> 4.59 us  [last_call(): pl.pallas_call(last_kernel, out_shape=tuple((sds(a.shape, a.dtype) for a...]
    slice x3 -> x0, local copies, waits for them, and re-layouts: 2.62 us -> none  [the longest x1 1.26 us: per_device_tuned(): red[:3]]
where the time goes in v6:
time: 197 us; the launch traced here: 194 us
  Pallas kernels  193 us (98%)
    pallas_call x1, Pallas kernels, forward_call(): pl.pallas_call(forward_kernel, out_shape=tuple((jax.ShapeDtypeStruct(s, t...  95.8 us
    pallas_call x1, Pallas kernels, backward_call(): pl.pallas_call(backward_kernel, out_shape=(sds((24, 3200), f32), sds((24,...  92.6 us
    pallas_call x1, Pallas kernels, last_call(): pl.pallas_call(last_kernel, out_shape=tuple((sds(a.shape, a.dtype) for a...  4.59 us

profile of v6, /device:TPU:0, one launch (start us, length us, event | category | flops | bytes accessed | tf_op | source)
XLA Modules:
  0.0 193.9 jit_solution(17045259875057779967)
XLA Ops:
  0.6 95.8 %shard_map.228 = (bf16[768,6400]{1,0:T(8,128)(2,1)}, bf16[1536,1536]{1,0:T(8,128)(2,1)}, bf16[512,1536]{1,0:T(8,128)(2,1)}, bf16[512,1536]{1,0:T(8,128)(2,1)}, b...) custom-call(s32[2]{0:T(128)} %lens.3, ...), custom_call_target="tpu_custom_call" | custom-call | tf_op jit(solution)/shard_map/pallas_call | solution.py:1051
  96.4 92.6 %shard_map.229 = (f32[24,3200]{1,0:T(8,128)}, f32[24,1536]{1,0:T(8,128)}, f32[24,1536]{1,0:T(8,128)}, f32[48,768]{1,0:T(8,128)}, f32[48,768]{1,0:T(8,128)}, /*in...) custom-call(s32[2]{0:T(128)} %lens.3, bf16[3,128]{1,0:T(4,128)(2,1)} %qk.3, f32[24,768]{1,0:T(8,128)} %get-tuple-element.58.sq, ...), custom_call_target="tpu_custom_call" | custom-call | tf_op jit(solution)/shard_map/pallas_call | solution.py:1326
  189.1 4.6 %shard_map.230 = (bf16[512,768]{1,0:T(8,128)(2,1)}, f32[512,768]{1,0:T(8,128)}, f32[24,3200]{1,0:T(8,128)}, f32[24,1536]{1,0:T(8,128)}, f32[48,768]{1,0:T(8,128)...) custom-call(bf16[512,768]{1,0:T(8,128)(2,1)} %get-tuple-element.57.r, ...), custom_call_target="tpu_custom_call" | custom-call | tf_op jit(solution)/shard_map/pallas_call | solution.py:1363

commit v7 on v6

--- a/solution.py
+++ b/solution.py
@@ -374,8 +374,8 @@
 
 MXL, VAL, UPL, ONE, DWL = 1664, 1664, 2432, 768, 384
 KINDS = ((0, 0, 1664), (0, 1664, 768), (0, 2432, 768), (1, 0, 384), (1, 384, 384))
-GATHER_CHUNKS = ((0, 1664, 128, "xy"), (0, 1792, 256, "yx"), (0, 2048, 256, "xy"), (0, 2304, 128, "yx"), (0, 0, 256, "xy"), (0, 256, 256, "yx"), (0, 512, 256, "xy"), (0, 768, 384, "yx"), (0, 1152, 256, "xy"), (0, 1408, 256, "yx"), (1, 0, 128, "xy"), (1, 128, 256, "yx"), (0, 2432, 128, "xy"), (0, 2560, 128, "yx"), (0, 2688, 128, "z"), (0, 2816, 128, "z"), (0, 2944, 128, "z"), (0, 3072, 128, "z"), (1, 384, 128, "xy"), (1, 512, 128, "yx"), (1, 640, 128, "xy"))
-SCATTER_CHUNKS = ((1, 384, 128, "xy"), (1, 512, 128, "yx"), (1, 640, 128, "yx"), (0, 2432, 512, "xy"), (0, 2944, 256, "yx"), (1, 0, 128, "yx"), (1, 128, 256, "xy"), (0, 1664, 512, "yx"), (0, 2176, 256, "xy"), (0, 0, 384, "yx"), (0, 384, 384, "xy"), (0, 768, 384, "yx"), (0, 1152, 256, "xy"), (0, 1408, 256, "yx"))
+GATHER_CHUNKS = ((0, 1664, 128, "xy"), (0, 1792, 128, "yx"), (0, 1920, 256, "xy"), (0, 2176, 256, "yx"), (0, 0, 384, "xy"), (0, 384, 384, "yx"), (0, 768, 384, "xy"), (0, 1152, 512, "yx"), (1, 0, 128, "xy"), (1, 128, 256, "yx"), (0, 2432, 128, "xy"), (0, 2560, 128, "yx"), (0, 2688, 512, "z"), (1, 384, 128, "xy"), (1, 512, 256, "yx"))
+SCATTER_CHUNKS = ((1, 384, 128, "xy"), (1, 512, 128, "yx"), (1, 640, 128, "yx"), (0, 2432, 384, "xy"), (0, 2816, 384, "yx"), (1, 0, 256, "xy"), (1, 256, 128, "yx"), (0, 1664, 512, "yx"), (0, 2176, 256, "xy"), (0, 0, 384, "xy"), (0, 384, 384, "yx"), (0, 768, 256, "xy"), (0, 1024, 256, "yx"), (0, 1280, 128, "xy"), (0, 1408, 256, "yx"))
 
 class Pos:
     def __init__(s):
@@ -391,11 +391,11 @@
 def rcopy(src, dst, ss, rs, dev):
     return pltpu.make_async_remote_copy(src_ref=src, dst_ref=dst, send_sem=ss, recv_sem=rs, device_id=dev, device_id_type=MESH)
 
-def full_barrier(p):
+def full_barrier(p, *more):
     bar = pltpu.get_barrier_semaphore()
     sig = lambda d: pl.semaphore_signal(bar, inc=1, device_id=d, device_id_type=MESH)
-    for d in (p.sib, p.xn, p.yn, p.zn(1), p.zn(2), p.zn(3)): sig(d)
-    pl.semaphore_wait(bar, 6)
+    for d in (p.sib, p.xn, p.yn, p.zn(1), p.zn(2), p.zn(3)) + more: sig(d)
+    pl.semaphore_wait(bar, 6 + len(more))
 
 def at(ref, rows, nrows, half, w, off, width):
     return ref.at[pl.ds(pl.multiple_of(rows, 48), nrows), pl.ds(pl.multiple_of(half * w + off, 128), width)]
@@ -483,7 +483,8 @@
 
 class Scatter:
     NS = 11
-    def __init__(s, pos, P, L1, L2, L3, L4, F, G, out, ss, rs):
+    def __init__(s, pos, P, L1, L2, L3, L4, F, FS, G, out, ss, rs):
+        s.FS = FS
         s.p, s.P, s.L1, s.L2, s.L3, s.L4, s.F, s.G, s.out, s.ss, s.rs = pos, P, L1, L2, L3, L4, F, G, out, ss, rs
     def geom(s, i):
         b, off, w, order = SCATTER_CHUNKS[i]
@@ -555,19 +556,21 @@
             l = s.l4(i, k)
             s.cp(i, 7 + k, l, l, p.sib).wait_recv()
             t = t + l[...].astype(f32)
-        F[:, pl.ds(off, w)] = t
-        src = F.at[pl.ds(pl.multiple_of((1 - p.y) * h, 8), h), pl.ds(off, w)]
-        s.cp(i, 10, src, G.at[:, pl.ds(off, w)], p.yn).start()
+        cols = pl.ds(off, w)
         for yy in (0, 1):
             @pl.when(p.y == yy)
-            def _(): out(b, yy, off, w, lambda o, k: F[pl.ds(yy * h, h), pl.ds(off + o, k)])
+            def _():
+                F[:, cols] = t[yy * h:yy * h + h, :]
+                s.FS[b][:, cols] = t[(1 - yy) * h:(2 - yy) * h, :].astype(bf16)
+                out(b, yy, off, w, lambda o, k: F[:, pl.ds(off + o, k)])
+        s.cp(i, 10, s.FS[b].at[:, cols], G.at[:, cols], p.yn).start()
     def last(s, i):
         p = s.p; b, R, W, off, w, _ = s.geom(i)
         l = s.G[b].at[:, pl.ds(off, w)]
         s.cp(i, 10, l, l, p.yn).wait_recv()
         for yy in (0, 1):
             @pl.when(p.y == 1 - yy)
-            def _(): s.out(b, yy, off, w, lambda o, k: l[:, pl.ds(o, k)])
+            def _(): s.out(b, yy, off, w, lambda o, k: l[:, pl.ds(o, k)].astype(f32))
     def r0(s, i): s.st0(i)
     def r1(s, i): s.a0(i); s.st1(i)
     def r2(s, i): s.a1(i); s.st2(i)
@@ -586,7 +589,7 @@
     v = pltpu.VMEM
     return [v((768, 2 * HA), bf16), v((1536, 2 * HB), bf16), v((2, 192, 2 * HA), bf16), v((2, 384, 2 * HB), bf16),
         v((2, 192, HA), bf16), v((2, 384, HB), bf16), v((192, HA), bf16), v((384, HB), bf16),
-        v((3, 48, HA), bf16), v((3, 96, HB), bf16), v((48, HA), f32), v((96, HB), f32), v((24, HA), f32), v((48, HB), f32)]
+        v((3, 48, HA), bf16), v((3, 96, HB), bf16), v((24, HA), f32), v((48, HB), f32), v((24, HA), bf16), v((48, HB), bf16), v((24, HA), bf16), v((48, HB), bf16)]
 
 NK = 32
 NB = 2
@@ -724,11 +727,9 @@
 def dot(a, b): return jnp.dot(a, b, preferred_element_type=f32)
 def dot_nt(a, b): return lax.dot_general(a, b, (((1,), (1,)), ((), ())), preferred_element_type=f32)
 def dot_tn(a, b): return lax.dot_general(a, b, (((0,), (0,)), ((), ())), preferred_element_type=f32)
-def loop(n, f, unroll=1):
-    def body(i, _):
-        f(i); return 0
-    lax.fori_loop(0, n, body, 0, unroll=unroll)
-def ds(i, n): return pl.ds(pl.multiple_of(i * n, n), n)
+def loop(n, f):
+    for i in range(n): f(i)
+def ds(i, n): return pl.ds(i * n if isinstance(i, int) else pl.multiple_of(i * n, n), n)
 def silu_and_slope(v):
     s = sigmoid(v)
     y = v * s
@@ -738,24 +739,21 @@
     def __init__(s, pos, ref, PRM, ss, rs):
         s.p, s.ref, s.PRM, s.ss, s.rs = pos, ref, PRM, ss, rs
     def r(s, row, n): return s.PRM.at[pl.ds(pl.multiple_of(row, 8), n), :]
-    def cp(s, k, src, dst, dev, kr=None):
-        return rcopy(src, dst, s.ss.at[k], s.rs.at[k if kr is None else kr], dev)
+    def cp(s, k, src, dst, dev): return rcopy(src, dst, s.ss.at[k], s.rs.at[k], dev)
+    def others(s):
+        return tuple((d, f) for d in (0, 1, 3, 2) for f in (1, 0) if d or f)
     def y0(s):
-        p = s.p; row = (p.dp * 4 + p.z) * 48 + p.y * 24
-        s.cp(0, s.ref, s.r(row, 24), p.yn).start()
-        s.PRM[pl.ds(pl.multiple_of(row, 8), 24), :] = s.ref[...]
-    def y1(s):
-        p = s.p
-        l = s.r((p.dp * 4 + p.z) * 48, 24)
-        s.cp(0, l, l, p.yn).wait()
-    def z0(s):
-        p = s.p; u = s.r((p.dp * 4 + p.z) * 48, 48)
-        for d in (1, 3, 2): s.cp(d, u, u, p.zn(d), 1 + p.z).start()
+        p = s.p
+        own = (p.dp * 4 + p.z) * 48 + p.y * 24
+        s.PRM[pl.ds(pl.multiple_of(own, 8), 24), :] = s.ref[...]
+        for k, (d, f) in enumerate(s.others()):
+            y = 1 - p.y if f else p.y
+            s.cp(k, s.ref, s.r(own, 24), (p.dp, p.zof(d) * 2 + y)).start()
     def x0(s):
         p = s.p; u = s.r(p.dp * 192, 192)
-        for d in (1, 2, 3):
-            l = s.r((p.dp * 4 + p.zof(d)) * 48, 48)
-            s.cp(1, l, l, p.sib, 1 + p.zof(d)).wait_recv()
+        for k in range(7):
+            l = s.r(p.dp * 192, 24)
+            s.cp(k, l, l, p.sib).wait_recv()
         s.cp(7, u, u, p.xn).start()
         s.cp(8, u, u, p.sib).start()
     def x1(s):
@@ -767,9 +765,9 @@
         s.cp(8, u, u, p.sib).wait_recv()
         s.cp(9, u, u, p.sib).wait_recv()
     def drain(s):
-        p = s.p; u = s.r(p.dp * 192, 192); u1 = s.r(p.dp * 192, 48)
+        p = s.p; u = s.r(p.dp * 192, 192); u1 = s.r(p.dp * 192, 24)
         for k in (7, 8, 9): s.cp(k, u, u, p.sib).wait_send()
-        for k in (1, 2, 3): s.cp(k, u1, u1, p.sib).wait_send()
+        for k in range(7): s.cp(k, u1, u1, p.sib).wait_send()
 
 class Scan:
     def __init__(s, pos, way, rate, E, L, Z, ss, rs):
@@ -881,21 +879,21 @@
     ("mi", (512, 768), f32), ("sp", (512, 128), f32), ("pr", (512, 128), f32), ("st", (64, 16, 768), f32), ("pt", (128, 768), f32), ("res", (512, 768), bf16), ("sq", (24, 768), f32))
 
 FORWARD_PLAN = (
-    0, 100, 200, 300, 702, 500, 701, 703, 802, 400, 704, 1216, 1218, 600, 710, 801, 902, 709, 700, 901, 800, 804, 1001, 1002, 705, 803,
-    1316, 706, 810, 1, 2, 1101, 1318, 3, 4, 707, 809, 5, 1102, 1217, 903, 714, 6, 805, 900, 904, 910, 713, 708, 1215, 201, 1003, 711, 806,
-    909, 1000, 1103, 813, 1004, 807, 906, 808, 907, 202, 905, 908, 1104, 1010, 1006, 712, 1009, 1109, 811, 1110, 101, 102, 1007, 1107, 721,
-    103, 104, 812, 720, 913, 814, 1106, 105, 1008, 1005, 106, 821, 1105, 719, 1418, 1100, 203, 820, 912, 1317, 1108, 1315, 301, 401, 1416,
-    302, 819, 911, 914, 402, 303, 1415, 1012, 1013, 403, 921, 920, 1200, 501, 1011, 1516, 502, 1111, 1112, 1113, 503, 1417, 1518, 504, 919,
-    1300, 1014, 1114, 1021, 1515, 1121, 1400, 601, 1517, 602, 1020, 1019, 1119, 1120, 603, 1500,
+    0, 100, 300, 704, 200, 702, 500, 701, 703, 400, 600, 804, 1213, 706, 802, 700, 711, 712, 801, 800, 1313, 803, 1, 2, 901, 705, 902, 904,
+    806, 3, 714, 1001, 812, 1101, 4, 707, 708, 811, 710, 5, 6, 900, 805, 906, 1004, 903, 905, 807, 1003, 1006, 1000, 808, 912, 1005, 1002,
+    1103, 709, 814, 907, 1104, 908, 1102, 201, 1012, 810, 1105, 715, 1007, 911, 101, 102, 103, 1413, 104, 809, 202, 1008, 105, 910, 815,
+    1108, 106, 1107, 1100, 909, 203, 1011, 1106, 401, 402, 1200, 914, 1111, 1010, 301, 302, 915, 303, 403, 501, 1110, 502, 1009, 1109, 1112,
+    503, 504, 1300, 1513, 1014, 1114, 1015, 1400, 601, 1115, 602, 603, 1500,
 )
 
-def forward_kernel(lens, tok, qk, rate_t, in_t, out_t, gain_t, mx, va, wo, wu, wd, *refs):
+def forward_kernel(lens, qk, rate_t, in_t, out_t, gain_t, *refs):
+    far, refs = refs[:6], refs[6:]
     no = len(FORWARD_OUT)
     outs, bufs, rest = refs[:no], refs[no:2 * no], refs[2 * no:]
     B = {name: r for (name, _, _), r in zip(FORWARD_OUT, bufs)}
     O = {name: r for (name, _, _), r in zip(FORWARD_OUT, outs)}
     osem = {name: i for i, (name, _, _) in enumerate(FORWARD_OUT)}
-    (PRM, land, U, NL, BL, RSF, UPD, DIR, ACC, KS, E, L, Z, valid, affine, prm, s0, r0, sp_, rp_, ss, rs, sx, rx, so, sw) = rest
+    (PRM, land, U, NL, BL, RSF, UPD, DIR, ACC, KS, E, L, Z, valid, affine, prm, tok, mx, va, wo, wu, wd, si, s0, r0, sp_, rp_, ss, rs, sx, rx, so, sw) = rest
     WA, WB, PT, S = B["wa"], B["wb"], B["pt"], B["st"]
     p = Pos()
     out = lambda name: pltpu.make_async_copy(B[name], O[name], so.at[osem[name]])
@@ -915,8 +913,11 @@
         PT[16:32, 0:24] = out_t[...].astype(f32) * state_scale(r) * in_t[...].astype(f32)
         PT[32:35, 0:24] = gain_t[...].astype(f32)
         prm[...] = PT[:, 0:128].T[0:24, :]
+    near = [pltpu.make_async_copy(a, b, si.at[k]) for k, (a, b) in enumerate(zip(far, (va, mx, wu, wo, wd, tok)))]
+    for cp in near: cp.start()
     small()
-    full_barrier(p)
+    full_barrier(p, *((p.dp, p.zof(d) * 2 + 1 - p.y) for d in (1, 2, 3)))
+    for cp in near: cp.wait()
     row_masks(lens, valid, p)
     affine[0:3, :] = qk[...].astype(f32)
     par = Params(p, prm, PRM, sp_, rp_)
@@ -925,7 +926,7 @@
     rate, ec, omega = PT.at[0:16, :], PT.at[16:32, :], PT.at[34:35, :]
     sc = Scan(p, 1, PT, E, L, Z, sx, rx)
     SQ = B["sq"]
-    def par1(): par.y1(); par.z0()
+    def par1(): pass
     def pt():
         par.end()
         for j in range(6): PT[:, j * 128:(j + 1) * 128] = PRM[j * 128:(j + 1) * 128, :].T
@@ -1019,8 +1020,8 @@
         for h in (0, 1):
             mul(B["n2"], WA, h * HA + UPL + 256 * k)
             both("hi", "hs", 3 * h + k, 0)
+        if k == 2: keep("hi", "hs"); keep_weight(2)
     def do():
-        keep("hi", "hs"); keep_weight(2)
         g.need(1, DWL, 2 * DWL)
         keep_weight(4)
         for m in range(2):
@@ -1050,12 +1051,13 @@
     D_ = pltpu.SemaphoreType.DMA
     return pl.pallas_call(forward_kernel,
         out_shape=tuple(jax.ShapeDtypeStruct(s, t) for _, s, t in FORWARD_OUT),
-        in_specs=[pl.BlockSpec(memory_space=pltpu.SMEM)] + [pl.BlockSpec(memory_space=pltpu.VMEM)] * 11,
+        in_specs=[pl.BlockSpec(memory_space=pltpu.SMEM)] + [pl.BlockSpec(memory_space=pltpu.VMEM)] * 5 + [pl.BlockSpec(memory_space=pl.ANY)] * 6,
         out_specs=[pl.BlockSpec(memory_space=pl.ANY)] * len(FORWARD_OUT),
         scratch_shapes=[v(s, t) for _, s, t in FORWARD_OUT] + [v((768, 128), f32), v((24, HA), bf16), v((64, 8, 768), f32), v((512, 768), bf16),
             v((64, 8, 768), f32), v((512, 1536), f32), v((512, 768), f32), v((512, 768), f32), v((512, 384), f32), v((8, 128), f32),
             v((2, 2, 16, 768), SCAN_TYPE), v((4, 2, 16, 768), SCAN_TYPE), v((2, 16, 768), f32),
             v((512, 1), f32), v((8, 128), f32), v((24, 128), f32),
+            v((512, 768), bf16), v((24, 3200), bf16), v((24, 1536), bf16), v((48, 768), bf16), v((24, 1536), bf16), v((48, 768), bf16), D_((6,)),
             D_((7,)), D_((5,)), D_((10,)), D_((10,)), D_((n, 23)), D_((n, 23)), D_((4,)), D_((4,)), D_((len(FORWARD_OUT),)), D_((len(KINDS), 2))],
         compiler_params=pltpu.CompilerParams(collective_id=0, has_side_effects=True, vmem_limit_bytes=62 * 2**20),
     )(*args)
@@ -1120,22 +1122,22 @@
         for k in range(5): s.cp(k).wait_send()
 
 BACK_IN = ("wa", "wb", "vl", "vs", "re", "rs", "at", "gt", "hi", "hs", "uc", "du", "om", "sh", "bs", "n2", "mi", "sp", "pr", "st", "pt", "tok", "cot")
-MX_PARTS = ((0, 384), (384, 384), (768, 384), (1152, 256), (1408, 256))
+MX_PARTS = ((0, 384), (384, 384), (768, 256), (1024, 256), (1280, 128), (1408, 256))
 BACKWARD_PLAN = (
-    800, 701, 702, 703, 704, 705, 706, 1, 801, 3, 802, 803, 5, 4, 101, 103, 2, 900, 104, 901, 105, 1000, 902, 102, 903, 203, 904, 905, 906,
-    205, 6, 1001, 1002, 201, 1003, 7, 1004, 701, 702, 703, 202, 106, 204, 801, 802, 803, 8, 301, 107, 901, 108, 902, 9, 305, 903, 109, 303,
-    1001, 304, 1002, 1003, 1004, 1005, 1006, 207, 0, 206, 302, 800, 1101, 10, 100, 208, 700, 209, 1102, 601, 1104, 110, 307, 1105, 11, 1103,
-    13, 12, 306, 111, 14, 602, 112, 1201, 1202, 308, 210, 1203, 1204, 211, 113, 309, 212, 114, 310, 1205, 1206, 406, 311, 900, 214, 312,
-    200, 409, 300, 603, 403, 407, 314, 401, 213, 410, 412, 503, 400, 404, 507, 411, 313, 402, 414, 408, 405, 509, 500, 504, 604, 512, 514,
-    502, 413, 506, 605, 511, 510, 508, 501, 600, 505, 513,
+    800, 701, 702, 703, 704, 705, 706, 3, 801, 1, 802, 803, 103, 2, 4, 5, 101, 900, 901, 102, 104, 902, 903, 904, 905, 906, 1001, 1002, 6,
+    7, 105, 1003, 1000, 1004, 701, 106, 702, 201, 703, 204, 901, 902, 107, 903, 800, 205, 301, 1102, 11, 304, 203, 1103, 12, 202, 1001, 111,
+    1002, 206, 305, 1003, 112, 1004, 303, 1005, 1006, 302, 0, 207, 700, 801, 802, 803, 211, 8, 601, 9, 212, 100, 1101, 10, 108, 602, 109,
+    1104, 306, 110, 307, 603, 1106, 13, 1105, 1201, 209, 113, 14, 1202, 312, 208, 311, 1203, 1204, 15, 114, 604, 210, 309, 1205, 308, 115,
+    1206, 213, 402, 900, 200, 310, 403, 215, 214, 300, 404, 313, 412, 409, 314, 406, 503, 410, 315, 401, 411, 502, 405, 407, 512, 504, 400,
+    605, 506, 408, 507, 413, 415, 414, 510, 500, 509, 513, 515, 508, 505, 511, 514, 501, 600,
 )
-CUT = 37
+CUT = 34
 
 def backward_kernel(lens, qk, sq, *refs):
     ni = len(BACK_IN)
     I = dict(zip(BACK_IN, refs[:ni]))
     (o_mx, o_va, o_up, o_wo, o_wd, o_gt, o_tiny, o_red) = refs[ni:ni + 8]
-    (WA, WB, L1A, L1B, L2A, L2B, L3A, L3B, L4A, L4B, FA, FB, GA, GB_, TOK, PT, U, X0, X1, GT, GG, G1, H, KS, AT, ACC, E, L, Zb,
+    (WA, WB, L1A, L1B, L2A, L2B, L3A, L3B, L4A, L4B, FA, FB, FSA, FSB, GA, GB_, TOK, PT, U, X0, X1, GT, GG, G1, H, KS, AT, ACC, E, L, Zb,
      T, TL1, TL2, TL4, TG, TP, RR, RL, P6, GMX, Q0, Q1, Q2, SHT, SP, valid, affine, ss, rs, sx, rx, st_, rt_, sr, rr_, li, lo, lw) = refs[ni + 8:]
     p = Pos()
     sem = {name: i for i, name in enumerate(BACK_IN)}
@@ -1156,7 +1158,7 @@
         for o, lo_, hi_, step in outs:
             a, e = max(off, lo_), min(off + w, hi_)
             if a < e: o[:, pl.ds(a - lo_ + half * step, e - a)] = get(a - off, e - a)
-    g = Scatter(p, (WA, WB), (L1A, L1B), (L2A, L2B), (L3A, L3B), (L4A, L4B), (FA, FB), (GA, GB_), put, ss, rs)
+    g = Scatter(p, (WA, WB), (L1A, L1B), (L2A, L2B), (L3A, L3B), (L4A, L4B), (FA, FB), (FSA, FSB), (GA, GB_), put, ss, rs)
     tot = Total(p, RR, RL, sr, rr_)
     sc = Scan(p, -1, PT, E, L, Zb, sx, rx)
     tiny = Tiny(p, T, TL1, TL2, TL4, o_tiny, TG, st_, rt_)
@@ -1176,8 +1178,7 @@
     alone = (sc.sc0, sc.sc1, tiny.st0, tiny.a0, ti2, tiny.fin, tiny.last, to0)
     many = g.steps() + (tot.step,)
     def first(P0, P1, P2, P3, P4, P5, Q3, Q4, PR):
-        load("cot", Q4); part(4); load("hs", P0); load("hi", P1); part(2); load("n2", Q1); load("mi", X0); load("uc", Q2); load("du", Q3); load("pt", PT)
-        part(3); load("gt", P3); load("rs", P4); load("vl", P5); load("vs", P6); load("sp", SP); load("pr", PR); part(1); load("tok", TOK); part(0)
+        load("cot", Q4); part(4); load("hs", P0); load("hi", P1)
         full_barrier(p)
         row_masks(lens, valid, p)
         affine[0:3, :] = qk[...].astype(f32)
@@ -1188,6 +1189,8 @@
             def rows(i): Q0[ds(i, 64), :] = (Q4[ds(i, 64), :].astype(f32) * valid[ds(i, 64), :]).astype(bf16)
             loop(8, rows)
             part_ready(4); ready(("hs", P0), ("hi", P1))
+            part(2); load("n2", Q1); load("mi", X0); load("uc", Q2); load("du", Q3); load("pt", PT)
+            load("gt", P3); load("rs", P4); part(3)
         def hi(m):
             c = pl.ds(m * 256, 256)
             ACC[...] = dot_nt(Q0[...], pair(WB, c, DWL, DWL, HB))
@@ -1197,7 +1200,9 @@
                 r = ds(i, 64)
                 P2[r, c] = (ACC[r, :] * P0[r, c].astype(f32)).astype(bf16)
             loop(8, rows)
-            if m == 5: load("at", P0); load("re", P1)
+            if m == 5:
+                load("at", P0); load("re", P1)
+                load("vl", P5); load("vs", P6); load("sp", SP); load("pr", PR); load("tok", TOK); part(1)
         def ub(m):
             if m == 0: part_ready(2); ready(("n2", Q1))
             c = pl.ds(m * 256, 256)
@@ -1221,6 +1226,7 @@
                 GT[r, :] = gm * Q1[r, :].astype(f32)
             loop(8, rows)
             load("bs", Q1)
+            part(0)
         def ga(m):
             if m == 0: part_ready(3); ready(("gt", P3), ("at", P0), ("re", P1), ("rs", P4))
             c = pl.ds(m * 256, 256)
@@ -1371,7 +1377,7 @@
 def per_device_tuned(tokens, cotangent, lengths, w_mx, w_value, w_out, w_up, w_down, ema_rate, ema_in, ema_out, gains, qk_affine):
     tok = tokens.reshape(512, D)
     rate_t, in_t, out_t, gain_t = ema_rate.T, ema_in.T, ema_out.T, gains.T
-    kept = forward_call(lengths, tok, qk_affine, rate_t, in_t, out_t, gain_t, w_mx, w_value, w_out, w_up, w_down)
+    kept = forward_call(lengths, qk_affine, rate_t, in_t, out_t, gain_t, w_value, w_mx, w_up, w_out, w_down, tok)
     K = {name: t for (name, _, _), t in zip(FORWARD_OUT, kept)}
     K["tok"], K["cot"], K["mi"] = tok, cotangent.reshape(512, D), K["mi"].reshape(64, 8, 768)
     g_mx, g_va, g_up, g_wo, g_wd, g_tok, tiny, red = backward_call(lengths, qk_affine, K["sq"], [K[name] for name in BACK_IN])

time: 197 us -> 184 us (0.934)
  Pallas kernels: 193 us -> 179 us
    pallas_call x1, Pallas kernels: 95.8 us -> 85 us  [forward_call(): pl.pallas_call(forward_kernel, out_shape=tuple((jax.ShapeDtypeStruct(s, t...]
    pallas_call x1, Pallas kernels: 92.6 us -> 89.7 us  [backward_call(): pl.pallas_call(backward_kernel, out_shape=(sds((24, 3200), f32), sds((24,...]
where the time goes in v7:
time: 184 us; the launch traced here: 180 us
  Pallas kernels  179 us (97%)
    pallas_call x1, Pallas kernels, backward_call(): pl.pallas_call(backward_kernel, out_shape=(sds((24, 3200), f32), sds((24,...  89.7 us
    pallas_call x1, Pallas kernels, forward_call(): pl.pallas_call(forward_kernel, out_shape=tuple((jax.ShapeDtypeStruct(s, t...  85 us
    pallas_call x1, Pallas kernels, last_call(): pl.pallas_call(last_kernel, out_shape=tuple((sds(a.shape, a.dtype) for a...  4.59 us

profile of v7, /device:TPU:0, one launch (start us, length us, event | category | flops | bytes accessed | tf_op | source)
XLA Modules:
  0.0 180.2 jit_solution(1072116810942964037)
XLA Ops:
  0.6 85.0 %shard_map.228 = (bf16[768,6400]{1,0:T(8,128)(2,1)}, bf16[1536,1536]{1,0:T(8,128)(2,1)}, bf16[512,1536]{1,0:T(8,128)(2,1)}, bf16[512,1536]{1,0:T(8,128)(2,1)}, b...) custom-call(s32[2]{0:T(128)} %lens.3, ...), custom_call_target="tpu_custom_call" | custom-call | tf_op jit(solution)/shard_map/pallas_call | solution.py:1052
  85.7 89.7 %shard_map.229 = (f32[24,3200]{1,0:T(8,128)}, f32[24,1536]{1,0:T(8,128)}, f32[24,1536]{1,0:T(8,128)}, f32[48,768]{1,0:T(8,128)}, f32[48,768]{1,0:T(8,128)}, /*in...) custom-call(s32[2]{0:T(128)} %lens.3, bf16[3,128]{1,0:T(4,128)(2,1)} %qk.3, f32[24,768]{1,0:T(8,128)} %get-tuple-element.58.sq, ...), custom_call_target="tpu_custom_call" | custom-call | tf_op jit(solution)/shard_map/pallas_call | solution.py:1332
  175.4 4.6 %shard_map.230 = (bf16[512,768]{1,0:T(8,128)(2,1)}, f32[512,768]{1,0:T(8,128)}, f32[24,3200]{1,0:T(8,128)}, f32[24,1536]{1,0:T(8,128)}, f32[48,768]{1,0:T(8,128)...) custom-call(bf16[512,768]{1,0:T(8,128)(2,1)} %get-tuple-element.57.r, ...), custom_call_target="tpu_custom_call" | custom-call | tf_op jit(solution)/shard_map/pallas_call | solution.py:1369

commit v8 on v7

--- a/solution.py
+++ b/solution.py
@@ -391,10 +391,11 @@
 def rcopy(src, dst, ss, rs, dev):
     return pltpu.make_async_remote_copy(src_ref=src, dst_ref=dst, send_sem=ss, recv_sem=rs, device_id=dev, device_id_type=MESH)
 
-def full_barrier(p, *more):
+def full_barrier(p, *more, between=lambda: None):
     bar = pltpu.get_barrier_semaphore()
-    sig = lambda d: pl.semaphore_signal(bar, inc=1, device_id=d, device_id_type=MESH)
-    for d in (p.sib, p.xn, p.yn, p.zn(1), p.zn(2), p.zn(3)) + more: sig(d)
+    for d in (p.sib, p.xn, p.yn, p.zn(1), p.zn(2), p.zn(3)) + more:
+        pl.semaphore_signal(bar, inc=1, device_id=d, device_id_type=MESH)
+    between()
     pl.semaphore_wait(bar, 6 + len(more))
 
 def at(ref, rows, nrows, half, w, off, width):
@@ -915,11 +916,12 @@
         prm[...] = PT[:, 0:128].T[0:24, :]
     near = [pltpu.make_async_copy(a, b, si.at[k]) for k, (a, b) in enumerate(zip(far, (va, mx, wu, wo, wd, tok)))]
     for cp in near: cp.start()
-    small()
-    full_barrier(p, *((p.dp, p.zof(d) * 2 + 1 - p.y) for d in (1, 2, 3)))
-    for cp in near: cp.wait()
-    row_masks(lens, valid, p)
-    affine[0:3, :] = qk[...].astype(f32)
+    def between():
+        small()
+        row_masks(lens, valid, p)
+        affine[0:3, :] = qk[...].astype(f32)
+        for cp in near: cp.wait()
+    full_barrier(p, *((p.dp, p.zof(d) * 2 + 1 - p.y) for d in (1, 2, 3)), between=between)
     par = Params(p, prm, PRM, sp_, rp_)
     hv = Halves(p, mx, va, wo, wu, wd, WA, WB, land, s0, r0)
     g = Gather(p, (WA, WB), ss, rs)
@@ -1179,15 +1181,16 @@
     many = g.steps() + (tot.step,)
     def first(P0, P1, P2, P3, P4, P5, Q3, Q4, PR):
         load("cot", Q4); part(4); load("hs", P0); load("hi", P1)
-        full_barrier(p)
-        row_masks(lens, valid, p)
-        affine[0:3, :] = qk[...].astype(f32)
-        def lo_():
+        def between():
+            row_masks(lens, valid, p)
+            affine[0:3, :] = qk[...].astype(f32)
             GG[...] = jnp.zeros_like(GG)
             RR[0] = jnp.zeros((8, 128), f32)
             ready(("cot", Q4))
             def rows(i): Q0[ds(i, 64), :] = (Q4[ds(i, 64), :].astype(f32) * valid[ds(i, 64), :]).astype(bf16)
             loop(8, rows)
+        full_barrier(p, between=between)
+        def lo_():
             part_ready(4); ready(("hs", P0), ("hi", P1))
             part(2); load("n2", Q1); load("mi", X0); load("uc", Q2); load("du", Q3); load("pt", PT)
             load("gt", P3); load("rs", P4); part(3)
@@ -1344,8 +1347,10 @@
 
 def last_kernel(res, gtok, mx, va, wo, wu, wd, tiny, red, rate_t, in_t, out_t, o_res, o_gtok, o_mx, o_va, o_wo, o_wu, o_wd, o_rate, o_in, o_out, o_gain, o_qk, o_rms, *rest):
     mid, ss = rest[:7], rest[7]
-    into = [pltpu.make_async_copy(a, m, ss.at[0, k]) for k, (a, m) in enumerate(zip((res, gtok, mx, va, wo, wu, wd), mid))]
-    big = [pltpu.make_async_copy(m, o, ss.at[1, k]) for k, (m, o) in enumerate(zip(mid, (o_res, o_gtok, o_mx, o_va, o_wo, o_wu, o_wd)))]
+    pieces = [(a, m, o, r, a.shape[0] // n) for a, m, o, n in zip((gtok, res, mx, va, wo, wu, wd), mid, (o_gtok, o_res, o_mx, o_va, o_wo, o_wu, o_wd), (4, 2, 1, 1, 1, 1, 1)) for r in range(n)]
+    part = lambda ref, r, n: ref.at[pl.ds(r * n, n), :]
+    into = [pltpu.make_async_copy(part(a, r, n), part(m, r, n), ss.at[0, k]) for k, (a, m, o, r, n) in enumerate(pieces)]
+    big = [pltpu.make_async_copy(part(m, r, n), part(o, r, n), ss.at[1, k]) for k, (a, m, o, r, n) in enumerate(pieces)]
     for cp in into: cp.start()
     for a, b in zip(into, big):
         a.wait()
@@ -1370,7 +1375,7 @@
         out_shape=tuple(sds(a.shape, a.dtype) for a in args[:7]) + (sds((16, 24), f32),) * 3 + (sds((3, 24), f32), sds((3, 128), f32), sds((1, 3), f32)),
         in_specs=[any_] * 7 + [vm_] * 5,
         out_specs=[any_] * 7 + [vm_] * 6,
-        scratch_shapes=[pltpu.VMEM(a.shape, a.dtype) for a in args[:7]] + [pltpu.SemaphoreType.DMA((2, 7))],
+        scratch_shapes=[pltpu.VMEM(args[k].shape, args[k].dtype) for k in (1, 0, 2, 3, 4, 5, 6)] + [pltpu.SemaphoreType.DMA((2, 11))],
         compiler_params=pltpu.CompilerParams(vmem_limit_bytes=63 * 2**20))(*args)
 
 

time: 184 us -> 183 us (level)
  no operation moved by 1% of the time
where the time goes in v8:
time: 183 us; the launch traced here: 180 us
  Pallas kernels  179 us (98%)
    pallas_call x1, Pallas kernels, backward_call(): pl.pallas_call(backward_kernel, out_shape=(sds((24, 3200), f32), sds((24,...  89.7 us
    pallas_call x1, Pallas kernels, forward_call(): pl.pallas_call(forward_kernel, out_shape=tuple((jax.ShapeDtypeStruct(s, t...  85 us
    pallas_call x1, Pallas kernels, last_call(): pl.pallas_call(last_kernel, out_shape=tuple((sds(a.shape, a.dtype) for a...  4.26 us

profile of v8, /device:TPU:0, one launch (start us, length us, event | category | flops | bytes accessed | tf_op | source)
XLA Modules:
  0.0 179.9 jit_solution(6519886351953660161)
XLA Ops:
  0.6 85.0 %shard_map.228 = (bf16[768,6400]{1,0:T(8,128)(2,1)}, bf16[1536,1536]{1,0:T(8,128)(2,1)}, bf16[512,1536]{1,0:T(8,128)(2,1)}, bf16[512,1536]{1,0:T(8,128)(2,1)}, b...) custom-call(s32[2]{0:T(128)} %lens.3, ...), custom_call_target="tpu_custom_call" | custom-call | tf_op jit(solution)/shard_map/pallas_call | solution.py:1054
  85.6 89.7 %shard_map.229 = (f32[24,3200]{1,0:T(8,128)}, f32[24,1536]{1,0:T(8,128)}, f32[24,1536]{1,0:T(8,128)}, f32[48,768]{1,0:T(8,128)}, f32[48,768]{1,0:T(8,128)}, /*in...) custom-call(s32[2]{0:T(128)} %lens.3, bf16[3,128]{1,0:T(4,128)(2,1)} %qk.3, f32[24,768]{1,0:T(8,128)} %get-tuple-element.58.sq, ...), custom_call_target="tpu_custom_call" | custom-call | tf_op jit(solution)/shard_map/pallas_call | solution.py:1335
  175.4 4.3 %shard_map.230 = (bf16[512,768]{1,0:T(8,128)(2,1)}, f32[512,768]{1,0:T(8,128)}, f32[24,3200]{1,0:T(8,128)}, f32[24,1536]{1,0:T(8,128)}, f32[48,768]{1,0:T(8,128)...) custom-call(bf16[512,768]{1,0:T(8,128)(2,1)} %get-tuple-element.57.r, ...), custom_call_target="tpu_custom_call" | custom-call | tf_op jit(solution)/shard_map/pallas_call | solution.py:1374
